TPU v7x, 32 devices: a whole 2x2x4 slice. The times are simulated.
32 devices in a mesh: groups: 2 (over y), ep: 8 (over z, x), tp: 2 (over core).
Axes of the slice: x: 2, y: 2, z: 4, core: 2. Of those that a mesh axis runs over, the one named last changes fastest.
Arguments:
- tokens: bfloat16 [1024, 3584], P(('groups', 'ep'), 'tp'), parts along dimension 0, may hold values from -6 to 6
- expert_ids: int32 [1024, 1], P(('groups', 'ep')), parts along dimension 0, may hold values from 0 to 1; in each aligned block of 64 rows (0 to 63, 64 to 127, ...) at most 64 rows name the same one
- gate_fixed: int32 [1024, 1], P(('groups', 'ep')), parts along dimension 0, may hold values from 256 to 4095
- w_gate: bfloat16 [8, 3584, 256], P('ep', None, 'tp'), may hold values from -0.09375 to 0.09375
- w_up: bfloat16 [8, 3584, 256], P('ep', None, 'tp'), may hold values from -0.09375 to 0.09375
- w_down: bfloat16 [8, 256, 3584], P('ep', 'tp'), may hold values from -0.1875 to 0.1875
Outputs:
- mixed: bfloat16 [1024, 3584], P(('groups', 'ep'), 'tp'), parts along dimension 0
There are 2 independent parts, one for each index of `groups`. A program takes and returns all parts, laid end to end along the dimension named above; an argument that names none is the same for every part. Nothing has to cross between parts.
Inputs may be any that keep to these rules, and one draw needn't show every extreme that they name: `expert_ids`: in each aligned block of 64 tokens no expert is named by more than 64 routes, and in some blocks one is named by exactly 64; a token's ids differ. `gate_fixed`: gate weight times 2048.
All inputs are finite; a program needn't handle non-finite values.
Results may differ from a plain program's by a relative error of at most 0.0066.
Values may be sent and summed in bfloat16 or wider, within the bound.
No kernel may reach another device: no remote copies, remote signals or barrier semaphores. Data moves between devices by JAX's collectives and lax.ppermute only.
A program may use at most 64 MiB of HBM per device.

v0:
```python
import jax
import jax.numpy as jnp
from jax import lax
from jax.sharding import PartitionSpec as P

ESPLIT = 4


def earlier_ranks(labels):
    position = jnp.arange(labels.shape[0])
    matches = (labels[:, None] == labels[None, :]) & (position[:, None] < position[None, :])
    return jnp.sum(matches, axis=0)


def body(tokens, expert_ids, gate_fixed, w_gate, w_up, w_down):
    ep_count = lax.axis_size("ep")
    tok_dev, topk = expert_ids.shape
    experts = ep_count // ESPLIT
    capacity = max(2, min(tok_dev, 2 * tok_dev * topk // experts))
    flat_ids = expert_ids.reshape(-1)
    slot_index = flat_ids * capacity + earlier_ranks(flat_ids)
    chooser = (slot_index[None, :] == jnp.arange(experts * capacity)[:, None]).astype(jnp.bfloat16)
    whole = lax.all_gather(tokens, "tp", axis=1, tiled=True)
    width = whole.shape[1]
    routed_rows = jnp.repeat(whole, topk, axis=0)
    grouped = jnp.dot(chooser, routed_rows, preferred_element_type=jnp.float32).astype(jnp.bfloat16)
    grouped = grouped.reshape(experts, 1, capacity, width)
    copies = jnp.broadcast_to(grouped, (experts, ESPLIT, capacity, width))
    arrived = lax.all_to_all(
        copies.reshape(ep_count, capacity, width), "ep", split_axis=0, concat_axis=0, tiled=True
    )
    expert_rows = arrived.reshape(ep_count * capacity, arrived.shape[2])
    gate_act = jnp.dot(expert_rows, w_gate[0], preferred_element_type=jnp.float32)
    up_act = jnp.dot(expert_rows, w_up[0], preferred_element_type=jnp.float32)
    hidden = (jax.nn.silu(gate_act) * up_act).astype(jnp.bfloat16)
    partial_out = jnp.dot(hidden, w_down[0], preferred_element_type=jnp.float32).astype(
        jnp.bfloat16
    )
    summed = (
        lax.psum_scatter(partial_out, "tp", scatter_dimension=1, tiled=True)
        .astype(jnp.float32)
        .astype(jnp.bfloat16)
    )
    returned = lax.all_to_all(
        summed.reshape(ep_count, capacity, summed.shape[1]),
        "ep",
        split_axis=0,
        concat_axis=0,
        tiled=True,
    )
    quarters = jnp.sum(
        returned.reshape(experts, ESPLIT, capacity, returned.shape[2]).astype(jnp.float32), axis=1
    )
    quarters = quarters.reshape(experts * capacity, returned.shape[2])
    weights_route = gate_fixed.reshape(-1).astype(jnp.float32) / 2048.0
    routed = quarters[slot_index] * weights_route[:, None]
    return jnp.sum(routed.reshape(tok_dev, topk, routed.shape[1]), axis=1).astype(jnp.bfloat16)


def solution(mesh):
    placed = (
        P(("groups", "ep"), "tp"),
        P(("groups", "ep"), None),
        P(("groups", "ep"), None),
        P("ep", None, "tp"),
        P("ep", None, "tp"),
        P("ep", "tp", None),
    )
    return jax.shard_map(
        body, mesh=mesh, in_specs=placed, out_specs=P(("groups", "ep"), "tp"), check_vma=False
    )
```

profile of v0, /device:TPU:0, one launch (start us, length us, event | category | flops | bytes accessed | tf_op | source)
XLA Modules:
  0.0 181.2 jit_solution(5763716614983102959)
XLA Ops:
  6.5 0.0 copy-start
  6.5 0.0 reduce-scatter.2.cloned.1.call-start
  6.5 0.8 convert_reduce_fusion.1
  7.4 0.7 multiply_add_fusion
  8.0 2.4 %all_gather.3 = bf16[64,3584]{1,0:T(8,128)(2,1)S(1)} all-gather(bf16[64,1792]{1,0:T(8,128)(2,1)} %param.6), channel_id=1, replica_groups=mesh['groups'=2,'ep'=8,'tp'=2] {'tp'}, dimensions={1}, use_global_device_ids=true | all-gather | bytes 688128 | tf_op jit(solution)/shard_map/all_gather | solution.py:23
  10.5 0.4 convolution_convert_fusion.1
  10.8 0.3 broadcast_in_dim.5
  11.2 0.0 copy-start.3
  11.2 89.3 %all_to_all.10 = bf16[8,64,3584]{2,1,0:T(8,128)(2,1)S(1)} all-to-all(bf16[8,64,3584]{2,1,0:T(8,128)(2,1)S(1)} %bitcast.34), channel_id=1, replica_groups=mesh['groups'=2,'ep'=8,'tp'=2] {'ep'}, dimensions={0} | all-to-all | bytes 7340032 | tf_op jit(solution)/shard_map/all_to_all | solution.py:29
  100.5 0.0 copy-start.1
  100.5 0.0 copy-start.2
  100.5 1.8 %copy-done.1 = bf16[8,64,3584]{2,1,0:T(8,128)(2,1)} copy-done((bf16[8,64,3584]{2,1,0:T(8,128)(2,1)}, bf16[8,64,3584]{2,1,0:T(8,128)(2,1)S(1)}, u32[]{:S(2)}) %copy-start.1) | copy-done | bytes 3670040
  102.3 0.0 copy-done.3
  102.3 1.1 fusion.4
  103.4 0.0 copy-done
  103.4 0.0 copy-done.2
  103.4 7.8 %convolution_convert_fusion = bf16[512,3584]{1,0:T(8,128)(2,1)} fusion(bf16[512,3584]{1,0:T(8,128)(2,1)} %bitcast.32, bf16[1,128,3584]{2,1,0:T(8,128)(2,1)S(1)} %copy-done, bf16[1,3584,128]{2,1,0:T(8,128)(2,1)S(1)} %copy-done.2, f32[512,128]{1,0:T(8,128)S(1)} %fusion.4), kind=kOutput, calls=%fused_computation.1 | convolution fusion | flops 941752320 | bytes 9437184 | tf_op jit(solution)/shard_map/dot_general | solution.py:36
  111.2 0.0 copy-start.4
  111.2 0.0 copy-start.5
  111.2 0.0 reduce-scatter.2.cloned.1.call-update
  111.2 10.8 %reduce-scatter.2.cloned.1.call-done = bf16[512,1792]{1,0:T(8,128)(2,1)} async-done(((bf16[512,3584]{1,0:T(8,128)(2,1)}), bf16[512,1792]{1,0:T(8,128)(2,1)}) %reduce-scatter.2.cloned.1.call-update) | async-done | bytes 1835024 | tf_op jit(solution)/shard_map/reduce_scatter | solution.py:40
  122.0 5.7 %all-to-all-start.1 = ((bf16[8,64,1792]{2,1,0:T(8,128)(2,1)}), bf16[8,64,1792]{2,1,0:T(8,128)(2,1)}, u32[]{:S(2)}, u32[]{:S(2)}) async-start(bf16[8,64,1792]{2,1,0:T(8,128)(2,1)} %bitcast.36), calls=%async_computation.2 | async-start | bytes 3670016 | tf_op jit(solution)/shard_map/all_to_all | solution.py:44
  127.8 0.0 copy-done.4
  127.8 0.0 copy-done.5
  127.8 43.2 %all-to-all-done.1 = bf16[8,64,1792]{2,1,0:T(8,128)(2,1)} async-done(((bf16[8,64,1792]{2,1,0:T(8,128)(2,1)}), bf16[8,64,1792]{2,1,0:T(8,128)(2,1)}, u32[]{:S(2)}, u32[]{:S(2)}) %all-to-all-start.1) | async-done | bytes 1835040 | tf_op jit(solution)/shard_map/all_to_all | solution.py:44
  171.0 1.8 %convert_reduce_fusion = f32[2,64,1792]{2,1,0:T(8,128)S(1)} fusion(bf16[8,64,1792]{2,1,0:T(8,128)(2,1)} %all-to-all-done.1), kind=kLoop, calls=%fused_computation.3 | loop fusion | flops 1605632 | bytes 2752512 | tf_op jit(solution)/shard_map/reduce_sum | solution.py:51
  172.8 0.8 gather_fusion
  173.6 0.8 multiply_convert_fusion
  (3 shorter events, 0.0 us)
Async XLA Ops:
  6.5 96.9 %copy-start = (bf16[1,128,3584]{2,1,0:T(8,128)(2,1)S(1)}, bf16[1,128,3584]{2,1,0:T(8,128)(2,1)}, u32[]{:S(2)}) copy-start(bf16[1,128,3584]{2,1,0:T(8,128)(2,1)} %param.11) | copy-start | bytes 2752516
  6.5 115.5 %reduce-scatter.2.cloned.1.call-start = ((), (), s32[]{:S(2)}) async-start(), calls=%async_computation.3 | async-start | bytes 5505024 | tf_op jit(solution)/shard_map/reduce_scatter | solution.py:40
  11.2 91.2 %copy-start.3 = (bf16[1,3584,128]{2,1,0:T(8,128)(2,1)S(1)}, bf16[1,3584,128]{2,1,0:T(8,128)(2,1)}, u32[]{:S(2)}) copy-start(bf16[1,3584,128]{2,1,0:T(8,128)(2,1)} %param.9) | copy-start | bytes 2752516
  100.5 1.8 %copy-start.1 = (bf16[8,64,3584]{2,1,0:T(8,128)(2,1)}, bf16[8,64,3584]{2,1,0:T(8,128)(2,1)S(1)}, u32[]{:S(2)}) copy-start(bf16[8,64,3584]{2,1,0:T(8,128)(2,1)S(1)} %all_to_all.10) | copy-start | bytes 11010052
  100.5 3.0 %copy-start.2 = (bf16[1,3584,128]{2,1,0:T(8,128)(2,1)S(1)}, bf16[1,3584,128]{2,1,0:T(8,128)(2,1)}, u32[]{:S(2)}) copy-start(bf16[1,3584,128]{2,1,0:T(8,128)(2,1)} %param.10) | copy-start | bytes 2752516
  111.2 16.6 %copy-start.4 = (s32[64,1]{0,1:T(1,128)S(1)}, s32[64,1]{0,1:T(1,128)}, u32[]{:S(2)}) copy-start(s32[64,1]{0,1:T(1,128)} %param.7) | copy-start | bytes 772
  111.2 16.6 %copy-start.5 = (s32[64,1]{0,1:T(1,128)S(1)}, s32[64,1]{0,1:T(1,128)}, u32[]{:S(2)}) copy-start(s32[64,1]{0,1:T(1,128)} %param.8) | copy-start | bytes 772
  122.0 49.0 %all-to-all-start.1 = ((bf16[8,64,1792]{2,1,0:T(8,128)(2,1)}), bf16[8,64,1792]{2,1,0:T(8,128)(2,1)}, u32[]{:S(2)}, u32[]{:S(2)}) async-start(bf16[8,64,1792]{2,1,0:T(8,128)(2,1)} %bitcast.36), calls=%async_computation.2 | async-start | bytes 3670016 | tf_op jit(solution)/shard_map/all_to_all | solution.py:44
Sparse Core Ops, SparseCore 0:
  111.4 10.6 reduce-scatter.1
where the time goes:
time: 182 us; the launch traced here: 181 us
  blocking collectives  91.7 us (50%)
  waiting for transfers between devices  54 us (30%)
  between operations  13.5 us (7%)
  matrix products  9.25 us (5%)
  starting transfers between devices  5.74 us (3%)
  other arithmetic  4.15 us (2%)
  local copies, waits for them, and re-layouts  2.92 us (2%)
    all_to_all x1, blocking collectives, body(): lax.all_to_all(copies.reshape(ep_count, capacity, width), 'ep', split_axi...  89.3 us
    all_to_all x1, waiting for transfers between devices, body(): lax.all_to_all(summed.reshape(ep_count, capacity, summed.shape[1]), 'ep',...  43.2 us
    reduce_scatter x1, waiting for transfers between devices, body(): lax.psum_scatter(partial_out, 'tp', scatter_dimension=1, tiled=True)  10.8 us
    dot_general x1, matrix products, body(): jnp.dot(hidden, w_down[0], preferred_element_type=jnp.float32)  7.76 us
    all_to_all x1, starting transfers between devices, body(): lax.all_to_all(summed.reshape(ep_count, capacity, summed.shape[1]), 'ep',...  5.74 us
  transfers between devices with their start and end apart: 2, of which 2 were waited for; matrix products, arithmetic and copies ran while one was open for 0% of the time, Pallas kernels for 0%

commit v1 on v0

--- a/solution.py
+++ b/solution.py
@@ -12,7 +12,67 @@
     return jnp.sum(matches, axis=0)
 
 
-def body(tokens, expert_ids, gate_fixed, w_gate, w_up, w_down):
+def swap(value, bit):
+    pairs = [(i, i ^ bit) for i in range(lax.axis_size("ep"))]
+    return lax.ppermute(value, "ep", pairs)
+
+
+def swap_core(value):
+    return lax.ppermute(value, "tp", [(0, 1), (1, 0)])
+
+
+def dense_body(tokens, expert_ids, gate_fixed, w_gate, w_up, w_down):
+    core = lax.axis_index("tp")
+    first = core == 0
+    half = tokens.shape[0] // 2
+    top, bottom = tokens[:half], tokens[half:]
+    mine = jnp.where(first, top, bottom)
+    theirs = swap_core(jnp.where(first, bottom, top))
+    block = jnp.concatenate(
+        [jnp.where(first, mine, theirs), jnp.where(first, theirs, mine)], axis=1
+    )
+    w_gate, w_up, w_down = w_gate[0], w_up[0], w_down[0]
+    weights = [(w_gate, w_up, w_down), (swap_core(w_gate), swap_core(w_up), swap_core(w_down))]
+
+    held = {0: block}
+    held[4] = swap(block, 4)
+    held[2] = swap(block, 2)
+    held[1] = swap(block, 1)
+    held[6] = swap(held[4], 2)
+    for m in (2, 4, 6):
+        held[m | 1] = swap(held[m], 1)
+
+    def expert(m):
+        rows = jnp.concatenate([held[m], held[m | 1]], axis=0)
+        out = None
+        for gate, up, down in weights:
+            gate_act = jnp.dot(rows, gate, preferred_element_type=jnp.float32)
+            up_act = jnp.dot(rows, up, preferred_element_type=jnp.float32)
+            hidden = (jax.nn.silu(gate_act) * up_act).astype(jnp.bfloat16)
+            part = jnp.dot(hidden, down, preferred_element_type=jnp.float32)
+            out = part if out is None else out + part
+        return out[:half], out[half:].astype(jnp.bfloat16)
+
+    pair = {}
+    for m in (6, 4, 2, 0):
+        own, sent = expert(m)
+        pair[m] = own + swap(sent, 1).astype(jnp.float32)
+    far = pair[4] + swap(pair[6].astype(jnp.bfloat16), 2).astype(jnp.float32)
+    near = pair[0] + swap(pair[2].astype(jnp.bfloat16), 2).astype(jnp.float32)
+    other = swap(far.astype(jnp.bfloat16), 4).astype(jnp.float32)
+
+    ids = lax.dynamic_slice_in_dim(expert_ids, core * half, half, 0)
+    scale = lax.dynamic_slice_in_dim(gate_fixed, core * half, half, 0).astype(jnp.float32) / 2048.0
+    here = lax.axis_index("ep") // ESPLIT
+    mixed = (jnp.where(ids == here, near, other) * scale).astype(jnp.bfloat16)
+    width = tokens.shape[1]
+    left, right = mixed[:, :width], mixed[:, width:]
+    keep = jnp.where(first, left, right)
+    got = swap_core(jnp.where(first, right, left))
+    return jnp.concatenate([jnp.where(first, keep, got), jnp.where(first, got, keep)], axis=0)
+
+
+def routed_body(tokens, expert_ids, gate_fixed, w_gate, w_up, w_down):
     ep_count = lax.axis_size("ep")
     tok_dev, topk = expert_ids.shape
     experts = ep_count // ESPLIT
@@ -57,6 +117,12 @@
     return jnp.sum(routed.reshape(tok_dev, topk, routed.shape[1]), axis=1).astype(jnp.bfloat16)
 
 
+def body(tokens, expert_ids, *rest):
+    experts = lax.axis_size("ep") // ESPLIT
+    dense = experts == 2 and expert_ids.shape[1] == 1
+    return (dense_body if dense else routed_body)(tokens, expert_ids, *rest)
+
+
 def solution(mesh):
     placed = (
         P(("groups", "ep"), "tp"),

time: 182 us -> 95.9 us (0.53)
  blocking collectives: 91.7 us -> 0 us
  waiting for transfers between devices: 54 us -> 24.8 us
  matrix products: 9.25 us -> 28.3 us
  starting transfers between devices: 5.74 us -> 20.9 us
  between operations: 13.5 us -> 0.29 us
  local copies, waits for them, and re-layouts: 2.92 us -> 15.4 us
    all_to_all x1 -> x0, blocking collectives: 89.3 us -> none  [body(): lax.all_to_all(copies.reshape(ep_count, capacity, width), 'ep', split_axi...]
    all_to_all x1 -> x0, waiting for transfers between devices: 43.2 us -> none  [body(): lax.all_to_all(summed.reshape(ep_count, capacity, summed.shape[1]), 'ep',...]
    ppermute x0 -> x19, waiting for transfers between devices: none -> 24.8 us  [the longest x14 22.5 us: swap(): return lax.ppermute(value, 'ep', pairs)]
    ppermute x0 -> x19, starting transfers between devices: none -> 20.9 us  [the longest x14 19.8 us: swap(): return lax.ppermute(value, 'ep', pairs)]
    dot_general x3 -> x16, matrix products: 9.25 us -> 28.3 us  [the longest x8 19.8 us: expert(): part = jnp.dot(hidden, down, preferred_element_type=jnp.float32)]
    reduce_scatter x1 -> x0, waiting for transfers between devices: 10.8 us -> none  [body(): lax.psum_scatter(partial_out, 'tp', scatter_dimension=1, tiled=True)]
    all_to_all x1 -> x0, starting transfers between devices: 5.74 us -> none  [body(): lax.all_to_all(summed.reshape(ep_count, capacity, summed.shape[1]), 'ep',...]
    slice x0 -> x4, local copies, waits for them, and re-layouts: none -> 4.81 us  [expert(): return (out[:half], out[half:].astype(jnp.bfloat16))]
  transfers between devices with their start and end apart: 2 -> 19, of which waited for: 2 -> 8; matrix products, arithmetic and copies ran while one was open for 0% -> 42% of each run, Pallas kernels for 0% -> 0%
where the time goes in v1:
time: 95.9 us; the launch traced here: 95 us
  matrix products  28.3 us (30%)
  waiting for transfers between devices  24.8 us (26%)
  starting transfers between devices  20.9 us (22%)
  local copies, waits for them, and re-layouts  15.4 us (16%)
  other arithmetic  5.32 us (6%)
    ppermute x14, waiting for transfers between devices, swap(): return lax.ppermute(value, 'ep', pairs)  22.5 us
    ppermute x14, starting transfers between devices, swap(): return lax.ppermute(value, 'ep', pairs)  19.8 us
    dot_general x8, matrix products, expert(): part = jnp.dot(hidden, down, preferred_element_type=jnp.float32)  19.8 us
    dot_general x7, matrix products, expert(): gate_act = jnp.dot(rows, gate, preferred_element_type=jnp.float32)  7.04 us
    unnamed x33, local copies, waits for them, and re-layouts  6.36 us
    slice x4, local copies, waits for them, and re-layouts, expert(): return (out[:half], out[half:].astype(jnp.bfloat16))  4.81 us
    concatenate x3, local copies, waits for them, and re-layouts, expert(): rows = jnp.concatenate([held[m], held[m | 1]], axis=0)  4.25 us
    ppermute x5, waiting for transfers between devices, swap_core(): return lax.ppermute(value, 'tp', [(0, 1), (1, 0)])  2.28 us
  transfers between devices with their start and end apart: 19, of which 8 were waited for; matrix products, arithmetic and copies ran while one was open for 42% of the time, Pallas kernels for 0%

profile of v1, /device:TPU:0, one launch (start us, length us, event | category | flops | bytes accessed | tf_op | source)
XLA Modules:
  0.0 95.0 jit_solution(14668333758939164048)
XLA Ops:
  2.6 3.0 %collective-permute-start.6 = (bf16[32,3584]{1,0:T(8,128)(2,1)S(1)}, bf16[32,3584]{1,0:T(8,128)(2,1)}, u32[]{:S(2)}, u32[]{:S(2)}) collective-permute-start(bf16[32,3584]{1,0:T(8,128)(2,1)S(1)} %pad_maximum_fusion.1), channel_id=1, source_target_pairs={{0,4},{2,6},{4,0},{6,2},{8,12},{10,14},{12,8},{14,10},{1,5},{3,7},... | collective-permute-start | bytes 688136 | tf_op jit(solution)/shard_map/ppermute | solution.py:17
  6.1 2.6 %collective-permute-start.10 = (bf16[32,3584]{1,0:T(8,128)(2,1)S(1)}, bf16[32,3584]{1,0:T(8,128)(2,1)}, u32[]{:S(2)}, u32[]{:S(2)}) collective-permute-start(bf16[32,3584]{1,0:T(8,128)(2,1)S(1)} %pad_maximum_fusion.1), channel_id=1, source_target_pairs={{0,8},{2,10},{4,12},{6,14},{8,0},{10,2},{12,4},{14,6},{1,9},{3,11}... | collective-permute-start | bytes 688136 | tf_op jit(solution)/shard_map/ppermute | solution.py:17
  8.7 6.6 %collective-permute-done.6 = bf16[32,3584]{1,0:T(8,128)(2,1)} collective-permute-done((bf16[32,3584]{1,0:T(8,128)(2,1)S(1)}, bf16[32,3584]{1,0:T(8,128)(2,1)}, u32[]{:S(2)}, u32[]{:S(2)}) %collective-permute-start.6) | collective-permute-done | bytes 229408 | tf_op jit(solution)/shard_map/ppermute | solution.py:17
  15.3 1.7 %collective-permute-start.1 = (bf16[32,3584]{1,0:T(8,128)(2,1)S(1)}, bf16[32,3584]{1,0:T(8,128)(2,1)S(1)}, u32[]{:S(2)}, u32[]{:S(2)}) collective-permute-start(bf16[32,3584]{1,0:T(8,128)(2,1)S(1)} %pad_maximum_fusion.1), channel_id=1, source_target_pairs={{0,2},{2,0},{4,6},{6,4},{8,10},{10,8},{12,14},{14,12},{1,3},{3,1},... | collective-permute-start | bytes 688136 | tf_op jit(solution)/shard_map/ppermute | solution.py:17
  16.9 1.6 %constant_dynamic-update-slice_fusion.1 = bf16[64,3584]{1,0:T(8,128)(2,1)} fusion(bf16[32,3584]{1,0:T(8,128)(2,1)} %collective-permute-done.6), kind=kLoop, calls=%fused_computation.52 | loop fusion | bytes 458752
  18.6 1.5 %collective-permute-done.10 = bf16[32,3584]{1,0:T(8,128)(2,1)} collective-permute-done((bf16[32,3584]{1,0:T(8,128)(2,1)S(1)}, bf16[32,3584]{1,0:T(8,128)(2,1)}, u32[]{:S(2)}, u32[]{:S(2)}) %collective-permute-start.10) | collective-permute-done | bytes 229408 | tf_op jit(solution)/shard_map/ppermute | solution.py:17
  20.1 1.5 %collective-permute-start.7 = (bf16[32,3584]{1,0:T(8,128)(2,1)}, bf16[32,3584]{1,0:T(8,128)(2,1)}, u32[]{:S(2)}, u32[]{:S(2)}) collective-permute-start(bf16[32,3584]{1,0:T(8,128)(2,1)} %collective-permute-done.6), channel_id=1, source_target_pairs={{0,2},{2,0},{4,6},{6,4},{8,10},{10,8},{12,14},{14,12},{1,3},{3,1},... | collective-permute-start | bytes 688136 | tf_op jit(solution)/shard_map/ppermute | solution.py:17
  23.8 2.4 %fusion.8 = f32[64,3584]{1,0:T(8,128)} fusion(f32[64,128]{1,0:T(8,128)S(1)} %fusion.54, bf16[1,128,3584]{2,1,0:T(8,128)(2,1)S(1)} %copy-done.1, bf16[1,3584,128]{2,1,0:T(8,128)(2,1)S(1)} %copy-done, bf16[32,3584]{1,0:T(8,128)(2,1)} %copy-done.10, bf16[32,1792]{1,0:T(8,128)(2,1)S(1)} %get-tuple-element.8, bf16[32,1792]{1,0:T(8,128)(2,1)S(1)} %get-tuple-element.7), kind=kOutput, calls=%fused_computation.39 | convolution fusion | flops 118865920 | bytes 3244032 | tf_op jit(solution)/shard_map/dot_general | solution.py:52
  26.2 1.4 %collective-permute-done.7 = bf16[32,3584]{1,0:T(8,128)(2,1)} collective-permute-done((bf16[32,3584]{1,0:T(8,128)(2,1)}, bf16[32,3584]{1,0:T(8,128)(2,1)}, u32[]{:S(2)}, u32[]{:S(2)}) %collective-permute-start.7) | collective-permute-done | bytes 229408 | tf_op jit(solution)/shard_map/ppermute | solution.py:17
  27.7 1.5 %collective-permute-start.11 = (bf16[32,3584]{1,0:T(8,128)(2,1)}, bf16[32,3584]{1,0:T(8,128)(2,1)}, u32[]{:S(2)}, u32[]{:S(2)}) collective-permute-start(bf16[32,3584]{1,0:T(8,128)(2,1)} %collective-permute-done.10), channel_id=1, source_target_pairs={{0,2},{2,0},{4,6},{6,4},{8,10},{10,8},{12,14},{14,12},{1,3},{3,1},... | collective-permute-start | bytes 688136 | tf_op jit(solution)/shard_map/ppermute | solution.py:17
  29.2 1.6 %constant_dynamic-update-slice_fusion = bf16[64,3584]{1,0:T(8,128)(2,1)} fusion(bf16[64,3584]{1,0:T(8,128)(2,1)} %constant_dynamic-update-slice_fusion.1, bf16[32,3584]{1,0:T(8,128)(2,1)} %collective-permute-done.7), kind=kLoop, calls=%fused_computation.51 | loop fusion | bytes 458752 | tf_op jit(solution)/shard_map/concatenate | solution.py:46
  30.8 1.6 %fusion.52 = f32[64,128]{1,0:T(8,128)S(1)} fusion(bf16[64,3584]{1,0:T(8,128)(2,1)} %constant_dynamic-update-slice_fusion, bf16[1,3584,128]{2,1,0:T(8,128)(2,1)} %param.9), kind=kOutput, calls=%fused_computation.75 | convolution fusion | flops 58720256 | bytes 1409024 | tf_op jit(solution)/shard_map/dot_general | solution.py:49
  32.4 2.5 %fusion.9 = f32[64,3584]{1,0:T(8,128)} fusion(f32[64,128]{1,0:T(8,128)S(1)} %fusion.52, bf16[1,128,3584]{2,1,0:T(8,128)(2,1)S(1)} %copy-done.1, bf16[64,3584]{1,0:T(8,128)(2,1)} %constant_dynamic-update-slice_fusion, bf16[1,3584,128]{2,1,0:T(8,128)(2,1)S(1)} %copy-done), kind=kOutput, calls=%fused_computation.40 | convolution fusion | flops 117489664 | bytes 3244032 | tf_op jit(solution)/shard_map/dot_general | solution.py:52
  35.9 1.5 %fusion.50 = f32[64,128]{1,0:T(8,128)S(1)} fusion(bf16[64,3584]{1,0:T(8,128)(2,1)S(1)} %constant_dynamic-update-slice_fusion.2, bf16[1,3584,128]{2,1,0:T(8,128)(2,1)} %param.9), kind=kOutput, calls=%fused_computation.73 | convolution fusion | flops 58720256 | bytes 1409024 | tf_op jit(solution)/shard_map/dot_general | solution.py:49
  37.4 1.6 %constant_dynamic-update-slice_fusion.5 = bf16[64,3584]{1,0:T(8,128)(2,1)} fusion(bf16[32,3584]{1,0:T(8,128)(2,1)} %collective-permute-done.13), kind=kLoop, calls=%fused_computation.56 | loop fusion | bytes 458752
  39.9 1.5 %fusion.10 = f32[64,3584]{1,0:T(8,128)} fusion(f32[64,128]{1,0:T(8,128)S(1)} %fusion.50, bf16[1,128,3584]{2,1,0:T(8,128)(2,1)S(1)} %copy-done.1, bf16[64,3584]{1,0:T(8,128)(2,1)S(1)} %constant_dynamic-update-slice_fusion.2, bf16[1,3584,128]{2,1,0:T(8,128)(2,1)S(1)} %copy-done), kind=kOutput, calls=%fused_computation.41 | convolution fusion | flops 117489664 | bytes 3244032 | tf_op jit(solution)/shard_map/dot_general | solution.py:52
  41.4 4.0 %collective-permute-done.14 = bf16[32,3584]{1,0:T(8,128)(2,1)} collective-permute-done((bf16[32,3584]{1,0:T(8,128)(2,1)}, bf16[32,3584]{1,0:T(8,128)(2,1)}, u32[]{:S(2)}, u32[]{:S(2)}) %collective-permute-start.14) | collective-permute-done | bytes 229408 | tf_op jit(solution)/shard_map/ppermute | solution.py:17
  45.4 1.6 %constant_dynamic-update-slice_fusion.4 = bf16[64,3584]{1,0:T(8,128)(2,1)} fusion(bf16[64,3584]{1,0:T(8,128)(2,1)} %constant_dynamic-update-slice_fusion.5, bf16[32,3584]{1,0:T(8,128)(2,1)} %collective-permute-done.14), kind=kLoop, calls=%fused_computation.55 | loop fusion | bytes 458752 | tf_op jit(solution)/shard_map/concatenate | solution.py:46
  47.1 1.6 %fusion.48 = f32[64,128]{1,0:T(8,128)S(1)} fusion(bf16[64,3584]{1,0:T(8,128)(2,1)} %constant_dynamic-update-slice_fusion.4, bf16[1,3584,128]{2,1,0:T(8,128)(2,1)} %param.9), kind=kOutput, calls=%fused_computation.71 | convolution fusion | flops 58720256 | bytes 1409024 | tf_op jit(solution)/shard_map/dot_general | solution.py:49
  48.7 2.5 %fusion.11 = f32[64,3584]{1,0:T(8,128)} fusion(f32[64,128]{1,0:T(8,128)S(1)} %fusion.48, bf16[1,128,3584]{2,1,0:T(8,128)(2,1)S(1)} %copy-done.1, bf16[64,3584]{1,0:T(8,128)(2,1)} %constant_dynamic-update-slice_fusion.4, bf16[1,3584,128]{2,1,0:T(8,128)(2,1)S(1)} %copy-done), kind=kOutput, calls=%fused_computation.42 | convolution fusion | flops 117489664 | bytes 3244032 | tf_op jit(solution)/shard_map/dot_general | solution.py:52
  51.2 1.4 %fusion.72 = f32[64,128]{1,0:T(8,128)S(1)} fusion(bf16[64,3584]{1,0:T(8,128)(2,1)} %constant_dynamic-update-slice_fusion, bf16[3584,128]{1,0:T(8,128)(2,1)S(1)} %collective-permute-done.2), kind=kOutput, calls=%fused_computation.92 | convolution fusion | flops 58720256 | bytes 1409024 | tf_op jit(solution)/shard_map/dot_general | solution.py:49
  52.6 3.2 %convolution_add_fusion.2 = f32[64,3584]{1,0:T(8,128)} fusion(f32[64,3584]{1,0:T(8,128)} %fusion.9, bf16[128,3584]{1,0:T(8,128)(2,1)} %collective-permute-done.4, f32[64,128]{1,0:T(8,128)S(1)} %fusion.72, bf16[64,3584]{1,0:T(8,128)(2,1)S(1)} %copy-done.2, bf16[3584,128]{1,0:T(8,128)(2,1)} %collective-permute-done.3), kind=kOutput, calls=%fused_computation.2 | convolution fusion | flops 117719040 | bytes 4161536 | tf_op jit(solution)/shard_map/dot_general | solution.py:52
  55.8 1.8 %slice.112 = bf16[32,3584]{1,0:T(8,128)(2,1)} slice(f32[64,3584]{1,0:T(8,128)} %convolution_add_fusion.2), slice={[32:64], [0:3584]} | slice | bytes 458752 | tf_op jit(solution)/shard_map/slice | solution.py:54
  58.9 3.0 %convolution_add_fusion = f32[64,3584]{1,0:T(8,128)} fusion(f32[64,3584]{1,0:T(8,128)S(1)} %copy-done.7, bf16[128,3584]{1,0:T(8,128)(2,1)} %collective-permute-done.4, f32[64,128]{1,0:T(8,128)S(1)} %fusion.74, bf16[64,3584]{1,0:T(8,128)(2,1)S(1)} %copy-done.3, bf16[3584,128]{1,0:T(8,128)(2,1)} %collective-permute-done.3), kind=kOutput, calls=%fused_computation | convolution fusion | flops 117719040 | bytes 4161536 | tf_op jit(solution)/shard_map/dot_general | solution.py:52
  61.8 1.8 %slice.110 = bf16[32,3584]{1,0:T(8,128)(2,1)} slice(f32[64,3584]{1,0:T(8,128)} %convolution_add_fusion), slice={[32:64], [0:3584]} | slice | bytes 458752 | tf_op jit(solution)/shard_map/slice | solution.py:54
  65.1 2.0 %convolution_add_fusion.1 = f32[64,3584]{1,0:T(8,128)S(1)} fusion(f32[64,3584]{1,0:T(8,128)S(1)} %copy-done.6, bf16[128,3584]{1,0:T(8,128)(2,1)} %collective-permute-done.4, f32[64,128]{1,0:T(8,128)S(1)} %fusion.73, bf16[64,3584]{1,0:T(8,128)(2,1)S(1)} %constant_dynamic-update-slice_fusion.2, bf16[3584,128]{1,0:T(8,128)(2,1)} %collective-permute-done.3), kind=kOutput, calls=%fused_computation.1 | convolution fusion | flops 117719040 | bytes 4161536 | tf_op jit(solution)/shard_map/dot_general | solution.py:52
  68.1 1.5 %fusion.64 = f32[64,128]{1,0:T(8,128)S(1)} fusion(bf16[3584,128]{1,0:T(8,128)(2,1)} %collective-permute-done.3, bf16[32,3584]{1,0:T(8,128)(2,1)S(1)} %copy-done.11, bf16[32,1792]{1,0:T(8,128)(2,1)S(1)} %get-tuple-element.8, bf16[32,1792]{1,0:T(8,128)(2,1)S(1)} %get-tuple-element.7), kind=kOutput, calls=%fused_computation.87 | convolution fusion | flops 60096512 | bytes 1409024 | tf_op jit(solution)/shard_map/dot_general | solution.py:50
  69.6 2.7 %convolution_add_fusion.3 = f32[64,3584]{1,0:T(8,128)} fusion(f32[64,3584]{1,0:T(8,128)S(1)} %copy-done.5, bf16[128,3584]{1,0:T(8,128)(2,1)} %collective-permute-done.4, f32[64,128]{1,0:T(8,128)S(1)} %fusion.64, bf16[3584,128]{1,0:T(8,128)(2,1)S(1)} %collective-permute-done.2, bf16[32,3584]{1,0:T(8,128)(2,1)S(1)} %copy-done.11, ...), kind=kOutput, calls=%fused_computation.3 | convolution fusion | flops 119095296 | bytes 4161536 | tf_op jit(solution)/shard_map/dot_general | solution.py:52
  77.0 2.0 %collective-permute-start.9 = (bf16[32,3584]{1,0:T(8,128)(2,1)S(1)}, bf16[32,3584]{1,0:T(8,128)(2,1)S(1)}, u32[]{:S(2)}, u32[]{:S(2)}) collective-permute-start(bf16[32,3584]{1,0:T(8,128)(2,1)S(1)} %fusion.3), channel_id=1, source_target_pairs={{0,4},{2,6},{4,0},{6,2},{8,12},{10,14},{12,8},{14,10},{1,5},{3,7},... | collective-permute-start | bytes 688136 | tf_op jit(solution)/shard_map/ppermute | solution.py:17
  79.0 3.4 %collective-permute-done.16 = bf16[32,3584]{1,0:T(8,128)(2,1)S(1)} collective-permute-done((bf16[32,3584]{1,0:T(8,128)(2,1)S(1)}, bf16[32,3584]{1,0:T(8,128)(2,1)S(1)}, u32[]{:S(2)}, u32[]{:S(2)}) %collective-permute-start.16) | collective-permute-done | bytes 229408 | tf_op jit(solution)/shard_map/ppermute | solution.py:17
  83.3 2.3 %collective-permute-start.17 = (bf16[32,3584]{1,0:T(8,128)(2,1)S(1)}, bf16[32,3584]{1,0:T(8,128)(2,1)S(1)}, u32[]{:S(2)}, u32[]{:S(2)}) collective-permute-start(bf16[32,3584]{1,0:T(8,128)(2,1)S(1)} %fusion.2), channel_id=1, source_target_pairs={{0,8},{2,10},{4,12},{6,14},{8,0},{10,2},{12,4},{14,6},{1,9},{3,11}... | collective-permute-start | bytes 688136 | tf_op jit(solution)/shard_map/ppermute | solution.py:17
  87.1 5.7 %collective-permute-done.17 = bf16[32,3584]{1,0:T(8,128)(2,1)S(1)} collective-permute-done((bf16[32,3584]{1,0:T(8,128)(2,1)S(1)}, bf16[32,3584]{1,0:T(8,128)(2,1)S(1)}, u32[]{:S(2)}, u32[]{:S(2)}) %collective-permute-start.17) | collective-permute-done | bytes 229408 | tf_op jit(solution)/shard_map/ppermute | solution.py:17
  (74 shorter events, 20.0 us)
Async XLA Ops:
  0.0 2.6 %copy-start.12 = (bf16[64,1792]{1,0:T(8,128)(2,1)S(1)}, bf16[64,1792]{1,0:T(8,128)(2,1)}, u32[]{:S(2)}) copy-start(bf16[64,1792]{1,0:T(8,128)(2,1)} %param.6) | copy-start | bytes 688132
  0.0 5.6 %copy-start = (bf16[1,3584,128]{2,1,0:T(8,128)(2,1)S(1)}, bf16[1,3584,128]{2,1,0:T(8,128)(2,1)}, u32[]{:S(2)}) copy-start(bf16[1,3584,128]{2,1,0:T(8,128)(2,1)} %param.10) | copy-start | bytes 2752516
  1.1 22.2 %copy-start.4 = (bf16[1,3584,128]{2,1,0:T(8,128)(2,1)S(1)}, bf16[1,3584,128]{2,1,0:T(8,128)(2,1)}, u32[]{:S(2)}) copy-start(bf16[1,3584,128]{2,1,0:T(8,128)(2,1)} %param.9) | copy-start | bytes 2752516
  1.1 1.5 %collective-permute-start = (bf16[32,1792]{1,0:T(8,128)(2,1)S(1)}, bf16[32,1792]{1,0:T(8,128)(2,1)S(1)}, u32[]{:S(2)}, u32[]{:S(2)}) collective-permute-start(bf16[32,1792]{1,0:T(8,128)(2,1)S(1)} %broadcast_select_fusion.6), channel_id=1, source_target_pairs={{0,1},{1,0},{2,3},{3,2},{4,5},{5,4},{6,7},{7,6},{8,9},{9,8},{10,11... | collective-permute-start | bytes 344072 | tf_op jit(solution)/shard_map/ppermute | solution.py:21
  2.6 12.7 %collective-permute-start.6 = (bf16[32,3584]{1,0:T(8,128)(2,1)S(1)}, bf16[32,3584]{1,0:T(8,128)(2,1)}, u32[]{:S(2)}, u32[]{:S(2)}) collective-permute-start(bf16[32,3584]{1,0:T(8,128)(2,1)S(1)} %pad_maximum_fusion.1), channel_id=1, source_target_pairs={{0,4},{2,6},{4,0},{6,2},{8,12},{10,14},{12,8},{14,10},{1,5},{3,7},... | collective-permute-start | bytes 688136 | tf_op jit(solution)/shard_map/ppermute | solution.py:17
  5.6 45.6 %collective-permute-start.2 = (bf16[3584,128]{1,0:T(8,128)(2,1)}, bf16[3584,128]{1,0:T(8,128)(2,1)S(1)}, u32[]{:S(2)}, u32[]{:S(2)}) collective-permute-start(bf16[3584,128]{1,0:T(8,128)(2,1)} %bitcast.73), channel_id=1, source_target_pairs={{0,1},{1,0},{2,3},{3,2},{4,5},{5,4},{6,7},{7,6},{8,9},{9,8},{10,11... | collective-permute-start | bytes 2752520 | tf_op jit(solution)/shard_map/ppermute | solution.py:21
  5.6 47.0 %collective-permute-start.3 = (bf16[3584,128]{1,0:T(8,128)(2,1)S(1)}, bf16[3584,128]{1,0:T(8,128)(2,1)}, u32[]{:S(2)}, u32[]{:S(2)}) collective-permute-start(bf16[3584,128]{1,0:T(8,128)(2,1)S(1)} %bitcast.71), channel_id=1, source_target_pairs={{0,1},{1,0},{2,3},{3,2},{4,5},{5,4},{6,7},{7,6},{8,9},{9,8},{10,11... | collective-permute-start | bytes 2752520 | tf_op jit(solution)/shard_map/ppermute | solution.py:21
  6.1 46.5 %collective-permute-start.4 = (bf16[128,3584]{1,0:T(8,128)(2,1)}, bf16[128,3584]{1,0:T(8,128)(2,1)}, u32[]{:S(2)}, u32[]{:S(2)}) collective-permute-start(bf16[128,3584]{1,0:T(8,128)(2,1)} %bitcast.72), channel_id=1, source_target_pairs={{0,1},{1,0},{2,3},{3,2},{4,5},{5,4},{6,7},{7,6},{8,9},{9,8},{10,11... | collective-permute-start | bytes 2752520 | tf_op jit(solution)/shard_map/ppermute | solution.py:21
  6.1 14.0 %collective-permute-start.10 = (bf16[32,3584]{1,0:T(8,128)(2,1)S(1)}, bf16[32,3584]{1,0:T(8,128)(2,1)}, u32[]{:S(2)}, u32[]{:S(2)}) collective-permute-start(bf16[32,3584]{1,0:T(8,128)(2,1)S(1)} %pad_maximum_fusion.1), channel_id=1, source_target_pairs={{0,8},{2,10},{4,12},{6,14},{8,0},{10,2},{12,4},{14,6},{1,9},{3,11}... | collective-permute-start | bytes 688136 | tf_op jit(solution)/shard_map/ppermute | solution.py:17
  15.3 7.3 %collective-permute-start.1 = (bf16[32,3584]{1,0:T(8,128)(2,1)S(1)}, bf16[32,3584]{1,0:T(8,128)(2,1)S(1)}, u32[]{:S(2)}, u32[]{:S(2)}) collective-permute-start(bf16[32,3584]{1,0:T(8,128)(2,1)S(1)} %pad_maximum_fusion.1), channel_id=1, source_target_pairs={{0,2},{2,0},{4,6},{6,4},{8,10},{10,8},{12,14},{14,12},{1,3},{3,1},... | collective-permute-start | bytes 688136 | tf_op jit(solution)/shard_map/ppermute | solution.py:17
  20.1 7.6 %collective-permute-start.7 = (bf16[32,3584]{1,0:T(8,128)(2,1)}, bf16[32,3584]{1,0:T(8,128)(2,1)}, u32[]{:S(2)}, u32[]{:S(2)}) collective-permute-start(bf16[32,3584]{1,0:T(8,128)(2,1)} %collective-permute-done.6), channel_id=1, source_target_pairs={{0,2},{2,0},{4,6},{6,4},{8,10},{10,8},{12,14},{14,12},{1,3},{3,1},... | collective-permute-start | bytes 688136 | tf_op jit(solution)/shard_map/ppermute | solution.py:17
  22.6 1.3 %copy-start.1 = (bf16[1,128,3584]{2,1,0:T(8,128)(2,1)S(1)}, bf16[1,128,3584]{2,1,0:T(8,128)(2,1)}, u32[]{:S(2)}) copy-start(bf16[1,128,3584]{2,1,0:T(8,128)(2,1)} %param.11) | copy-start | bytes 2752516
  22.6 0.7 copy-start.10
  22.6 14.8 %collective-permute-start.13 = (bf16[32,3584]{1,0:T(8,128)(2,1)}, bf16[32,3584]{1,0:T(8,128)(2,1)}, u32[]{:S(2)}, u32[]{:S(2)}) collective-permute-start(bf16[32,3584]{1,0:T(8,128)(2,1)} %collective-permute-done.10), channel_id=1, source_target_pairs={{0,4},{2,6},{4,0},{6,2},{8,12},{10,14},{12,8},{14,10},{1,5},{3,7},... | collective-permute-start | bytes 688136 | tf_op jit(solution)/shard_map/ppermute | solution.py:17
  27.7 7.3 %collective-permute-start.11 = (bf16[32,3584]{1,0:T(8,128)(2,1)}, bf16[32,3584]{1,0:T(8,128)(2,1)}, u32[]{:S(2)}, u32[]{:S(2)}) collective-permute-start(bf16[32,3584]{1,0:T(8,128)(2,1)} %collective-permute-done.10), channel_id=1, source_target_pairs={{0,2},{2,0},{4,6},{6,4},{8,10},{10,8},{12,14},{14,12},{1,3},{3,1},... | collective-permute-start | bytes 688136 | tf_op jit(solution)/shard_map/ppermute | solution.py:17
  39.0 6.4 %collective-permute-start.14 = (bf16[32,3584]{1,0:T(8,128)(2,1)}, bf16[32,3584]{1,0:T(8,128)(2,1)}, u32[]{:S(2)}, u32[]{:S(2)}) collective-permute-start(bf16[32,3584]{1,0:T(8,128)(2,1)} %collective-permute-done.13), channel_id=1, source_target_pairs={{0,2},{2,0},{4,6},{6,4},{8,10},{10,8},{12,14},{14,12},{1,3},{3,1},... | collective-permute-start | bytes 688136 | tf_op jit(solution)/shard_map/ppermute | solution.py:17
  51.2 1.4 %copy-start.2 = (bf16[64,3584]{1,0:T(8,128)(2,1)S(1)}, bf16[64,3584]{1,0:T(8,128)(2,1)}, u32[]{:S(2)}) copy-start(bf16[64,3584]{1,0:T(8,128)(2,1)} %constant_dynamic-update-slice_fusion) | copy-start | bytes 1376260
  55.8 2.7 %copy-start.3 = (bf16[64,3584]{1,0:T(8,128)(2,1)S(1)}, bf16[64,3584]{1,0:T(8,128)(2,1)}, u32[]{:S(2)}) copy-start(bf16[64,3584]{1,0:T(8,128)(2,1)} %constant_dynamic-update-slice_fusion.4) | copy-start | bytes 1376260
  55.8 3.0 %copy-start.7 = (f32[64,3584]{1,0:T(8,128)S(1)}, f32[64,3584]{1,0:T(8,128)}, u32[]{:S(2)}) copy-start(f32[64,3584]{1,0:T(8,128)} %fusion.11) | copy-start | bytes 2752516
  57.7 18.2 %collective-permute-start.8 = (bf16[32,3584]{1,0:T(8,128)(2,1)}, bf16[32,3584]{1,0:T(8,128)(2,1)}, u32[]{:S(2)}, u32[]{:S(2)}) collective-permute-start(bf16[32,3584]{1,0:T(8,128)(2,1)} %slice.112), channel_id=1, source_target_pairs={{0,2},{2,0},{4,6},{6,4},{8,10},{10,8},{12,14},{14,12},{1,3},{3,1},... | collective-permute-start | bytes 688136 | tf_op jit(solution)/shard_map/ppermute | solution.py:17
  61.8 3.3 %copy-start.6 = (f32[64,3584]{1,0:T(8,128)S(1)}, f32[64,3584]{1,0:T(8,128)}, u32[]{:S(2)}) copy-start(f32[64,3584]{1,0:T(8,128)} %fusion.10) | copy-start | bytes 2752516
  63.6 11.0 %collective-permute-start.15 = (bf16[32,3584]{1,0:T(8,128)(2,1)}, bf16[32,3584]{1,0:T(8,128)(2,1)}, u32[]{:S(2)}, u32[]{:S(2)}) collective-permute-start(bf16[32,3584]{1,0:T(8,128)(2,1)} %slice.110), channel_id=1, source_target_pairs={{0,2},{2,0},{4,6},{6,4},{8,10},{10,8},{12,14},{14,12},{1,3},{3,1},... | collective-permute-start | bytes 688136 | tf_op jit(solution)/shard_map/ppermute | solution.py:17
  67.1 1.0 %copy-start.11 = (bf16[32,3584]{1,0:T(8,128)(2,1)S(1)}, bf16[32,3584]{1,0:T(8,128)(2,1)}, u32[]{:S(2)}) copy-start(bf16[32,3584]{1,0:T(8,128)(2,1)} %copy-done.10) | copy-start | bytes 688132
  67.2 2.4 %copy-start.5 = (f32[64,3584]{1,0:T(8,128)S(1)}, f32[64,3584]{1,0:T(8,128)}, u32[]{:S(2)}) copy-start(f32[64,3584]{1,0:T(8,128)} %fusion.8) | copy-start | bytes 2752516
  67.2 11.8 %collective-permute-start.12 = (bf16[32,3584]{1,0:T(8,128)(2,1)S(1)}, bf16[32,3584]{1,0:T(8,128)(2,1)}, u32[]{:S(2)}, u32[]{:S(2)}) collective-permute-start(bf16[32,3584]{1,0:T(8,128)(2,1)S(1)} %slice.111), channel_id=1, source_target_pairs={{0,2},{2,0},{4,6},{6,4},{8,10},{10,8},{12,14},{14,12},{1,3},{3,1},... | collective-permute-start | bytes 688136 | tf_op jit(solution)/shard_map/ppermute | solution.py:17
  72.3 3.6 %copy-start.8 = (f32[64,3584]{1,0:T(8,128)S(1)}, f32[64,3584]{1,0:T(8,128)}, u32[]{:S(2)}) copy-start(f32[64,3584]{1,0:T(8,128)} %convolution_add_fusion.2) | copy-start | bytes 2752516
  73.4 13.6 %collective-permute-start.5 = (bf16[32,3584]{1,0:T(8,128)(2,1)S(1)}, bf16[32,3584]{1,0:T(8,128)(2,1)S(1)}, u32[]{:S(2)}, u32[]{:S(2)}) collective-permute-start(bf16[32,3584]{1,0:T(8,128)(2,1)S(1)} %slice.113), channel_id=1, source_target_pairs={{0,2},{2,0},{4,6},{6,4},{8,10},{10,8},{12,14},{14,12},{1,3},{3,1},... | collective-permute-start | bytes 688136 | tf_op jit(solution)/shard_map/ppermute | solution.py:17
  75.8 16.9 %copy-start.9 = (f32[64,3584]{1,0:T(8,128)S(1)}, f32[64,3584]{1,0:T(8,128)}, u32[]{:S(2)}) copy-start(f32[64,3584]{1,0:T(8,128)} %convolution_add_fusion.3) | copy-start | bytes 2752516
  75.8 6.5 %collective-permute-start.16 = (bf16[32,3584]{1,0:T(8,128)(2,1)S(1)}, bf16[32,3584]{1,0:T(8,128)(2,1)S(1)}, u32[]{:S(2)}, u32[]{:S(2)}) collective-permute-start(bf16[32,3584]{1,0:T(8,128)(2,1)S(1)} %fusion), channel_id=1, source_target_pairs={{0,4},{2,6},{4,0},{6,2},{8,12},{10,14},{12,8},{14,10},{1,5},{3,7},... | collective-permute-start | bytes 688136 | tf_op jit(solution)/shard_map/ppermute | solution.py:17
  77.0 10.1 %collective-permute-start.9 = (bf16[32,3584]{1,0:T(8,128)(2,1)S(1)}, bf16[32,3584]{1,0:T(8,128)(2,1)S(1)}, u32[]{:S(2)}, u32[]{:S(2)}) collective-permute-start(bf16[32,3584]{1,0:T(8,128)(2,1)S(1)} %fusion.3), channel_id=1, source_target_pairs={{0,4},{2,6},{4,0},{6,2},{8,12},{10,14},{12,8},{14,10},{1,5},{3,7},... | collective-permute-start | bytes 688136 | tf_op jit(solution)/shard_map/ppermute | solution.py:17
  83.3 9.4 %collective-permute-start.17 = (bf16[32,3584]{1,0:T(8,128)(2,1)S(1)}, bf16[32,3584]{1,0:T(8,128)(2,1)S(1)}, u32[]{:S(2)}, u32[]{:S(2)}) collective-permute-start(bf16[32,3584]{1,0:T(8,128)(2,1)S(1)} %fusion.2), channel_id=1, source_target_pairs={{0,8},{2,10},{4,12},{6,14},{8,0},{10,2},{12,4},{14,6},{1,9},{3,11}... | collective-permute-start | bytes 688136 | tf_op jit(solution)/shard_map/ppermute | solution.py:17
  92.9 1.4 %collective-permute-start.18 = (bf16[32,1792]{1,0:T(8,128)(2,1)S(1)}, bf16[32,1792]{1,0:T(8,128)(2,1)S(1)}, u32[]{:S(2)}, u32[]{:S(2)}) collective-permute-start(bf16[32,1792]{1,0:T(8,128)(2,1)S(1)} %broadcast_select_fusion.2), channel_id=1, source_target_pairs={{0,1},{1,0},{2,3},{3,2},{4,5},{5,4},{6,7},{7,6},{8,9},{9,8},{10,11... | collective-permute-start | bytes 344072 | tf_op jit(solution)/shard_map/ppermute | solution.py:21
  (2 other events, 1.3 us)

commit v2 on v0

--- a/solution.py
+++ b/solution.py
@@ -1,9 +1,14 @@
+import functools
+
 import jax
 import jax.numpy as jnp
 from jax import lax
+from jax.experimental import pallas as pl
+from jax.experimental.pallas import tpu as pltpu
 from jax.sharding import PartitionSpec as P
 
 ESPLIT = 4
+VMEM = pl.BlockSpec(memory_space=pltpu.VMEM)
 
 
 def earlier_ranks(labels):
@@ -12,7 +17,161 @@
     return jnp.sum(matches, axis=0)
 
 
-def body(tokens, expert_ids, gate_fixed, w_gate, w_up, w_down):
+def swap(value, bit):
+    pairs = [(i, i ^ bit) for i in range(lax.axis_size("ep"))]
+    return lax.ppermute(value, "ep", pairs)
+
+
+def swap_core(value):
+    return lax.ppermute(value, "tp", [(0, 1), (1, 0)])
+
+
+def expert_kernel(count, *refs):
+    split, at = [], 0
+    for n in (*count[:2], 2, *count[2:]):
+        split.append(refs[at : at + n])
+        at += n
+    near, far, (w_in, w_out), near_out, far_out = split
+    first = lax.axis_index("tp") == 0
+
+    def halves(refs):
+        return [r[...] for r in refs] if len(refs) == 2 else [refs[0][0], refs[0][1]]
+
+    def run(order):
+        rows = jnp.concatenate(
+            [jnp.concatenate([halves(near)[i], halves(far)[i]], axis=0) for i in order], axis=1
+        )
+        act = jnp.dot(rows, w_in[...], preferred_element_type=jnp.float32)
+        units = act.shape[1] // 2
+        gate, up = act[:, :units], act[:, units:]
+        hidden = (gate / (1 + jnp.exp(-gate)) * up).astype(jnp.bfloat16)
+        out = jnp.dot(hidden, w_out[...], preferred_element_type=jnp.float32)
+        half, width = rows.shape[0] // 2, rows.shape[1] // 2
+        for place, i in enumerate(order):
+            part = out[:, place * width : (place + 1) * width]
+            for refs, low in ((near_out, 0), (far_out, half)):
+                ref = refs[i] if len(refs) == 2 else refs[0].at[i]
+                ref[...] = part[low : low + half].astype(ref.dtype)
+
+    @pl.when(first)
+    def _():
+        run((0, 1))
+
+    @pl.when(jnp.logical_not(first))
+    def _():
+        run((1, 0))
+
+
+def pack_kernel(*refs):
+    w_in, w_out = refs[6:]
+    units = refs[0].shape[1]
+    for i, ref in enumerate((refs[0], refs[3], refs[1], refs[4])):
+        w_in[:, i * units : (i + 1) * units] = ref[...]
+    w_out[:units] = refs[2][...]
+    w_out[units:] = refs[5][...]
+
+
+def pack(own, theirs):
+    depth, units = own[0].shape
+    return pl.pallas_call(
+        pack_kernel,
+        out_shape=[
+            jax.ShapeDtypeStruct((depth, 4 * units), own[0].dtype),
+            jax.ShapeDtypeStruct((2 * units, depth), own[0].dtype),
+        ],
+        in_specs=[VMEM] * 6,
+        out_specs=[VMEM] * 2,
+        compiler_params=pltpu.CompilerParams(vmem_limit_bytes=24 * 1024 * 1024),
+    )(*own, *theirs)
+
+
+def split_kernel(both_ref, a_ref, b_ref):
+    a_ref[...] = both_ref[0]
+    b_ref[...] = both_ref[1]
+
+
+def split(both):
+    part = jax.ShapeDtypeStruct(both.shape[1:], both.dtype)
+    return pl.pallas_call(
+        split_kernel, out_shape=[part] * 2, in_specs=[VMEM], out_specs=[VMEM] * 2
+    )(both)
+
+
+def expert_block(near, far, weights, near_types, far_types):
+    half, width = near[0].shape[-2:]
+    shapes = []
+    for types in (near_types, far_types):
+        part = (half, width) if len(types) == 2 else (2, half, width)
+        shapes += [jax.ShapeDtypeStruct(part, t) for t in types]
+    count = (len(near), len(far), len(near_types), len(far_types))
+    return pl.pallas_call(
+        functools.partial(expert_kernel, count),
+        out_shape=shapes,
+        in_specs=[VMEM] * (len(near) + len(far) + 2),
+        out_specs=[VMEM] * len(shapes),
+        compiler_params=pltpu.CompilerParams(vmem_limit_bytes=8 * 1024 * 1024),
+    )(*near, *far, *weights)
+
+
+def dense_body(tokens, expert_ids, gate_fixed, w_gate, w_up, w_down):
+    tie = lax.optimization_barrier
+    f32, bf16 = jnp.float32, jnp.bfloat16
+    core = lax.axis_index("tp")
+    first = core == 0
+    half = tokens.shape[0] // 2
+    top, bottom = tokens[:half], tokens[half:]
+    ids = jnp.where(first, expert_ids[:half], expert_ids[half:])
+    scale = jnp.where(first, gate_fixed[:half], gate_fixed[half:]).astype(f32) / 2048.0
+    offset = lax.axis_index("ep") - ids * ESPLIT
+    here = jnp.where((offset >= 0) & (offset < ESPLIT), 1.0, 0.0)
+    a0, b0, here, scale = tie(
+        (jnp.where(first, top, bottom), jnp.where(first, bottom, top), here, scale)
+    )
+    here = here > 0
+    b0 = swap_core(b0)
+    b0, own = tie((b0, (w_gate[0], w_up[0], w_down[0])))
+    theirs = tuple(swap_core(w) for w in own)
+
+    def expert(near, far, near_types, far_types):
+        return expert_block(near, far, weights, near_types, far_types)
+
+    both0 = jnp.stack([a0, b0])
+    z2 = swap(both0, 4)
+    z1 = swap(both0, 2)
+    held, theirs = tie((both0, theirs))
+    x0 = swap(held, 1)
+    weights = pack(own, theirs)
+    z2, z1, x0, weights = tie((z2, z1, x0, weights))
+    m6 = swap(z2, 2)
+    m5 = swap(z2, 1)
+    m6, m5, held = tie((m6, m5, x0))
+    m7 = swap(m6, 1)
+    m3 = swap(held, 2)
+    p0, p1 = expert((both0,), (x0,), (f32,), (f32,))
+    p4, p5 = expert((z2,), (m5,), (f32,), (bf16,))
+    m7, m3, p0, p1, p4, p5 = tie((m7, m3, p0, p1, p4, p5))
+    p6, p7 = expert((m6,), (m7,), (f32,), (bf16,))
+    p7, p5, m3 = tie((p7, p5, m3))
+    p2, p3 = expert((z1,), (m3,), (bf16,), (bf16,))
+    r7 = swap(p7, 1).astype(f32)
+    r5 = swap(p5, 1).astype(f32)
+    r3 = swap(p3, 2).astype(f32)
+    r6 = swap((p6 + r7).astype(bf16), 2).astype(f32)
+    sent = (p4 + r6 + r5).astype(bf16)
+    sent, p2, p1, r3 = tie((sent, p2, p1, r3))
+    other = swap(sent, 4).astype(f32)
+    r2 = swap(p2, 2).astype(f32)
+    r1 = swap((p1 + r3).astype(bf16), 1).astype(f32)
+    near = p0 + r2 + r1
+    near_a, near_b = near[0], near[1]
+    other_a, other_b = other[0], other[1]
+    left = (jnp.where(here, near_a, other_a) * scale).astype(bf16)
+    right = (jnp.where(here, near_b, other_b) * scale).astype(bf16)
+    got = swap_core(right)
+    return jnp.concatenate([jnp.where(first, left, got), jnp.where(first, got, left)], axis=0)
+
+
+def routed_body(tokens, expert_ids, gate_fixed, w_gate, w_up, w_down):
     ep_count = lax.axis_size("ep")
     tok_dev, topk = expert_ids.shape
     experts = ep_count // ESPLIT
@@ -57,6 +216,12 @@
     return jnp.sum(routed.reshape(tok_dev, topk, routed.shape[1]), axis=1).astype(jnp.bfloat16)
 
 
+def body(tokens, expert_ids, *rest):
+    experts = lax.axis_size("ep") // ESPLIT
+    dense = experts == 2 and expert_ids.shape[1] == 1
+    return (dense_body if dense else routed_body)(tokens, expert_ids, *rest)
+
+
 def solution(mesh):
     placed = (
         P(("groups", "ep"), "tp"),

time: 182 us -> 66.5 us (0.37)
  blocking collectives: 91.7 us -> 0 us
  waiting for transfers between devices: 54 us -> 30.1 us
  starting transfers between devices: 5.74 us -> 24 us
  between operations: 13.5 us -> 0.11 us
  matrix products: 9.25 us -> 0 us
  Pallas kernels: 0 us -> 5.37 us
    all_to_all x1 -> x0, blocking collectives: 89.3 us -> none  [body(): lax.all_to_all(copies.reshape(ep_count, capacity, width), 'ep', split_axi...]
    all_to_all x1 -> x0, waiting for transfers between devices: 43.2 us -> none  [body(): lax.all_to_all(summed.reshape(ep_count, capacity, summed.shape[1]), 'ep',...]
    ppermute x0 -> x19, waiting for transfers between devices: none -> 30.1 us  [the longest x14 27.8 us: swap(): return lax.ppermute(value, 'ep', pairs)]
    ppermute x0 -> x19, starting transfers between devices: none -> 24 us  [the longest x14 22.6 us: swap(): return lax.ppermute(value, 'ep', pairs)]
    reduce_scatter x1 -> x0, waiting for transfers between devices: 10.8 us -> none  [body(): lax.psum_scatter(partial_out, 'tp', scatter_dimension=1, tiled=True)]
    dot_general x3 -> x0, matrix products: 9.25 us -> none  [the longest x1 7.76 us: body(): jnp.dot(hidden, w_down[0], preferred_element_type=jnp.float32)]
    all_to_all x1 -> x0, starting transfers between devices: 5.74 us -> none  [body(): lax.all_to_all(summed.reshape(ep_count, capacity, summed.shape[1]), 'ep',...]
    pallas_call x0 -> x5, Pallas kernels: none -> 5.37 us  [the longest x4 4.62 us: expert_block(): pl.pallas_call(functools.partial(expert_kernel, count), out_shape=shapes,...]
  transfers between devices with their start and end apart: 2 -> 19, of which waited for: 2 -> 14; matrix products, arithmetic and copies ran while one was open for 0% -> 0% of each run, Pallas kernels for 0% -> 6%
where the time goes in v2:
time: 66.5 us; the launch traced here: 66.2 us
  waiting for transfers between devices  30.1 us (45%)
  starting transfers between devices  24 us (36%)
  Pallas kernels  5.37 us (8%)
  local copies, waits for them, and re-layouts  3.54 us (5%)
  other arithmetic  3.07 us (5%)
    ppermute x14, waiting for transfers between devices, swap(): return lax.ppermute(value, 'ep', pairs)  27.8 us
    ppermute x14, starting transfers between devices, swap(): return lax.ppermute(value, 'ep', pairs)  22.6 us
    pallas_call x4, Pallas kernels, expert_block(): pl.pallas_call(functools.partial(expert_kernel, count), out_shape=shapes,...  4.62 us
    unnamed x6, local copies, waits for them, and re-layouts  3.54 us
    ppermute x5, waiting for transfers between devices, swap_core(): return lax.ppermute(value, 'tp', [(0, 1), (1, 0)])  2.28 us
    ppermute x5, starting transfers between devices, swap_core(): return lax.ppermute(value, 'tp', [(0, 1), (1, 0)])  1.4 us
  transfers between devices with their start and end apart: 19, of which 14 were waited for; matrix products, arithmetic and copies ran while one was open for 0% of the time, Pallas kernels for 6%

profile of v2, /device:TPU:0, one launch (start us, length us, event | category | flops | bytes accessed | tf_op | source)
XLA Modules:
  0.0 66.2 jit_solution(11345694416100948784)
XLA Ops:
  0.0 1.0 %broadcast_select_fusion.2 = (bf16[32,1792]{1,0:T(8,128)(2,1)S(1)}, bf16[32,1792]{1,0:T(8,128)(2,1)S(1)}) fusion(pred[]{:T(512)S(6)} %eq.3, bf16[64,1792]{1,0:T(8,128)(2,1)} %param.6), kind=kLoop, calls=%fused_computation.18 | loop fusion | flops 114688 | bytes 458753 | tf_op jit(solution)/shard_map/jit(_where)/select_n | solution.py:128
  1.0 0.8 %and_select_fusion = (f32[32,1]{0,1:T(1,128)S(1)}, f32[32,1]{0,1:T(1,128)S(1)}) fusion(s32[64,1]{0,1:T(1,128)} %param.7, pred[]{:T(512)S(6)} %eq.3, s32[]{:T(128)S(6)} %axis_index.25, s32[64,1]{0,1:T(1,128)} %param.8), kind=kLoop, calls=%fused_computation.21 | loop fusion | flops 320 | bytes 773 | tf_op jit(solution)/shard_map/jit(_where)/select_n | solution.py:126
  2.2 1.0 %collective-permute-done = bf16[32,1792]{1,0:T(8,128)(2,1)S(1)} collective-permute-done((bf16[32,1792]{1,0:T(8,128)(2,1)S(1)}, bf16[32,1792]{1,0:T(8,128)(2,1)S(1)}, u32[]{:S(2)}, u32[]{:S(2)}) %collective-permute-start) | collective-permute-done | bytes 114720 | tf_op jit(solution)/shard_map/ppermute | solution.py:26
  4.1 3.8 %collective-permute-start.1 = (bf16[2,32,1792]{2,1,0:T(8,128)(2,1)S(1)}, bf16[2,32,1792]{2,1,0:T(8,128)(2,1)S(1)}, u32[]{:S(2)}, u32[]{:S(2)}) collective-permute-start(bf16[2,32,1792]{2,1,0:T(8,128)(2,1)S(1)} %pad_maximum_fusion.refs_0_), channel_id=1, source_target_pairs={{0,8},{2,10},{4,12},{6,14},{8,0},{10,2},{12,4},{14,6},{1,9},{3,11}... | collective-permute-start | bytes 688136 | tf_op jit(solution)/shard_map/ppermute | solution.py:22
  7.9 1.6 %collective-permute-start.2 = (bf16[2,32,1792]{2,1,0:T(8,128)(2,1)S(1)}, bf16[2,32,1792]{2,1,0:T(8,128)(2,1)S(1)}, u32[]{:S(2)}, u32[]{:S(2)}) collective-permute-start(bf16[2,32,1792]{2,1,0:T(8,128)(2,1)S(1)} %pad_maximum_fusion.refs_0_), channel_id=1, source_target_pairs={{0,4},{2,6},{4,0},{6,2},{8,12},{10,14},{12,8},{14,10},{1,5},{3,7},... | collective-permute-start | bytes 688136 | tf_op jit(solution)/shard_map/ppermute | solution.py:22
  9.5 1.9 %collective-permute-start.6 = (bf16[2,32,1792]{2,1,0:T(8,128)(2,1)S(1)}, bf16[2,32,1792]{2,1,0:T(8,128)(2,1)S(1)}, u32[]{:S(2)}, u32[]{:S(2)}) collective-permute-start(bf16[2,32,1792]{2,1,0:T(8,128)(2,1)S(1)} %pad_maximum_fusion.refs_0_), channel_id=1, source_target_pairs={{0,2},{2,0},{4,6},{6,4},{8,10},{10,8},{12,14},{14,12},{1,3},{3,1},... | collective-permute-start | bytes 688136 | tf_op jit(solution)/shard_map/ppermute | solution.py:22
  11.4 1.2 %copy-done = bf16[1,3584,128]{2,1,0:T(8,128)(2,1)S(1)} copy-done((bf16[1,3584,128]{2,1,0:T(8,128)(2,1)S(1)}, bf16[1,3584,128]{2,1,0:T(8,128)(2,1)}, u32[]{:S(2)}) %copy-start) | copy-done | bytes 917528
  12.5 1.2 %copy-done.1 = bf16[1,3584,128]{2,1,0:T(8,128)(2,1)S(1)} copy-done((bf16[1,3584,128]{2,1,0:T(8,128)(2,1)S(1)}, bf16[1,3584,128]{2,1,0:T(8,128)(2,1)}, u32[]{:S(2)}) %copy-start.1) | copy-done | bytes 917528
  13.7 1.2 %copy-done.2 = bf16[1,128,3584]{2,1,0:T(8,128)(2,1)S(1)} copy-done((bf16[1,128,3584]{2,1,0:T(8,128)(2,1)S(1)}, bf16[1,128,3584]{2,1,0:T(8,128)(2,1)}, u32[]{:S(2)}) %copy-start.2) | copy-done | bytes 917528
  14.9 0.7 %shard_map.64 = (bf16[3584,512]{1,0:T(8,128)(2,1)S(1)}, bf16[256,3584]{1,0:T(8,128)(2,1)S(1)}) custom-call(bf16[3584,128]{1,0:T(8,128)(2,1)S(1)} %bitcast.35, bf16[3584,128]{1,0:T(8,128)(2,1)S(1)} %bitcast.37, bf16[128,3584]{1,0:T(8,128)(2,1)S(1)} %bitcast.39, bf16[3584,128]{1,0:T(8,128)(2,1)S(1)} %collective-permute-done.3.refs_3_, ...), custom_call_target="tpu_custom_call" | custom-call | tf_op jit(solution)/shard_map/pallas_call | solution.py:76
  15.7 3.4 %collective-permute-done.1.refs_0_ = bf16[2,32,1792]{2,1,0:T(8,128)(2,1)S(1)} collective-permute-done((bf16[2,32,1792]{2,1,0:T(8,128)(2,1)S(1)}, bf16[2,32,1792]{2,1,0:T(8,128)(2,1)S(1)}, u32[]{:S(2)}, u32[]{:S(2)}) %collective-permute-start.1) | collective-permute-done | bytes 229408 | tf_op jit(solution)/shard_map/ppermute | solution.py:22
  19.3 1.5 %collective-permute-start.7 = (bf16[2,32,1792]{2,1,0:T(8,128)(2,1)S(1)}, bf16[2,32,1792]{2,1,0:T(8,128)(2,1)S(1)}, u32[]{:S(2)}, u32[]{:S(2)}) collective-permute-start(bf16[2,32,1792]{2,1,0:T(8,128)(2,1)S(1)} %collective-permute-done.1.refs_0_), channel_id=1, source_target_pairs={{0,4},{2,6},{4,0},{6,2},{8,12},{10,14},{12,8},{14,10},{1,5},{3,7},... | collective-permute-start | bytes 688136 | tf_op jit(solution)/shard_map/ppermute | solution.py:22
  20.7 1.5 %collective-permute-start.8 = (bf16[2,32,1792]{2,1,0:T(8,128)(2,1)S(1)}, bf16[2,32,1792]{2,1,0:T(8,128)(2,1)S(1)}, u32[]{:S(2)}, u32[]{:S(2)}) collective-permute-start(bf16[2,32,1792]{2,1,0:T(8,128)(2,1)S(1)} %collective-permute-done.1.refs_0_), channel_id=1, source_target_pairs={{0,2},{2,0},{4,6},{6,4},{8,10},{10,8},{12,14},{14,12},{1,3},{3,1},... | collective-permute-start | bytes 688136 | tf_op jit(solution)/shard_map/ppermute | solution.py:22
  22.2 4.1 %collective-permute-done.7.refs_0_ = bf16[2,32,1792]{2,1,0:T(8,128)(2,1)S(1)} collective-permute-done((bf16[2,32,1792]{2,1,0:T(8,128)(2,1)S(1)}, bf16[2,32,1792]{2,1,0:T(8,128)(2,1)S(1)}, u32[]{:S(2)}, u32[]{:S(2)}) %collective-permute-start.7) | collective-permute-done | bytes 229408 | tf_op jit(solution)/shard_map/ppermute | solution.py:22
  26.3 1.2 %collective-permute-done.8.refs_1_ = bf16[2,32,1792]{2,1,0:T(8,128)(2,1)S(1)} collective-permute-done((bf16[2,32,1792]{2,1,0:T(8,128)(2,1)S(1)}, bf16[2,32,1792]{2,1,0:T(8,128)(2,1)S(1)}, u32[]{:S(2)}, u32[]{:S(2)}) %collective-permute-start.8) | collective-permute-done | bytes 229408 | tf_op jit(solution)/shard_map/ppermute | solution.py:22
  28.0 1.3 %collective-permute-start.9 = (bf16[2,32,1792]{2,1,0:T(8,128)(2,1)S(1)}, bf16[2,32,1792]{2,1,0:T(8,128)(2,1)S(1)}, u32[]{:S(2)}, u32[]{:S(2)}) collective-permute-start(bf16[2,32,1792]{2,1,0:T(8,128)(2,1)S(1)} %collective-permute-done.7.refs_0_), channel_id=1, source_target_pairs={{0,2},{2,0},{4,6},{6,4},{8,10},{10,8},{12,14},{14,12},{1,3},{3,1},... | collective-permute-start | bytes 688136 | tf_op jit(solution)/shard_map/ppermute | solution.py:22
  29.3 1.2 %shard_map.65 = (f32[2,32,1792]{2,1,0:T(8,128)S(1)}, f32[2,32,1792]{2,1,0:T(8,128)S(1)}) custom-call(bf16[2,32,1792]{2,1,0:T(8,128)(2,1)S(1)} %pad_maximum_fusion.refs_0_, bf16[2,32,1792]{2,1,0:T(8,128)(2,1)S(1)} %collective-permute-done.6.refs_1_, bf16[3584,512]{1,0:T(8,128)(2,1)S(1)} %get-tuple-element.65.refs_2_, ...), custom_call_target="tpu_custom_call" | custom-call | tf_op jit(solution)/shard_map/pallas_call | solution.py:107
  30.5 1.2 %shard_map.66 = (f32[2,32,1792]{2,1,0:T(8,128)S(1)}, bf16[2,32,1792]{2,1,0:T(8,128)(2,1)S(1)}) custom-call(bf16[2,32,1792]{2,1,0:T(8,128)(2,1)S(1)} %collective-permute-done.1.refs_0_, bf16[2,32,1792]{2,1,0:T(8,128)(2,1)S(1)} %collective-permute-done.8.refs_1_, bf16[3584,512]{1,0:T(8,128)(2,1)S(1)} %get-tuple-element.65.refs_2_, ...), custom_call_target="tpu_custom_call" | custom-call | tf_op jit(solution)/shard_map/pallas_call | solution.py:107
  31.7 1.9 %collective-permute-done.10.refs_1_ = bf16[2,32,1792]{2,1,0:T(8,128)(2,1)S(1)} collective-permute-done((bf16[2,32,1792]{2,1,0:T(8,128)(2,1)S(1)}, bf16[2,32,1792]{2,1,0:T(8,128)(2,1)S(1)}, u32[]{:S(2)}, u32[]{:S(2)}) %collective-permute-start.10) | collective-permute-done | bytes 229408 | tf_op jit(solution)/shard_map/ppermute | solution.py:22
  34.1 1.2 %shard_map.67 = (f32[2,32,1792]{2,1,0:T(8,128)S(1)}, bf16[2,32,1792]{2,1,0:T(8,128)(2,1)S(1)}) custom-call(bf16[2,32,1792]{2,1,0:T(8,128)(2,1)S(1)} %collective-permute-done.7.refs_0_, bf16[2,32,1792]{2,1,0:T(8,128)(2,1)S(1)} %collective-permute-done.9.refs_1_, bf16[3584,512]{1,0:T(8,128)(2,1)S(1)} %get-tuple-element.65.refs_2_, ...), custom_call_target="tpu_custom_call" | custom-call | tf_op jit(solution)/shard_map/pallas_call | solution.py:107
  35.2 1.4 %collective-permute-start.11 = (bf16[2,32,1792]{2,1,0:T(8,128)(2,1)S(1)}, bf16[2,32,1792]{2,1,0:T(8,128)(2,1)S(1)}, u32[]{:S(2)}, u32[]{:S(2)}) collective-permute-start(bf16[2,32,1792]{2,1,0:T(8,128)(2,1)S(1)} %get-tuple-element.79), channel_id=1, source_target_pairs={{0,2},{2,0},{4,6},{6,4},{8,10},{10,8},{12,14},{14,12},{1,3},{3,1},... | collective-permute-start | bytes 688136 | tf_op jit(solution)/shard_map/ppermute | solution.py:22
  36.6 1.2 %shard_map.68 = (bf16[2,32,1792]{2,1,0:T(8,128)(2,1)S(1)}, bf16[2,32,1792]{2,1,0:T(8,128)(2,1)S(1)}) custom-call(bf16[2,32,1792]{2,1,0:T(8,128)(2,1)S(1)} %collective-permute-done.2.refs_0_, bf16[2,32,1792]{2,1,0:T(8,128)(2,1)S(1)} %collective-permute-done.10.refs_1_, bf16[3584,512]{1,0:T(8,128)(2,1)S(1)} %get-tuple-element.65.refs_2_, ...), custom_call_target="tpu_custom_call" | custom-call | tf_op jit(solution)/shard_map/pallas_call | solution.py:107
  37.8 1.8 %collective-permute-start.14 = (bf16[2,32,1792]{2,1,0:T(8,128)(2,1)S(1)}, bf16[2,32,1792]{2,1,0:T(8,128)(2,1)S(1)}, u32[]{:S(2)}, u32[]{:S(2)}) collective-permute-start(bf16[2,32,1792]{2,1,0:T(8,128)(2,1)S(1)} %get-tuple-element.85), channel_id=1, source_target_pairs={{0,4},{2,6},{4,0},{6,2},{8,12},{10,14},{12,8},{14,10},{1,5},{3,7},... | collective-permute-start | bytes 688136 | tf_op jit(solution)/shard_map/ppermute | solution.py:22
  40.0 3.6 %collective-permute-done.11 = bf16[2,32,1792]{2,1,0:T(8,128)(2,1)S(1)} collective-permute-done((bf16[2,32,1792]{2,1,0:T(8,128)(2,1)S(1)}, bf16[2,32,1792]{2,1,0:T(8,128)(2,1)S(1)}, u32[]{:S(2)}, u32[]{:S(2)}) %collective-permute-start.11) | collective-permute-done | bytes 229408 | tf_op jit(solution)/shard_map/ppermute | solution.py:22
  44.4 0.7 %collective-permute-done.14 = bf16[2,32,1792]{2,1,0:T(8,128)(2,1)S(1)} collective-permute-done((bf16[2,32,1792]{2,1,0:T(8,128)(2,1)S(1)}, bf16[2,32,1792]{2,1,0:T(8,128)(2,1)S(1)}, u32[]{:S(2)}, u32[]{:S(2)}) %collective-permute-start.14) | collective-permute-done | bytes 229408 | tf_op jit(solution)/shard_map/ppermute | solution.py:22
  45.1 1.0 %collective-permute-done.13 = bf16[2,32,1792]{2,1,0:T(8,128)(2,1)S(1)} collective-permute-done((bf16[2,32,1792]{2,1,0:T(8,128)(2,1)S(1)}, bf16[2,32,1792]{2,1,0:T(8,128)(2,1)S(1)}, u32[]{:S(2)}, u32[]{:S(2)}) %collective-permute-start.13) | collective-permute-done | bytes 229408 | tf_op jit(solution)/shard_map/ppermute | solution.py:22
  46.1 3.9 %collective-permute-done.12 = bf16[2,32,1792]{2,1,0:T(8,128)(2,1)S(1)} collective-permute-done((bf16[2,32,1792]{2,1,0:T(8,128)(2,1)S(1)}, bf16[2,32,1792]{2,1,0:T(8,128)(2,1)S(1)}, u32[]{:S(2)}, u32[]{:S(2)}) %collective-permute-start.12) | collective-permute-done | bytes 229408 | tf_op jit(solution)/shard_map/ppermute | solution.py:22
  50.1 5.2 %collective-permute-start.17 = (bf16[2,32,1792]{2,1,0:T(8,128)(2,1)S(1)}, bf16[2,32,1792]{2,1,0:T(8,128)(2,1)S(1)}, u32[]{:S(2)}, u32[]{:S(2)}) collective-permute-start(bf16[2,32,1792]{2,1,0:T(8,128)(2,1)S(1)} %add_convert_fusion.1), channel_id=1, source_target_pairs={{0,8},{2,10},{4,12},{6,14},{8,0},{10,2},{12,4},{14,6},{1,9},{3,11}... | collective-permute-start | bytes 688136 | tf_op jit(solution)/shard_map/ppermute | solution.py:22
  56.5 5.5 %collective-permute-done.17 = bf16[2,32,1792]{2,1,0:T(8,128)(2,1)S(1)} collective-permute-done((bf16[2,32,1792]{2,1,0:T(8,128)(2,1)S(1)}, bf16[2,32,1792]{2,1,0:T(8,128)(2,1)S(1)}, u32[]{:S(2)}, u32[]{:S(2)}) %collective-permute-start.17) | collective-permute-done | bytes 229408 | tf_op jit(solution)/shard_map/ppermute | solution.py:22
  62.0 1.8 %collective-permute-done.15 = bf16[2,32,1792]{2,1,0:T(8,128)(2,1)S(1)} collective-permute-done((bf16[2,32,1792]{2,1,0:T(8,128)(2,1)S(1)}, bf16[2,32,1792]{2,1,0:T(8,128)(2,1)S(1)}, u32[]{:S(2)}, u32[]{:S(2)}) %collective-permute-start.15) | collective-permute-done | bytes 229408 | tf_op jit(solution)/shard_map/ppermute | solution.py:22
  64.1 1.3 %collective-permute-done.18 = bf16[32,1792]{1,0:T(8,128)(2,1)S(1)} collective-permute-done((bf16[32,1792]{1,0:T(8,128)(2,1)S(1)}, bf16[32,1792]{1,0:T(8,128)(2,1)S(1)}, u32[]{:S(2)}, u32[]{:S(2)}) %collective-permute-start.18) | collective-permute-done | bytes 114720 | tf_op jit(solution)/shard_map/ppermute | solution.py:26
  65.5 0.7 %pad_maximum_fusion.1 = bf16[64,1792]{1,0:T(8,128)(2,1)} fusion(bf16[32,1792]{1,0:T(8,128)(2,1)S(1)} %broadcast_select_fusion, bf16[32,1792]{1,0:T(8,128)(2,1)S(1)} %get-tuple-element.91), kind=kLoop, calls=%fused_computation.15 | loop fusion | flops 458752 | bytes 458752 | tf_op jit(solution)/shard_map/concatenate | solution.py:171
  (31 shorter events, 5.5 us)
Async XLA Ops:
  1.8 1.4 %collective-permute-start = (bf16[32,1792]{1,0:T(8,128)(2,1)S(1)}, bf16[32,1792]{1,0:T(8,128)(2,1)S(1)}, u32[]{:S(2)}, u32[]{:S(2)}) collective-permute-start(bf16[32,1792]{1,0:T(8,128)(2,1)S(1)} %get-tuple-element.50), channel_id=1, source_target_pairs={{0,1},{1,0},{2,3},{3,2},{4,5},{5,4},{6,7},{7,6},{8,9},{9,8},{10,11... | collective-permute-start | bytes 344072 | tf_op jit(solution)/shard_map/ppermute | solution.py:26
  3.2 6.3 %collective-permute-start.3 = (bf16[3584,128]{1,0:T(8,128)(2,1)}, bf16[3584,128]{1,0:T(8,128)(2,1)S(1)}, u32[]{:S(2)}, u32[]{:S(2)}) collective-permute-start(bf16[3584,128]{1,0:T(8,128)(2,1)} %bitcast.34), channel_id=1, source_target_pairs={{0,1},{1,0},{2,3},{3,2},{4,5},{5,4},{6,7},{7,6},{8,9},{9,8},{10,11... | collective-permute-start | bytes 2752520 | tf_op jit(solution)/shard_map/ppermute | solution.py:26
  3.6 5.9 %collective-permute-start.4 = (bf16[3584,128]{1,0:T(8,128)(2,1)}, bf16[3584,128]{1,0:T(8,128)(2,1)S(1)}, u32[]{:S(2)}, u32[]{:S(2)}) collective-permute-start(bf16[3584,128]{1,0:T(8,128)(2,1)} %bitcast.36), channel_id=1, source_target_pairs={{0,1},{1,0},{2,3},{3,2},{4,5},{5,4},{6,7},{7,6},{8,9},{9,8},{10,11... | collective-permute-start | bytes 2752520 | tf_op jit(solution)/shard_map/ppermute | solution.py:26
  3.7 5.8 %collective-permute-start.5 = (bf16[128,3584]{1,0:T(8,128)(2,1)}, bf16[128,3584]{1,0:T(8,128)(2,1)S(1)}, u32[]{:S(2)}, u32[]{:S(2)}) collective-permute-start(bf16[128,3584]{1,0:T(8,128)(2,1)} %bitcast.38), channel_id=1, source_target_pairs={{0,1},{1,0},{2,3},{3,2},{4,5},{5,4},{6,7},{7,6},{8,9},{9,8},{10,11... | collective-permute-start | bytes 2752520 | tf_op jit(solution)/shard_map/ppermute | solution.py:26
  4.1 14.9 %collective-permute-start.1 = (bf16[2,32,1792]{2,1,0:T(8,128)(2,1)S(1)}, bf16[2,32,1792]{2,1,0:T(8,128)(2,1)S(1)}, u32[]{:S(2)}, u32[]{:S(2)}) collective-permute-start(bf16[2,32,1792]{2,1,0:T(8,128)(2,1)S(1)} %pad_maximum_fusion.refs_0_), channel_id=1, source_target_pairs={{0,8},{2,10},{4,12},{6,14},{8,0},{10,2},{12,4},{14,6},{1,9},{3,11}... | collective-permute-start | bytes 688136 | tf_op jit(solution)/shard_map/ppermute | solution.py:22
  7.9 11.3 %collective-permute-start.2 = (bf16[2,32,1792]{2,1,0:T(8,128)(2,1)S(1)}, bf16[2,32,1792]{2,1,0:T(8,128)(2,1)S(1)}, u32[]{:S(2)}, u32[]{:S(2)}) collective-permute-start(bf16[2,32,1792]{2,1,0:T(8,128)(2,1)S(1)} %pad_maximum_fusion.refs_0_), channel_id=1, source_target_pairs={{0,4},{2,6},{4,0},{6,2},{8,12},{10,14},{12,8},{14,10},{1,5},{3,7},... | collective-permute-start | bytes 688136 | tf_op jit(solution)/shard_map/ppermute | solution.py:22
  9.5 9.7 %collective-permute-start.6 = (bf16[2,32,1792]{2,1,0:T(8,128)(2,1)S(1)}, bf16[2,32,1792]{2,1,0:T(8,128)(2,1)S(1)}, u32[]{:S(2)}, u32[]{:S(2)}) collective-permute-start(bf16[2,32,1792]{2,1,0:T(8,128)(2,1)S(1)} %pad_maximum_fusion.refs_0_), channel_id=1, source_target_pairs={{0,2},{2,0},{4,6},{6,4},{8,10},{10,8},{12,14},{14,12},{1,3},{3,1},... | collective-permute-start | bytes 688136 | tf_op jit(solution)/shard_map/ppermute | solution.py:22
  11.4 1.2 %copy-start = (bf16[1,3584,128]{2,1,0:T(8,128)(2,1)S(1)}, bf16[1,3584,128]{2,1,0:T(8,128)(2,1)}, u32[]{:S(2)}) copy-start(bf16[1,3584,128]{2,1,0:T(8,128)(2,1)} %param.9) | copy-start | bytes 2752516
  12.5 1.2 %copy-start.1 = (bf16[1,3584,128]{2,1,0:T(8,128)(2,1)S(1)}, bf16[1,3584,128]{2,1,0:T(8,128)(2,1)}, u32[]{:S(2)}) copy-start(bf16[1,3584,128]{2,1,0:T(8,128)(2,1)} %param.10) | copy-start | bytes 2752516
  13.7 1.2 %copy-start.2 = (bf16[1,128,3584]{2,1,0:T(8,128)(2,1)S(1)}, bf16[1,128,3584]{2,1,0:T(8,128)(2,1)}, u32[]{:S(2)}) copy-start(bf16[1,128,3584]{2,1,0:T(8,128)(2,1)} %param.11) | copy-start | bytes 2752516
  19.3 7.0 %collective-permute-start.7 = (bf16[2,32,1792]{2,1,0:T(8,128)(2,1)S(1)}, bf16[2,32,1792]{2,1,0:T(8,128)(2,1)S(1)}, u32[]{:S(2)}, u32[]{:S(2)}) collective-permute-start(bf16[2,32,1792]{2,1,0:T(8,128)(2,1)S(1)} %collective-permute-done.1.refs_0_), channel_id=1, source_target_pairs={{0,4},{2,6},{4,0},{6,2},{8,12},{10,14},{12,8},{14,10},{1,5},{3,7},... | collective-permute-start | bytes 688136 | tf_op jit(solution)/shard_map/ppermute | solution.py:22
  20.7 6.8 %collective-permute-start.8 = (bf16[2,32,1792]{2,1,0:T(8,128)(2,1)S(1)}, bf16[2,32,1792]{2,1,0:T(8,128)(2,1)S(1)}, u32[]{:S(2)}, u32[]{:S(2)}) collective-permute-start(bf16[2,32,1792]{2,1,0:T(8,128)(2,1)S(1)} %collective-permute-done.1.refs_0_), channel_id=1, source_target_pairs={{0,2},{2,0},{4,6},{6,4},{8,10},{10,8},{12,14},{14,12},{1,3},{3,1},... | collective-permute-start | bytes 688136 | tf_op jit(solution)/shard_map/ppermute | solution.py:22
  27.5 6.0 %collective-permute-start.10 = (bf16[2,32,1792]{2,1,0:T(8,128)(2,1)S(1)}, bf16[2,32,1792]{2,1,0:T(8,128)(2,1)S(1)}, u32[]{:S(2)}, u32[]{:S(2)}) collective-permute-start(bf16[2,32,1792]{2,1,0:T(8,128)(2,1)S(1)} %collective-permute-done.6.refs_1_), channel_id=1, source_target_pairs={{0,4},{2,6},{4,0},{6,2},{8,12},{10,14},{12,8},{14,10},{1,5},{3,7},... | collective-permute-start | bytes 688136 | tf_op jit(solution)/shard_map/ppermute | solution.py:22
  28.0 6.0 %collective-permute-start.9 = (bf16[2,32,1792]{2,1,0:T(8,128)(2,1)S(1)}, bf16[2,32,1792]{2,1,0:T(8,128)(2,1)S(1)}, u32[]{:S(2)}, u32[]{:S(2)}) collective-permute-start(bf16[2,32,1792]{2,1,0:T(8,128)(2,1)S(1)} %collective-permute-done.7.refs_0_), channel_id=1, source_target_pairs={{0,2},{2,0},{4,6},{6,4},{8,10},{10,8},{12,14},{14,12},{1,3},{3,1},... | collective-permute-start | bytes 688136 | tf_op jit(solution)/shard_map/ppermute | solution.py:22
  35.2 8.4 %collective-permute-start.11 = (bf16[2,32,1792]{2,1,0:T(8,128)(2,1)S(1)}, bf16[2,32,1792]{2,1,0:T(8,128)(2,1)S(1)}, u32[]{:S(2)}, u32[]{:S(2)}) collective-permute-start(bf16[2,32,1792]{2,1,0:T(8,128)(2,1)S(1)} %get-tuple-element.79), channel_id=1, source_target_pairs={{0,2},{2,0},{4,6},{6,4},{8,10},{10,8},{12,14},{14,12},{1,3},{3,1},... | collective-permute-start | bytes 688136 | tf_op jit(solution)/shard_map/ppermute | solution.py:22
  37.8 7.3 %collective-permute-start.14 = (bf16[2,32,1792]{2,1,0:T(8,128)(2,1)S(1)}, bf16[2,32,1792]{2,1,0:T(8,128)(2,1)S(1)}, u32[]{:S(2)}, u32[]{:S(2)}) collective-permute-start(bf16[2,32,1792]{2,1,0:T(8,128)(2,1)S(1)} %get-tuple-element.85), channel_id=1, source_target_pairs={{0,4},{2,6},{4,0},{6,2},{8,12},{10,14},{12,8},{14,10},{1,5},{3,7},... | collective-permute-start | bytes 688136 | tf_op jit(solution)/shard_map/ppermute | solution.py:22
  39.5 6.6 %collective-permute-start.13 = (bf16[2,32,1792]{2,1,0:T(8,128)(2,1)S(1)}, bf16[2,32,1792]{2,1,0:T(8,128)(2,1)S(1)}, u32[]{:S(2)}, u32[]{:S(2)}) collective-permute-start(bf16[2,32,1792]{2,1,0:T(8,128)(2,1)S(1)} %get-tuple-element.80), channel_id=1, source_target_pairs={{0,2},{2,0},{4,6},{6,4},{8,10},{10,8},{12,14},{14,12},{1,3},{3,1},... | collective-permute-start | bytes 688136 | tf_op jit(solution)/shard_map/ppermute | solution.py:22
  43.7 6.3 %collective-permute-start.12 = (bf16[2,32,1792]{2,1,0:T(8,128)(2,1)S(1)}, bf16[2,32,1792]{2,1,0:T(8,128)(2,1)S(1)}, u32[]{:S(2)}, u32[]{:S(2)}) collective-permute-start(bf16[2,32,1792]{2,1,0:T(8,128)(2,1)S(1)} %add_convert_fusion.2), channel_id=1, source_target_pairs={{0,4},{2,6},{4,0},{6,2},{8,12},{10,14},{12,8},{14,10},{1,5},{3,7},... | collective-permute-start | bytes 688136 | tf_op jit(solution)/shard_map/ppermute | solution.py:22
  50.1 11.8 %collective-permute-start.17 = (bf16[2,32,1792]{2,1,0:T(8,128)(2,1)S(1)}, bf16[2,32,1792]{2,1,0:T(8,128)(2,1)S(1)}, u32[]{:S(2)}, u32[]{:S(2)}) collective-permute-start(bf16[2,32,1792]{2,1,0:T(8,128)(2,1)S(1)} %add_convert_fusion.1), channel_id=1, source_target_pairs={{0,8},{2,10},{4,12},{6,14},{8,0},{10,2},{12,4},{14,6},{1,9},{3,11}... | collective-permute-start | bytes 688136 | tf_op jit(solution)/shard_map/ppermute | solution.py:22
  55.4 6.6 %collective-permute-start.16 = (bf16[2,32,1792]{2,1,0:T(8,128)(2,1)S(1)}, bf16[2,32,1792]{2,1,0:T(8,128)(2,1)S(1)}, u32[]{:S(2)}, u32[]{:S(2)}) collective-permute-start(bf16[2,32,1792]{2,1,0:T(8,128)(2,1)S(1)} %add_convert_fusion), channel_id=1, source_target_pairs={{0,2},{2,0},{4,6},{6,4},{8,10},{10,8},{12,14},{14,12},{1,3},{3,1},... | collective-permute-start | bytes 688136 | tf_op jit(solution)/shard_map/ppermute | solution.py:22
  55.8 8.0 %collective-permute-start.15 = (bf16[2,32,1792]{2,1,0:T(8,128)(2,1)S(1)}, bf16[2,32,1792]{2,1,0:T(8,128)(2,1)S(1)}, u32[]{:S(2)}, u32[]{:S(2)}) collective-permute-start(bf16[2,32,1792]{2,1,0:T(8,128)(2,1)S(1)} %get-tuple-element.86), channel_id=1, source_target_pairs={{0,4},{2,6},{4,0},{6,2},{8,12},{10,14},{12,8},{14,10},{1,5},{3,7},... | collective-permute-start | bytes 688136 | tf_op jit(solution)/shard_map/ppermute | solution.py:22
  64.0 1.4 %collective-permute-start.18 = (bf16[32,1792]{1,0:T(8,128)(2,1)S(1)}, bf16[32,1792]{1,0:T(8,128)(2,1)S(1)}, u32[]{:S(2)}, u32[]{:S(2)}) collective-permute-start(bf16[32,1792]{1,0:T(8,128)(2,1)S(1)} %fusion.2), channel_id=1, source_target_pairs={{0,1},{1,0},{2,3},{3,2},{4,5},{5,4},{6,7},{7,6},{8,9},{9,8},{10,11... | collective-permute-start | bytes 344072 | tf_op jit(solution)/shard_map/ppermute | solution.py:26

commit v3 on v0

--- a/solution.py
+++ b/solution.py
@@ -1,9 +1,15 @@
+import functools
+
 import jax
 import jax.numpy as jnp
 from jax import lax
+from jax.experimental import pallas as pl
+from jax.experimental.pallas import tpu as pltpu
 from jax.sharding import PartitionSpec as P
 
 ESPLIT = 4
+FLOPS_US = 1.15e9
+VMEM = pl.BlockSpec(memory_space=pltpu.VMEM)
 
 
 def earlier_ranks(labels):
@@ -12,7 +18,247 @@
     return jnp.sum(matches, axis=0)
 
 
-def body(tokens, expert_ids, gate_fixed, w_gate, w_up, w_down):
+def swap(value, bit):
+    pairs = [(i, i ^ bit) for i in range(lax.axis_size("ep"))]
+    return lax.ppermute(value, "ep", pairs)
+
+
+def swap_of(value, bit, core):
+    pairs = [(2 * i + core, 2 * (i ^ bit) + core) for i in range(lax.axis_size("ep"))]
+    return lax.ppermute(value, ("ep", "tp"), pairs)
+
+
+def swap_core(value):
+    return lax.ppermute(value, "tp", [(0, 1), (1, 0)])
+
+
+def pack_kernel(turn, *refs):
+    w_in, w_out, sems = refs[-3:]
+    units = refs[0].shape[1]
+    gate, up = (w_in.at[:, i * units : (i + 1) * units] for i in (turn, 2 + turn))
+    down = w_out.at[turn * units : (turn + 1) * units]
+    copies = [
+        pltpu.make_async_copy(ref, place, sems.at[i])
+        for i, (ref, place) in enumerate(zip(refs[:3], (gate, up, down)))
+    ]
+    for copy in copies:
+        copy.start()
+    for copy in copies:
+        copy.wait()
+
+
+def pack(turn, parts, held=()):
+    depth, units = parts[0].shape
+    return pl.pallas_call(
+        functools.partial(pack_kernel, turn),
+        out_shape=[
+            jax.ShapeDtypeStruct((depth, 4 * units), parts[0].dtype),
+            jax.ShapeDtypeStruct((2 * units, depth), parts[0].dtype),
+        ],
+        in_specs=[pl.BlockSpec(memory_space=pl.ANY)] * 3 + [VMEM] * len(held),
+        out_specs=[VMEM] * 2,
+        scratch_shapes=[pltpu.SemaphoreType.DMA((3,))],
+        input_output_aliases={3 + i: i for i in range(len(held))},
+        compiler_params=pltpu.CompilerParams(vmem_limit_bytes=24 * 1024 * 1024),
+    )(*parts, *held)
+
+
+def expert_kernel(blocks_in, blocks_out, *refs):
+    def take(shape):
+        nonlocal refs
+        taken, refs = refs[: len(shape)], refs[len(shape) :]
+        return taken
+
+    def parts(held):
+        return held if len(held) == 2 else (held[0].at[0], held[0].at[1])
+
+    blocks = [parts(take(block)) for block in blocks_in]
+    w_in, w_out = take((None, None))
+    sums = [parts(take(block)) for block in blocks_out]
+    rows, width = blocks[0][0].shape
+    first = lax.axis_index("tp") == 0
+
+    def run(order):
+        whole = jnp.concatenate(
+            [jnp.concatenate([block[i][...] for block in blocks], axis=0) for i in order], axis=1
+        )
+        act = jnp.dot(whole, w_in[...], preferred_element_type=jnp.float32)
+        units = act.shape[1] // 2
+        gate, up = act[:, :units], act[:, units:]
+        hidden = (gate / (1 + jnp.exp(-gate)) * up).astype(jnp.bfloat16)
+        out = jnp.dot(hidden, w_out[...], preferred_element_type=jnp.float32)
+        for place, i in enumerate(order):
+            for j, held in enumerate(sums):
+                part = out[j * rows : (j + 1) * rows, place * width : (place + 1) * width]
+                held[i][...] = part.astype(held[i].dtype)
+
+    @pl.when(first)
+    def _():
+        run((0, 1))
+
+    @pl.when(jnp.logical_not(first))
+    def _():
+        run((1, 0))
+
+
+def expert_block(blocks, weights, types, work):
+    half, width = blocks[0][0].shape[-2:]
+    shapes = [
+        jax.ShapeDtypeStruct((half, width) if len(pair) == 2 else (2, half, width), t)
+        for pair in types
+        for t in pair
+    ]
+    flat = [array for block in blocks for array in block]
+    return pl.pallas_call(
+        functools.partial(
+            expert_kernel, [(None,) * len(b) for b in blocks], [(None,) * len(t) for t in types]
+        ),
+        out_shape=shapes,
+        in_specs=[VMEM] * (len(flat) + 2),
+        out_specs=[VMEM] * len(shapes),
+        cost_estimate=pl.CostEstimate(
+            flops=int(work * FLOPS_US), bytes_accessed=0, transcendentals=0
+        ),
+        compiler_params=pltpu.CompilerParams(vmem_limit_bytes=16 * 1024 * 1024),
+    )(*flat, *weights)
+
+
+def part_kernel(index, both_ref, part_ref):
+    part_ref[...] = both_ref[index]
+
+
+def part_of(both, index):
+    return pl.pallas_call(
+        functools.partial(part_kernel, index),
+        out_shape=jax.ShapeDtypeStruct(both.shape[1:], both.dtype),
+        in_specs=[VMEM],
+        out_specs=VMEM,
+        cost_estimate=pl.CostEstimate(flops=int(FLOPS_US / 5), bytes_accessed=0, transcendentals=0),
+        compiler_params=pltpu.CompilerParams(vmem_limit_bytes=4 * 1024 * 1024),
+    )(both)
+
+
+def widen_kernel(sum_ref, out_ref):
+    out_ref[...] = sum_ref[...].astype(jnp.float32)
+
+
+def widen(sums, work):
+    return pl.pallas_call(
+        widen_kernel,
+        out_shape=jax.ShapeDtypeStruct(sums.shape, jnp.float32),
+        in_specs=[VMEM],
+        out_specs=VMEM,
+        cost_estimate=pl.CostEstimate(
+            flops=int(work * FLOPS_US), bytes_accessed=0, transcendentals=0
+        ),
+        compiler_params=pltpu.CompilerParams(vmem_limit_bytes=4 * 1024 * 1024),
+    )(sums)
+
+
+def add_kernel(one_ref, two_ref, out_ref):
+    out_ref[...] = (one_ref[...] + two_ref[...].astype(jnp.float32)).astype(out_ref.dtype)
+
+
+def add(one, two, work):
+    return pl.pallas_call(
+        add_kernel,
+        out_shape=jax.ShapeDtypeStruct(two.shape, two.dtype),
+        in_specs=[VMEM] * 2,
+        out_specs=VMEM,
+        cost_estimate=pl.CostEstimate(
+            flops=int(work * FLOPS_US), bytes_accessed=0, transcendentals=0
+        ),
+        compiler_params=pltpu.CompilerParams(vmem_limit_bytes=4 * 1024 * 1024),
+    )(one, two)
+
+
+def pick_kernel(one_ref, two_ref, out_ref):
+    first = lax.axis_index("tp") == 0
+
+    @pl.when(first)
+    def _():
+        out_ref[...] = one_ref[...]
+
+    @pl.when(jnp.logical_not(first))
+    def _():
+        out_ref[...] = two_ref[...]
+
+
+def pick(one, two):
+    return pl.pallas_call(
+        pick_kernel,
+        out_shape=jax.ShapeDtypeStruct(one.shape, one.dtype),
+        in_specs=[VMEM] * 2,
+        out_specs=VMEM,
+        cost_estimate=pl.CostEstimate(flops=int(FLOPS_US / 5), bytes_accessed=0, transcendentals=0),
+        compiler_params=pltpu.CompilerParams(vmem_limit_bytes=4 * 1024 * 1024),
+    )(one, two)
+
+
+def dense_body(tokens, expert_ids, gate_fixed, w_gate, w_up, w_down):
+    tie = lax.optimization_barrier
+    f32, bf16 = jnp.float32, jnp.bfloat16
+    core = lax.axis_index("tp")
+    first = core == 0
+    half = tokens.shape[0] // 2
+    top, bottom = tokens[:half], tokens[half:]
+    a0, b0, place = tie(
+        (jnp.where(first, top, bottom), jnp.where(first, bottom, top), lax.axis_index("ep"))
+    )
+    b0 = swap_core(b0)
+    b0, own = tie((b0, (w_gate[0], w_up[0], w_down[0])))
+    theirs = tuple(swap_core(w) for w in own)
+
+    def expert(blocks, types, work=1.0):
+        return expert_block(blocks, weights, types, work)
+
+    both0 = jnp.stack([a0, b0])
+    one, two, three = theirs
+    z2 = swap(both0, 4)
+    z1 = swap(both0, 2)
+    held, one = tie((both0, one))
+    x0 = swap(held, 1)
+    packed = pack(0, own)
+    weights = pack(1, (one, two, three), packed)
+    z2, z1, x0, weights = tie((z2, z1, x0, weights))
+    m6 = swap(z2, 2)
+    m5 = swap(z2, 1)
+    h6, h5 = part_of(m6, 0), part_of(m5, 1)
+    z1, h5 = tie((z1, h5))
+    m7a = swap(h6, 1)
+    m7b = swap(h5, 2)
+    m3 = swap(z1, 1)
+    p4, p5 = expert(((z2,), (m5,)), ((f32,), (f32,)))
+    m7a, m7b, p4, p5 = tie((m7a, m7b, p4, p5))
+    p6, p7a, p7b = expert(((m6,), (m7a, m7b)), ((f32,), (bf16, bf16)))
+    p0, p1, p2, p3 = expert(
+        ((both0,), (x0,), (z1,), (m3,)), ((f32,), (bf16,), (f32,), (bf16,)), 1.0
+    )
+    r7a = swap(p7a, 1).astype(f32)
+    r7b = swap(p7b, 2).astype(f32)
+    s6 = jnp.stack([p6[0] + r7a, p6[1]]).astype(bf16)
+    s5 = jnp.stack([p5[0], p5[1] + r7b]).astype(bf16)
+    r6 = swap(s6, 2).astype(f32)
+    r5 = swap(s5, 1).astype(f32)
+    sent = (p4 + r6 + r5).astype(bf16)
+    r3 = swap(p3, 1)
+    s2 = add(p2, r3, 0.1)
+    sent, p1 = tie((sent, p1))
+    other = widen(swap(sent, 4), 0.5)
+    r2 = swap(s2, 2)
+    r1 = swap(p1, 1)
+    near = p0 + r1.astype(f32) + r2.astype(f32)
+    ids = jnp.where(first, expert_ids[:half], expert_ids[half:])
+    scale = jnp.where(first, gate_fixed[:half], gate_fixed[half:]).astype(f32) / 2048.0
+    offset = place - ids * ESPLIT
+    here = (offset >= 0) & (offset < ESPLIT)
+    mixed = jnp.where(here, near, other) * scale
+    left, right = mixed[0].astype(bf16), mixed[1].astype(bf16)
+    got = swap_core(right)
+    return jnp.concatenate([jnp.where(first, left, got), jnp.where(first, got, left)], axis=0)
+
+
+def routed_body(tokens, expert_ids, gate_fixed, w_gate, w_up, w_down):
     ep_count = lax.axis_size("ep")
     tok_dev, topk = expert_ids.shape
     experts = ep_count // ESPLIT
@@ -57,6 +303,12 @@
     return jnp.sum(routed.reshape(tok_dev, topk, routed.shape[1]), axis=1).astype(jnp.bfloat16)
 
 
+def body(tokens, expert_ids, *rest):
+    experts = lax.axis_size("ep") // ESPLIT
+    dense = experts == 2 and expert_ids.shape[1] == 1
+    return (dense_body if dense else routed_body)(tokens, expert_ids, *rest)
+
+
 def solution(mesh):
     placed = (
         P(("groups", "ep"), "tp"),

time: 182 us -> 61.3 us (0.34)
  blocking collectives: 91.7 us -> 0 us
  waiting for transfers between devices: 54 us -> 24 us
  starting transfers between devices: 5.74 us -> 26.7 us
  between operations: 13.5 us -> 0.15 us
  matrix products: 9.25 us -> 0 us
  Pallas kernels: 0 us -> 4.54 us
  other arithmetic: 4.15 us -> 2.16 us
    all_to_all x1 -> x0, blocking collectives: 89.3 us -> none  [body(): lax.all_to_all(copies.reshape(ep_count, capacity, width), 'ep', split_axi...]
    all_to_all x1 -> x0, waiting for transfers between devices: 43.2 us -> none  [body(): lax.all_to_all(summed.reshape(ep_count, capacity, summed.shape[1]), 'ep',...]
    ppermute x0 -> x21, starting transfers between devices: none -> 26.7 us  [the longest x16 25.2 us: swap(): return lax.ppermute(value, 'ep', pairs)]
    ppermute x0 -> x21, waiting for transfers between devices: none -> 24 us  [the longest x16 21.7 us: swap(): return lax.ppermute(value, 'ep', pairs)]
    reduce_scatter x1 -> x0, waiting for transfers between devices: 10.8 us -> none  [body(): lax.psum_scatter(partial_out, 'tp', scatter_dimension=1, tiled=True)]
    dot_general x3 -> x0, matrix products: 9.25 us -> none  [the longest x1 7.76 us: body(): jnp.dot(hidden, w_down[0], preferred_element_type=jnp.float32)]
    all_to_all x1 -> x0, starting transfers between devices: 5.74 us -> none  [body(): lax.all_to_all(summed.reshape(ep_count, capacity, summed.shape[1]), 'ep',...]
    pallas_call x0 -> x9, Pallas kernels: none -> 4.54 us  [the longest x3 3.31 us: expert_block(): pl.pallas_call(functools.partial(expert_kernel, [(None,) * len(b) for b i...]
  transfers between devices with their start and end apart: 2 -> 21, of which waited for: 2 -> 14; matrix products, arithmetic and copies ran while one was open for 0% -> 1% of each run, Pallas kernels for 0% -> 6%
where the time goes in v3:
time: 61.3 us; the launch traced here: 61.1 us
  starting transfers between devices  26.7 us (44%)
  waiting for transfers between devices  24 us (39%)
  Pallas kernels  4.54 us (7%)
  local copies, waits for them, and re-layouts  3.58 us (6%)
  other arithmetic  2.16 us (4%)
    ppermute x16, starting transfers between devices, swap(): return lax.ppermute(value, 'ep', pairs)  25.2 us
    ppermute x16, waiting for transfers between devices, swap(): return lax.ppermute(value, 'ep', pairs)  21.7 us
    unnamed x10, local copies, waits for them, and re-layouts  3.54 us
    pallas_call x3, Pallas kernels, expert_block(): pl.pallas_call(functools.partial(expert_kernel, [(None,) * len(b) for b i...  3.31 us
    ppermute x5, waiting for transfers between devices, swap_core(): return lax.ppermute(value, 'tp', [(0, 1), (1, 0)])  2.28 us
    ppermute x5, starting transfers between devices, swap_core(): return lax.ppermute(value, 'tp', [(0, 1), (1, 0)])  1.46 us
  transfers between devices with their start and end apart: 21, of which 14 were waited for; matrix products, arithmetic and copies ran while one was open for 1% of the time, Pallas kernels for 6%

profile of v3, /device:TPU:0, one launch (start us, length us, event | category | flops | bytes accessed | tf_op | source)
XLA Modules:
  0.0 61.1 jit_solution(11670217295211541428)
XLA Ops:
  0.0 1.0 %broadcast_select_fusion.2 = (bf16[32,1792]{1,0:T(8,128)(2,1)S(1)}, bf16[32,1792]{1,0:T(8,128)(2,1)S(1)}) fusion(pred[]{:T(512)S(6)} %eq.3, bf16[64,1792]{1,0:T(8,128)(2,1)} %param.6), kind=kLoop, calls=%fused_computation.18 | loop fusion | flops 114688 | bytes 458753 | tf_op jit(solution)/shard_map/jit(_where)/select_n | solution.py:206
  1.5 1.0 %collective-permute-done = bf16[32,1792]{1,0:T(8,128)(2,1)S(1)} collective-permute-done((bf16[32,1792]{1,0:T(8,128)(2,1)S(1)}, bf16[32,1792]{1,0:T(8,128)(2,1)S(1)}, u32[]{:S(2)}, u32[]{:S(2)}) %collective-permute-start) | collective-permute-done | bytes 114720 | tf_op jit(solution)/shard_map/ppermute | solution.py:32
  3.4 3.8 %collective-permute-start.1 = (bf16[2,32,1792]{2,1,0:T(8,128)(2,1)S(1)}, bf16[2,32,1792]{2,1,0:T(8,128)(2,1)S(1)}, u32[]{:S(2)}, u32[]{:S(2)}) collective-permute-start(bf16[2,32,1792]{2,1,0:T(8,128)(2,1)S(1)} %pad_maximum_fusion.refs_0_), channel_id=1, source_target_pairs={{0,8},{2,10},{4,12},{6,14},{8,0},{10,2},{12,4},{14,6},{1,9},{3,11}... | collective-permute-start | bytes 688136 | tf_op jit(solution)/shard_map/ppermute | solution.py:23
  7.2 1.6 %collective-permute-start.2 = (bf16[2,32,1792]{2,1,0:T(8,128)(2,1)S(1)}, bf16[2,32,1792]{2,1,0:T(8,128)(2,1)S(1)}, u32[]{:S(2)}, u32[]{:S(2)}) collective-permute-start(bf16[2,32,1792]{2,1,0:T(8,128)(2,1)S(1)} %pad_maximum_fusion.refs_0_), channel_id=1, source_target_pairs={{0,4},{2,6},{4,0},{6,2},{8,12},{10,14},{12,8},{14,10},{1,5},{3,7},... | collective-permute-start | bytes 688136 | tf_op jit(solution)/shard_map/ppermute | solution.py:23
  8.8 1.5 %collective-permute-start.4 = (bf16[2,32,1792]{2,1,0:T(8,128)(2,1)S(1)}, bf16[2,32,1792]{2,1,0:T(8,128)(2,1)S(1)}, u32[]{:S(2)}, u32[]{:S(2)}) collective-permute-start(bf16[2,32,1792]{2,1,0:T(8,128)(2,1)S(1)} %pad_maximum_fusion.refs_0_), channel_id=1, source_target_pairs={{0,2},{2,0},{4,6},{6,4},{8,10},{10,8},{12,14},{14,12},{1,3},{3,1},... | collective-permute-start | bytes 688136 | tf_op jit(solution)/shard_map/ppermute | solution.py:23
  10.2 1.2 %copy-done = bf16[1,3584,128]{2,1,0:T(8,128)(2,1)S(1)} copy-done((bf16[1,3584,128]{2,1,0:T(8,128)(2,1)S(1)}, bf16[1,3584,128]{2,1,0:T(8,128)(2,1)}, u32[]{:S(2)}) %copy-start) | copy-done | bytes 917528
  11.4 1.2 %copy-done.1 = bf16[1,3584,128]{2,1,0:T(8,128)(2,1)S(1)} copy-done((bf16[1,3584,128]{2,1,0:T(8,128)(2,1)S(1)}, bf16[1,3584,128]{2,1,0:T(8,128)(2,1)}, u32[]{:S(2)}) %copy-start.1) | copy-done | bytes 917528
  12.6 1.2 %copy-done.2 = bf16[1,128,3584]{2,1,0:T(8,128)(2,1)S(1)} copy-done((bf16[1,128,3584]{2,1,0:T(8,128)(2,1)S(1)}, bf16[1,128,3584]{2,1,0:T(8,128)(2,1)}, u32[]{:S(2)}) %copy-start.2) | copy-done | bytes 917528
  15.0 3.3 %collective-permute-done.1.refs_0_ = bf16[2,32,1792]{2,1,0:T(8,128)(2,1)S(1)} collective-permute-done((bf16[2,32,1792]{2,1,0:T(8,128)(2,1)S(1)}, bf16[2,32,1792]{2,1,0:T(8,128)(2,1)S(1)}, u32[]{:S(2)}, u32[]{:S(2)}) %collective-permute-start.1) | collective-permute-done | bytes 229408 | tf_op jit(solution)/shard_map/ppermute | solution.py:23
  18.5 1.5 %collective-permute-start.7 = (bf16[2,32,1792]{2,1,0:T(8,128)(2,1)S(1)}, bf16[2,32,1792]{2,1,0:T(8,128)(2,1)S(1)}, u32[]{:S(2)}, u32[]{:S(2)}) collective-permute-start(bf16[2,32,1792]{2,1,0:T(8,128)(2,1)S(1)} %collective-permute-done.1.refs_0_), channel_id=1, source_target_pairs={{0,2},{2,0},{4,6},{6,4},{8,10},{10,8},{12,14},{14,12},{1,3},{3,1},... | collective-permute-start | bytes 688136 | tf_op jit(solution)/shard_map/ppermute | solution.py:23
  20.0 1.4 %collective-permute-start.9 = (bf16[2,32,1792]{2,1,0:T(8,128)(2,1)S(1)}, bf16[2,32,1792]{2,1,0:T(8,128)(2,1)S(1)}, u32[]{:S(2)}, u32[]{:S(2)}) collective-permute-start(bf16[2,32,1792]{2,1,0:T(8,128)(2,1)S(1)} %collective-permute-done.1.refs_0_), channel_id=1, source_target_pairs={{0,4},{2,6},{4,0},{6,2},{8,12},{10,14},{12,8},{14,10},{1,5},{3,7},... | collective-permute-start | bytes 688136 | tf_op jit(solution)/shard_map/ppermute | solution.py:23
  21.5 4.1 %collective-permute-done.7.both_ref.refs_1_ = bf16[2,32,1792]{2,1,0:T(8,128)(2,1)S(1)} collective-permute-done((bf16[2,32,1792]{2,1,0:T(8,128)(2,1)S(1)}, bf16[2,32,1792]{2,1,0:T(8,128)(2,1)S(1)}, u32[]{:S(2)}, u32[]{:S(2)}) %collective-permute-start.7) | collective-permute-done | bytes 229408 | tf_op jit(solution)/shard_map/ppermute | solution.py:23
  25.6 1.6 %collective-permute-start.11 = (bf16[32,1792]{1,0:T(8,128)(2,1)S(1)}, bf16[32,1792]{1,0:T(8,128)(2,1)S(1)}, u32[]{:S(2)}, u32[]{:S(2)}) collective-permute-start(bf16[32,1792]{1,0:T(8,128)(2,1)S(1)} %shard_map.66), channel_id=1, source_target_pairs={{0,4},{2,6},{4,0},{6,2},{8,12},{10,14},{12,8},{14,10},{1,5},{3,7},... | collective-permute-start | bytes 344072 | tf_op jit(solution)/shard_map/ppermute | solution.py:23
  27.1 1.6 %collective-permute-start.10 = (bf16[32,1792]{1,0:T(8,128)(2,1)S(1)}, bf16[32,1792]{1,0:T(8,128)(2,1)S(1)}, u32[]{:S(2)}, u32[]{:S(2)}) collective-permute-start(bf16[32,1792]{1,0:T(8,128)(2,1)S(1)} %shard_map.68), channel_id=1, source_target_pairs={{0,2},{2,0},{4,6},{6,4},{8,10},{10,8},{12,14},{14,12},{1,3},{3,1},... | collective-permute-start | bytes 344072 | tf_op jit(solution)/shard_map/ppermute | solution.py:23
  28.7 1.2 %shard_map.69 = (f32[2,32,1792]{2,1,0:T(8,128)S(1)}, f32[2,32,1792]{2,1,0:T(8,128)S(1)}) custom-call(bf16[2,32,1792]{2,1,0:T(8,128)(2,1)S(1)} %collective-permute-done.1.refs_0_, bf16[2,32,1792]{2,1,0:T(8,128)(2,1)S(1)} %collective-permute-done.7.both_ref.refs_1_, bf16[3584,512]{1,0:T(8,128)(2,1)S(1)} %get-tuple-element.57.refs_4_.refs_2_.refs_3_, ...), custom_call_target="tpu_custom_call" | custom-call | flops 1150000000 | tf_op jit(solution)/shard_map/pallas_call | solution.py:112
  30.4 1.6 %collective-permute-done.10.refs_1_ = bf16[32,1792]{1,0:T(8,128)(2,1)S(1)} collective-permute-done((bf16[32,1792]{1,0:T(8,128)(2,1)S(1)}, bf16[32,1792]{1,0:T(8,128)(2,1)S(1)}, u32[]{:S(2)}, u32[]{:S(2)}) %collective-permute-start.10) | collective-permute-done | bytes 114720 | tf_op jit(solution)/shard_map/ppermute | solution.py:23
  32.0 1.2 %shard_map.70 = (f32[2,32,1792]{2,1,0:T(8,128)S(1)}, bf16[32,1792]{1,0:T(8,128)(2,1)S(1)}, bf16[32,1792]{1,0:T(8,128)(2,1)S(1)}) custom-call(bf16[2,32,1792]{2,1,0:T(8,128)(2,1)S(1)} %collective-permute-done.9.both_ref.refs_0_, bf16[32,1792]{1,0:T(8,128)(2,1)S(1)} %collective-permute-done.10.refs_1_, bf16[32,1792]{1,0:T(8,128)(2,1)S(1)} %collective-permute-done.11.refs_2_, ...), custom_call_target="tpu_custom_call" | custom-call | flops 1150000000 | tf_op jit(solution)/shard_map/pallas_call | solution.py:112
  33.2 1.6 %collective-permute-start.12 = (bf16[32,1792]{1,0:T(8,128)(2,1)S(1)}, bf16[32,1792]{1,0:T(8,128)(2,1)S(1)}, u32[]{:S(2)}, u32[]{:S(2)}) collective-permute-start(bf16[32,1792]{1,0:T(8,128)(2,1)S(1)} %get-tuple-element.67), channel_id=1, source_target_pairs={{0,2},{2,0},{4,6},{6,4},{8,10},{10,8},{12,14},{14,12},{1,3},{3,1},... | collective-permute-start | bytes 344072 | tf_op jit(solution)/shard_map/ppermute | solution.py:23
  35.3 1.2 %collective-permute-start.14 = (bf16[32,1792]{1,0:T(8,128)(2,1)S(1)}, bf16[32,1792]{1,0:T(8,128)(2,1)S(1)}, u32[]{:S(2)}, u32[]{:S(2)}) collective-permute-start(bf16[32,1792]{1,0:T(8,128)(2,1)S(1)} %get-tuple-element.69), channel_id=1, source_target_pairs={{0,4},{2,6},{4,0},{6,2},{8,12},{10,14},{12,8},{14,10},{1,5},{3,7},... | collective-permute-start | bytes 344072 | tf_op jit(solution)/shard_map/ppermute | solution.py:23
  36.5 1.8 %collective-permute-done.12 = bf16[32,1792]{1,0:T(8,128)(2,1)S(1)} collective-permute-done((bf16[32,1792]{1,0:T(8,128)(2,1)S(1)}, bf16[32,1792]{1,0:T(8,128)(2,1)S(1)}, u32[]{:S(2)}, u32[]{:S(2)}) %collective-permute-start.12) | collective-permute-done | bytes 114720 | tf_op jit(solution)/shard_map/ppermute | solution.py:23
  38.3 1.0 %collective-permute-start.13 = (bf16[2,32,1792]{2,1,0:T(8,128)(2,1)S(1)}, bf16[2,32,1792]{2,1,0:T(8,128)(2,1)S(1)}, u32[]{:S(2)}, u32[]{:S(2)}) collective-permute-start(bf16[2,32,1792]{2,1,0:T(8,128)(2,1)S(1)} %pad_maximum_fusion.1), channel_id=1, source_target_pairs={{0,4},{2,6},{4,0},{6,2},{8,12},{10,14},{12,8},{14,10},{1,5},{3,7},... | collective-permute-start | bytes 688136 | tf_op jit(solution)/shard_map/ppermute | solution.py:23
  39.3 1.5 %collective-permute-done.14 = bf16[32,1792]{1,0:T(8,128)(2,1)S(1)} collective-permute-done((bf16[32,1792]{1,0:T(8,128)(2,1)S(1)}, bf16[32,1792]{1,0:T(8,128)(2,1)S(1)}, u32[]{:S(2)}, u32[]{:S(2)}) %collective-permute-start.14) | collective-permute-done | bytes 114720 | tf_op jit(solution)/shard_map/ppermute | solution.py:23
  40.8 1.6 %collective-permute-start.15 = (bf16[2,32,1792]{2,1,0:T(8,128)(2,1)S(1)}, bf16[2,32,1792]{2,1,0:T(8,128)(2,1)S(1)}, u32[]{:S(2)}, u32[]{:S(2)}) collective-permute-start(bf16[2,32,1792]{2,1,0:T(8,128)(2,1)S(1)} %pad_maximum_fusion.2), channel_id=1, source_target_pairs={{0,2},{2,0},{4,6},{6,4},{8,10},{10,8},{12,14},{14,12},{1,3},{3,1},... | collective-permute-start | bytes 688136 | tf_op jit(solution)/shard_map/ppermute | solution.py:23
  42.9 1.0 %shard_map.67 = (f32[2,32,1792]{2,1,0:T(8,128)S(1)}, bf16[2,32,1792]{2,1,0:T(8,128)(2,1)S(1)}, f32[2,32,1792]{2,1,0:T(8,128)S(1)}, bf16[2,32,1792]{2,1,0:T(8,128)(2,1)S(1)}) custom-call(bf16[2,32,1792]{2,1,0:T(8,128)(2,1)S(1)} %pad_maximum_fusion.refs_0_, bf16[2,32,1792]{2,1,0:T(8,128)(2,1)S(1)} %collective-permute-done.4.refs_1_, ...), custom_call_target="tpu_custom_call" | custom-call | flops 1150000000 | tf_op jit(solution)/shard_map/pallas_call | solution.py:112
  43.9 1.3 %collective-permute-start.17 = (bf16[2,32,1792]{2,1,0:T(8,128)(2,1)S(1)}, bf16[2,32,1792]{2,1,0:T(8,128)(2,1)S(1)}, u32[]{:S(2)}, u32[]{:S(2)}) collective-permute-start(bf16[2,32,1792]{2,1,0:T(8,128)(2,1)S(1)} %get-tuple-element.73), channel_id=1, source_target_pairs={{0,2},{2,0},{4,6},{6,4},{8,10},{10,8},{12,14},{14,12},{1,3},{3,1},... | collective-permute-start | bytes 688136 | tf_op jit(solution)/shard_map/ppermute | solution.py:23
  45.3 2.8 %collective-permute-done.15 = bf16[2,32,1792]{2,1,0:T(8,128)(2,1)S(1)} collective-permute-done((bf16[2,32,1792]{2,1,0:T(8,128)(2,1)S(1)}, bf16[2,32,1792]{2,1,0:T(8,128)(2,1)S(1)}, u32[]{:S(2)}, u32[]{:S(2)}) %collective-permute-start.15) | collective-permute-done | bytes 229408 | tf_op jit(solution)/shard_map/ppermute | solution.py:23
  48.2 3.4 %collective-permute-start.19 = (bf16[2,32,1792]{2,1,0:T(8,128)(2,1)S(1)}, bf16[2,32,1792]{2,1,0:T(8,128)(2,1)S(1)}, u32[]{:S(2)}, u32[]{:S(2)}) collective-permute-start(bf16[2,32,1792]{2,1,0:T(8,128)(2,1)S(1)} %add_convert_fusion), channel_id=1, source_target_pairs={{0,8},{2,10},{4,12},{6,14},{8,0},{10,2},{12,4},{14,6},{1,9},{3,11}... | collective-permute-start | bytes 688136 | tf_op jit(solution)/shard_map/ppermute | solution.py:23
  51.6 1.2 %collective-permute-start.18 = (bf16[2,32,1792]{2,1,0:T(8,128)(2,1)S(1)}, bf16[2,32,1792]{2,1,0:T(8,128)(2,1)S(1)}, u32[]{:S(2)}, u32[]{:S(2)}) collective-permute-start(bf16[2,32,1792]{2,1,0:T(8,128)(2,1)S(1)} %shard_map.71), channel_id=1, source_target_pairs={{0,4},{2,6},{4,0},{6,2},{8,12},{10,14},{12,8},{14,10},{1,5},{3,7},... | collective-permute-start | bytes 688136 | tf_op jit(solution)/shard_map/ppermute | solution.py:23
  53.4 4.7 %collective-permute-done.19.sum_ref = bf16[2,32,1792]{2,1,0:T(8,128)(2,1)S(1)} collective-permute-done((bf16[2,32,1792]{2,1,0:T(8,128)(2,1)S(1)}, bf16[2,32,1792]{2,1,0:T(8,128)(2,1)S(1)}, u32[]{:S(2)}, u32[]{:S(2)}) %collective-permute-start.19) | collective-permute-done | bytes 229408 | tf_op jit(solution)/shard_map/ppermute | solution.py:23
  58.1 0.6 collective-permute-done.18
  59.0 1.3 %collective-permute-done.20 = bf16[32,1792]{1,0:T(8,128)(2,1)S(1)} collective-permute-done((bf16[32,1792]{1,0:T(8,128)(2,1)S(1)}, bf16[32,1792]{1,0:T(8,128)(2,1)S(1)}, u32[]{:S(2)}, u32[]{:S(2)}) %collective-permute-start.20) | collective-permute-done | bytes 114720 | tf_op jit(solution)/shard_map/ppermute | solution.py:32
  60.4 0.7 %pad_maximum_fusion.3 = bf16[64,1792]{1,0:T(8,128)(2,1)} fusion(bf16[32,1792]{1,0:T(8,128)(2,1)S(1)} %get-tuple-element.76, bf16[32,1792]{1,0:T(8,128)(2,1)S(1)} %get-tuple-element.75), kind=kLoop, calls=%fused_computation.7 | loop fusion | flops 458752 | bytes 458752 | tf_op jit(solution)/shard_map/concatenate | solution.py:258
  (44 shorter events, 5.6 us)
Async XLA Ops:
  1.0 1.5 %collective-permute-start = (bf16[32,1792]{1,0:T(8,128)(2,1)S(1)}, bf16[32,1792]{1,0:T(8,128)(2,1)S(1)}, u32[]{:S(2)}, u32[]{:S(2)}) collective-permute-start(bf16[32,1792]{1,0:T(8,128)(2,1)S(1)} %get-tuple-element.42), channel_id=1, source_target_pairs={{0,1},{1,0},{2,3},{3,2},{4,5},{5,4},{6,7},{7,6},{8,9},{9,8},{10,11... | collective-permute-start | bytes 344072 | tf_op jit(solution)/shard_map/ppermute | solution.py:32
  2.5 6.3 %collective-permute-start.3 = (bf16[3584,128]{1,0:T(8,128)(2,1)}, bf16[3584,128]{1,0:T(8,128)(2,1)S(1)}, u32[]{:S(2)}, u32[]{:S(2)}) collective-permute-start(bf16[3584,128]{1,0:T(8,128)(2,1)} %bitcast.33), channel_id=1, source_target_pairs={{0,1},{1,0},{2,3},{3,2},{4,5},{5,4},{6,7},{7,6},{8,9},{9,8},{10,11... | collective-permute-start | bytes 2752520 | tf_op jit(solution)/shard_map/ppermute | solution.py:32
  2.8 11.5 %collective-permute-start.5 = (bf16[3584,128]{1,0:T(8,128)(2,1)}, bf16[3584,128]{1,0:T(8,128)(2,1)S(1)}, u32[]{:S(2)}, u32[]{:S(2)}) collective-permute-start(bf16[3584,128]{1,0:T(8,128)(2,1)} %bitcast.35), channel_id=1, source_target_pairs={{0,1},{1,0},{2,3},{3,2},{4,5},{5,4},{6,7},{7,6},{8,9},{9,8},{10,11... | collective-permute-start | bytes 2752520 | tf_op jit(solution)/shard_map/ppermute | solution.py:32
  3.0 11.4 %collective-permute-start.6 = (bf16[128,3584]{1,0:T(8,128)(2,1)}, bf16[128,3584]{1,0:T(8,128)(2,1)S(1)}, u32[]{:S(2)}, u32[]{:S(2)}) collective-permute-start(bf16[128,3584]{1,0:T(8,128)(2,1)} %bitcast.37), channel_id=1, source_target_pairs={{0,1},{1,0},{2,3},{3,2},{4,5},{5,4},{6,7},{7,6},{8,9},{9,8},{10,11... | collective-permute-start | bytes 2752520 | tf_op jit(solution)/shard_map/ppermute | solution.py:32
  3.4 14.9 %collective-permute-start.1 = (bf16[2,32,1792]{2,1,0:T(8,128)(2,1)S(1)}, bf16[2,32,1792]{2,1,0:T(8,128)(2,1)S(1)}, u32[]{:S(2)}, u32[]{:S(2)}) collective-permute-start(bf16[2,32,1792]{2,1,0:T(8,128)(2,1)S(1)} %pad_maximum_fusion.refs_0_), channel_id=1, source_target_pairs={{0,8},{2,10},{4,12},{6,14},{8,0},{10,2},{12,4},{14,6},{1,9},{3,11}... | collective-permute-start | bytes 688136 | tf_op jit(solution)/shard_map/ppermute | solution.py:23
  7.2 11.3 %collective-permute-start.2 = (bf16[2,32,1792]{2,1,0:T(8,128)(2,1)S(1)}, bf16[2,32,1792]{2,1,0:T(8,128)(2,1)S(1)}, u32[]{:S(2)}, u32[]{:S(2)}) collective-permute-start(bf16[2,32,1792]{2,1,0:T(8,128)(2,1)S(1)} %pad_maximum_fusion.refs_0_), channel_id=1, source_target_pairs={{0,4},{2,6},{4,0},{6,2},{8,12},{10,14},{12,8},{14,10},{1,5},{3,7},... | collective-permute-start | bytes 688136 | tf_op jit(solution)/shard_map/ppermute | solution.py:23
  8.8 9.7 %collective-permute-start.4 = (bf16[2,32,1792]{2,1,0:T(8,128)(2,1)S(1)}, bf16[2,32,1792]{2,1,0:T(8,128)(2,1)S(1)}, u32[]{:S(2)}, u32[]{:S(2)}) collective-permute-start(bf16[2,32,1792]{2,1,0:T(8,128)(2,1)S(1)} %pad_maximum_fusion.refs_0_), channel_id=1, source_target_pairs={{0,2},{2,0},{4,6},{6,4},{8,10},{10,8},{12,14},{14,12},{1,3},{3,1},... | collective-permute-start | bytes 688136 | tf_op jit(solution)/shard_map/ppermute | solution.py:23
  10.2 1.2 %copy-start = (bf16[1,3584,128]{2,1,0:T(8,128)(2,1)S(1)}, bf16[1,3584,128]{2,1,0:T(8,128)(2,1)}, u32[]{:S(2)}) copy-start(bf16[1,3584,128]{2,1,0:T(8,128)(2,1)} %param.9) | copy-start | bytes 2752516
  11.4 1.2 %copy-start.1 = (bf16[1,3584,128]{2,1,0:T(8,128)(2,1)S(1)}, bf16[1,3584,128]{2,1,0:T(8,128)(2,1)}, u32[]{:S(2)}) copy-start(bf16[1,3584,128]{2,1,0:T(8,128)(2,1)} %param.10) | copy-start | bytes 2752516
  12.6 1.2 %copy-start.2 = (bf16[1,128,3584]{2,1,0:T(8,128)(2,1)S(1)}, bf16[1,128,3584]{2,1,0:T(8,128)(2,1)}, u32[]{:S(2)}) copy-start(bf16[1,128,3584]{2,1,0:T(8,128)(2,1)} %param.11) | copy-start | bytes 2752516
  18.5 7.0 %collective-permute-start.7 = (bf16[2,32,1792]{2,1,0:T(8,128)(2,1)S(1)}, bf16[2,32,1792]{2,1,0:T(8,128)(2,1)S(1)}, u32[]{:S(2)}, u32[]{:S(2)}) collective-permute-start(bf16[2,32,1792]{2,1,0:T(8,128)(2,1)S(1)} %collective-permute-done.1.refs_0_), channel_id=1, source_target_pairs={{0,2},{2,0},{4,6},{6,4},{8,10},{10,8},{12,14},{14,12},{1,3},{3,1},... | collective-permute-start | bytes 688136 | tf_op jit(solution)/shard_map/ppermute | solution.py:23
  20.0 7.1 %collective-permute-start.9 = (bf16[2,32,1792]{2,1,0:T(8,128)(2,1)S(1)}, bf16[2,32,1792]{2,1,0:T(8,128)(2,1)S(1)}, u32[]{:S(2)}, u32[]{:S(2)}) collective-permute-start(bf16[2,32,1792]{2,1,0:T(8,128)(2,1)S(1)} %collective-permute-done.1.refs_0_), channel_id=1, source_target_pairs={{0,4},{2,6},{4,0},{6,2},{8,12},{10,14},{12,8},{14,10},{1,5},{3,7},... | collective-permute-start | bytes 688136 | tf_op jit(solution)/shard_map/ppermute | solution.py:23
  25.6 4.9 %collective-permute-start.11 = (bf16[32,1792]{1,0:T(8,128)(2,1)S(1)}, bf16[32,1792]{1,0:T(8,128)(2,1)S(1)}, u32[]{:S(2)}, u32[]{:S(2)}) collective-permute-start(bf16[32,1792]{1,0:T(8,128)(2,1)S(1)} %shard_map.66), channel_id=1, source_target_pairs={{0,4},{2,6},{4,0},{6,2},{8,12},{10,14},{12,8},{14,10},{1,5},{3,7},... | collective-permute-start | bytes 344072 | tf_op jit(solution)/shard_map/ppermute | solution.py:23
  27.1 4.9 %collective-permute-start.10 = (bf16[32,1792]{1,0:T(8,128)(2,1)S(1)}, bf16[32,1792]{1,0:T(8,128)(2,1)S(1)}, u32[]{:S(2)}, u32[]{:S(2)}) collective-permute-start(bf16[32,1792]{1,0:T(8,128)(2,1)S(1)} %shard_map.68), channel_id=1, source_target_pairs={{0,2},{2,0},{4,6},{6,4},{8,10},{10,8},{12,14},{14,12},{1,3},{3,1},... | collective-permute-start | bytes 344072 | tf_op jit(solution)/shard_map/ppermute | solution.py:23
  32.0 10.4 %copy-start.3 = (s32[64,1]{0,1:T(1,128)S(1)}, s32[64,1]{0,1:T(1,128)}, u32[]{:S(2)}) copy-start(s32[64,1]{0,1:T(1,128)} %param.8) | copy-start | bytes 772
  33.2 5.1 %collective-permute-start.12 = (bf16[32,1792]{1,0:T(8,128)(2,1)S(1)}, bf16[32,1792]{1,0:T(8,128)(2,1)S(1)}, u32[]{:S(2)}, u32[]{:S(2)}) collective-permute-start(bf16[32,1792]{1,0:T(8,128)(2,1)S(1)} %get-tuple-element.67), channel_id=1, source_target_pairs={{0,2},{2,0},{4,6},{6,4},{8,10},{10,8},{12,14},{14,12},{1,3},{3,1},... | collective-permute-start | bytes 344072 | tf_op jit(solution)/shard_map/ppermute | solution.py:23
  34.7 8.2 %collective-permute-start.8 = (bf16[2,32,1792]{2,1,0:T(8,128)(2,1)S(1)}, bf16[2,32,1792]{2,1,0:T(8,128)(2,1)S(1)}, u32[]{:S(2)}, u32[]{:S(2)}) collective-permute-start(bf16[2,32,1792]{2,1,0:T(8,128)(2,1)S(1)} %collective-permute-done.2.refs_2_), channel_id=1, source_target_pairs={{0,2},{2,0},{4,6},{6,4},{8,10},{10,8},{12,14},{14,12},{1,3},{3,1},... | collective-permute-start | bytes 688136 | tf_op jit(solution)/shard_map/ppermute | solution.py:23
  35.3 5.5 %collective-permute-start.14 = (bf16[32,1792]{1,0:T(8,128)(2,1)S(1)}, bf16[32,1792]{1,0:T(8,128)(2,1)S(1)}, u32[]{:S(2)}, u32[]{:S(2)}) collective-permute-start(bf16[32,1792]{1,0:T(8,128)(2,1)S(1)} %get-tuple-element.69), channel_id=1, source_target_pairs={{0,4},{2,6},{4,0},{6,2},{8,12},{10,14},{12,8},{14,10},{1,5},{3,7},... | collective-permute-start | bytes 344072 | tf_op jit(solution)/shard_map/ppermute | solution.py:23
  38.3 7.0 %collective-permute-start.13 = (bf16[2,32,1792]{2,1,0:T(8,128)(2,1)S(1)}, bf16[2,32,1792]{2,1,0:T(8,128)(2,1)S(1)}, u32[]{:S(2)}, u32[]{:S(2)}) collective-permute-start(bf16[2,32,1792]{2,1,0:T(8,128)(2,1)S(1)} %pad_maximum_fusion.1), channel_id=1, source_target_pairs={{0,4},{2,6},{4,0},{6,2},{8,12},{10,14},{12,8},{14,10},{1,5},{3,7},... | collective-permute-start | bytes 688136 | tf_op jit(solution)/shard_map/ppermute | solution.py:23
  40.8 7.3 %collective-permute-start.15 = (bf16[2,32,1792]{2,1,0:T(8,128)(2,1)S(1)}, bf16[2,32,1792]{2,1,0:T(8,128)(2,1)S(1)}, u32[]{:S(2)}, u32[]{:S(2)}) collective-permute-start(bf16[2,32,1792]{2,1,0:T(8,128)(2,1)S(1)} %pad_maximum_fusion.2), channel_id=1, source_target_pairs={{0,2},{2,0},{4,6},{6,4},{8,10},{10,8},{12,14},{14,12},{1,3},{3,1},... | collective-permute-start | bytes 688136 | tf_op jit(solution)/shard_map/ppermute | solution.py:23
  42.5 10.9 %copy-start.4 = (s32[64,1]{0,1:T(1,128)S(1)}, s32[64,1]{0,1:T(1,128)}, u32[]{:S(2)}) copy-start(s32[64,1]{0,1:T(1,128)} %param.7) | copy-start | bytes 772
  43.9 7.6 %collective-permute-start.17 = (bf16[2,32,1792]{2,1,0:T(8,128)(2,1)S(1)}, bf16[2,32,1792]{2,1,0:T(8,128)(2,1)S(1)}, u32[]{:S(2)}, u32[]{:S(2)}) collective-permute-start(bf16[2,32,1792]{2,1,0:T(8,128)(2,1)S(1)} %get-tuple-element.73), channel_id=1, source_target_pairs={{0,2},{2,0},{4,6},{6,4},{8,10},{10,8},{12,14},{14,12},{1,3},{3,1},... | collective-permute-start | bytes 688136 | tf_op jit(solution)/shard_map/ppermute | solution.py:23
  48.2 9.9 %collective-permute-start.19 = (bf16[2,32,1792]{2,1,0:T(8,128)(2,1)S(1)}, bf16[2,32,1792]{2,1,0:T(8,128)(2,1)S(1)}, u32[]{:S(2)}, u32[]{:S(2)}) collective-permute-start(bf16[2,32,1792]{2,1,0:T(8,128)(2,1)S(1)} %add_convert_fusion), channel_id=1, source_target_pairs={{0,8},{2,10},{4,12},{6,14},{8,0},{10,2},{12,4},{14,6},{1,9},{3,11}... | collective-permute-start | bytes 688136 | tf_op jit(solution)/shard_map/ppermute | solution.py:23
  51.6 7.2 %collective-permute-start.18 = (bf16[2,32,1792]{2,1,0:T(8,128)(2,1)S(1)}, bf16[2,32,1792]{2,1,0:T(8,128)(2,1)S(1)}, u32[]{:S(2)}, u32[]{:S(2)}) collective-permute-start(bf16[2,32,1792]{2,1,0:T(8,128)(2,1)S(1)} %shard_map.71), channel_id=1, source_target_pairs={{0,4},{2,6},{4,0},{6,2},{8,12},{10,14},{12,8},{14,10},{1,5},{3,7},... | collective-permute-start | bytes 688136 | tf_op jit(solution)/shard_map/ppermute | solution.py:23
  52.8 6.0 %collective-permute-start.16 = (bf16[2,32,1792]{2,1,0:T(8,128)(2,1)S(1)}, bf16[2,32,1792]{2,1,0:T(8,128)(2,1)S(1)}, u32[]{:S(2)}, u32[]{:S(2)}) collective-permute-start(bf16[2,32,1792]{2,1,0:T(8,128)(2,1)S(1)} %get-tuple-element.71), channel_id=1, source_target_pairs={{0,2},{2,0},{4,6},{6,4},{8,10},{10,8},{12,14},{14,12},{1,3},{3,1},... | collective-permute-start | bytes 688136 | tf_op jit(solution)/shard_map/ppermute | solution.py:23
  59.0 1.4 %collective-permute-start.20 = (bf16[32,1792]{1,0:T(8,128)(2,1)S(1)}, bf16[32,1792]{1,0:T(8,128)(2,1)S(1)}, u32[]{:S(2)}, u32[]{:S(2)}) collective-permute-start(bf16[32,1792]{1,0:T(8,128)(2,1)S(1)} %slice_bitcast_fusion), channel_id=1, source_target_pairs={{0,1},{1,0},{2,3},{3,2},{4,5},{5,4},{6,7},{7,6},{8,9},{9,8},{10,11... | collective-permute-start | bytes 344072 | tf_op jit(solution)/shard_map/ppermute | solution.py:32

commit v4 on v3

--- a/solution.py
+++ b/solution.py
@@ -32,35 +32,29 @@
     return lax.ppermute(value, "tp", [(0, 1), (1, 0)])
 
 
-def pack_kernel(turn, *refs):
-    w_in, w_out, sems = refs[-3:]
-    units = refs[0].shape[1]
-    gate, up = (w_in.at[:, i * units : (i + 1) * units] for i in (turn, 2 + turn))
-    down = w_out.at[turn * units : (turn + 1) * units]
-    copies = [
-        pltpu.make_async_copy(ref, place, sems.at[i])
-        for i, (ref, place) in enumerate(zip(refs[:3], (gate, up, down)))
-    ]
+def pack_kernel(gate_ref, up_ref, down_ref, pack_ref, sems):
+    depth, units = gate_ref.shape
+    pairs = [(gate_ref, pack_ref.at[:, :units]), (up_ref, pack_ref.at[:, units : 2 * units])]
+    for at in range(0, depth, units):
+        pairs.append((down_ref.at[:, at : at + units], pack_ref.at[at : at + units, 2 * units :]))
+    copies = [pltpu.make_async_copy(*pair, sems.at[i]) for i, pair in enumerate(pairs)]
     for copy in copies:
         copy.start()
     for copy in copies:
         copy.wait()
 
 
-def pack(turn, parts, held=()):
-    depth, units = parts[0].shape
-    return pl.pallas_call(
-        functools.partial(pack_kernel, turn),
-        out_shape=[
-            jax.ShapeDtypeStruct((depth, 4 * units), parts[0].dtype),
-            jax.ShapeDtypeStruct((2 * units, depth), parts[0].dtype),
-        ],
-        in_specs=[pl.BlockSpec(memory_space=pl.ANY)] * 3 + [VMEM] * len(held),
-        out_specs=[VMEM] * 2,
-        scratch_shapes=[pltpu.SemaphoreType.DMA((3,))],
-        input_output_aliases={3 + i: i for i in range(len(held))},
-        compiler_params=pltpu.CompilerParams(vmem_limit_bytes=24 * 1024 * 1024),
-    )(*parts, *held)
+def pack(gate, up, down):
+    depth, units = gate.shape
+    return pl.pallas_call(
+        pack_kernel,
+        out_shape=jax.ShapeDtypeStruct((depth, 3 * units), gate.dtype),
+        in_specs=[pl.BlockSpec(memory_space=pl.ANY)] * 3,
+        out_specs=VMEM,
+        scratch_shapes=[pltpu.SemaphoreType.DMA((2 + depth // units,))],
+        cost_estimate=pl.CostEstimate(flops=int(2 * FLOPS_US), bytes_accessed=0, transcendentals=0),
+        compiler_params=pltpu.CompilerParams(vmem_limit_bytes=8 * 1024 * 1024),
+    )(gate, up, down)
 
 
 def expert_kernel(blocks_in, blocks_out, *refs):
@@ -73,7 +67,7 @@
         return held if len(held) == 2 else (held[0].at[0], held[0].at[1])
 
     blocks = [parts(take(block)) for block in blocks_in]
-    w_in, w_out = take((None, None))
+    packs = take((None, None))
     sums = [parts(take(block)) for block in blocks_out]
     rows, width = blocks[0][0].shape
     first = lax.axis_index("tp") == 0
@@ -82,11 +76,17 @@
         whole = jnp.concatenate(
             [jnp.concatenate([block[i][...] for block in blocks], axis=0) for i in order], axis=1
         )
-        act = jnp.dot(whole, w_in[...], preferred_element_type=jnp.float32)
-        units = act.shape[1] // 2
-        gate, up = act[:, :units], act[:, units:]
-        hidden = (gate / (1 + jnp.exp(-gate)) * up).astype(jnp.bfloat16)
-        out = jnp.dot(hidden, w_out[...], preferred_element_type=jnp.float32)
+        out = None
+        for held in packs:
+            depth, units = held.shape[0], held.shape[1] // 3
+            act = jnp.dot(whole, held[:, : 2 * units], preferred_element_type=jnp.float32)
+            w_out = jnp.concatenate(
+                [held[at : at + units, 2 * units :] for at in range(0, depth, units)], axis=1
+            )
+            gate, up = act[:, :units], act[:, units:]
+            hidden = (gate / (1 + jnp.exp(-gate)) * up).astype(jnp.bfloat16)
+            part = jnp.dot(hidden, w_out, preferred_element_type=jnp.float32)
+            out = part if out is None else out + part
         for place, i in enumerate(order):
             for j, held in enumerate(sums):
                 part = out[j * rows : (j + 1) * rows, place * width : (place + 1) * width]
@@ -138,21 +138,21 @@
     )(both)
 
 
-def widen_kernel(sum_ref, out_ref):
-    out_ref[...] = sum_ref[...].astype(jnp.float32)
-
-
-def widen(sums, work):
-    return pl.pallas_call(
-        widen_kernel,
-        out_shape=jax.ShapeDtypeStruct(sums.shape, jnp.float32),
+def cast_kernel(from_ref, to_ref):
+    to_ref[...] = from_ref[...].astype(to_ref.dtype)
+
+
+def cast(array, dtype, work):
+    return pl.pallas_call(
+        cast_kernel,
+        out_shape=jax.ShapeDtypeStruct(array.shape, dtype),
         in_specs=[VMEM],
         out_specs=VMEM,
         cost_estimate=pl.CostEstimate(
             flops=int(work * FLOPS_US), bytes_accessed=0, transcendentals=0
         ),
         compiler_params=pltpu.CompilerParams(vmem_limit_bytes=4 * 1024 * 1024),
-    )(sums)
+    )(array)
 
 
 def add_kernel(one_ref, two_ref, out_ref):
@@ -206,45 +206,42 @@
         (jnp.where(first, top, bottom), jnp.where(first, bottom, top), lax.axis_index("ep"))
     )
     b0 = swap_core(b0)
-    b0, own = tie((b0, (w_gate[0], w_up[0], w_down[0])))
-    theirs = tuple(swap_core(w) for w in own)
+    ours = pack(w_gate[0], w_up[0], w_down[0])
 
     def expert(blocks, types, work=1.0):
         return expert_block(blocks, weights, types, work)
 
     both0 = jnp.stack([a0, b0])
-    one, two, three = theirs
     z2 = swap(both0, 4)
     z1 = swap(both0, 2)
-    held, one = tie((both0, one))
-    x0 = swap(held, 1)
-    packed = pack(0, own)
-    weights = pack(1, (one, two, three), packed)
-    z2, z1, x0, weights = tie((z2, z1, x0, weights))
+    x0 = swap(both0, 1)
+    z2, z1, x0, ours = tie((z2, z1, x0, ours))
+    weights = [ours, swap_core(ours)]
     m6 = swap(z2, 2)
     m5 = swap(z2, 1)
-    h6, h5 = part_of(m6, 0), part_of(m5, 1)
-    z1, h5 = tie((z1, h5))
-    m7a = swap(h6, 1)
-    m7b = swap(h5, 2)
-    m3 = swap(z1, 1)
+    m6a, m5b = part_of(m6, 0), part_of(m5, 1)
+    m5b, held = tie((m5b, x0))
+    m3 = swap(held, 2)
+    m7a = swap(m6a, 1)
+    m7b = swap(m5b, 2)
     p4, p5 = expert(((z2,), (m5,)), ((f32,), (f32,)))
     m7a, m7b, p4, p5 = tie((m7a, m7b, p4, p5))
     p6, p7a, p7b = expert(((m6,), (m7a, m7b)), ((f32,), (bf16, bf16)))
     p0, p1, p2, p3 = expert(
         ((both0,), (x0,), (z1,), (m3,)), ((f32,), (bf16,), (f32,), (bf16,)), 1.0
     )
-    r7a = swap(p7a, 1).astype(f32)
-    r7b = swap(p7b, 2).astype(f32)
-    s6 = jnp.stack([p6[0] + r7a, p6[1]]).astype(bf16)
-    s5 = jnp.stack([p5[0], p5[1] + r7b]).astype(bf16)
+    r7a = swap(p7a, 1)
+    r7b = swap(p7b, 2)
+    r7a, p1, p2, p3 = tie((r7a, p1, p2, p3))
+    s6 = jnp.stack([p6[0] + r7a.astype(f32), p6[1]]).astype(bf16)
+    s5 = jnp.stack([p5[0], p5[1] + r7b.astype(f32)]).astype(bf16)
     r6 = swap(s6, 2).astype(f32)
     r5 = swap(s5, 1).astype(f32)
     sent = (p4 + r6 + r5).astype(bf16)
     r3 = swap(p3, 1)
     s2 = add(p2, r3, 0.1)
     sent, p1 = tie((sent, p1))
-    other = widen(swap(sent, 4), 0.5)
+    other = cast(swap(sent, 4), f32, 0.5)
     r2 = swap(s2, 2)
     r1 = swap(p1, 1)
     near = p0 + r1.astype(f32) + r2.astype(f32)

time: 61.3 us -> 60.2 us (0.982)
  starting transfers between devices: 26.7 us -> 25.3 us
    ppermute x5 -> x3, starting transfers between devices: 1.46 us -> 0.59 us  [swap_core(): return lax.ppermute(value, 'tp', [(0, 1), (1, 0)])]
    ppermute x5 -> x3, waiting for transfers between devices: 2.28 us -> 2.28 us  [swap_core(): return lax.ppermute(value, 'tp', [(0, 1), (1, 0)])]
  transfers between devices with their start and end apart: 21 -> 19, of which waited for: 14 -> 13; matrix products, arithmetic and copies ran while one was open for 1% -> 1% of each run, Pallas kernels for 6% -> 7%
where the time goes in v4:
time: 60.2 us; the launch traced here: 60 us
  starting transfers between devices  25.3 us (42%)
  waiting for transfers between devices  24.3 us (40%)
  Pallas kernels  4.41 us (7%)
  local copies, waits for them, and re-layouts  3.58 us (6%)
  other arithmetic  2.16 us (4%)
    ppermute x16, starting transfers between devices, swap(): return lax.ppermute(value, 'ep', pairs)  24.7 us
    ppermute x16, waiting for transfers between devices, swap(): return lax.ppermute(value, 'ep', pairs)  22 us
    unnamed x10, local copies, waits for them, and re-layouts  3.55 us
    pallas_call x3, Pallas kernels, expert_block(): pl.pallas_call(functools.partial(expert_kernel, [(None,) * len(b) for b i...  3.51 us
    ppermute x3, waiting for transfers between devices, swap_core(): return lax.ppermute(value, 'tp', [(0, 1), (1, 0)])  2.28 us
  transfers between devices with their start and end apart: 19, of which 13 were waited for; matrix products, arithmetic and copies ran while one was open for 1% of the time, Pallas kernels for 7%

profile of v4, /device:TPU:0, one launch (start us, length us, event | category | flops | bytes accessed | tf_op | source)
XLA Modules:
  0.0 60.0 jit_solution(15324379719602104038)
XLA Ops:
  0.0 1.0 %broadcast_select_fusion.2 = (bf16[32,1792]{1,0:T(8,128)(2,1)S(1)}, bf16[32,1792]{1,0:T(8,128)(2,1)S(1)}) fusion(pred[]{:T(512)S(6)} %eq.3, bf16[64,1792]{1,0:T(8,128)(2,1)} %param.6), kind=kLoop, calls=%fused_computation.18 | loop fusion | flops 114688 | bytes 458753 | tf_op jit(solution)/shard_map/jit(_where)/select_n | solution.py:206
  1.5 1.0 %collective-permute-done = bf16[32,1792]{1,0:T(8,128)(2,1)S(1)} collective-permute-done((bf16[32,1792]{1,0:T(8,128)(2,1)S(1)}, bf16[32,1792]{1,0:T(8,128)(2,1)S(1)}, u32[]{:S(2)}, u32[]{:S(2)}) %collective-permute-start) | collective-permute-done | bytes 114720 | tf_op jit(solution)/shard_map/ppermute | solution.py:32
  2.5 4.0 %collective-permute-start.1 = (bf16[2,32,1792]{2,1,0:T(8,128)(2,1)S(1)}, bf16[2,32,1792]{2,1,0:T(8,128)(2,1)S(1)}, u32[]{:S(2)}, u32[]{:S(2)}) collective-permute-start(bf16[2,32,1792]{2,1,0:T(8,128)(2,1)S(1)} %pad_maximum_fusion.refs_0_), channel_id=1, source_target_pairs={{0,8},{2,10},{4,12},{6,14},{8,0},{10,2},{12,4},{14,6},{1,9},{3,11}... | collective-permute-start | bytes 688136 | tf_op jit(solution)/shard_map/ppermute | solution.py:23
  6.5 1.6 %collective-permute-start.2 = (bf16[2,32,1792]{2,1,0:T(8,128)(2,1)S(1)}, bf16[2,32,1792]{2,1,0:T(8,128)(2,1)S(1)}, u32[]{:S(2)}, u32[]{:S(2)}) collective-permute-start(bf16[2,32,1792]{2,1,0:T(8,128)(2,1)S(1)} %pad_maximum_fusion.refs_0_), channel_id=1, source_target_pairs={{0,4},{2,6},{4,0},{6,2},{8,12},{10,14},{12,8},{14,10},{1,5},{3,7},... | collective-permute-start | bytes 688136 | tf_op jit(solution)/shard_map/ppermute | solution.py:23
  8.1 1.5 %collective-permute-start.3 = (bf16[2,32,1792]{2,1,0:T(8,128)(2,1)S(1)}, bf16[2,32,1792]{2,1,0:T(8,128)(2,1)S(1)}, u32[]{:S(2)}, u32[]{:S(2)}) collective-permute-start(bf16[2,32,1792]{2,1,0:T(8,128)(2,1)S(1)} %pad_maximum_fusion.refs_0_), channel_id=1, source_target_pairs={{0,2},{2,0},{4,6},{6,4},{8,10},{10,8},{12,14},{14,12},{1,3},{3,1},... | collective-permute-start | bytes 688136 | tf_op jit(solution)/shard_map/ppermute | solution.py:23
  9.6 1.2 %copy-done = bf16[1,3584,128]{2,1,0:T(8,128)(2,1)S(1)} copy-done((bf16[1,3584,128]{2,1,0:T(8,128)(2,1)S(1)}, bf16[1,3584,128]{2,1,0:T(8,128)(2,1)}, u32[]{:S(2)}) %copy-start) | copy-done | bytes 917528
  10.7 1.2 %copy-done.1 = bf16[1,3584,128]{2,1,0:T(8,128)(2,1)S(1)} copy-done((bf16[1,3584,128]{2,1,0:T(8,128)(2,1)S(1)}, bf16[1,3584,128]{2,1,0:T(8,128)(2,1)}, u32[]{:S(2)}) %copy-start.1) | copy-done | bytes 917528
  11.9 1.2 %copy-done.2 = bf16[1,128,3584]{2,1,0:T(8,128)(2,1)S(1)} copy-done((bf16[1,128,3584]{2,1,0:T(8,128)(2,1)S(1)}, bf16[1,128,3584]{2,1,0:T(8,128)(2,1)}, u32[]{:S(2)}) %copy-start.2) | copy-done | bytes 917528
  13.1 0.8 %shard_map.64.refs_4_.refs_2_.refs_3_ = bf16[3584,384]{1,0:T(8,128)(2,1)S(1)} custom-call(bf16[3584,128]{1,0:T(8,128)(2,1)S(1)} %bitcast.33, bf16[3584,128]{1,0:T(8,128)(2,1)S(1)} %bitcast.34, bf16[128,3584]{1,0:T(8,128)(2,1)S(1)} %bitcast.35), custom_call_target="tpu_custom_call" | custom-call | flops 2300000000 | tf_op jit(solution)/shard_map/pallas_call | solution.py:49
  13.9 3.5 %collective-permute-done.1.refs_0_ = bf16[2,32,1792]{2,1,0:T(8,128)(2,1)S(1)} collective-permute-done((bf16[2,32,1792]{2,1,0:T(8,128)(2,1)S(1)}, bf16[2,32,1792]{2,1,0:T(8,128)(2,1)S(1)}, u32[]{:S(2)}, u32[]{:S(2)}) %collective-permute-start.1) | collective-permute-done | bytes 229408 | tf_op jit(solution)/shard_map/ppermute | solution.py:23
  17.6 1.5 %collective-permute-start.4 = (bf16[2,32,1792]{2,1,0:T(8,128)(2,1)S(1)}, bf16[2,32,1792]{2,1,0:T(8,128)(2,1)S(1)}, u32[]{:S(2)}, u32[]{:S(2)}) collective-permute-start(bf16[2,32,1792]{2,1,0:T(8,128)(2,1)S(1)} %collective-permute-done.1.refs_0_), channel_id=1, source_target_pairs={{0,2},{2,0},{4,6},{6,4},{8,10},{10,8},{12,14},{14,12},{1,3},{3,1},... | collective-permute-start | bytes 688136 | tf_op jit(solution)/shard_map/ppermute | solution.py:23
  19.2 1.4 %collective-permute-start.7 = (bf16[2,32,1792]{2,1,0:T(8,128)(2,1)S(1)}, bf16[2,32,1792]{2,1,0:T(8,128)(2,1)S(1)}, u32[]{:S(2)}, u32[]{:S(2)}) collective-permute-start(bf16[2,32,1792]{2,1,0:T(8,128)(2,1)S(1)} %collective-permute-done.1.refs_0_), channel_id=1, source_target_pairs={{0,4},{2,6},{4,0},{6,2},{8,12},{10,14},{12,8},{14,10},{1,5},{3,7},... | collective-permute-start | bytes 688136 | tf_op jit(solution)/shard_map/ppermute | solution.py:23
  20.6 5.0 %collective-permute-done.4.both_ref.refs_1_ = bf16[2,32,1792]{2,1,0:T(8,128)(2,1)S(1)} collective-permute-done((bf16[2,32,1792]{2,1,0:T(8,128)(2,1)S(1)}, bf16[2,32,1792]{2,1,0:T(8,128)(2,1)S(1)}, u32[]{:S(2)}, u32[]{:S(2)}) %collective-permute-start.4) | collective-permute-done | bytes 229408 | tf_op jit(solution)/shard_map/ppermute | solution.py:23
  25.7 1.6 %collective-permute-start.9 = (bf16[32,1792]{1,0:T(8,128)(2,1)S(1)}, bf16[32,1792]{1,0:T(8,128)(2,1)S(1)}, u32[]{:S(2)}, u32[]{:S(2)}) collective-permute-start(bf16[32,1792]{1,0:T(8,128)(2,1)S(1)} %shard_map.65), channel_id=1, source_target_pairs={{0,4},{2,6},{4,0},{6,2},{8,12},{10,14},{12,8},{14,10},{1,5},{3,7},... | collective-permute-start | bytes 344072 | tf_op jit(solution)/shard_map/ppermute | solution.py:23
  27.2 1.6 %collective-permute-start.8 = (bf16[32,1792]{1,0:T(8,128)(2,1)S(1)}, bf16[32,1792]{1,0:T(8,128)(2,1)S(1)}, u32[]{:S(2)}, u32[]{:S(2)}) collective-permute-start(bf16[32,1792]{1,0:T(8,128)(2,1)S(1)} %shard_map.67), channel_id=1, source_target_pairs={{0,2},{2,0},{4,6},{6,4},{8,10},{10,8},{12,14},{14,12},{1,3},{3,1},... | collective-permute-start | bytes 344072 | tf_op jit(solution)/shard_map/ppermute | solution.py:23
  29.4 1.1 %shard_map.68 = (f32[2,32,1792]{2,1,0:T(8,128)S(1)}, f32[2,32,1792]{2,1,0:T(8,128)S(1)}) custom-call(bf16[2,32,1792]{2,1,0:T(8,128)(2,1)S(1)} %collective-permute-done.1.refs_0_, bf16[2,32,1792]{2,1,0:T(8,128)(2,1)S(1)} %collective-permute-done.4.both_ref.refs_1_, bf16[3584,384]{1,0:T(8,128)(2,1)S(1)} %shard_map.64.refs_4_.refs_2_.refs_3_, ...), custom_call_target="tpu_custom_call" | custom-call | flops 1150000000 | tf_op jit(solution)/shard_map/pallas_call | solution.py:112
  30.5 1.6 %collective-permute-done.8.refs_1_ = bf16[32,1792]{1,0:T(8,128)(2,1)S(1)} collective-permute-done((bf16[32,1792]{1,0:T(8,128)(2,1)S(1)}, bf16[32,1792]{1,0:T(8,128)(2,1)S(1)}, u32[]{:S(2)}, u32[]{:S(2)}) %collective-permute-start.8) | collective-permute-done | bytes 114720 | tf_op jit(solution)/shard_map/ppermute | solution.py:23
  32.1 1.1 %shard_map.69 = (f32[2,32,1792]{2,1,0:T(8,128)S(1)}, bf16[32,1792]{1,0:T(8,128)(2,1)S(1)}, bf16[32,1792]{1,0:T(8,128)(2,1)S(1)}) custom-call(bf16[2,32,1792]{2,1,0:T(8,128)(2,1)S(1)} %collective-permute-done.7.both_ref.refs_0_, bf16[32,1792]{1,0:T(8,128)(2,1)S(1)} %collective-permute-done.8.refs_1_, bf16[32,1792]{1,0:T(8,128)(2,1)S(1)} %collective-permute-done.9.refs_2_, ...), custom_call_target="tpu_custom_call" | custom-call | flops 1150000000 | tf_op jit(solution)/shard_map/pallas_call | solution.py:112
  33.2 1.6 %collective-permute-start.10 = (bf16[32,1792]{1,0:T(8,128)(2,1)S(1)}, bf16[32,1792]{1,0:T(8,128)(2,1)S(1)}, u32[]{:S(2)}, u32[]{:S(2)}) collective-permute-start(bf16[32,1792]{1,0:T(8,128)(2,1)S(1)} %get-tuple-element.49), channel_id=1, source_target_pairs={{0,2},{2,0},{4,6},{6,4},{8,10},{10,8},{12,14},{14,12},{1,3},{3,1},... | collective-permute-start | bytes 344072 | tf_op jit(solution)/shard_map/ppermute | solution.py:23
  34.8 1.2 %collective-permute-start.12 = (bf16[32,1792]{1,0:T(8,128)(2,1)S(1)}, bf16[32,1792]{1,0:T(8,128)(2,1)S(1)}, u32[]{:S(2)}, u32[]{:S(2)}) collective-permute-start(bf16[32,1792]{1,0:T(8,128)(2,1)S(1)} %get-tuple-element.55), channel_id=1, source_target_pairs={{0,4},{2,6},{4,0},{6,2},{8,12},{10,14},{12,8},{14,10},{1,5},{3,7},... | collective-permute-start | bytes 344072 | tf_op jit(solution)/shard_map/ppermute | solution.py:23
  36.1 1.2 %shard_map.66 = (f32[2,32,1792]{2,1,0:T(8,128)S(1)}, bf16[2,32,1792]{2,1,0:T(8,128)(2,1)S(1)}, f32[2,32,1792]{2,1,0:T(8,128)S(1)}, bf16[2,32,1792]{2,1,0:T(8,128)(2,1)S(1)}) custom-call(bf16[2,32,1792]{2,1,0:T(8,128)(2,1)S(1)} %pad_maximum_fusion.refs_0_, bf16[2,32,1792]{2,1,0:T(8,128)(2,1)S(1)} %collective-permute-done.3.refs_1_, ...), custom_call_target="tpu_custom_call" | custom-call | flops 1150000000 | tf_op jit(solution)/shard_map/pallas_call | solution.py:112
  38.1 1.2 %collective-permute-start.11 = (bf16[2,32,1792]{2,1,0:T(8,128)(2,1)S(1)}, bf16[2,32,1792]{2,1,0:T(8,128)(2,1)S(1)}, u32[]{:S(2)}, u32[]{:S(2)}) collective-permute-start(bf16[2,32,1792]{2,1,0:T(8,128)(2,1)S(1)} %pad_maximum_fusion.1), channel_id=1, source_target_pairs={{0,4},{2,6},{4,0},{6,2},{8,12},{10,14},{12,8},{14,10},{1,5},{3,7},... | collective-permute-start | bytes 688136 | tf_op jit(solution)/shard_map/ppermute | solution.py:23
  39.3 1.5 %collective-permute-done.12 = bf16[32,1792]{1,0:T(8,128)(2,1)S(1)} collective-permute-done((bf16[32,1792]{1,0:T(8,128)(2,1)S(1)}, bf16[32,1792]{1,0:T(8,128)(2,1)S(1)}, u32[]{:S(2)}, u32[]{:S(2)}) %collective-permute-start.12) | collective-permute-done | bytes 114720 | tf_op jit(solution)/shard_map/ppermute | solution.py:23
  41.1 2.0 %collective-permute-start.15 = (bf16[2,32,1792]{2,1,0:T(8,128)(2,1)S(1)}, bf16[2,32,1792]{2,1,0:T(8,128)(2,1)S(1)}, u32[]{:S(2)}, u32[]{:S(2)}) collective-permute-start(bf16[2,32,1792]{2,1,0:T(8,128)(2,1)S(1)} %get-tuple-element.59), channel_id=1, source_target_pairs={{0,2},{2,0},{4,6},{6,4},{8,10},{10,8},{12,14},{14,12},{1,3},{3,1},... | collective-permute-start | bytes 688136 | tf_op jit(solution)/shard_map/ppermute | solution.py:23
  43.1 1.4 %collective-permute-done.11 = bf16[2,32,1792]{2,1,0:T(8,128)(2,1)S(1)} collective-permute-done((bf16[2,32,1792]{2,1,0:T(8,128)(2,1)S(1)}, bf16[2,32,1792]{2,1,0:T(8,128)(2,1)S(1)}, u32[]{:S(2)}, u32[]{:S(2)}) %collective-permute-start.11) | collective-permute-done | bytes 229408 | tf_op jit(solution)/shard_map/ppermute | solution.py:23
  44.5 2.8 %collective-permute-done.13 = bf16[2,32,1792]{2,1,0:T(8,128)(2,1)S(1)} collective-permute-done((bf16[2,32,1792]{2,1,0:T(8,128)(2,1)S(1)}, bf16[2,32,1792]{2,1,0:T(8,128)(2,1)S(1)}, u32[]{:S(2)}, u32[]{:S(2)}) %collective-permute-start.13) | collective-permute-done | bytes 229408 | tf_op jit(solution)/shard_map/ppermute | solution.py:23
  47.4 2.2 %collective-permute-start.17 = (bf16[2,32,1792]{2,1,0:T(8,128)(2,1)S(1)}, bf16[2,32,1792]{2,1,0:T(8,128)(2,1)S(1)}, u32[]{:S(2)}, u32[]{:S(2)}) collective-permute-start(bf16[2,32,1792]{2,1,0:T(8,128)(2,1)S(1)} %add_convert_fusion), channel_id=1, source_target_pairs={{0,8},{2,10},{4,12},{6,14},{8,0},{10,2},{12,4},{14,6},{1,9},{3,11}... | collective-permute-start | bytes 688136 | tf_op jit(solution)/shard_map/ppermute | solution.py:23
  49.8 1.5 %collective-permute-start.16 = (bf16[2,32,1792]{2,1,0:T(8,128)(2,1)S(1)}, bf16[2,32,1792]{2,1,0:T(8,128)(2,1)S(1)}, u32[]{:S(2)}, u32[]{:S(2)}) collective-permute-start(bf16[2,32,1792]{2,1,0:T(8,128)(2,1)S(1)} %shard_map.70), channel_id=1, source_target_pairs={{0,4},{2,6},{4,0},{6,2},{8,12},{10,14},{12,8},{14,10},{1,5},{3,7},... | collective-permute-start | bytes 688136 | tf_op jit(solution)/shard_map/ppermute | solution.py:23
  51.2 1.2 %collective-permute-start.14 = (bf16[2,32,1792]{2,1,0:T(8,128)(2,1)S(1)}, bf16[2,32,1792]{2,1,0:T(8,128)(2,1)S(1)}, u32[]{:S(2)}, u32[]{:S(2)}) collective-permute-start(bf16[2,32,1792]{2,1,0:T(8,128)(2,1)S(1)} %get-tuple-element.57), channel_id=1, source_target_pairs={{0,2},{2,0},{4,6},{6,4},{8,10},{10,8},{12,14},{14,12},{1,3},{3,1},... | collective-permute-start | bytes 688136 | tf_op jit(solution)/shard_map/ppermute | solution.py:23
  52.5 4.4 %collective-permute-done.17.from_ref = bf16[2,32,1792]{2,1,0:T(8,128)(2,1)S(1)} collective-permute-done((bf16[2,32,1792]{2,1,0:T(8,128)(2,1)S(1)}, bf16[2,32,1792]{2,1,0:T(8,128)(2,1)S(1)}, u32[]{:S(2)}, u32[]{:S(2)}) %collective-permute-start.17) | collective-permute-done | bytes 229408 | tf_op jit(solution)/shard_map/ppermute | solution.py:23
  56.9 0.8 %collective-permute-done.16 = bf16[2,32,1792]{2,1,0:T(8,128)(2,1)S(1)} collective-permute-done((bf16[2,32,1792]{2,1,0:T(8,128)(2,1)S(1)}, bf16[2,32,1792]{2,1,0:T(8,128)(2,1)S(1)}, u32[]{:S(2)}, u32[]{:S(2)}) %collective-permute-start.16) | collective-permute-done | bytes 229408 | tf_op jit(solution)/shard_map/ppermute | solution.py:23
  57.9 1.3 %collective-permute-done.18 = bf16[32,1792]{1,0:T(8,128)(2,1)S(1)} collective-permute-done((bf16[32,1792]{1,0:T(8,128)(2,1)S(1)}, bf16[32,1792]{1,0:T(8,128)(2,1)S(1)}, u32[]{:S(2)}, u32[]{:S(2)}) %collective-permute-start.18) | collective-permute-done | bytes 114720 | tf_op jit(solution)/shard_map/ppermute | solution.py:32
  (39 shorter events, 3.7 us)
Async XLA Ops:
  1.0 1.5 %collective-permute-start = (bf16[32,1792]{1,0:T(8,128)(2,1)S(1)}, bf16[32,1792]{1,0:T(8,128)(2,1)S(1)}, u32[]{:S(2)}, u32[]{:S(2)}) collective-permute-start(bf16[32,1792]{1,0:T(8,128)(2,1)S(1)} %get-tuple-element.35), channel_id=1, source_target_pairs={{0,1},{1,0},{2,3},{3,2},{4,5},{5,4},{6,7},{7,6},{8,9},{9,8},{10,11... | collective-permute-start | bytes 344072 | tf_op jit(solution)/shard_map/ppermute | solution.py:32
  2.5 14.9 %collective-permute-start.1 = (bf16[2,32,1792]{2,1,0:T(8,128)(2,1)S(1)}, bf16[2,32,1792]{2,1,0:T(8,128)(2,1)S(1)}, u32[]{:S(2)}, u32[]{:S(2)}) collective-permute-start(bf16[2,32,1792]{2,1,0:T(8,128)(2,1)S(1)} %pad_maximum_fusion.refs_0_), channel_id=1, source_target_pairs={{0,8},{2,10},{4,12},{6,14},{8,0},{10,2},{12,4},{14,6},{1,9},{3,11}... | collective-permute-start | bytes 688136 | tf_op jit(solution)/shard_map/ppermute | solution.py:23
  6.5 11.1 %collective-permute-start.2 = (bf16[2,32,1792]{2,1,0:T(8,128)(2,1)S(1)}, bf16[2,32,1792]{2,1,0:T(8,128)(2,1)S(1)}, u32[]{:S(2)}, u32[]{:S(2)}) collective-permute-start(bf16[2,32,1792]{2,1,0:T(8,128)(2,1)S(1)} %pad_maximum_fusion.refs_0_), channel_id=1, source_target_pairs={{0,4},{2,6},{4,0},{6,2},{8,12},{10,14},{12,8},{14,10},{1,5},{3,7},... | collective-permute-start | bytes 688136 | tf_op jit(solution)/shard_map/ppermute | solution.py:23
  8.1 9.6 %collective-permute-start.3 = (bf16[2,32,1792]{2,1,0:T(8,128)(2,1)S(1)}, bf16[2,32,1792]{2,1,0:T(8,128)(2,1)S(1)}, u32[]{:S(2)}, u32[]{:S(2)}) collective-permute-start(bf16[2,32,1792]{2,1,0:T(8,128)(2,1)S(1)} %pad_maximum_fusion.refs_0_), channel_id=1, source_target_pairs={{0,2},{2,0},{4,6},{6,4},{8,10},{10,8},{12,14},{14,12},{1,3},{3,1},... | collective-permute-start | bytes 688136 | tf_op jit(solution)/shard_map/ppermute | solution.py:23
  9.6 1.2 %copy-start = (bf16[1,3584,128]{2,1,0:T(8,128)(2,1)S(1)}, bf16[1,3584,128]{2,1,0:T(8,128)(2,1)}, u32[]{:S(2)}) copy-start(bf16[1,3584,128]{2,1,0:T(8,128)(2,1)} %param.9) | copy-start | bytes 2752516
  10.7 1.2 %copy-start.1 = (bf16[1,3584,128]{2,1,0:T(8,128)(2,1)S(1)}, bf16[1,3584,128]{2,1,0:T(8,128)(2,1)}, u32[]{:S(2)}) copy-start(bf16[1,3584,128]{2,1,0:T(8,128)(2,1)} %param.10) | copy-start | bytes 2752516
  11.9 1.2 %copy-start.2 = (bf16[1,128,3584]{2,1,0:T(8,128)(2,1)S(1)}, bf16[1,128,3584]{2,1,0:T(8,128)(2,1)}, u32[]{:S(2)}) copy-start(bf16[1,128,3584]{2,1,0:T(8,128)(2,1)} %param.11) | copy-start | bytes 2752516
  17.6 11.7 %collective-permute-start.6 = (bf16[3584,384]{1,0:T(8,128)(2,1)S(1)}, bf16[3584,384]{1,0:T(8,128)(2,1)S(1)}, u32[]{:S(2)}, u32[]{:S(2)}) collective-permute-start(bf16[3584,384]{1,0:T(8,128)(2,1)S(1)} %shard_map.64.refs_4_.refs_2_.refs_3_), channel_id=1, source_target_pairs={{0,1},{1,0},{2,3},{3,2},{4,5},{5,4},{6,7},{7,6},{8,9},{9,8},{10,11... | collective-permute-start | bytes 8257544 | tf_op jit(solution)/shard_map/ppermute | solution.py:32
  17.6 8.0 %collective-permute-start.4 = (bf16[2,32,1792]{2,1,0:T(8,128)(2,1)S(1)}, bf16[2,32,1792]{2,1,0:T(8,128)(2,1)S(1)}, u32[]{:S(2)}, u32[]{:S(2)}) collective-permute-start(bf16[2,32,1792]{2,1,0:T(8,128)(2,1)S(1)} %collective-permute-done.1.refs_0_), channel_id=1, source_target_pairs={{0,2},{2,0},{4,6},{6,4},{8,10},{10,8},{12,14},{14,12},{1,3},{3,1},... | collective-permute-start | bytes 688136 | tf_op jit(solution)/shard_map/ppermute | solution.py:23
  19.2 8.0 %collective-permute-start.7 = (bf16[2,32,1792]{2,1,0:T(8,128)(2,1)S(1)}, bf16[2,32,1792]{2,1,0:T(8,128)(2,1)S(1)}, u32[]{:S(2)}, u32[]{:S(2)}) collective-permute-start(bf16[2,32,1792]{2,1,0:T(8,128)(2,1)S(1)} %collective-permute-done.1.refs_0_), channel_id=1, source_target_pairs={{0,4},{2,6},{4,0},{6,2},{8,12},{10,14},{12,8},{14,10},{1,5},{3,7},... | collective-permute-start | bytes 688136 | tf_op jit(solution)/shard_map/ppermute | solution.py:23
  25.7 4.9 %collective-permute-start.9 = (bf16[32,1792]{1,0:T(8,128)(2,1)S(1)}, bf16[32,1792]{1,0:T(8,128)(2,1)S(1)}, u32[]{:S(2)}, u32[]{:S(2)}) collective-permute-start(bf16[32,1792]{1,0:T(8,128)(2,1)S(1)} %shard_map.65), channel_id=1, source_target_pairs={{0,4},{2,6},{4,0},{6,2},{8,12},{10,14},{12,8},{14,10},{1,5},{3,7},... | collective-permute-start | bytes 344072 | tf_op jit(solution)/shard_map/ppermute | solution.py:23
  27.2 4.9 %collective-permute-start.8 = (bf16[32,1792]{1,0:T(8,128)(2,1)S(1)}, bf16[32,1792]{1,0:T(8,128)(2,1)S(1)}, u32[]{:S(2)}, u32[]{:S(2)}) collective-permute-start(bf16[32,1792]{1,0:T(8,128)(2,1)S(1)} %shard_map.67), channel_id=1, source_target_pairs={{0,2},{2,0},{4,6},{6,4},{8,10},{10,8},{12,14},{14,12},{1,3},{3,1},... | collective-permute-start | bytes 344072 | tf_op jit(solution)/shard_map/ppermute | solution.py:23
  28.8 7.3 %collective-permute-start.5 = (bf16[2,32,1792]{2,1,0:T(8,128)(2,1)S(1)}, bf16[2,32,1792]{2,1,0:T(8,128)(2,1)S(1)}, u32[]{:S(2)}, u32[]{:S(2)}) collective-permute-start(bf16[2,32,1792]{2,1,0:T(8,128)(2,1)S(1)} %collective-permute-done.3.refs_1_), channel_id=1, source_target_pairs={{0,4},{2,6},{4,0},{6,2},{8,12},{10,14},{12,8},{14,10},{1,5},{3,7},... | collective-permute-start | bytes 688136 | tf_op jit(solution)/shard_map/ppermute | solution.py:23
  33.2 4.9 %collective-permute-start.10 = (bf16[32,1792]{1,0:T(8,128)(2,1)S(1)}, bf16[32,1792]{1,0:T(8,128)(2,1)S(1)}, u32[]{:S(2)}, u32[]{:S(2)}) collective-permute-start(bf16[32,1792]{1,0:T(8,128)(2,1)S(1)} %get-tuple-element.49), channel_id=1, source_target_pairs={{0,2},{2,0},{4,6},{6,4},{8,10},{10,8},{12,14},{14,12},{1,3},{3,1},... | collective-permute-start | bytes 344072 | tf_op jit(solution)/shard_map/ppermute | solution.py:23
  34.8 6.1 %collective-permute-start.12 = (bf16[32,1792]{1,0:T(8,128)(2,1)S(1)}, bf16[32,1792]{1,0:T(8,128)(2,1)S(1)}, u32[]{:S(2)}, u32[]{:S(2)}) collective-permute-start(bf16[32,1792]{1,0:T(8,128)(2,1)S(1)} %get-tuple-element.55), channel_id=1, source_target_pairs={{0,4},{2,6},{4,0},{6,2},{8,12},{10,14},{12,8},{14,10},{1,5},{3,7},... | collective-permute-start | bytes 344072 | tf_op jit(solution)/shard_map/ppermute | solution.py:23
  36.1 5.0 %copy-start.3 = (s32[64,1]{0,1:T(1,128)S(1)}, s32[64,1]{0,1:T(1,128)}, u32[]{:S(2)}) copy-start(s32[64,1]{0,1:T(1,128)} %param.8) | copy-start | bytes 772
  37.3 15.1 %copy-start.4 = (s32[64,1]{0,1:T(1,128)S(1)}, s32[64,1]{0,1:T(1,128)}, u32[]{:S(2)}) copy-start(s32[64,1]{0,1:T(1,128)} %param.7) | copy-start | bytes 772
  38.1 6.3 %collective-permute-start.11 = (bf16[2,32,1792]{2,1,0:T(8,128)(2,1)S(1)}, bf16[2,32,1792]{2,1,0:T(8,128)(2,1)S(1)}, u32[]{:S(2)}, u32[]{:S(2)}) collective-permute-start(bf16[2,32,1792]{2,1,0:T(8,128)(2,1)S(1)} %pad_maximum_fusion.1), channel_id=1, source_target_pairs={{0,4},{2,6},{4,0},{6,2},{8,12},{10,14},{12,8},{14,10},{1,5},{3,7},... | collective-permute-start | bytes 688136 | tf_op jit(solution)/shard_map/ppermute | solution.py:23
  40.9 6.3 %collective-permute-start.13 = (bf16[2,32,1792]{2,1,0:T(8,128)(2,1)S(1)}, bf16[2,32,1792]{2,1,0:T(8,128)(2,1)S(1)}, u32[]{:S(2)}, u32[]{:S(2)}) collective-permute-start(bf16[2,32,1792]{2,1,0:T(8,128)(2,1)S(1)} %pad_maximum_fusion.2), channel_id=1, source_target_pairs={{0,2},{2,0},{4,6},{6,4},{8,10},{10,8},{12,14},{14,12},{1,3},{3,1},... | collective-permute-start | bytes 688136 | tf_op jit(solution)/shard_map/ppermute | solution.py:23
  41.1 8.6 %collective-permute-start.15 = (bf16[2,32,1792]{2,1,0:T(8,128)(2,1)S(1)}, bf16[2,32,1792]{2,1,0:T(8,128)(2,1)S(1)}, u32[]{:S(2)}, u32[]{:S(2)}) collective-permute-start(bf16[2,32,1792]{2,1,0:T(8,128)(2,1)S(1)} %get-tuple-element.59), channel_id=1, source_target_pairs={{0,2},{2,0},{4,6},{6,4},{8,10},{10,8},{12,14},{14,12},{1,3},{3,1},... | collective-permute-start | bytes 688136 | tf_op jit(solution)/shard_map/ppermute | solution.py:23
  47.4 9.6 %collective-permute-start.17 = (bf16[2,32,1792]{2,1,0:T(8,128)(2,1)S(1)}, bf16[2,32,1792]{2,1,0:T(8,128)(2,1)S(1)}, u32[]{:S(2)}, u32[]{:S(2)}) collective-permute-start(bf16[2,32,1792]{2,1,0:T(8,128)(2,1)S(1)} %add_convert_fusion), channel_id=1, source_target_pairs={{0,8},{2,10},{4,12},{6,14},{8,0},{10,2},{12,4},{14,6},{1,9},{3,11}... | collective-permute-start | bytes 688136 | tf_op jit(solution)/shard_map/ppermute | solution.py:23
  49.8 7.9 %collective-permute-start.16 = (bf16[2,32,1792]{2,1,0:T(8,128)(2,1)S(1)}, bf16[2,32,1792]{2,1,0:T(8,128)(2,1)S(1)}, u32[]{:S(2)}, u32[]{:S(2)}) collective-permute-start(bf16[2,32,1792]{2,1,0:T(8,128)(2,1)S(1)} %shard_map.70), channel_id=1, source_target_pairs={{0,4},{2,6},{4,0},{6,2},{8,12},{10,14},{12,8},{14,10},{1,5},{3,7},... | collective-permute-start | bytes 688136 | tf_op jit(solution)/shard_map/ppermute | solution.py:23
  51.2 6.5 %collective-permute-start.14 = (bf16[2,32,1792]{2,1,0:T(8,128)(2,1)S(1)}, bf16[2,32,1792]{2,1,0:T(8,128)(2,1)S(1)}, u32[]{:S(2)}, u32[]{:S(2)}) collective-permute-start(bf16[2,32,1792]{2,1,0:T(8,128)(2,1)S(1)} %get-tuple-element.57), channel_id=1, source_target_pairs={{0,2},{2,0},{4,6},{6,4},{8,10},{10,8},{12,14},{14,12},{1,3},{3,1},... | collective-permute-start | bytes 688136 | tf_op jit(solution)/shard_map/ppermute | solution.py:23
  57.9 1.4 %collective-permute-start.18 = (bf16[32,1792]{1,0:T(8,128)(2,1)S(1)}, bf16[32,1792]{1,0:T(8,128)(2,1)S(1)}, u32[]{:S(2)}, u32[]{:S(2)}) collective-permute-start(bf16[32,1792]{1,0:T(8,128)(2,1)S(1)} %slice_bitcast_fusion), channel_id=1, source_target_pairs={{0,1},{1,0},{2,3},{3,2},{4,5},{5,4},{6,7},{7,6},{8,9},{9,8},{10,11... | collective-permute-start | bytes 344072 | tf_op jit(solution)/shard_map/ppermute | solution.py:32

commit v5 on v4

--- a/solution.py
+++ b/solution.py
@@ -212,21 +212,24 @@
         return expert_block(blocks, weights, types, work)
 
     both0 = jnp.stack([a0, b0])
-    z2 = swap(both0, 4)
+    z2a = cast(swap(a0, 4), bf16, 0.3)
+    z2b = cast(swap(b0, 4), bf16, 0.3)
     z1 = swap(both0, 2)
     x0 = swap(both0, 1)
-    z2, z1, x0, ours = tie((z2, z1, x0, ours))
+    z2a, z2b, z1, x0, ours = tie((z2a, z2b, z1, x0, ours))
     weights = [ours, swap_core(ours)]
-    m6 = swap(z2, 2)
-    m5 = swap(z2, 1)
-    m6a, m5b = part_of(m6, 0), part_of(m5, 1)
+    m5b = swap(z2b, 1)
+    m5a = swap(z2a, 1)
+    m6a = swap(z2a, 2)
+    m6b = swap(z2b, 2)
+    m5a, m6b = tie((m5a, m6b))
     m5b, held = tie((m5b, x0))
     m3 = swap(held, 2)
     m7a = swap(m6a, 1)
     m7b = swap(m5b, 2)
-    p4, p5 = expert(((z2,), (m5,)), ((f32,), (f32,)))
-    m7a, m7b, p4, p5 = tie((m7a, m7b, p4, p5))
-    p6, p7a, p7b = expert(((m6,), (m7a, m7b)), ((f32,), (bf16, bf16)))
+    p4, p5a, p5b = expert(((z2a, z2b), (m5a, m5b)), ((f32,), (bf16, f32)))
+    m7a, m7b, p4, p5a, p5b = tie((m7a, m7b, p4, p5a, p5b))
+    p6, p7a, p7b = expert(((m6a, m6b), (m7a, m7b)), ((f32,), (bf16, bf16)))
     p0, p1, p2, p3 = expert(
         ((both0,), (x0,), (z1,), (m3,)), ((f32,), (bf16,), (f32,), (bf16,)), 1.0
     )
@@ -234,9 +237,12 @@
     r7b = swap(p7b, 2)
     r7a, p1, p2, p3 = tie((r7a, p1, p2, p3))
     s6 = jnp.stack([p6[0] + r7a.astype(f32), p6[1]]).astype(bf16)
-    s5 = jnp.stack([p5[0], p5[1] + r7b.astype(f32)]).astype(bf16)
+    r5a = swap(p5a, 1)
+    r7b, r5a = tie((r7b, r5a))
+    s5b = (p5b + r7b.astype(f32)).astype(bf16)
     r6 = swap(s6, 2).astype(f32)
-    r5 = swap(s5, 1).astype(f32)
+    r5b = swap(s5b, 1)
+    r5 = jnp.stack([r5a, r5b]).astype(f32)
     sent = (p4 + r6 + r5).astype(bf16)
     r3 = swap(p3, 1)
     s2 = add(p2, r3, 0.1)

time: 60.2 us -> 56.5 us (0.939)
  waiting for transfers between devices: 24.3 us -> 17.1 us
  starting transfers between devices: 25.3 us -> 28.9 us
    ppermute x16 -> x20, waiting for transfers between devices: 22 us -> 15.8 us  [swap(): return lax.ppermute(value, 'ep', pairs)]
    ppermute x16 -> x20, starting transfers between devices: 24.7 us -> 28.3 us  [swap(): return lax.ppermute(value, 'ep', pairs)]
    ppermute x3, waiting for transfers between devices: 2.28 us -> 1.32 us  [swap_core(): return lax.ppermute(value, 'tp', [(0, 1), (1, 0)])]
  transfers between devices with their start and end apart: 19 -> 23, of which waited for: 13 -> 13; matrix products, arithmetic and copies ran while one was open for 1% -> 1% of each run, Pallas kernels for 7% -> 8%
where the time goes in v5:
time: 56.5 us; the launch traced here: 56.2 us
  starting transfers between devices  28.9 us (51%)
  waiting for transfers between devices  17.1 us (30%)
  Pallas kernels  4.4 us (8%)
  local copies, waits for them, and re-layouts  3.57 us (6%)
  other arithmetic  2.13 us (4%)
    ppermute x20, starting transfers between devices, swap(): return lax.ppermute(value, 'ep', pairs)  28.3 us
    ppermute x20, waiting for transfers between devices, swap(): return lax.ppermute(value, 'ep', pairs)  15.8 us
    unnamed x10, local copies, waits for them, and re-layouts  3.55 us
    pallas_call x3, Pallas kernels, expert_block(): pl.pallas_call(functools.partial(expert_kernel, [(None,) * len(b) for b i...  3.5 us
    ppermute x3, waiting for transfers between devices, swap_core(): return lax.ppermute(value, 'tp', [(0, 1), (1, 0)])  1.32 us
  transfers between devices with their start and end apart: 23, of which 13 were waited for; matrix products, arithmetic and copies ran while one was open for 1% of the time, Pallas kernels for 8%

profile of v5, /device:TPU:0, one launch (start us, length us, event | category | flops | bytes accessed | tf_op | source)
XLA Modules:
  0.0 56.2 jit_solution(11366726452623296145)
XLA Ops:
  0.0 1.0 %broadcast_select_fusion.2 = (bf16[32,1792]{1,0:T(8,128)(2,1)S(1)}, bf16[32,1792]{1,0:T(8,128)(2,1)S(1)}) fusion(pred[]{:T(512)S(6)} %eq.3, bf16[64,1792]{1,0:T(8,128)(2,1)} %param.6), kind=kLoop, calls=%fused_computation.14 | loop fusion | flops 114688 | bytes 458753 | tf_op jit(solution)/shard_map/jit(_where)/select_n | solution.py:206
  1.5 3.7 %collective-permute-start.1 = (bf16[32,1792]{1,0:T(8,128)(2,1)S(1)}, bf16[32,1792]{1,0:T(8,128)(2,1)S(1)}, u32[]{:S(2)}, u32[]{:S(2)}) collective-permute-start(bf16[32,1792]{1,0:T(8,128)(2,1)S(1)} %get-tuple-element.41), channel_id=1, source_target_pairs={{0,8},{2,10},{4,12},{6,14},{8,0},{10,2},{12,4},{14,6},{1,9},{3,11}... | collective-permute-start | bytes 344072 | tf_op jit(solution)/shard_map/ppermute | solution.py:23
  5.2 1.6 %collective-permute-start.3 = (bf16[2,32,1792]{2,1,0:T(8,128)(2,1)S(1)}, bf16[2,32,1792]{2,1,0:T(8,128)(2,1)S(1)}, u32[]{:S(2)}, u32[]{:S(2)}) collective-permute-start(bf16[2,32,1792]{2,1,0:T(8,128)(2,1)S(1)} %pad_maximum_fusion.refs_0_), channel_id=1, source_target_pairs={{0,4},{2,6},{4,0},{6,2},{8,12},{10,14},{12,8},{14,10},{1,5},{3,7},... | collective-permute-start | bytes 688136 | tf_op jit(solution)/shard_map/ppermute | solution.py:23
  6.8 1.5 %collective-permute-start.4 = (bf16[2,32,1792]{2,1,0:T(8,128)(2,1)S(1)}, bf16[2,32,1792]{2,1,0:T(8,128)(2,1)S(1)}, u32[]{:S(2)}, u32[]{:S(2)}) collective-permute-start(bf16[2,32,1792]{2,1,0:T(8,128)(2,1)S(1)} %pad_maximum_fusion.refs_0_), channel_id=1, source_target_pairs={{0,2},{2,0},{4,6},{6,4},{8,10},{10,8},{12,14},{14,12},{1,3},{3,1},... | collective-permute-start | bytes 688136 | tf_op jit(solution)/shard_map/ppermute | solution.py:23
  8.3 1.2 %collective-permute-start.2 = (bf16[32,1792]{1,0:T(8,128)(2,1)S(1)}, bf16[32,1792]{1,0:T(8,128)(2,1)S(1)}, u32[]{:S(2)}, u32[]{:S(2)}) collective-permute-start(bf16[32,1792]{1,0:T(8,128)(2,1)S(1)} %collective-permute-done), channel_id=1, source_target_pairs={{0,8},{2,10},{4,12},{6,14},{8,0},{10,2},{12,4},{14,6},{1,9},{3,11}... | collective-permute-start | bytes 344072 | tf_op jit(solution)/shard_map/ppermute | solution.py:23
  9.6 1.2 %copy-done = bf16[1,3584,128]{2,1,0:T(8,128)(2,1)S(1)} copy-done((bf16[1,3584,128]{2,1,0:T(8,128)(2,1)S(1)}, bf16[1,3584,128]{2,1,0:T(8,128)(2,1)}, u32[]{:S(2)}) %copy-start) | copy-done | bytes 917528
  10.7 1.2 %copy-done.1 = bf16[1,3584,128]{2,1,0:T(8,128)(2,1)S(1)} copy-done((bf16[1,3584,128]{2,1,0:T(8,128)(2,1)S(1)}, bf16[1,3584,128]{2,1,0:T(8,128)(2,1)}, u32[]{:S(2)}) %copy-start.1) | copy-done | bytes 917528
  11.9 1.2 %copy-done.2 = bf16[1,128,3584]{2,1,0:T(8,128)(2,1)S(1)} copy-done((bf16[1,128,3584]{2,1,0:T(8,128)(2,1)S(1)}, bf16[1,128,3584]{2,1,0:T(8,128)(2,1)}, u32[]{:S(2)}) %copy-start.2) | copy-done | bytes 917528
  13.1 0.8 %shard_map.66.refs_4_ = bf16[3584,384]{1,0:T(8,128)(2,1)S(1)} custom-call(bf16[3584,128]{1,0:T(8,128)(2,1)S(1)} %bitcast.27, bf16[3584,128]{1,0:T(8,128)(2,1)S(1)} %bitcast.28, bf16[128,3584]{1,0:T(8,128)(2,1)S(1)} %bitcast.29), custom_call_target="tpu_custom_call" | custom-call | flops 2300000000 | tf_op jit(solution)/shard_map/pallas_call | solution.py:49
  13.9 1.6 %collective-permute-done.2.from_ref = bf16[32,1792]{1,0:T(8,128)(2,1)S(1)} collective-permute-done((bf16[32,1792]{1,0:T(8,128)(2,1)S(1)}, bf16[32,1792]{1,0:T(8,128)(2,1)S(1)}, u32[]{:S(2)}, u32[]{:S(2)}) %collective-permute-start.2) | collective-permute-done | bytes 114720 | tf_op jit(solution)/shard_map/ppermute | solution.py:23
  15.6 1.1 %collective-permute-done.3.refs_2_ = bf16[2,32,1792]{2,1,0:T(8,128)(2,1)S(1)} collective-permute-done((bf16[2,32,1792]{2,1,0:T(8,128)(2,1)S(1)}, bf16[2,32,1792]{2,1,0:T(8,128)(2,1)S(1)}, u32[]{:S(2)}, u32[]{:S(2)}) %collective-permute-start.3) | collective-permute-done | bytes 229408 | tf_op jit(solution)/shard_map/ppermute | solution.py:23
  16.7 1.6 %collective-permute-start.5 = (bf16[32,1792]{1,0:T(8,128)(2,1)S(1)}, bf16[32,1792]{1,0:T(8,128)(2,1)S(1)}, u32[]{:S(2)}, u32[]{:S(2)}) collective-permute-start(bf16[32,1792]{1,0:T(8,128)(2,1)S(1)} %shard_map.65.refs_1_), channel_id=1, source_target_pairs={{0,2},{2,0},{4,6},{6,4},{8,10},{10,8},{12,14},{14,12},{1,3},{3,1},... | collective-permute-start | bytes 344072 | tf_op jit(solution)/shard_map/ppermute | solution.py:23
  18.2 1.4 %collective-permute-start.8 = (bf16[32,1792]{1,0:T(8,128)(2,1)S(1)}, bf16[32,1792]{1,0:T(8,128)(2,1)S(1)}, u32[]{:S(2)}, u32[]{:S(2)}) collective-permute-start(bf16[32,1792]{1,0:T(8,128)(2,1)S(1)} %shard_map.64.refs_0_), channel_id=1, source_target_pairs={{0,4},{2,6},{4,0},{6,2},{8,12},{10,14},{12,8},{14,10},{1,5},{3,7},... | collective-permute-start | bytes 344072 | tf_op jit(solution)/shard_map/ppermute | solution.py:23
  20.7 1.6 %collective-permute-done.5.refs_3_ = bf16[32,1792]{1,0:T(8,128)(2,1)S(1)} collective-permute-done((bf16[32,1792]{1,0:T(8,128)(2,1)S(1)}, bf16[32,1792]{1,0:T(8,128)(2,1)S(1)}, u32[]{:S(2)}, u32[]{:S(2)}) %collective-permute-start.5) | collective-permute-done | bytes 114720 | tf_op jit(solution)/shard_map/ppermute | solution.py:23
  22.3 1.8 %collective-permute-start.10 = (bf16[32,1792]{1,0:T(8,128)(2,1)S(1)}, bf16[32,1792]{1,0:T(8,128)(2,1)S(1)}, u32[]{:S(2)}, u32[]{:S(2)}) collective-permute-start(bf16[32,1792]{1,0:T(8,128)(2,1)S(1)} %collective-permute-done.5.refs_3_), channel_id=1, source_target_pairs={{0,4},{2,6},{4,0},{6,2},{8,12},{10,14},{12,8},{14,10},{1,5},{3,7},... | collective-permute-start | bytes 344072 | tf_op jit(solution)/shard_map/ppermute | solution.py:23
  24.2 1.4 %collective-permute-start.9 = (bf16[32,1792]{1,0:T(8,128)(2,1)S(1)}, bf16[32,1792]{1,0:T(8,128)(2,1)S(1)}, u32[]{:S(2)}, u32[]{:S(2)}) collective-permute-start(bf16[32,1792]{1,0:T(8,128)(2,1)S(1)} %collective-permute-done.8.refs_0_), channel_id=1, source_target_pairs={{0,2},{2,0},{4,6},{6,4},{8,10},{10,8},{12,14},{14,12},{1,3},{3,1},... | collective-permute-start | bytes 344072 | tf_op jit(solution)/shard_map/ppermute | solution.py:23
  26.7 1.1 %shard_map.68 = (f32[2,32,1792]{2,1,0:T(8,128)S(1)}, bf16[32,1792]{1,0:T(8,128)(2,1)S(1)}, f32[32,1792]{1,0:T(8,128)S(1)}) custom-call(bf16[32,1792]{1,0:T(8,128)(2,1)S(1)} %shard_map.64.refs_0_, bf16[32,1792]{1,0:T(8,128)(2,1)S(1)} %shard_map.65.refs_1_, bf16[32,1792]{1,0:T(8,128)(2,1)S(1)} %collective-permute-done.11.refs_2_, ...), custom_call_target="tpu_custom_call" | custom-call | flops 1150000000 | tf_op jit(solution)/shard_map/pallas_call | solution.py:112
  27.8 1.3 %collective-permute-done.10.refs_3_ = bf16[32,1792]{1,0:T(8,128)(2,1)S(1)} collective-permute-done((bf16[32,1792]{1,0:T(8,128)(2,1)S(1)}, bf16[32,1792]{1,0:T(8,128)(2,1)S(1)}, u32[]{:S(2)}, u32[]{:S(2)}) %collective-permute-start.10) | collective-permute-done | bytes 114720 | tf_op jit(solution)/shard_map/ppermute | solution.py:23
  29.1 1.1 %shard_map.69 = (f32[2,32,1792]{2,1,0:T(8,128)S(1)}, bf16[32,1792]{1,0:T(8,128)(2,1)S(1)}, bf16[32,1792]{1,0:T(8,128)(2,1)S(1)}) custom-call(bf16[32,1792]{1,0:T(8,128)(2,1)S(1)} %collective-permute-done.8.refs_0_, bf16[32,1792]{1,0:T(8,128)(2,1)S(1)} %collective-permute-done.12.refs_1_, bf16[32,1792]{1,0:T(8,128)(2,1)S(1)} %collective-permute-done.9.refs_2_, ...), custom_call_target="tpu_custom_call" | custom-call | flops 1150000000 | tf_op jit(solution)/shard_map/pallas_call | solution.py:112
  30.3 1.3 %collective-permute-start.13 = (bf16[32,1792]{1,0:T(8,128)(2,1)S(1)}, bf16[32,1792]{1,0:T(8,128)(2,1)S(1)}, u32[]{:S(2)}, u32[]{:S(2)}) collective-permute-start(bf16[32,1792]{1,0:T(8,128)(2,1)S(1)} %get-tuple-element.60), channel_id=1, source_target_pairs={{0,2},{2,0},{4,6},{6,4},{8,10},{10,8},{12,14},{14,12},{1,3},{3,1},... | collective-permute-start | bytes 344072 | tf_op jit(solution)/shard_map/ppermute | solution.py:23
  32.2 1.6 %collective-permute-start.16 = (bf16[32,1792]{1,0:T(8,128)(2,1)S(1)}, bf16[32,1792]{1,0:T(8,128)(2,1)S(1)}, u32[]{:S(2)}, u32[]{:S(2)}) collective-permute-start(bf16[32,1792]{1,0:T(8,128)(2,1)S(1)} %get-tuple-element.66), channel_id=1, source_target_pairs={{0,2},{2,0},{4,6},{6,4},{8,10},{10,8},{12,14},{14,12},{1,3},{3,1},... | collective-permute-start | bytes 344072 | tf_op jit(solution)/shard_map/ppermute | solution.py:23
  34.1 1.2 %shard_map.67 = (f32[2,32,1792]{2,1,0:T(8,128)S(1)}, bf16[2,32,1792]{2,1,0:T(8,128)(2,1)S(1)}, f32[2,32,1792]{2,1,0:T(8,128)S(1)}, bf16[2,32,1792]{2,1,0:T(8,128)(2,1)S(1)}) custom-call(bf16[2,32,1792]{2,1,0:T(8,128)(2,1)S(1)} %pad_maximum_fusion.refs_0_, bf16[2,32,1792]{2,1,0:T(8,128)(2,1)S(1)} %collective-permute-done.4.refs_1_, ...), custom_call_target="tpu_custom_call" | custom-call | flops 1150000000 | tf_op jit(solution)/shard_map/pallas_call | solution.py:112
  35.4 1.0 %collective-permute-done.15 = bf16[32,1792]{1,0:T(8,128)(2,1)S(1)} collective-permute-done((bf16[32,1792]{1,0:T(8,128)(2,1)S(1)}, bf16[32,1792]{1,0:T(8,128)(2,1)S(1)}, u32[]{:S(2)}, u32[]{:S(2)}) %collective-permute-start.15) | collective-permute-done | bytes 114720 | tf_op jit(solution)/shard_map/ppermute | solution.py:23
  37.1 1.5 %collective-permute-start.14 = (bf16[2,32,1792]{2,1,0:T(8,128)(2,1)S(1)}, bf16[2,32,1792]{2,1,0:T(8,128)(2,1)S(1)}, u32[]{:S(2)}, u32[]{:S(2)}) collective-permute-start(bf16[2,32,1792]{2,1,0:T(8,128)(2,1)S(1)} %pad_maximum_fusion.1), channel_id=1, source_target_pairs={{0,4},{2,6},{4,0},{6,2},{8,12},{10,14},{12,8},{14,10},{1,5},{3,7},... | collective-permute-start | bytes 688136 | tf_op jit(solution)/shard_map/ppermute | solution.py:23
  38.5 0.9 %collective-permute-start.17 = (bf16[32,1792]{1,0:T(8,128)(2,1)S(1)}, bf16[32,1792]{1,0:T(8,128)(2,1)S(1)}, u32[]{:S(2)}, u32[]{:S(2)}) collective-permute-start(bf16[32,1792]{1,0:T(8,128)(2,1)S(1)} %add_convert_fusion.1), channel_id=1, source_target_pairs={{0,2},{2,0},{4,6},{6,4},{8,10},{10,8},{12,14},{14,12},{1,3},{3,1},... | collective-permute-start | bytes 344072 | tf_op jit(solution)/shard_map/ppermute | solution.py:23
  39.5 1.2 %collective-permute-start.19 = (bf16[2,32,1792]{2,1,0:T(8,128)(2,1)S(1)}, bf16[2,32,1792]{2,1,0:T(8,128)(2,1)S(1)}, u32[]{:S(2)}, u32[]{:S(2)}) collective-permute-start(bf16[2,32,1792]{2,1,0:T(8,128)(2,1)S(1)} %get-tuple-element.73), channel_id=1, source_target_pairs={{0,2},{2,0},{4,6},{6,4},{8,10},{10,8},{12,14},{14,12},{1,3},{3,1},... | collective-permute-start | bytes 688136 | tf_op jit(solution)/shard_map/ppermute | solution.py:23
  40.7 2.8 %collective-permute-done.17 = bf16[32,1792]{1,0:T(8,128)(2,1)S(1)} collective-permute-done((bf16[32,1792]{1,0:T(8,128)(2,1)S(1)}, bf16[32,1792]{1,0:T(8,128)(2,1)S(1)}, u32[]{:S(2)}, u32[]{:S(2)}) %collective-permute-start.17) | collective-permute-done | bytes 114720 | tf_op jit(solution)/shard_map/ppermute | solution.py:23
  43.6 2.9 %collective-permute-start.21 = (bf16[2,32,1792]{2,1,0:T(8,128)(2,1)S(1)}, bf16[2,32,1792]{2,1,0:T(8,128)(2,1)S(1)}, u32[]{:S(2)}, u32[]{:S(2)}) collective-permute-start(bf16[2,32,1792]{2,1,0:T(8,128)(2,1)S(1)} %add_convert_fusion), channel_id=1, source_target_pairs={{0,8},{2,10},{4,12},{6,14},{8,0},{10,2},{12,4},{14,6},{1,9},{3,11}... | collective-permute-start | bytes 688136 | tf_op jit(solution)/shard_map/ppermute | solution.py:23
  46.5 0.8 %collective-permute-start.20 = (bf16[2,32,1792]{2,1,0:T(8,128)(2,1)S(1)}, bf16[2,32,1792]{2,1,0:T(8,128)(2,1)S(1)}, u32[]{:S(2)}, u32[]{:S(2)}) collective-permute-start(bf16[2,32,1792]{2,1,0:T(8,128)(2,1)S(1)} %shard_map.70), channel_id=1, source_target_pairs={{0,4},{2,6},{4,0},{6,2},{8,12},{10,14},{12,8},{14,10},{1,5},{3,7},... | collective-permute-start | bytes 688136 | tf_op jit(solution)/shard_map/ppermute | solution.py:23
  47.3 1.7 %collective-permute-start.18 = (bf16[2,32,1792]{2,1,0:T(8,128)(2,1)S(1)}, bf16[2,32,1792]{2,1,0:T(8,128)(2,1)S(1)}, u32[]{:S(2)}, u32[]{:S(2)}) collective-permute-start(bf16[2,32,1792]{2,1,0:T(8,128)(2,1)S(1)} %get-tuple-element.71), channel_id=1, source_target_pairs={{0,2},{2,0},{4,6},{6,4},{8,10},{10,8},{12,14},{14,12},{1,3},{3,1},... | collective-permute-start | bytes 688136 | tf_op jit(solution)/shard_map/ppermute | solution.py:23
  49.1 4.2 %collective-permute-done.21.from_ref = bf16[2,32,1792]{2,1,0:T(8,128)(2,1)S(1)} collective-permute-done((bf16[2,32,1792]{2,1,0:T(8,128)(2,1)S(1)}, bf16[2,32,1792]{2,1,0:T(8,128)(2,1)S(1)}, u32[]{:S(2)}, u32[]{:S(2)}) %collective-permute-start.21) | collective-permute-done | bytes 229408 | tf_op jit(solution)/shard_map/ppermute | solution.py:23
  54.2 1.3 %collective-permute-done.22 = bf16[32,1792]{1,0:T(8,128)(2,1)S(1)} collective-permute-done((bf16[32,1792]{1,0:T(8,128)(2,1)S(1)}, bf16[32,1792]{1,0:T(8,128)(2,1)S(1)}, u32[]{:S(2)}, u32[]{:S(2)}) %collective-permute-start.22) | collective-permute-done | bytes 114720 | tf_op jit(solution)/shard_map/ppermute | solution.py:32
  (45 shorter events, 6.4 us)
Async XLA Ops:
  1.0 4.2 %collective-permute-start = (bf16[32,1792]{1,0:T(8,128)(2,1)S(1)}, bf16[32,1792]{1,0:T(8,128)(2,1)S(1)}, u32[]{:S(2)}, u32[]{:S(2)}) collective-permute-start(bf16[32,1792]{1,0:T(8,128)(2,1)S(1)} %get-tuple-element.42), channel_id=1, source_target_pairs={{0,1},{1,0},{2,3},{3,2},{4,5},{5,4},{6,7},{7,6},{8,9},{9,8},{10,11... | collective-permute-start | bytes 344072 | tf_op jit(solution)/shard_map/ppermute | solution.py:32
  1.5 12.4 %collective-permute-start.1 = (bf16[32,1792]{1,0:T(8,128)(2,1)S(1)}, bf16[32,1792]{1,0:T(8,128)(2,1)S(1)}, u32[]{:S(2)}, u32[]{:S(2)}) collective-permute-start(bf16[32,1792]{1,0:T(8,128)(2,1)S(1)} %get-tuple-element.41), channel_id=1, source_target_pairs={{0,8},{2,10},{4,12},{6,14},{8,0},{10,2},{12,4},{14,6},{1,9},{3,11}... | collective-permute-start | bytes 344072 | tf_op jit(solution)/shard_map/ppermute | solution.py:23
  5.2 11.5 %collective-permute-start.3 = (bf16[2,32,1792]{2,1,0:T(8,128)(2,1)S(1)}, bf16[2,32,1792]{2,1,0:T(8,128)(2,1)S(1)}, u32[]{:S(2)}, u32[]{:S(2)}) collective-permute-start(bf16[2,32,1792]{2,1,0:T(8,128)(2,1)S(1)} %pad_maximum_fusion.refs_0_), channel_id=1, source_target_pairs={{0,4},{2,6},{4,0},{6,2},{8,12},{10,14},{12,8},{14,10},{1,5},{3,7},... | collective-permute-start | bytes 688136 | tf_op jit(solution)/shard_map/ppermute | solution.py:23
  6.8 9.8 %collective-permute-start.4 = (bf16[2,32,1792]{2,1,0:T(8,128)(2,1)S(1)}, bf16[2,32,1792]{2,1,0:T(8,128)(2,1)S(1)}, u32[]{:S(2)}, u32[]{:S(2)}) collective-permute-start(bf16[2,32,1792]{2,1,0:T(8,128)(2,1)S(1)} %pad_maximum_fusion.refs_0_), channel_id=1, source_target_pairs={{0,2},{2,0},{4,6},{6,4},{8,10},{10,8},{12,14},{14,12},{1,3},{3,1},... | collective-permute-start | bytes 688136 | tf_op jit(solution)/shard_map/ppermute | solution.py:23
  8.3 7.3 %collective-permute-start.2 = (bf16[32,1792]{1,0:T(8,128)(2,1)S(1)}, bf16[32,1792]{1,0:T(8,128)(2,1)S(1)}, u32[]{:S(2)}, u32[]{:S(2)}) collective-permute-start(bf16[32,1792]{1,0:T(8,128)(2,1)S(1)} %collective-permute-done), channel_id=1, source_target_pairs={{0,8},{2,10},{4,12},{6,14},{8,0},{10,2},{12,4},{14,6},{1,9},{3,11}... | collective-permute-start | bytes 344072 | tf_op jit(solution)/shard_map/ppermute | solution.py:23
  9.6 1.2 %copy-start = (bf16[1,3584,128]{2,1,0:T(8,128)(2,1)S(1)}, bf16[1,3584,128]{2,1,0:T(8,128)(2,1)}, u32[]{:S(2)}) copy-start(bf16[1,3584,128]{2,1,0:T(8,128)(2,1)} %param.9) | copy-start | bytes 2752516
  10.7 1.2 %copy-start.1 = (bf16[1,3584,128]{2,1,0:T(8,128)(2,1)S(1)}, bf16[1,3584,128]{2,1,0:T(8,128)(2,1)}, u32[]{:S(2)}) copy-start(bf16[1,3584,128]{2,1,0:T(8,128)(2,1)} %param.10) | copy-start | bytes 2752516
  11.9 1.2 %copy-start.2 = (bf16[1,128,3584]{2,1,0:T(8,128)(2,1)S(1)}, bf16[1,128,3584]{2,1,0:T(8,128)(2,1)}, u32[]{:S(2)}) copy-start(bf16[1,128,3584]{2,1,0:T(8,128)(2,1)} %param.11) | copy-start | bytes 2752516
  16.7 10.0 %collective-permute-start.7 = (bf16[3584,384]{1,0:T(8,128)(2,1)S(1)}, bf16[3584,384]{1,0:T(8,128)(2,1)S(1)}, u32[]{:S(2)}, u32[]{:S(2)}) collective-permute-start(bf16[3584,384]{1,0:T(8,128)(2,1)S(1)} %shard_map.66.refs_4_), channel_id=1, source_target_pairs={{0,1},{1,0},{2,3},{3,2},{4,5},{5,4},{6,7},{7,6},{8,9},{9,8},{10,11... | collective-permute-start | bytes 8257544 | tf_op jit(solution)/shard_map/ppermute | solution.py:32
  16.7 5.6 %collective-permute-start.5 = (bf16[32,1792]{1,0:T(8,128)(2,1)S(1)}, bf16[32,1792]{1,0:T(8,128)(2,1)S(1)}, u32[]{:S(2)}, u32[]{:S(2)}) collective-permute-start(bf16[32,1792]{1,0:T(8,128)(2,1)S(1)} %shard_map.65.refs_1_), channel_id=1, source_target_pairs={{0,2},{2,0},{4,6},{6,4},{8,10},{10,8},{12,14},{14,12},{1,3},{3,1},... | collective-permute-start | bytes 344072 | tf_op jit(solution)/shard_map/ppermute | solution.py:23
  18.2 6.0 %collective-permute-start.8 = (bf16[32,1792]{1,0:T(8,128)(2,1)S(1)}, bf16[32,1792]{1,0:T(8,128)(2,1)S(1)}, u32[]{:S(2)}, u32[]{:S(2)}) collective-permute-start(bf16[32,1792]{1,0:T(8,128)(2,1)S(1)} %shard_map.64.refs_0_), channel_id=1, source_target_pairs={{0,4},{2,6},{4,0},{6,2},{8,12},{10,14},{12,8},{14,10},{1,5},{3,7},... | collective-permute-start | bytes 344072 | tf_op jit(solution)/shard_map/ppermute | solution.py:23
  19.6 6.0 %collective-permute-start.11 = (bf16[32,1792]{1,0:T(8,128)(2,1)S(1)}, bf16[32,1792]{1,0:T(8,128)(2,1)S(1)}, u32[]{:S(2)}, u32[]{:S(2)}) collective-permute-start(bf16[32,1792]{1,0:T(8,128)(2,1)S(1)} %shard_map.64.refs_0_), channel_id=1, source_target_pairs={{0,2},{2,0},{4,6},{6,4},{8,10},{10,8},{12,14},{14,12},{1,3},{3,1},... | collective-permute-start | bytes 344072 | tf_op jit(solution)/shard_map/ppermute | solution.py:23
  20.2 6.5 %collective-permute-start.12 = (bf16[32,1792]{1,0:T(8,128)(2,1)S(1)}, bf16[32,1792]{1,0:T(8,128)(2,1)S(1)}, u32[]{:S(2)}, u32[]{:S(2)}) collective-permute-start(bf16[32,1792]{1,0:T(8,128)(2,1)S(1)} %shard_map.65.refs_1_), channel_id=1, source_target_pairs={{0,4},{2,6},{4,0},{6,2},{8,12},{10,14},{12,8},{14,10},{1,5},{3,7},... | collective-permute-start | bytes 344072 | tf_op jit(solution)/shard_map/ppermute | solution.py:23
  22.3 6.8 %collective-permute-start.10 = (bf16[32,1792]{1,0:T(8,128)(2,1)S(1)}, bf16[32,1792]{1,0:T(8,128)(2,1)S(1)}, u32[]{:S(2)}, u32[]{:S(2)}) collective-permute-start(bf16[32,1792]{1,0:T(8,128)(2,1)S(1)} %collective-permute-done.5.refs_3_), channel_id=1, source_target_pairs={{0,4},{2,6},{4,0},{6,2},{8,12},{10,14},{12,8},{14,10},{1,5},{3,7},... | collective-permute-start | bytes 344072 | tf_op jit(solution)/shard_map/ppermute | solution.py:23
  24.2 4.9 %collective-permute-start.9 = (bf16[32,1792]{1,0:T(8,128)(2,1)S(1)}, bf16[32,1792]{1,0:T(8,128)(2,1)S(1)}, u32[]{:S(2)}, u32[]{:S(2)}) collective-permute-start(bf16[32,1792]{1,0:T(8,128)(2,1)S(1)} %collective-permute-done.8.refs_0_), channel_id=1, source_target_pairs={{0,2},{2,0},{4,6},{6,4},{8,10},{10,8},{12,14},{14,12},{1,3},{3,1},... | collective-permute-start | bytes 344072 | tf_op jit(solution)/shard_map/ppermute | solution.py:23
  25.6 8.5 %collective-permute-start.6 = (bf16[2,32,1792]{2,1,0:T(8,128)(2,1)S(1)}, bf16[2,32,1792]{2,1,0:T(8,128)(2,1)S(1)}, u32[]{:S(2)}, u32[]{:S(2)}) collective-permute-start(bf16[2,32,1792]{2,1,0:T(8,128)(2,1)S(1)} %collective-permute-done.4.refs_1_), channel_id=1, source_target_pairs={{0,4},{2,6},{4,0},{6,2},{8,12},{10,14},{12,8},{14,10},{1,5},{3,7},... | collective-permute-start | bytes 688136 | tf_op jit(solution)/shard_map/ppermute | solution.py:23
  30.3 5.1 %collective-permute-start.13 = (bf16[32,1792]{1,0:T(8,128)(2,1)S(1)}, bf16[32,1792]{1,0:T(8,128)(2,1)S(1)}, u32[]{:S(2)}, u32[]{:S(2)}) collective-permute-start(bf16[32,1792]{1,0:T(8,128)(2,1)S(1)} %get-tuple-element.60), channel_id=1, source_target_pairs={{0,2},{2,0},{4,6},{6,4},{8,10},{10,8},{12,14},{14,12},{1,3},{3,1},... | collective-permute-start | bytes 344072 | tf_op jit(solution)/shard_map/ppermute | solution.py:23
  31.6 4.8 %collective-permute-start.15 = (bf16[32,1792]{1,0:T(8,128)(2,1)S(1)}, bf16[32,1792]{1,0:T(8,128)(2,1)S(1)}, u32[]{:S(2)}, u32[]{:S(2)}) collective-permute-start(bf16[32,1792]{1,0:T(8,128)(2,1)S(1)} %get-tuple-element.65), channel_id=1, source_target_pairs={{0,4},{2,6},{4,0},{6,2},{8,12},{10,14},{12,8},{14,10},{1,5},{3,7},... | collective-permute-start | bytes 344072 | tf_op jit(solution)/shard_map/ppermute | solution.py:23
  32.2 4.8 %collective-permute-start.16 = (bf16[32,1792]{1,0:T(8,128)(2,1)S(1)}, bf16[32,1792]{1,0:T(8,128)(2,1)S(1)}, u32[]{:S(2)}, u32[]{:S(2)}) collective-permute-start(bf16[32,1792]{1,0:T(8,128)(2,1)S(1)} %get-tuple-element.66), channel_id=1, source_target_pairs={{0,2},{2,0},{4,6},{6,4},{8,10},{10,8},{12,14},{14,12},{1,3},{3,1},... | collective-permute-start | bytes 344072 | tf_op jit(solution)/shard_map/ppermute | solution.py:23
  33.8 5.6 %copy-start.3 = (s32[64,1]{0,1:T(1,128)S(1)}, s32[64,1]{0,1:T(1,128)}, u32[]{:S(2)}) copy-start(s32[64,1]{0,1:T(1,128)} %param.8) | copy-start | bytes 772
  35.4 13.6 %copy-start.4 = (s32[64,1]{0,1:T(1,128)S(1)}, s32[64,1]{0,1:T(1,128)}, u32[]{:S(2)}) copy-start(s32[64,1]{0,1:T(1,128)} %param.7) | copy-start | bytes 772
  37.1 6.5 %collective-permute-start.14 = (bf16[2,32,1792]{2,1,0:T(8,128)(2,1)S(1)}, bf16[2,32,1792]{2,1,0:T(8,128)(2,1)S(1)}, u32[]{:S(2)}, u32[]{:S(2)}) collective-permute-start(bf16[2,32,1792]{2,1,0:T(8,128)(2,1)S(1)} %pad_maximum_fusion.1), channel_id=1, source_target_pairs={{0,4},{2,6},{4,0},{6,2},{8,12},{10,14},{12,8},{14,10},{1,5},{3,7},... | collective-permute-start | bytes 688136 | tf_op jit(solution)/shard_map/ppermute | solution.py:23
  38.5 5.0 %collective-permute-start.17 = (bf16[32,1792]{1,0:T(8,128)(2,1)S(1)}, bf16[32,1792]{1,0:T(8,128)(2,1)S(1)}, u32[]{:S(2)}, u32[]{:S(2)}) collective-permute-start(bf16[32,1792]{1,0:T(8,128)(2,1)S(1)} %add_convert_fusion.1), channel_id=1, source_target_pairs={{0,2},{2,0},{4,6},{6,4},{8,10},{10,8},{12,14},{14,12},{1,3},{3,1},... | collective-permute-start | bytes 344072 | tf_op jit(solution)/shard_map/ppermute | solution.py:23
  39.5 7.0 %collective-permute-start.19 = (bf16[2,32,1792]{2,1,0:T(8,128)(2,1)S(1)}, bf16[2,32,1792]{2,1,0:T(8,128)(2,1)S(1)}, u32[]{:S(2)}, u32[]{:S(2)}) collective-permute-start(bf16[2,32,1792]{2,1,0:T(8,128)(2,1)S(1)} %get-tuple-element.73), channel_id=1, source_target_pairs={{0,2},{2,0},{4,6},{6,4},{8,10},{10,8},{12,14},{14,12},{1,3},{3,1},... | collective-permute-start | bytes 688136 | tf_op jit(solution)/shard_map/ppermute | solution.py:23
  43.6 9.7 %collective-permute-start.21 = (bf16[2,32,1792]{2,1,0:T(8,128)(2,1)S(1)}, bf16[2,32,1792]{2,1,0:T(8,128)(2,1)S(1)}, u32[]{:S(2)}, u32[]{:S(2)}) collective-permute-start(bf16[2,32,1792]{2,1,0:T(8,128)(2,1)S(1)} %add_convert_fusion), channel_id=1, source_target_pairs={{0,8},{2,10},{4,12},{6,14},{8,0},{10,2},{12,4},{14,6},{1,9},{3,11}... | collective-permute-start | bytes 688136 | tf_op jit(solution)/shard_map/ppermute | solution.py:23
  46.5 7.5 %collective-permute-start.20 = (bf16[2,32,1792]{2,1,0:T(8,128)(2,1)S(1)}, bf16[2,32,1792]{2,1,0:T(8,128)(2,1)S(1)}, u32[]{:S(2)}, u32[]{:S(2)}) collective-permute-start(bf16[2,32,1792]{2,1,0:T(8,128)(2,1)S(1)} %shard_map.70), channel_id=1, source_target_pairs={{0,4},{2,6},{4,0},{6,2},{8,12},{10,14},{12,8},{14,10},{1,5},{3,7},... | collective-permute-start | bytes 688136 | tf_op jit(solution)/shard_map/ppermute | solution.py:23
  47.3 6.7 %collective-permute-start.18 = (bf16[2,32,1792]{2,1,0:T(8,128)(2,1)S(1)}, bf16[2,32,1792]{2,1,0:T(8,128)(2,1)S(1)}, u32[]{:S(2)}, u32[]{:S(2)}) collective-permute-start(bf16[2,32,1792]{2,1,0:T(8,128)(2,1)S(1)} %get-tuple-element.71), channel_id=1, source_target_pairs={{0,2},{2,0},{4,6},{6,4},{8,10},{10,8},{12,14},{14,12},{1,3},{3,1},... | collective-permute-start | bytes 688136 | tf_op jit(solution)/shard_map/ppermute | solution.py:23
  54.1 1.4 %collective-permute-start.22 = (bf16[32,1792]{1,0:T(8,128)(2,1)S(1)}, bf16[32,1792]{1,0:T(8,128)(2,1)S(1)}, u32[]{:S(2)}, u32[]{:S(2)}) collective-permute-start(bf16[32,1792]{1,0:T(8,128)(2,1)S(1)} %slice_bitcast_fusion), channel_id=1, source_target_pairs={{0,1},{1,0},{2,3},{3,2},{4,5},{5,4},{6,7},{7,6},{8,9},{9,8},{10,11... | collective-permute-start | bytes 344072 | tf_op jit(solution)/shard_map/ppermute | solution.py:32

commit v6 on v5

--- a/solution.py
+++ b/solution.py
@@ -237,13 +237,13 @@
     r7b = swap(p7b, 2)
     r7a, p1, p2, p3 = tie((r7a, p1, p2, p3))
     s6 = jnp.stack([p6[0] + r7a.astype(f32), p6[1]]).astype(bf16)
-    r5a = swap(p5a, 1)
-    r7b, r5a = tie((r7b, r5a))
-    s5b = (p5b + r7b.astype(f32)).astype(bf16)
+    r5a = cast(swap(p5a, 1), bf16, 2.0)
+    s5b = add(p5b, r7b, 1.0)
     r6 = swap(s6, 2).astype(f32)
     r5b = swap(s5b, 1)
     r5 = jnp.stack([r5a, r5b]).astype(f32)
     sent = (p4 + r6 + r5).astype(bf16)
+    s5b, p3 = tie((s5b, p3))
     r3 = swap(p3, 1)
     s2 = add(p2, r3, 0.1)
     sent, p1 = tie((sent, p1))

time: 56.5 us -> 55.3 us (0.979)
  waiting for transfers between devices: 17.1 us -> 15.7 us
    ppermute x20, waiting for transfers between devices: 15.8 us -> 14.4 us  [swap(): return lax.ppermute(value, 'ep', pairs)]
  transfers between devices with their start and end apart: 23 -> 23, of which waited for: 13 -> 11; matrix products, arithmetic and copies ran while one was open for 1% -> 1% of each run, Pallas kernels for 8% -> 8%
where the time goes in v6:
time: 55.3 us; the launch traced here: 55.1 us
  starting transfers between devices  29.1 us (53%)
  waiting for transfers between devices  15.7 us (28%)
  Pallas kernels  4.44 us (8%)
  local copies, waits for them, and re-layouts  3.57 us (6%)
  other arithmetic  2.11 us (4%)
    ppermute x20, starting transfers between devices, swap(): return lax.ppermute(value, 'ep', pairs)  28.5 us
    ppermute x20, waiting for transfers between devices, swap(): return lax.ppermute(value, 'ep', pairs)  14.4 us
    unnamed x10, local copies, waits for them, and re-layouts  3.55 us
    pallas_call x3, Pallas kernels, expert_block(): pl.pallas_call(functools.partial(expert_kernel, [(None,) * len(b) for b i...  3.51 us
    ppermute x3, waiting for transfers between devices, swap_core(): return lax.ppermute(value, 'tp', [(0, 1), (1, 0)])  1.32 us
  transfers between devices with their start and end apart: 23, of which 11 were waited for; matrix products, arithmetic and copies ran while one was open for 1% of the time, Pallas kernels for 8%

profile of v6, /device:TPU:0, one launch (start us, length us, event | category | flops | bytes accessed | tf_op | source)
XLA Modules:
  0.0 55.1 jit_solution(13905563442730846630)
XLA Ops:
  0.0 1.0 %broadcast_select_fusion.2 = (bf16[32,1792]{1,0:T(8,128)(2,1)S(1)}, bf16[32,1792]{1,0:T(8,128)(2,1)S(1)}) fusion(pred[]{:T(512)S(6)} %eq.3, bf16[64,1792]{1,0:T(8,128)(2,1)} %param.6), kind=kLoop, calls=%fused_computation.13 | loop fusion | flops 114688 | bytes 458753 | tf_op jit(solution)/shard_map/jit(_where)/select_n | solution.py:206
  1.5 3.7 %collective-permute-start.1 = (bf16[32,1792]{1,0:T(8,128)(2,1)S(1)}, bf16[32,1792]{1,0:T(8,128)(2,1)S(1)}, u32[]{:S(2)}, u32[]{:S(2)}) collective-permute-start(bf16[32,1792]{1,0:T(8,128)(2,1)S(1)} %get-tuple-element.40), channel_id=1, source_target_pairs={{0,8},{2,10},{4,12},{6,14},{8,0},{10,2},{12,4},{14,6},{1,9},{3,11}... | collective-permute-start | bytes 344072 | tf_op jit(solution)/shard_map/ppermute | solution.py:23
  5.2 1.6 %collective-permute-start.3 = (bf16[2,32,1792]{2,1,0:T(8,128)(2,1)S(1)}, bf16[2,32,1792]{2,1,0:T(8,128)(2,1)S(1)}, u32[]{:S(2)}, u32[]{:S(2)}) collective-permute-start(bf16[2,32,1792]{2,1,0:T(8,128)(2,1)S(1)} %pad_maximum_fusion.refs_0_), channel_id=1, source_target_pairs={{0,4},{2,6},{4,0},{6,2},{8,12},{10,14},{12,8},{14,10},{1,5},{3,7},... | collective-permute-start | bytes 688136 | tf_op jit(solution)/shard_map/ppermute | solution.py:23
  6.8 1.5 %collective-permute-start.4 = (bf16[2,32,1792]{2,1,0:T(8,128)(2,1)S(1)}, bf16[2,32,1792]{2,1,0:T(8,128)(2,1)S(1)}, u32[]{:S(2)}, u32[]{:S(2)}) collective-permute-start(bf16[2,32,1792]{2,1,0:T(8,128)(2,1)S(1)} %pad_maximum_fusion.refs_0_), channel_id=1, source_target_pairs={{0,2},{2,0},{4,6},{6,4},{8,10},{10,8},{12,14},{14,12},{1,3},{3,1},... | collective-permute-start | bytes 688136 | tf_op jit(solution)/shard_map/ppermute | solution.py:23
  8.3 1.2 %collective-permute-start.2 = (bf16[32,1792]{1,0:T(8,128)(2,1)S(1)}, bf16[32,1792]{1,0:T(8,128)(2,1)S(1)}, u32[]{:S(2)}, u32[]{:S(2)}) collective-permute-start(bf16[32,1792]{1,0:T(8,128)(2,1)S(1)} %collective-permute-done), channel_id=1, source_target_pairs={{0,8},{2,10},{4,12},{6,14},{8,0},{10,2},{12,4},{14,6},{1,9},{3,11}... | collective-permute-start | bytes 344072 | tf_op jit(solution)/shard_map/ppermute | solution.py:23
  9.6 1.2 %copy-done = bf16[1,3584,128]{2,1,0:T(8,128)(2,1)S(1)} copy-done((bf16[1,3584,128]{2,1,0:T(8,128)(2,1)S(1)}, bf16[1,3584,128]{2,1,0:T(8,128)(2,1)}, u32[]{:S(2)}) %copy-start) | copy-done | bytes 917528
  10.7 1.2 %copy-done.1 = bf16[1,3584,128]{2,1,0:T(8,128)(2,1)S(1)} copy-done((bf16[1,3584,128]{2,1,0:T(8,128)(2,1)S(1)}, bf16[1,3584,128]{2,1,0:T(8,128)(2,1)}, u32[]{:S(2)}) %copy-start.1) | copy-done | bytes 917528
  11.9 1.2 %copy-done.2 = bf16[1,128,3584]{2,1,0:T(8,128)(2,1)S(1)} copy-done((bf16[1,128,3584]{2,1,0:T(8,128)(2,1)S(1)}, bf16[1,128,3584]{2,1,0:T(8,128)(2,1)}, u32[]{:S(2)}) %copy-start.2) | copy-done | bytes 917528
  13.1 0.8 %shard_map.66.refs_4_ = bf16[3584,384]{1,0:T(8,128)(2,1)S(1)} custom-call(bf16[3584,128]{1,0:T(8,128)(2,1)S(1)} %bitcast.28, bf16[3584,128]{1,0:T(8,128)(2,1)S(1)} %bitcast.29, bf16[128,3584]{1,0:T(8,128)(2,1)S(1)} %bitcast.30), custom_call_target="tpu_custom_call" | custom-call | flops 2300000000 | tf_op jit(solution)/shard_map/pallas_call | solution.py:49
  13.9 1.6 %collective-permute-done.2.from_ref = bf16[32,1792]{1,0:T(8,128)(2,1)S(1)} collective-permute-done((bf16[32,1792]{1,0:T(8,128)(2,1)S(1)}, bf16[32,1792]{1,0:T(8,128)(2,1)S(1)}, u32[]{:S(2)}, u32[]{:S(2)}) %collective-permute-start.2) | collective-permute-done | bytes 114720 | tf_op jit(solution)/shard_map/ppermute | solution.py:23
  15.6 1.1 %collective-permute-done.3.refs_2_ = bf16[2,32,1792]{2,1,0:T(8,128)(2,1)S(1)} collective-permute-done((bf16[2,32,1792]{2,1,0:T(8,128)(2,1)S(1)}, bf16[2,32,1792]{2,1,0:T(8,128)(2,1)S(1)}, u32[]{:S(2)}, u32[]{:S(2)}) %collective-permute-start.3) | collective-permute-done | bytes 229408 | tf_op jit(solution)/shard_map/ppermute | solution.py:23
  16.7 1.6 %collective-permute-start.5 = (bf16[32,1792]{1,0:T(8,128)(2,1)S(1)}, bf16[32,1792]{1,0:T(8,128)(2,1)S(1)}, u32[]{:S(2)}, u32[]{:S(2)}) collective-permute-start(bf16[32,1792]{1,0:T(8,128)(2,1)S(1)} %shard_map.65.refs_1_), channel_id=1, source_target_pairs={{0,2},{2,0},{4,6},{6,4},{8,10},{10,8},{12,14},{14,12},{1,3},{3,1},... | collective-permute-start | bytes 344072 | tf_op jit(solution)/shard_map/ppermute | solution.py:23
  18.2 1.4 %collective-permute-start.8 = (bf16[32,1792]{1,0:T(8,128)(2,1)S(1)}, bf16[32,1792]{1,0:T(8,128)(2,1)S(1)}, u32[]{:S(2)}, u32[]{:S(2)}) collective-permute-start(bf16[32,1792]{1,0:T(8,128)(2,1)S(1)} %shard_map.64.refs_0_), channel_id=1, source_target_pairs={{0,4},{2,6},{4,0},{6,2},{8,12},{10,14},{12,8},{14,10},{1,5},{3,7},... | collective-permute-start | bytes 344072 | tf_op jit(solution)/shard_map/ppermute | solution.py:23
  20.7 1.6 %collective-permute-done.5.refs_3_ = bf16[32,1792]{1,0:T(8,128)(2,1)S(1)} collective-permute-done((bf16[32,1792]{1,0:T(8,128)(2,1)S(1)}, bf16[32,1792]{1,0:T(8,128)(2,1)S(1)}, u32[]{:S(2)}, u32[]{:S(2)}) %collective-permute-start.5) | collective-permute-done | bytes 114720 | tf_op jit(solution)/shard_map/ppermute | solution.py:23
  22.3 1.8 %collective-permute-start.10 = (bf16[32,1792]{1,0:T(8,128)(2,1)S(1)}, bf16[32,1792]{1,0:T(8,128)(2,1)S(1)}, u32[]{:S(2)}, u32[]{:S(2)}) collective-permute-start(bf16[32,1792]{1,0:T(8,128)(2,1)S(1)} %collective-permute-done.5.refs_3_), channel_id=1, source_target_pairs={{0,4},{2,6},{4,0},{6,2},{8,12},{10,14},{12,8},{14,10},{1,5},{3,7},... | collective-permute-start | bytes 344072 | tf_op jit(solution)/shard_map/ppermute | solution.py:23
  24.2 1.4 %collective-permute-start.9 = (bf16[32,1792]{1,0:T(8,128)(2,1)S(1)}, bf16[32,1792]{1,0:T(8,128)(2,1)S(1)}, u32[]{:S(2)}, u32[]{:S(2)}) collective-permute-start(bf16[32,1792]{1,0:T(8,128)(2,1)S(1)} %collective-permute-done.8.refs_0_), channel_id=1, source_target_pairs={{0,2},{2,0},{4,6},{6,4},{8,10},{10,8},{12,14},{14,12},{1,3},{3,1},... | collective-permute-start | bytes 344072 | tf_op jit(solution)/shard_map/ppermute | solution.py:23
  25.6 1.1 %collective-permute-done.12.refs_1_ = bf16[32,1792]{1,0:T(8,128)(2,1)S(1)} collective-permute-done((bf16[32,1792]{1,0:T(8,128)(2,1)S(1)}, bf16[32,1792]{1,0:T(8,128)(2,1)S(1)}, u32[]{:S(2)}, u32[]{:S(2)}) %collective-permute-start.12) | collective-permute-done | bytes 114720 | tf_op jit(solution)/shard_map/ppermute | solution.py:23
  26.7 1.4 %collective-permute-start.6 = (bf16[2,32,1792]{2,1,0:T(8,128)(2,1)S(1)}, bf16[2,32,1792]{2,1,0:T(8,128)(2,1)S(1)}, u32[]{:S(2)}, u32[]{:S(2)}) collective-permute-start(bf16[2,32,1792]{2,1,0:T(8,128)(2,1)S(1)} %collective-permute-done.4.refs_1_), channel_id=1, source_target_pairs={{0,4},{2,6},{4,0},{6,2},{8,12},{10,14},{12,8},{14,10},{1,5},{3,7},... | collective-permute-start | bytes 688136 | tf_op jit(solution)/shard_map/ppermute | solution.py:23
  28.1 1.1 %shard_map.68 = (f32[2,32,1792]{2,1,0:T(8,128)S(1)}, bf16[32,1792]{1,0:T(8,128)(2,1)S(1)}, f32[32,1792]{1,0:T(8,128)S(1)}) custom-call(bf16[32,1792]{1,0:T(8,128)(2,1)S(1)} %shard_map.64.refs_0_, bf16[32,1792]{1,0:T(8,128)(2,1)S(1)} %shard_map.65.refs_1_, bf16[32,1792]{1,0:T(8,128)(2,1)S(1)} %collective-permute-done.11.refs_2_, ...), custom_call_target="tpu_custom_call" | custom-call | flops 1150000000 | tf_op jit(solution)/shard_map/pallas_call | solution.py:112
  29.3 1.1 %shard_map.69 = (f32[2,32,1792]{2,1,0:T(8,128)S(1)}, bf16[32,1792]{1,0:T(8,128)(2,1)S(1)}, bf16[32,1792]{1,0:T(8,128)(2,1)S(1)}) custom-call(bf16[32,1792]{1,0:T(8,128)(2,1)S(1)} %collective-permute-done.8.refs_0_, bf16[32,1792]{1,0:T(8,128)(2,1)S(1)} %collective-permute-done.12.refs_1_, bf16[32,1792]{1,0:T(8,128)(2,1)S(1)} %collective-permute-done.9.refs_2_, ...), custom_call_target="tpu_custom_call" | custom-call | flops 1150000000 | tf_op jit(solution)/shard_map/pallas_call | solution.py:112
  30.4 1.2 %collective-permute-start.13 = (bf16[32,1792]{1,0:T(8,128)(2,1)S(1)}, bf16[32,1792]{1,0:T(8,128)(2,1)S(1)}, u32[]{:S(2)}, u32[]{:S(2)}) collective-permute-start(bf16[32,1792]{1,0:T(8,128)(2,1)S(1)} %get-tuple-element.59), channel_id=1, source_target_pairs={{0,2},{2,0},{4,6},{6,4},{8,10},{10,8},{12,14},{14,12},{1,3},{3,1},... | collective-permute-start | bytes 344072 | tf_op jit(solution)/shard_map/ppermute | solution.py:23
  32.3 1.5 %collective-permute-start.15 = (bf16[32,1792]{1,0:T(8,128)(2,1)S(1)}, bf16[32,1792]{1,0:T(8,128)(2,1)S(1)}, u32[]{:S(2)}, u32[]{:S(2)}) collective-permute-start(bf16[32,1792]{1,0:T(8,128)(2,1)S(1)} %get-tuple-element.64), channel_id=1, source_target_pairs={{0,2},{2,0},{4,6},{6,4},{8,10},{10,8},{12,14},{14,12},{1,3},{3,1},... | collective-permute-start | bytes 344072 | tf_op jit(solution)/shard_map/ppermute | solution.py:23
  33.8 0.8 %collective-permute-done.6.refs_3_ = bf16[2,32,1792]{2,1,0:T(8,128)(2,1)S(1)} collective-permute-done((bf16[2,32,1792]{2,1,0:T(8,128)(2,1)S(1)}, bf16[2,32,1792]{2,1,0:T(8,128)(2,1)S(1)}, u32[]{:S(2)}, u32[]{:S(2)}) %collective-permute-start.6) | collective-permute-done | bytes 229408 | tf_op jit(solution)/shard_map/ppermute | solution.py:23
  34.6 1.2 %shard_map.67 = (f32[2,32,1792]{2,1,0:T(8,128)S(1)}, bf16[2,32,1792]{2,1,0:T(8,128)(2,1)S(1)}, f32[2,32,1792]{2,1,0:T(8,128)S(1)}, bf16[2,32,1792]{2,1,0:T(8,128)(2,1)S(1)}) custom-call(bf16[2,32,1792]{2,1,0:T(8,128)(2,1)S(1)} %pad_maximum_fusion.refs_0_, bf16[2,32,1792]{2,1,0:T(8,128)(2,1)S(1)} %collective-permute-done.4.refs_1_, ...), custom_call_target="tpu_custom_call" | custom-call | flops 1150000000 | tf_op jit(solution)/shard_map/pallas_call | solution.py:112
  35.9 1.4 %collective-permute-start.14 = (bf16[2,32,1792]{2,1,0:T(8,128)(2,1)S(1)}, bf16[2,32,1792]{2,1,0:T(8,128)(2,1)S(1)}, u32[]{:S(2)}, u32[]{:S(2)}) collective-permute-start(bf16[2,32,1792]{2,1,0:T(8,128)(2,1)S(1)} %pad_maximum_fusion.1), channel_id=1, source_target_pairs={{0,4},{2,6},{4,0},{6,2},{8,12},{10,14},{12,8},{14,10},{1,5},{3,7},... | collective-permute-start | bytes 688136 | tf_op jit(solution)/shard_map/ppermute | solution.py:23
  37.3 1.1 %collective-permute-start.17 = (bf16[32,1792]{1,0:T(8,128)(2,1)S(1)}, bf16[32,1792]{1,0:T(8,128)(2,1)S(1)}, u32[]{:S(2)}, u32[]{:S(2)}) collective-permute-start(bf16[32,1792]{1,0:T(8,128)(2,1)S(1)} %shard_map.71), channel_id=1, source_target_pairs={{0,2},{2,0},{4,6},{6,4},{8,10},{10,8},{12,14},{14,12},{1,3},{3,1},... | collective-permute-start | bytes 344072 | tf_op jit(solution)/shard_map/ppermute | solution.py:23
  38.4 1.0 %collective-permute-start.19 = (bf16[2,32,1792]{2,1,0:T(8,128)(2,1)S(1)}, bf16[2,32,1792]{2,1,0:T(8,128)(2,1)S(1)}, u32[]{:S(2)}, u32[]{:S(2)}) collective-permute-start(bf16[2,32,1792]{2,1,0:T(8,128)(2,1)S(1)} %get-tuple-element.71), channel_id=1, source_target_pairs={{0,2},{2,0},{4,6},{6,4},{8,10},{10,8},{12,14},{14,12},{1,3},{3,1},... | collective-permute-start | bytes 688136 | tf_op jit(solution)/shard_map/ppermute | solution.py:23
  39.4 2.8 %collective-permute-done.17 = bf16[32,1792]{1,0:T(8,128)(2,1)S(1)} collective-permute-done((bf16[32,1792]{1,0:T(8,128)(2,1)S(1)}, bf16[32,1792]{1,0:T(8,128)(2,1)S(1)}, u32[]{:S(2)}, u32[]{:S(2)}) %collective-permute-start.17) | collective-permute-done | bytes 114720 | tf_op jit(solution)/shard_map/ppermute | solution.py:23
  42.4 2.6 %collective-permute-start.21 = (bf16[2,32,1792]{2,1,0:T(8,128)(2,1)S(1)}, bf16[2,32,1792]{2,1,0:T(8,128)(2,1)S(1)}, u32[]{:S(2)}, u32[]{:S(2)}) collective-permute-start(bf16[2,32,1792]{2,1,0:T(8,128)(2,1)S(1)} %add_convert_fusion), channel_id=1, source_target_pairs={{0,8},{2,10},{4,12},{6,14},{8,0},{10,2},{12,4},{14,6},{1,9},{3,11}... | collective-permute-start | bytes 688136 | tf_op jit(solution)/shard_map/ppermute | solution.py:23
  45.0 1.8 %collective-permute-start.20 = (bf16[2,32,1792]{2,1,0:T(8,128)(2,1)S(1)}, bf16[2,32,1792]{2,1,0:T(8,128)(2,1)S(1)}, u32[]{:S(2)}, u32[]{:S(2)}) collective-permute-start(bf16[2,32,1792]{2,1,0:T(8,128)(2,1)S(1)} %shard_map.72), channel_id=1, source_target_pairs={{0,4},{2,6},{4,0},{6,2},{8,12},{10,14},{12,8},{14,10},{1,5},{3,7},... | collective-permute-start | bytes 688136 | tf_op jit(solution)/shard_map/ppermute | solution.py:23
  47.5 4.8 %collective-permute-done.21.from_ref = bf16[2,32,1792]{2,1,0:T(8,128)(2,1)S(1)} collective-permute-done((bf16[2,32,1792]{2,1,0:T(8,128)(2,1)S(1)}, bf16[2,32,1792]{2,1,0:T(8,128)(2,1)S(1)}, u32[]{:S(2)}, u32[]{:S(2)}) %collective-permute-start.21) | collective-permute-done | bytes 229408 | tf_op jit(solution)/shard_map/ppermute | solution.py:23
  53.0 1.3 %collective-permute-done.22 = bf16[32,1792]{1,0:T(8,128)(2,1)S(1)} collective-permute-done((bf16[32,1792]{1,0:T(8,128)(2,1)S(1)}, bf16[32,1792]{1,0:T(8,128)(2,1)S(1)}, u32[]{:S(2)}, u32[]{:S(2)}) %collective-permute-start.22) | collective-permute-done | bytes 114720 | tf_op jit(solution)/shard_map/ppermute | solution.py:32
  (46 shorter events, 4.8 us)
Async XLA Ops:
  1.0 4.2 %collective-permute-start = (bf16[32,1792]{1,0:T(8,128)(2,1)S(1)}, bf16[32,1792]{1,0:T(8,128)(2,1)S(1)}, u32[]{:S(2)}, u32[]{:S(2)}) collective-permute-start(bf16[32,1792]{1,0:T(8,128)(2,1)S(1)} %get-tuple-element.41), channel_id=1, source_target_pairs={{0,1},{1,0},{2,3},{3,2},{4,5},{5,4},{6,7},{7,6},{8,9},{9,8},{10,11... | collective-permute-start | bytes 344072 | tf_op jit(solution)/shard_map/ppermute | solution.py:32
  1.5 12.4 %collective-permute-start.1 = (bf16[32,1792]{1,0:T(8,128)(2,1)S(1)}, bf16[32,1792]{1,0:T(8,128)(2,1)S(1)}, u32[]{:S(2)}, u32[]{:S(2)}) collective-permute-start(bf16[32,1792]{1,0:T(8,128)(2,1)S(1)} %get-tuple-element.40), channel_id=1, source_target_pairs={{0,8},{2,10},{4,12},{6,14},{8,0},{10,2},{12,4},{14,6},{1,9},{3,11}... | collective-permute-start | bytes 344072 | tf_op jit(solution)/shard_map/ppermute | solution.py:23
  5.2 11.5 %collective-permute-start.3 = (bf16[2,32,1792]{2,1,0:T(8,128)(2,1)S(1)}, bf16[2,32,1792]{2,1,0:T(8,128)(2,1)S(1)}, u32[]{:S(2)}, u32[]{:S(2)}) collective-permute-start(bf16[2,32,1792]{2,1,0:T(8,128)(2,1)S(1)} %pad_maximum_fusion.refs_0_), channel_id=1, source_target_pairs={{0,4},{2,6},{4,0},{6,2},{8,12},{10,14},{12,8},{14,10},{1,5},{3,7},... | collective-permute-start | bytes 688136 | tf_op jit(solution)/shard_map/ppermute | solution.py:23
  6.8 9.8 %collective-permute-start.4 = (bf16[2,32,1792]{2,1,0:T(8,128)(2,1)S(1)}, bf16[2,32,1792]{2,1,0:T(8,128)(2,1)S(1)}, u32[]{:S(2)}, u32[]{:S(2)}) collective-permute-start(bf16[2,32,1792]{2,1,0:T(8,128)(2,1)S(1)} %pad_maximum_fusion.refs_0_), channel_id=1, source_target_pairs={{0,2},{2,0},{4,6},{6,4},{8,10},{10,8},{12,14},{14,12},{1,3},{3,1},... | collective-permute-start | bytes 688136 | tf_op jit(solution)/shard_map/ppermute | solution.py:23
  8.3 7.3 %collective-permute-start.2 = (bf16[32,1792]{1,0:T(8,128)(2,1)S(1)}, bf16[32,1792]{1,0:T(8,128)(2,1)S(1)}, u32[]{:S(2)}, u32[]{:S(2)}) collective-permute-start(bf16[32,1792]{1,0:T(8,128)(2,1)S(1)} %collective-permute-done), channel_id=1, source_target_pairs={{0,8},{2,10},{4,12},{6,14},{8,0},{10,2},{12,4},{14,6},{1,9},{3,11}... | collective-permute-start | bytes 344072 | tf_op jit(solution)/shard_map/ppermute | solution.py:23
  9.6 1.2 %copy-start = (bf16[1,3584,128]{2,1,0:T(8,128)(2,1)S(1)}, bf16[1,3584,128]{2,1,0:T(8,128)(2,1)}, u32[]{:S(2)}) copy-start(bf16[1,3584,128]{2,1,0:T(8,128)(2,1)} %param.9) | copy-start | bytes 2752516
  10.7 1.2 %copy-start.1 = (bf16[1,3584,128]{2,1,0:T(8,128)(2,1)S(1)}, bf16[1,3584,128]{2,1,0:T(8,128)(2,1)}, u32[]{:S(2)}) copy-start(bf16[1,3584,128]{2,1,0:T(8,128)(2,1)} %param.10) | copy-start | bytes 2752516
  11.9 1.2 %copy-start.2 = (bf16[1,128,3584]{2,1,0:T(8,128)(2,1)S(1)}, bf16[1,128,3584]{2,1,0:T(8,128)(2,1)}, u32[]{:S(2)}) copy-start(bf16[1,128,3584]{2,1,0:T(8,128)(2,1)} %param.11) | copy-start | bytes 2752516
  16.7 11.4 %collective-permute-start.7 = (bf16[3584,384]{1,0:T(8,128)(2,1)S(1)}, bf16[3584,384]{1,0:T(8,128)(2,1)S(1)}, u32[]{:S(2)}, u32[]{:S(2)}) collective-permute-start(bf16[3584,384]{1,0:T(8,128)(2,1)S(1)} %shard_map.66.refs_4_), channel_id=1, source_target_pairs={{0,1},{1,0},{2,3},{3,2},{4,5},{5,4},{6,7},{7,6},{8,9},{9,8},{10,11... | collective-permute-start | bytes 8257544 | tf_op jit(solution)/shard_map/ppermute | solution.py:32
  16.7 5.6 %collective-permute-start.5 = (bf16[32,1792]{1,0:T(8,128)(2,1)S(1)}, bf16[32,1792]{1,0:T(8,128)(2,1)S(1)}, u32[]{:S(2)}, u32[]{:S(2)}) collective-permute-start(bf16[32,1792]{1,0:T(8,128)(2,1)S(1)} %shard_map.65.refs_1_), channel_id=1, source_target_pairs={{0,2},{2,0},{4,6},{6,4},{8,10},{10,8},{12,14},{14,12},{1,3},{3,1},... | collective-permute-start | bytes 344072 | tf_op jit(solution)/shard_map/ppermute | solution.py:23
  18.2 6.0 %collective-permute-start.8 = (bf16[32,1792]{1,0:T(8,128)(2,1)S(1)}, bf16[32,1792]{1,0:T(8,128)(2,1)S(1)}, u32[]{:S(2)}, u32[]{:S(2)}) collective-permute-start(bf16[32,1792]{1,0:T(8,128)(2,1)S(1)} %shard_map.64.refs_0_), channel_id=1, source_target_pairs={{0,4},{2,6},{4,0},{6,2},{8,12},{10,14},{12,8},{14,10},{1,5},{3,7},... | collective-permute-start | bytes 344072 | tf_op jit(solution)/shard_map/ppermute | solution.py:23
  19.6 6.0 %collective-permute-start.11 = (bf16[32,1792]{1,0:T(8,128)(2,1)S(1)}, bf16[32,1792]{1,0:T(8,128)(2,1)S(1)}, u32[]{:S(2)}, u32[]{:S(2)}) collective-permute-start(bf16[32,1792]{1,0:T(8,128)(2,1)S(1)} %shard_map.64.refs_0_), channel_id=1, source_target_pairs={{0,2},{2,0},{4,6},{6,4},{8,10},{10,8},{12,14},{14,12},{1,3},{3,1},... | collective-permute-start | bytes 344072 | tf_op jit(solution)/shard_map/ppermute | solution.py:23
  20.2 6.5 %collective-permute-start.12 = (bf16[32,1792]{1,0:T(8,128)(2,1)S(1)}, bf16[32,1792]{1,0:T(8,128)(2,1)S(1)}, u32[]{:S(2)}, u32[]{:S(2)}) collective-permute-start(bf16[32,1792]{1,0:T(8,128)(2,1)S(1)} %shard_map.65.refs_1_), channel_id=1, source_target_pairs={{0,4},{2,6},{4,0},{6,2},{8,12},{10,14},{12,8},{14,10},{1,5},{3,7},... | collective-permute-start | bytes 344072 | tf_op jit(solution)/shard_map/ppermute | solution.py:23
  22.3 6.9 %collective-permute-start.10 = (bf16[32,1792]{1,0:T(8,128)(2,1)S(1)}, bf16[32,1792]{1,0:T(8,128)(2,1)S(1)}, u32[]{:S(2)}, u32[]{:S(2)}) collective-permute-start(bf16[32,1792]{1,0:T(8,128)(2,1)S(1)} %collective-permute-done.5.refs_3_), channel_id=1, source_target_pairs={{0,4},{2,6},{4,0},{6,2},{8,12},{10,14},{12,8},{14,10},{1,5},{3,7},... | collective-permute-start | bytes 344072 | tf_op jit(solution)/shard_map/ppermute | solution.py:23
  24.2 5.0 %collective-permute-start.9 = (bf16[32,1792]{1,0:T(8,128)(2,1)S(1)}, bf16[32,1792]{1,0:T(8,128)(2,1)S(1)}, u32[]{:S(2)}, u32[]{:S(2)}) collective-permute-start(bf16[32,1792]{1,0:T(8,128)(2,1)S(1)} %collective-permute-done.8.refs_0_), channel_id=1, source_target_pairs={{0,2},{2,0},{4,6},{6,4},{8,10},{10,8},{12,14},{14,12},{1,3},{3,1},... | collective-permute-start | bytes 344072 | tf_op jit(solution)/shard_map/ppermute | solution.py:23
  26.7 7.9 %collective-permute-start.6 = (bf16[2,32,1792]{2,1,0:T(8,128)(2,1)S(1)}, bf16[2,32,1792]{2,1,0:T(8,128)(2,1)S(1)}, u32[]{:S(2)}, u32[]{:S(2)}) collective-permute-start(bf16[2,32,1792]{2,1,0:T(8,128)(2,1)S(1)} %collective-permute-done.4.refs_1_), channel_id=1, source_target_pairs={{0,4},{2,6},{4,0},{6,2},{8,12},{10,14},{12,8},{14,10},{1,5},{3,7},... | collective-permute-start | bytes 688136 | tf_op jit(solution)/shard_map/ppermute | solution.py:23
  29.2 2.3 %copy-start.3 = (s32[64,1]{0,1:T(1,128)S(1)}, s32[64,1]{0,1:T(1,128)}, u32[]{:S(2)}) copy-start(s32[64,1]{0,1:T(1,128)} %param.8) | copy-start | bytes 772
  30.4 5.4 %collective-permute-start.13 = (bf16[32,1792]{1,0:T(8,128)(2,1)S(1)}, bf16[32,1792]{1,0:T(8,128)(2,1)S(1)}, u32[]{:S(2)}, u32[]{:S(2)}) collective-permute-start(bf16[32,1792]{1,0:T(8,128)(2,1)S(1)} %get-tuple-element.59), channel_id=1, source_target_pairs={{0,2},{2,0},{4,6},{6,4},{8,10},{10,8},{12,14},{14,12},{1,3},{3,1},... | collective-permute-start | bytes 344072 | tf_op jit(solution)/shard_map/ppermute | solution.py:23
  31.7 5.6 %collective-permute-start.16 = (bf16[32,1792]{1,0:T(8,128)(2,1)S(1)}, bf16[32,1792]{1,0:T(8,128)(2,1)S(1)}, u32[]{:S(2)}, u32[]{:S(2)}) collective-permute-start(bf16[32,1792]{1,0:T(8,128)(2,1)S(1)} %get-tuple-element.66), channel_id=1, source_target_pairs={{0,4},{2,6},{4,0},{6,2},{8,12},{10,14},{12,8},{14,10},{1,5},{3,7},... | collective-permute-start | bytes 344072 | tf_op jit(solution)/shard_map/ppermute | solution.py:23
  32.3 7.1 %collective-permute-start.15 = (bf16[32,1792]{1,0:T(8,128)(2,1)S(1)}, bf16[32,1792]{1,0:T(8,128)(2,1)S(1)}, u32[]{:S(2)}, u32[]{:S(2)}) collective-permute-start(bf16[32,1792]{1,0:T(8,128)(2,1)S(1)} %get-tuple-element.64), channel_id=1, source_target_pairs={{0,2},{2,0},{4,6},{6,4},{8,10},{10,8},{12,14},{14,12},{1,3},{3,1},... | collective-permute-start | bytes 344072 | tf_op jit(solution)/shard_map/ppermute | solution.py:23
  35.9 6.4 %collective-permute-start.14 = (bf16[2,32,1792]{2,1,0:T(8,128)(2,1)S(1)}, bf16[2,32,1792]{2,1,0:T(8,128)(2,1)S(1)}, u32[]{:S(2)}, u32[]{:S(2)}) collective-permute-start(bf16[2,32,1792]{2,1,0:T(8,128)(2,1)S(1)} %pad_maximum_fusion.1), channel_id=1, source_target_pairs={{0,4},{2,6},{4,0},{6,2},{8,12},{10,14},{12,8},{14,10},{1,5},{3,7},... | collective-permute-start | bytes 688136 | tf_op jit(solution)/shard_map/ppermute | solution.py:23
  37.3 10.1 %copy-start.4 = (s32[64,1]{0,1:T(1,128)S(1)}, s32[64,1]{0,1:T(1,128)}, u32[]{:S(2)}) copy-start(s32[64,1]{0,1:T(1,128)} %param.7) | copy-start | bytes 772
  37.3 5.0 %collective-permute-start.17 = (bf16[32,1792]{1,0:T(8,128)(2,1)S(1)}, bf16[32,1792]{1,0:T(8,128)(2,1)S(1)}, u32[]{:S(2)}, u32[]{:S(2)}) collective-permute-start(bf16[32,1792]{1,0:T(8,128)(2,1)S(1)} %shard_map.71), channel_id=1, source_target_pairs={{0,2},{2,0},{4,6},{6,4},{8,10},{10,8},{12,14},{14,12},{1,3},{3,1},... | collective-permute-start | bytes 344072 | tf_op jit(solution)/shard_map/ppermute | solution.py:23
  38.4 6.5 %collective-permute-start.19 = (bf16[2,32,1792]{2,1,0:T(8,128)(2,1)S(1)}, bf16[2,32,1792]{2,1,0:T(8,128)(2,1)S(1)}, u32[]{:S(2)}, u32[]{:S(2)}) collective-permute-start(bf16[2,32,1792]{2,1,0:T(8,128)(2,1)S(1)} %get-tuple-element.71), channel_id=1, source_target_pairs={{0,2},{2,0},{4,6},{6,4},{8,10},{10,8},{12,14},{14,12},{1,3},{3,1},... | collective-permute-start | bytes 688136 | tf_op jit(solution)/shard_map/ppermute | solution.py:23
  42.4 10.0 %collective-permute-start.21 = (bf16[2,32,1792]{2,1,0:T(8,128)(2,1)S(1)}, bf16[2,32,1792]{2,1,0:T(8,128)(2,1)S(1)}, u32[]{:S(2)}, u32[]{:S(2)}) collective-permute-start(bf16[2,32,1792]{2,1,0:T(8,128)(2,1)S(1)} %add_convert_fusion), channel_id=1, source_target_pairs={{0,8},{2,10},{4,12},{6,14},{8,0},{10,2},{12,4},{14,6},{1,9},{3,11}... | collective-permute-start | bytes 688136 | tf_op jit(solution)/shard_map/ppermute | solution.py:23
  45.0 7.8 %collective-permute-start.20 = (bf16[2,32,1792]{2,1,0:T(8,128)(2,1)S(1)}, bf16[2,32,1792]{2,1,0:T(8,128)(2,1)S(1)}, u32[]{:S(2)}, u32[]{:S(2)}) collective-permute-start(bf16[2,32,1792]{2,1,0:T(8,128)(2,1)S(1)} %shard_map.72), channel_id=1, source_target_pairs={{0,4},{2,6},{4,0},{6,2},{8,12},{10,14},{12,8},{14,10},{1,5},{3,7},... | collective-permute-start | bytes 688136 | tf_op jit(solution)/shard_map/ppermute | solution.py:23
  46.8 6.0 %collective-permute-start.18 = (bf16[2,32,1792]{2,1,0:T(8,128)(2,1)S(1)}, bf16[2,32,1792]{2,1,0:T(8,128)(2,1)S(1)}, u32[]{:S(2)}, u32[]{:S(2)}) collective-permute-start(bf16[2,32,1792]{2,1,0:T(8,128)(2,1)S(1)} %get-tuple-element.68), channel_id=1, source_target_pairs={{0,2},{2,0},{4,6},{6,4},{8,10},{10,8},{12,14},{14,12},{1,3},{3,1},... | collective-permute-start | bytes 688136 | tf_op jit(solution)/shard_map/ppermute | solution.py:23
  53.0 1.4 %collective-permute-start.22 = (bf16[32,1792]{1,0:T(8,128)(2,1)S(1)}, bf16[32,1792]{1,0:T(8,128)(2,1)S(1)}, u32[]{:S(2)}, u32[]{:S(2)}) collective-permute-start(bf16[32,1792]{1,0:T(8,128)(2,1)S(1)} %slice_bitcast_fusion), channel_id=1, source_target_pairs={{0,1},{1,0},{2,3},{3,2},{4,5},{5,4},{6,7},{7,6},{8,9},{9,8},{10,11... | collective-permute-start | bytes 344072 | tf_op jit(solution)/shard_map/ppermute | solution.py:32

commit v7 on v6

--- a/solution.py
+++ b/solution.py
@@ -212,15 +212,16 @@
         return expert_block(blocks, weights, types, work)
 
     both0 = jnp.stack([a0, b0])
-    z2a = cast(swap(a0, 4), bf16, 0.3)
+    z2a = swap(a0, 4)
     z2b = cast(swap(b0, 4), bf16, 0.3)
     z1 = swap(both0, 2)
     x0 = swap(both0, 1)
-    z2a, z2b, z1, x0, ours = tie((z2a, z2b, z1, x0, ours))
+    z2a, ours = tie((z2a, ours))
+    m6a = cast(swap(z2a, 2), bf16, 40.0)
+    m5a = swap(z2a, 1)
+    z2b, z1, x0, ours = tie((z2b, z1, x0, ours))
     weights = [ours, swap_core(ours)]
     m5b = swap(z2b, 1)
-    m5a = swap(z2a, 1)
-    m6a = swap(z2a, 2)
     m6b = swap(z2b, 2)
     m5a, m6b = tie((m5a, m6b))
     m5b, held = tie((m5b, x0))
@@ -233,8 +234,8 @@
     p0, p1, p2, p3 = expert(
         ((both0,), (x0,), (z1,), (m3,)), ((f32,), (bf16,), (f32,), (bf16,)), 1.0
     )
+    r7b = swap(p7b, 2)
     r7a = swap(p7a, 1)
-    r7b = swap(p7b, 2)
     r7a, p1, p2, p3 = tie((r7a, p1, p2, p3))
     s6 = jnp.stack([p6[0] + r7a.astype(f32), p6[1]]).astype(bf16)
     r5a = cast(swap(p5a, 1), bf16, 2.0)

time: 55.3 us -> 55.2 us (level)
  starting transfers between devices: 29.1 us -> 26.2 us
  waiting for transfers between devices: 15.7 us -> 18.5 us
    ppermute x20, starting transfers between devices: 28.5 us -> 25.6 us  [swap(): return lax.ppermute(value, 'ep', pairs)]
    ppermute x20, waiting for transfers between devices: 14.4 us -> 16.9 us  [swap(): return lax.ppermute(value, 'ep', pairs)]
  transfers between devices with their start and end apart: 23 -> 23, of which waited for: 11 -> 12; matrix products, arithmetic and copies ran while one was open for 1% -> 1% of each run, Pallas kernels for 8% -> 8%
where the time goes in v7:
time: 55.2 us; the launch traced here: 54.9 us
  starting transfers between devices  26.2 us (47%)
  waiting for transfers between devices  18.5 us (34%)
  Pallas kernels  4.43 us (8%)
  local copies, waits for them, and re-layouts  3.57 us (6%)
  other arithmetic  2.11 us (4%)
    ppermute x20, starting transfers between devices, swap(): return lax.ppermute(value, 'ep', pairs)  25.6 us
    ppermute x20, waiting for transfers between devices, swap(): return lax.ppermute(value, 'ep', pairs)  16.9 us
    unnamed x10, local copies, waits for them, and re-layouts  3.55 us
    pallas_call x3, Pallas kernels, expert_block(): pl.pallas_call(functools.partial(expert_kernel, [(None,) * len(b) for b i...  3.5 us
    ppermute x3, waiting for transfers between devices, swap_core(): return lax.ppermute(value, 'tp', [(0, 1), (1, 0)])  1.62 us
  transfers between devices with their start and end apart: 23, of which 12 were waited for; matrix products, arithmetic and copies ran while one was open for 1% of the time, Pallas kernels for 8%

profile of v7, /device:TPU:0, one launch (start us, length us, event | category | flops | bytes accessed | tf_op | source)
XLA Modules:
  0.0 54.9 jit_solution(17056293219598452808)
XLA Ops:
  0.0 1.0 %broadcast_select_fusion.2 = (bf16[32,1792]{1,0:T(8,128)(2,1)S(1)}, bf16[32,1792]{1,0:T(8,128)(2,1)S(1)}) fusion(pred[]{:T(512)S(6)} %eq.3, bf16[64,1792]{1,0:T(8,128)(2,1)} %param.6), kind=kLoop, calls=%fused_computation.13 | loop fusion | flops 114688 | bytes 458753 | tf_op jit(solution)/shard_map/jit(_where)/select_n | solution.py:206
  1.5 3.7 %collective-permute-start.4 = (bf16[32,1792]{1,0:T(8,128)(2,1)S(1)}, bf16[32,1792]{1,0:T(8,128)(2,1)S(1)}, u32[]{:S(2)}, u32[]{:S(2)}) collective-permute-start(bf16[32,1792]{1,0:T(8,128)(2,1)S(1)} %get-tuple-element.41), channel_id=1, source_target_pairs={{0,8},{2,10},{4,12},{6,14},{8,0},{10,2},{12,4},{14,6},{1,9},{3,11}... | collective-permute-start | bytes 344072 | tf_op jit(solution)/shard_map/ppermute | solution.py:23
  5.2 1.6 %collective-permute-start.2 = (bf16[2,32,1792]{2,1,0:T(8,128)(2,1)S(1)}, bf16[2,32,1792]{2,1,0:T(8,128)(2,1)S(1)}, u32[]{:S(2)}, u32[]{:S(2)}) collective-permute-start(bf16[2,32,1792]{2,1,0:T(8,128)(2,1)S(1)} %pad_maximum_fusion.refs_0_), channel_id=1, source_target_pairs={{0,4},{2,6},{4,0},{6,2},{8,12},{10,14},{12,8},{14,10},{1,5},{3,7},... | collective-permute-start | bytes 688136 | tf_op jit(solution)/shard_map/ppermute | solution.py:23
  6.8 1.5 %collective-permute-start.3 = (bf16[2,32,1792]{2,1,0:T(8,128)(2,1)S(1)}, bf16[2,32,1792]{2,1,0:T(8,128)(2,1)S(1)}, u32[]{:S(2)}, u32[]{:S(2)}) collective-permute-start(bf16[2,32,1792]{2,1,0:T(8,128)(2,1)S(1)} %pad_maximum_fusion.refs_0_), channel_id=1, source_target_pairs={{0,2},{2,0},{4,6},{6,4},{8,10},{10,8},{12,14},{14,12},{1,3},{3,1},... | collective-permute-start | bytes 688136 | tf_op jit(solution)/shard_map/ppermute | solution.py:23
  8.3 1.2 %collective-permute-start.1 = (bf16[32,1792]{1,0:T(8,128)(2,1)S(1)}, bf16[32,1792]{1,0:T(8,128)(2,1)S(1)}, u32[]{:S(2)}, u32[]{:S(2)}) collective-permute-start(bf16[32,1792]{1,0:T(8,128)(2,1)S(1)} %collective-permute-done), channel_id=1, source_target_pairs={{0,8},{2,10},{4,12},{6,14},{8,0},{10,2},{12,4},{14,6},{1,9},{3,11}... | collective-permute-start | bytes 344072 | tf_op jit(solution)/shard_map/ppermute | solution.py:23
  9.6 1.2 %copy-done = bf16[1,3584,128]{2,1,0:T(8,128)(2,1)S(1)} copy-done((bf16[1,3584,128]{2,1,0:T(8,128)(2,1)S(1)}, bf16[1,3584,128]{2,1,0:T(8,128)(2,1)}, u32[]{:S(2)}) %copy-start) | copy-done | bytes 917528
  10.7 1.2 %copy-done.1 = bf16[1,3584,128]{2,1,0:T(8,128)(2,1)S(1)} copy-done((bf16[1,3584,128]{2,1,0:T(8,128)(2,1)S(1)}, bf16[1,3584,128]{2,1,0:T(8,128)(2,1)}, u32[]{:S(2)}) %copy-start.1) | copy-done | bytes 917528
  11.9 1.2 %copy-done.2 = bf16[1,128,3584]{2,1,0:T(8,128)(2,1)S(1)} copy-done((bf16[1,128,3584]{2,1,0:T(8,128)(2,1)S(1)}, bf16[1,128,3584]{2,1,0:T(8,128)(2,1)}, u32[]{:S(2)}) %copy-start.2) | copy-done | bytes 917528
  15.0 1.1 %collective-permute-done.1.from_ref = bf16[32,1792]{1,0:T(8,128)(2,1)S(1)} collective-permute-done((bf16[32,1792]{1,0:T(8,128)(2,1)S(1)}, bf16[32,1792]{1,0:T(8,128)(2,1)S(1)}, u32[]{:S(2)}, u32[]{:S(2)}) %collective-permute-start.1) | collective-permute-done | bytes 114720 | tf_op jit(solution)/shard_map/ppermute | solution.py:23
  16.1 1.3 %collective-permute-done.2.refs_2_ = bf16[2,32,1792]{2,1,0:T(8,128)(2,1)S(1)} collective-permute-done((bf16[2,32,1792]{2,1,0:T(8,128)(2,1)S(1)}, bf16[2,32,1792]{2,1,0:T(8,128)(2,1)S(1)}, u32[]{:S(2)}, u32[]{:S(2)}) %collective-permute-start.2) | collective-permute-done | bytes 229408 | tf_op jit(solution)/shard_map/ppermute | solution.py:23
  17.4 1.6 %collective-permute-start.5 = (bf16[32,1792]{1,0:T(8,128)(2,1)S(1)}, bf16[32,1792]{1,0:T(8,128)(2,1)S(1)}, u32[]{:S(2)}, u32[]{:S(2)}) collective-permute-start(bf16[32,1792]{1,0:T(8,128)(2,1)S(1)} %shard_map.64.refs_1_), channel_id=1, source_target_pairs={{0,2},{2,0},{4,6},{6,4},{8,10},{10,8},{12,14},{14,12},{1,3},{3,1},... | collective-permute-start | bytes 344072 | tf_op jit(solution)/shard_map/ppermute | solution.py:23
  19.0 1.0 %collective-permute-start.12 = (bf16[32,1792]{1,0:T(8,128)(2,1)S(1)}, bf16[32,1792]{1,0:T(8,128)(2,1)S(1)}, u32[]{:S(2)}, u32[]{:S(2)}) collective-permute-start(bf16[32,1792]{1,0:T(8,128)(2,1)S(1)} %shard_map.64.refs_1_), channel_id=1, source_target_pairs={{0,4},{2,6},{4,0},{6,2},{8,12},{10,14},{12,8},{14,10},{1,5},{3,7},... | collective-permute-start | bytes 344072 | tf_op jit(solution)/shard_map/ppermute | solution.py:23
  20.0 1.0 %collective-permute-start.9 = (bf16[32,1792]{1,0:T(8,128)(2,1)S(1)}, bf16[32,1792]{1,0:T(8,128)(2,1)S(1)}, u32[]{:S(2)}, u32[]{:S(2)}) collective-permute-start(bf16[32,1792]{1,0:T(8,128)(2,1)S(1)} %shard_map.67.refs_0_), channel_id=1, source_target_pairs={{0,2},{2,0},{4,6},{6,4},{8,10},{10,8},{12,14},{14,12},{1,3},{3,1},... | collective-permute-start | bytes 344072 | tf_op jit(solution)/shard_map/ppermute | solution.py:23
  21.0 1.1 %collective-permute-done.5.refs_3_ = bf16[32,1792]{1,0:T(8,128)(2,1)S(1)} collective-permute-done((bf16[32,1792]{1,0:T(8,128)(2,1)S(1)}, bf16[32,1792]{1,0:T(8,128)(2,1)S(1)}, u32[]{:S(2)}, u32[]{:S(2)}) %collective-permute-start.5) | collective-permute-done | bytes 114720 | tf_op jit(solution)/shard_map/ppermute | solution.py:23
  22.2 1.1 %collective-permute-start.10 = (bf16[32,1792]{1,0:T(8,128)(2,1)S(1)}, bf16[32,1792]{1,0:T(8,128)(2,1)S(1)}, u32[]{:S(2)}, u32[]{:S(2)}) collective-permute-start(bf16[32,1792]{1,0:T(8,128)(2,1)S(1)} %collective-permute-done.5.refs_3_), channel_id=1, source_target_pairs={{0,4},{2,6},{4,0},{6,2},{8,12},{10,14},{12,8},{14,10},{1,5},{3,7},... | collective-permute-start | bytes 344072 | tf_op jit(solution)/shard_map/ppermute | solution.py:23
  23.3 1.1 %collective-permute-done.12.refs_1_ = bf16[32,1792]{1,0:T(8,128)(2,1)S(1)} collective-permute-done((bf16[32,1792]{1,0:T(8,128)(2,1)S(1)}, bf16[32,1792]{1,0:T(8,128)(2,1)S(1)}, u32[]{:S(2)}, u32[]{:S(2)}) %collective-permute-start.12) | collective-permute-done | bytes 114720 | tf_op jit(solution)/shard_map/ppermute | solution.py:23
  25.1 1.1 %shard_map.68 = (f32[2,32,1792]{2,1,0:T(8,128)S(1)}, bf16[32,1792]{1,0:T(8,128)(2,1)S(1)}, f32[32,1792]{1,0:T(8,128)S(1)}) custom-call(bf16[32,1792]{1,0:T(8,128)(2,1)S(1)} %collective-permute-done.4.refs_0_, bf16[32,1792]{1,0:T(8,128)(2,1)S(1)} %shard_map.64.refs_1_, bf16[32,1792]{1,0:T(8,128)(2,1)S(1)} %collective-permute-done.11.refs_2_, ...), custom_call_target="tpu_custom_call" | custom-call | flops 1150000000 | tf_op jit(solution)/shard_map/pallas_call | solution.py:112
  26.2 2.0 %collective-permute-done.10.refs_3_ = bf16[32,1792]{1,0:T(8,128)(2,1)S(1)} collective-permute-done((bf16[32,1792]{1,0:T(8,128)(2,1)S(1)}, bf16[32,1792]{1,0:T(8,128)(2,1)S(1)}, u32[]{:S(2)}, u32[]{:S(2)}) %collective-permute-start.10) | collective-permute-done | bytes 114720 | tf_op jit(solution)/shard_map/ppermute | solution.py:23
  28.2 1.1 %shard_map.69 = (f32[2,32,1792]{2,1,0:T(8,128)S(1)}, bf16[32,1792]{1,0:T(8,128)(2,1)S(1)}, bf16[32,1792]{1,0:T(8,128)(2,1)S(1)}) custom-call(bf16[32,1792]{1,0:T(8,128)(2,1)S(1)} %shard_map.67.refs_0_, bf16[32,1792]{1,0:T(8,128)(2,1)S(1)} %collective-permute-done.12.refs_1_, bf16[32,1792]{1,0:T(8,128)(2,1)S(1)} %collective-permute-done.9.refs_2_, ...), custom_call_target="tpu_custom_call" | custom-call | flops 1150000000 | tf_op jit(solution)/shard_map/pallas_call | solution.py:112
  29.4 1.7 %collective-permute-start.13 = (bf16[32,1792]{1,0:T(8,128)(2,1)S(1)}, bf16[32,1792]{1,0:T(8,128)(2,1)S(1)}, u32[]{:S(2)}, u32[]{:S(2)}) collective-permute-start(bf16[32,1792]{1,0:T(8,128)(2,1)S(1)} %get-tuple-element.61), channel_id=1, source_target_pairs={{0,2},{2,0},{4,6},{6,4},{8,10},{10,8},{12,14},{14,12},{1,3},{3,1},... | collective-permute-start | bytes 344072 | tf_op jit(solution)/shard_map/ppermute | solution.py:23
  31.1 1.0 %collective-permute-start.16 = (bf16[32,1792]{1,0:T(8,128)(2,1)S(1)}, bf16[32,1792]{1,0:T(8,128)(2,1)S(1)}, u32[]{:S(2)}, u32[]{:S(2)}) collective-permute-start(bf16[32,1792]{1,0:T(8,128)(2,1)S(1)} %get-tuple-element.68), channel_id=1, source_target_pairs={{0,4},{2,6},{4,0},{6,2},{8,12},{10,14},{12,8},{14,10},{1,5},{3,7},... | collective-permute-start | bytes 344072 | tf_op jit(solution)/shard_map/ppermute | solution.py:23
  32.7 1.2 %shard_map.66 = (f32[2,32,1792]{2,1,0:T(8,128)S(1)}, bf16[2,32,1792]{2,1,0:T(8,128)(2,1)S(1)}, f32[2,32,1792]{2,1,0:T(8,128)S(1)}, bf16[2,32,1792]{2,1,0:T(8,128)(2,1)S(1)}) custom-call(bf16[2,32,1792]{2,1,0:T(8,128)(2,1)S(1)} %pad_maximum_fusion.refs_0_, bf16[2,32,1792]{2,1,0:T(8,128)(2,1)S(1)} %collective-permute-done.3.refs_1_, ...), custom_call_target="tpu_custom_call" | custom-call | flops 1150000000 | tf_op jit(solution)/shard_map/pallas_call | solution.py:112
  34.3 1.2 %collective-permute-start.14 = (bf16[2,32,1792]{2,1,0:T(8,128)(2,1)S(1)}, bf16[2,32,1792]{2,1,0:T(8,128)(2,1)S(1)}, u32[]{:S(2)}, u32[]{:S(2)}) collective-permute-start(bf16[2,32,1792]{2,1,0:T(8,128)(2,1)S(1)} %pad_maximum_fusion.1), channel_id=1, source_target_pairs={{0,4},{2,6},{4,0},{6,2},{8,12},{10,14},{12,8},{14,10},{1,5},{3,7},... | collective-permute-start | bytes 688136 | tf_op jit(solution)/shard_map/ppermute | solution.py:23
  35.5 1.6 %collective-permute-done.16.two_ref = bf16[32,1792]{1,0:T(8,128)(2,1)S(1)} collective-permute-done((bf16[32,1792]{1,0:T(8,128)(2,1)S(1)}, bf16[32,1792]{1,0:T(8,128)(2,1)S(1)}, u32[]{:S(2)}, u32[]{:S(2)}) %collective-permute-start.16) | collective-permute-done | bytes 114720 | tf_op jit(solution)/shard_map/ppermute | solution.py:23
  37.6 1.6 %collective-permute-start.19 = (bf16[2,32,1792]{2,1,0:T(8,128)(2,1)S(1)}, bf16[2,32,1792]{2,1,0:T(8,128)(2,1)S(1)}, u32[]{:S(2)}, u32[]{:S(2)}) collective-permute-start(bf16[2,32,1792]{2,1,0:T(8,128)(2,1)S(1)} %get-tuple-element.73), channel_id=1, source_target_pairs={{0,2},{2,0},{4,6},{6,4},{8,10},{10,8},{12,14},{14,12},{1,3},{3,1},... | collective-permute-start | bytes 688136 | tf_op jit(solution)/shard_map/ppermute | solution.py:23
  39.2 2.7 %collective-permute-done.17 = bf16[32,1792]{1,0:T(8,128)(2,1)S(1)} collective-permute-done((bf16[32,1792]{1,0:T(8,128)(2,1)S(1)}, bf16[32,1792]{1,0:T(8,128)(2,1)S(1)}, u32[]{:S(2)}, u32[]{:S(2)}) %collective-permute-start.17) | collective-permute-done | bytes 114720 | tf_op jit(solution)/shard_map/ppermute | solution.py:23
  42.0 2.9 %collective-permute-start.21 = (bf16[2,32,1792]{2,1,0:T(8,128)(2,1)S(1)}, bf16[2,32,1792]{2,1,0:T(8,128)(2,1)S(1)}, u32[]{:S(2)}, u32[]{:S(2)}) collective-permute-start(bf16[2,32,1792]{2,1,0:T(8,128)(2,1)S(1)} %add_convert_fusion), channel_id=1, source_target_pairs={{0,8},{2,10},{4,12},{6,14},{8,0},{10,2},{12,4},{14,6},{1,9},{3,11}... | collective-permute-start | bytes 688136 | tf_op jit(solution)/shard_map/ppermute | solution.py:23
  45.0 1.0 %collective-permute-start.20 = (bf16[2,32,1792]{2,1,0:T(8,128)(2,1)S(1)}, bf16[2,32,1792]{2,1,0:T(8,128)(2,1)S(1)}, u32[]{:S(2)}, u32[]{:S(2)}) collective-permute-start(bf16[2,32,1792]{2,1,0:T(8,128)(2,1)S(1)} %shard_map.72), channel_id=1, source_target_pairs={{0,4},{2,6},{4,0},{6,2},{8,12},{10,14},{12,8},{14,10},{1,5},{3,7},... | collective-permute-start | bytes 688136 | tf_op jit(solution)/shard_map/ppermute | solution.py:23
  46.0 0.9 %collective-permute-start.18 = (bf16[2,32,1792]{2,1,0:T(8,128)(2,1)S(1)}, bf16[2,32,1792]{2,1,0:T(8,128)(2,1)S(1)}, u32[]{:S(2)}, u32[]{:S(2)}) collective-permute-start(bf16[2,32,1792]{2,1,0:T(8,128)(2,1)S(1)} %get-tuple-element.70), channel_id=1, source_target_pairs={{0,2},{2,0},{4,6},{6,4},{8,10},{10,8},{12,14},{14,12},{1,3},{3,1},... | collective-permute-start | bytes 688136 | tf_op jit(solution)/shard_map/ppermute | solution.py:23
  47.0 4.7 %collective-permute-done.21.from_ref = bf16[2,32,1792]{2,1,0:T(8,128)(2,1)S(1)} collective-permute-done((bf16[2,32,1792]{2,1,0:T(8,128)(2,1)S(1)}, bf16[2,32,1792]{2,1,0:T(8,128)(2,1)S(1)}, u32[]{:S(2)}, u32[]{:S(2)}) %collective-permute-start.21) | collective-permute-done | bytes 229408 | tf_op jit(solution)/shard_map/ppermute | solution.py:23
  51.7 1.0 %collective-permute-done.20 = bf16[2,32,1792]{2,1,0:T(8,128)(2,1)S(1)} collective-permute-done((bf16[2,32,1792]{2,1,0:T(8,128)(2,1)S(1)}, bf16[2,32,1792]{2,1,0:T(8,128)(2,1)S(1)}, u32[]{:S(2)}, u32[]{:S(2)}) %collective-permute-start.20) | collective-permute-done | bytes 229408 | tf_op jit(solution)/shard_map/ppermute | solution.py:23
  52.9 1.3 %collective-permute-done.22 = bf16[32,1792]{1,0:T(8,128)(2,1)S(1)} collective-permute-done((bf16[32,1792]{1,0:T(8,128)(2,1)S(1)}, bf16[32,1792]{1,0:T(8,128)(2,1)S(1)}, u32[]{:S(2)}, u32[]{:S(2)}) %collective-permute-start.22) | collective-permute-done | bytes 114720 | tf_op jit(solution)/shard_map/ppermute | solution.py:32
  (46 shorter events, 5.8 us)
Async XLA Ops:
  1.0 4.2 %collective-permute-start = (bf16[32,1792]{1,0:T(8,128)(2,1)S(1)}, bf16[32,1792]{1,0:T(8,128)(2,1)S(1)}, u32[]{:S(2)}, u32[]{:S(2)}) collective-permute-start(bf16[32,1792]{1,0:T(8,128)(2,1)S(1)} %get-tuple-element.42), channel_id=1, source_target_pairs={{0,1},{1,0},{2,3},{3,2},{4,5},{5,4},{6,7},{7,6},{8,9},{9,8},{10,11... | collective-permute-start | bytes 344072 | tf_op jit(solution)/shard_map/ppermute | solution.py:32
  1.5 12.4 %collective-permute-start.4 = (bf16[32,1792]{1,0:T(8,128)(2,1)S(1)}, bf16[32,1792]{1,0:T(8,128)(2,1)S(1)}, u32[]{:S(2)}, u32[]{:S(2)}) collective-permute-start(bf16[32,1792]{1,0:T(8,128)(2,1)S(1)} %get-tuple-element.41), channel_id=1, source_target_pairs={{0,8},{2,10},{4,12},{6,14},{8,0},{10,2},{12,4},{14,6},{1,9},{3,11}... | collective-permute-start | bytes 344072 | tf_op jit(solution)/shard_map/ppermute | solution.py:23
  5.2 12.2 %collective-permute-start.2 = (bf16[2,32,1792]{2,1,0:T(8,128)(2,1)S(1)}, bf16[2,32,1792]{2,1,0:T(8,128)(2,1)S(1)}, u32[]{:S(2)}, u32[]{:S(2)}) collective-permute-start(bf16[2,32,1792]{2,1,0:T(8,128)(2,1)S(1)} %pad_maximum_fusion.refs_0_), channel_id=1, source_target_pairs={{0,4},{2,6},{4,0},{6,2},{8,12},{10,14},{12,8},{14,10},{1,5},{3,7},... | collective-permute-start | bytes 688136 | tf_op jit(solution)/shard_map/ppermute | solution.py:23
  6.8 10.5 %collective-permute-start.3 = (bf16[2,32,1792]{2,1,0:T(8,128)(2,1)S(1)}, bf16[2,32,1792]{2,1,0:T(8,128)(2,1)S(1)}, u32[]{:S(2)}, u32[]{:S(2)}) collective-permute-start(bf16[2,32,1792]{2,1,0:T(8,128)(2,1)S(1)} %pad_maximum_fusion.refs_0_), channel_id=1, source_target_pairs={{0,2},{2,0},{4,6},{6,4},{8,10},{10,8},{12,14},{14,12},{1,3},{3,1},... | collective-permute-start | bytes 688136 | tf_op jit(solution)/shard_map/ppermute | solution.py:23
  8.3 7.7 %collective-permute-start.1 = (bf16[32,1792]{1,0:T(8,128)(2,1)S(1)}, bf16[32,1792]{1,0:T(8,128)(2,1)S(1)}, u32[]{:S(2)}, u32[]{:S(2)}) collective-permute-start(bf16[32,1792]{1,0:T(8,128)(2,1)S(1)} %collective-permute-done), channel_id=1, source_target_pairs={{0,8},{2,10},{4,12},{6,14},{8,0},{10,2},{12,4},{14,6},{1,9},{3,11}... | collective-permute-start | bytes 344072 | tf_op jit(solution)/shard_map/ppermute | solution.py:23
  9.6 1.2 %copy-start = (bf16[1,3584,128]{2,1,0:T(8,128)(2,1)S(1)}, bf16[1,3584,128]{2,1,0:T(8,128)(2,1)}, u32[]{:S(2)}) copy-start(bf16[1,3584,128]{2,1,0:T(8,128)(2,1)} %param.9) | copy-start | bytes 2752516
  10.7 1.2 %copy-start.1 = (bf16[1,3584,128]{2,1,0:T(8,128)(2,1)S(1)}, bf16[1,3584,128]{2,1,0:T(8,128)(2,1)}, u32[]{:S(2)}) copy-start(bf16[1,3584,128]{2,1,0:T(8,128)(2,1)} %param.10) | copy-start | bytes 2752516
  11.9 1.2 %copy-start.2 = (bf16[1,128,3584]{2,1,0:T(8,128)(2,1)S(1)}, bf16[1,128,3584]{2,1,0:T(8,128)(2,1)}, u32[]{:S(2)}) copy-start(bf16[1,128,3584]{2,1,0:T(8,128)(2,1)} %param.11) | copy-start | bytes 2752516
  13.9 6.1 %collective-permute-start.8 = (bf16[32,1792]{1,0:T(8,128)(2,1)S(1)}, bf16[32,1792]{1,0:T(8,128)(2,1)S(1)}, u32[]{:S(2)}, u32[]{:S(2)}) collective-permute-start(bf16[32,1792]{1,0:T(8,128)(2,1)S(1)} %collective-permute-done.4.refs_0_), channel_id=1, source_target_pairs={{0,4},{2,6},{4,0},{6,2},{8,12},{10,14},{12,8},{14,10},{1,5},{3,7},... | collective-permute-start | bytes 344072 | tf_op jit(solution)/shard_map/ppermute | solution.py:23
  14.4 8.8 %collective-permute-start.11 = (bf16[32,1792]{1,0:T(8,128)(2,1)S(1)}, bf16[32,1792]{1,0:T(8,128)(2,1)S(1)}, u32[]{:S(2)}, u32[]{:S(2)}) collective-permute-start(bf16[32,1792]{1,0:T(8,128)(2,1)S(1)} %collective-permute-done.4.refs_0_), channel_id=1, source_target_pairs={{0,2},{2,0},{4,6},{6,4},{8,10},{10,8},{12,14},{14,12},{1,3},{3,1},... | collective-permute-start | bytes 344072 | tf_op jit(solution)/shard_map/ppermute | solution.py:23
  17.4 4.8 %collective-permute-start.5 = (bf16[32,1792]{1,0:T(8,128)(2,1)S(1)}, bf16[32,1792]{1,0:T(8,128)(2,1)S(1)}, u32[]{:S(2)}, u32[]{:S(2)}) collective-permute-start(bf16[32,1792]{1,0:T(8,128)(2,1)S(1)} %shard_map.64.refs_1_), channel_id=1, source_target_pairs={{0,2},{2,0},{4,6},{6,4},{8,10},{10,8},{12,14},{14,12},{1,3},{3,1},... | collective-permute-start | bytes 344072 | tf_op jit(solution)/shard_map/ppermute | solution.py:23
  19.0 5.3 %collective-permute-start.12 = (bf16[32,1792]{1,0:T(8,128)(2,1)S(1)}, bf16[32,1792]{1,0:T(8,128)(2,1)S(1)}, u32[]{:S(2)}, u32[]{:S(2)}) collective-permute-start(bf16[32,1792]{1,0:T(8,128)(2,1)S(1)} %shard_map.64.refs_1_), channel_id=1, source_target_pairs={{0,4},{2,6},{4,0},{6,2},{8,12},{10,14},{12,8},{14,10},{1,5},{3,7},... | collective-permute-start | bytes 344072 | tf_op jit(solution)/shard_map/ppermute | solution.py:23
  20.0 5.1 %collective-permute-start.7 = (bf16[3584,384]{1,0:T(8,128)(2,1)S(1)}, bf16[3584,384]{1,0:T(8,128)(2,1)S(1)}, u32[]{:S(2)}, u32[]{:S(2)}) collective-permute-start(bf16[3584,384]{1,0:T(8,128)(2,1)S(1)} %shard_map.65.refs_4_), channel_id=1, source_target_pairs={{0,1},{1,0},{2,3},{3,2},{4,5},{5,4},{6,7},{7,6},{8,9},{9,8},{10,11... | collective-permute-start | bytes 8257544 | tf_op jit(solution)/shard_map/ppermute | solution.py:32
  20.0 6.2 %collective-permute-start.9 = (bf16[32,1792]{1,0:T(8,128)(2,1)S(1)}, bf16[32,1792]{1,0:T(8,128)(2,1)S(1)}, u32[]{:S(2)}, u32[]{:S(2)}) collective-permute-start(bf16[32,1792]{1,0:T(8,128)(2,1)S(1)} %shard_map.67.refs_0_), channel_id=1, source_target_pairs={{0,2},{2,0},{4,6},{6,4},{8,10},{10,8},{12,14},{14,12},{1,3},{3,1},... | collective-permute-start | bytes 344072 | tf_op jit(solution)/shard_map/ppermute | solution.py:23
  22.2 6.1 %collective-permute-start.10 = (bf16[32,1792]{1,0:T(8,128)(2,1)S(1)}, bf16[32,1792]{1,0:T(8,128)(2,1)S(1)}, u32[]{:S(2)}, u32[]{:S(2)}) collective-permute-start(bf16[32,1792]{1,0:T(8,128)(2,1)S(1)} %collective-permute-done.5.refs_3_), channel_id=1, source_target_pairs={{0,4},{2,6},{4,0},{6,2},{8,12},{10,14},{12,8},{14,10},{1,5},{3,7},... | collective-permute-start | bytes 344072 | tf_op jit(solution)/shard_map/ppermute | solution.py:23
  24.3 8.4 %collective-permute-start.6 = (bf16[2,32,1792]{2,1,0:T(8,128)(2,1)S(1)}, bf16[2,32,1792]{2,1,0:T(8,128)(2,1)S(1)}, u32[]{:S(2)}, u32[]{:S(2)}) collective-permute-start(bf16[2,32,1792]{2,1,0:T(8,128)(2,1)S(1)} %collective-permute-done.3.refs_1_), channel_id=1, source_target_pairs={{0,4},{2,6},{4,0},{6,2},{8,12},{10,14},{12,8},{14,10},{1,5},{3,7},... | collective-permute-start | bytes 688136 | tf_op jit(solution)/shard_map/ppermute | solution.py:23
  28.2 2.8 %copy-start.3 = (s32[64,1]{0,1:T(1,128)S(1)}, s32[64,1]{0,1:T(1,128)}, u32[]{:S(2)}) copy-start(s32[64,1]{0,1:T(1,128)} %param.8) | copy-start | bytes 772
  29.4 4.9 %collective-permute-start.13 = (bf16[32,1792]{1,0:T(8,128)(2,1)S(1)}, bf16[32,1792]{1,0:T(8,128)(2,1)S(1)}, u32[]{:S(2)}, u32[]{:S(2)}) collective-permute-start(bf16[32,1792]{1,0:T(8,128)(2,1)S(1)} %get-tuple-element.61), channel_id=1, source_target_pairs={{0,2},{2,0},{4,6},{6,4},{8,10},{10,8},{12,14},{14,12},{1,3},{3,1},... | collective-permute-start | bytes 344072 | tf_op jit(solution)/shard_map/ppermute | solution.py:23
  31.1 5.9 %collective-permute-start.16 = (bf16[32,1792]{1,0:T(8,128)(2,1)S(1)}, bf16[32,1792]{1,0:T(8,128)(2,1)S(1)}, u32[]{:S(2)}, u32[]{:S(2)}) collective-permute-start(bf16[32,1792]{1,0:T(8,128)(2,1)S(1)} %get-tuple-element.68), channel_id=1, source_target_pairs={{0,4},{2,6},{4,0},{6,2},{8,12},{10,14},{12,8},{14,10},{1,5},{3,7},... | collective-permute-start | bytes 344072 | tf_op jit(solution)/shard_map/ppermute | solution.py:23
  32.2 7.0 %collective-permute-start.15 = (bf16[32,1792]{1,0:T(8,128)(2,1)S(1)}, bf16[32,1792]{1,0:T(8,128)(2,1)S(1)}, u32[]{:S(2)}, u32[]{:S(2)}) collective-permute-start(bf16[32,1792]{1,0:T(8,128)(2,1)S(1)} %get-tuple-element.66), channel_id=1, source_target_pairs={{0,2},{2,0},{4,6},{6,4},{8,10},{10,8},{12,14},{14,12},{1,3},{3,1},... | collective-permute-start | bytes 344072 | tf_op jit(solution)/shard_map/ppermute | solution.py:23
  34.3 7.7 %collective-permute-start.14 = (bf16[2,32,1792]{2,1,0:T(8,128)(2,1)S(1)}, bf16[2,32,1792]{2,1,0:T(8,128)(2,1)S(1)}, u32[]{:S(2)}, u32[]{:S(2)}) collective-permute-start(bf16[2,32,1792]{2,1,0:T(8,128)(2,1)S(1)} %pad_maximum_fusion.1), channel_id=1, source_target_pairs={{0,4},{2,6},{4,0},{6,2},{8,12},{10,14},{12,8},{14,10},{1,5},{3,7},... | collective-permute-start | bytes 688136 | tf_op jit(solution)/shard_map/ppermute | solution.py:23
  37.1 9.8 %copy-start.4 = (s32[64,1]{0,1:T(1,128)S(1)}, s32[64,1]{0,1:T(1,128)}, u32[]{:S(2)}) copy-start(s32[64,1]{0,1:T(1,128)} %param.7) | copy-start | bytes 772
  37.1 4.9 %collective-permute-start.17 = (bf16[32,1792]{1,0:T(8,128)(2,1)S(1)}, bf16[32,1792]{1,0:T(8,128)(2,1)S(1)}, u32[]{:S(2)}, u32[]{:S(2)}) collective-permute-start(bf16[32,1792]{1,0:T(8,128)(2,1)S(1)} %shard_map.71), channel_id=1, source_target_pairs={{0,2},{2,0},{4,6},{6,4},{8,10},{10,8},{12,14},{14,12},{1,3},{3,1},... | collective-permute-start | bytes 344072 | tf_op jit(solution)/shard_map/ppermute | solution.py:23
  37.6 7.4 %collective-permute-start.19 = (bf16[2,32,1792]{2,1,0:T(8,128)(2,1)S(1)}, bf16[2,32,1792]{2,1,0:T(8,128)(2,1)S(1)}, u32[]{:S(2)}, u32[]{:S(2)}) collective-permute-start(bf16[2,32,1792]{2,1,0:T(8,128)(2,1)S(1)} %get-tuple-element.73), channel_id=1, source_target_pairs={{0,2},{2,0},{4,6},{6,4},{8,10},{10,8},{12,14},{14,12},{1,3},{3,1},... | collective-permute-start | bytes 688136 | tf_op jit(solution)/shard_map/ppermute | solution.py:23
  42.0 9.6 %collective-permute-start.21 = (bf16[2,32,1792]{2,1,0:T(8,128)(2,1)S(1)}, bf16[2,32,1792]{2,1,0:T(8,128)(2,1)S(1)}, u32[]{:S(2)}, u32[]{:S(2)}) collective-permute-start(bf16[2,32,1792]{2,1,0:T(8,128)(2,1)S(1)} %add_convert_fusion), channel_id=1, source_target_pairs={{0,8},{2,10},{4,12},{6,14},{8,0},{10,2},{12,4},{14,6},{1,9},{3,11}... | collective-permute-start | bytes 688136 | tf_op jit(solution)/shard_map/ppermute | solution.py:23
  45.0 7.7 %collective-permute-start.20 = (bf16[2,32,1792]{2,1,0:T(8,128)(2,1)S(1)}, bf16[2,32,1792]{2,1,0:T(8,128)(2,1)S(1)}, u32[]{:S(2)}, u32[]{:S(2)}) collective-permute-start(bf16[2,32,1792]{2,1,0:T(8,128)(2,1)S(1)} %shard_map.72), channel_id=1, source_target_pairs={{0,4},{2,6},{4,0},{6,2},{8,12},{10,14},{12,8},{14,10},{1,5},{3,7},... | collective-permute-start | bytes 688136 | tf_op jit(solution)/shard_map/ppermute | solution.py:23
  46.0 6.7 %collective-permute-start.18 = (bf16[2,32,1792]{2,1,0:T(8,128)(2,1)S(1)}, bf16[2,32,1792]{2,1,0:T(8,128)(2,1)S(1)}, u32[]{:S(2)}, u32[]{:S(2)}) collective-permute-start(bf16[2,32,1792]{2,1,0:T(8,128)(2,1)S(1)} %get-tuple-element.70), channel_id=1, source_target_pairs={{0,2},{2,0},{4,6},{6,4},{8,10},{10,8},{12,14},{14,12},{1,3},{3,1},... | collective-permute-start | bytes 688136 | tf_op jit(solution)/shard_map/ppermute | solution.py:23
  52.8 1.4 %collective-permute-start.22 = (bf16[32,1792]{1,0:T(8,128)(2,1)S(1)}, bf16[32,1792]{1,0:T(8,128)(2,1)S(1)}, u32[]{:S(2)}, u32[]{:S(2)}) collective-permute-start(bf16[32,1792]{1,0:T(8,128)(2,1)S(1)} %slice_bitcast_fusion), channel_id=1, source_target_pairs={{0,1},{1,0},{2,3},{3,2},{4,5},{5,4},{6,7},{7,6},{8,9},{9,8},{10,11... | collective-permute-start | bytes 344072 | tf_op jit(solution)/shard_map/ppermute | solution.py:32

commit v8 on v7

--- a/solution.py
+++ b/solution.py
@@ -219,7 +219,8 @@
     z2a, ours = tie((z2a, ours))
     m6a = cast(swap(z2a, 2), bf16, 40.0)
     m5a = swap(z2a, 1)
-    z2b, z1, x0, ours = tie((z2b, z1, x0, ours))
+    z2b, x0 = tie((z2b, x0))
+    ours, z1 = tie((ours, z1))
     weights = [ours, swap_core(ours)]
     m5b = swap(z2b, 1)
     m6b = swap(z2b, 2)
@@ -234,8 +235,8 @@
     p0, p1, p2, p3 = expert(
         ((both0,), (x0,), (z1,), (m3,)), ((f32,), (bf16,), (f32,), (bf16,)), 1.0
     )
+    r7a = swap(p7a, 1)
     r7b = swap(p7b, 2)
-    r7a = swap(p7a, 1)
     r7a, p1, p2, p3 = tie((r7a, p1, p2, p3))
     s6 = jnp.stack([p6[0] + r7a.astype(f32), p6[1]]).astype(bf16)
     r5a = cast(swap(p5a, 1), bf16, 2.0)

time: 55.2 us -> 54.4 us (0.986)
  waiting for transfers between devices: 18.5 us -> 14.9 us
  starting transfers between devices: 26.2 us -> 29 us
    ppermute x20, waiting for transfers between devices: 16.9 us -> 13.3 us  [swap(): return lax.ppermute(value, 'ep', pairs)]
    ppermute x20, starting transfers between devices: 25.6 us -> 28.4 us  [swap(): return lax.ppermute(value, 'ep', pairs)]
  transfers between devices with their start and end apart: 23 -> 23, of which waited for: 12 -> 9; matrix products, arithmetic and copies ran while one was open for 1% -> 1% of each run, Pallas kernels for 8% -> 8%
where the time goes in v8:
time: 54.4 us; the launch traced here: 54.2 us
  starting transfers between devices  29 us (53%)
  waiting for transfers between devices  14.9 us (27%)
  Pallas kernels  4.43 us (8%)
  local copies, waits for them, and re-layouts  3.57 us (7%)
  other arithmetic  2.11 us (4%)
    ppermute x20, starting transfers between devices, swap(): return lax.ppermute(value, 'ep', pairs)  28.4 us
    ppermute x20, waiting for transfers between devices, swap(): return lax.ppermute(value, 'ep', pairs)  13.3 us
    unnamed x10, local copies, waits for them, and re-layouts  3.55 us
    pallas_call x3, Pallas kernels, expert_block(): pl.pallas_call(functools.partial(expert_kernel, [(None,) * len(b) for b i...  3.5 us
    ppermute x3, waiting for transfers between devices, swap_core(): return lax.ppermute(value, 'tp', [(0, 1), (1, 0)])  1.62 us
  transfers between devices with their start and end apart: 23, of which 9 were waited for; matrix products, arithmetic and copies ran while one was open for 1% of the time, Pallas kernels for 8%

profile of v8, /device:TPU:0, one launch (start us, length us, event | category | flops | bytes accessed | tf_op | source)
XLA Modules:
  0.0 54.2 jit_solution(8449354884039640312)
XLA Ops:
  0.0 1.0 %broadcast_select_fusion.2 = (bf16[32,1792]{1,0:T(8,128)(2,1)S(1)}, bf16[32,1792]{1,0:T(8,128)(2,1)S(1)}) fusion(pred[]{:T(512)S(6)} %eq.3, bf16[64,1792]{1,0:T(8,128)(2,1)} %param.6), kind=kLoop, calls=%fused_computation.13 | loop fusion | flops 114688 | bytes 458753 | tf_op jit(solution)/shard_map/jit(_where)/select_n | solution.py:206
  1.5 3.7 %collective-permute-start.3 = (bf16[32,1792]{1,0:T(8,128)(2,1)S(1)}, bf16[32,1792]{1,0:T(8,128)(2,1)S(1)}, u32[]{:S(2)}, u32[]{:S(2)}) collective-permute-start(bf16[32,1792]{1,0:T(8,128)(2,1)S(1)} %get-tuple-element.41), channel_id=1, source_target_pairs={{0,8},{2,10},{4,12},{6,14},{8,0},{10,2},{12,4},{14,6},{1,9},{3,11}... | collective-permute-start | bytes 344072 | tf_op jit(solution)/shard_map/ppermute | solution.py:23
  5.2 1.6 %collective-permute-start.2 = (bf16[2,32,1792]{2,1,0:T(8,128)(2,1)S(1)}, bf16[2,32,1792]{2,1,0:T(8,128)(2,1)S(1)}, u32[]{:S(2)}, u32[]{:S(2)}) collective-permute-start(bf16[2,32,1792]{2,1,0:T(8,128)(2,1)S(1)} %pad_maximum_fusion.refs_0_), channel_id=1, source_target_pairs={{0,2},{2,0},{4,6},{6,4},{8,10},{10,8},{12,14},{14,12},{1,3},{3,1},... | collective-permute-start | bytes 688136 | tf_op jit(solution)/shard_map/ppermute | solution.py:23
  6.7 1.6 %collective-permute-start.4 = (bf16[2,32,1792]{2,1,0:T(8,128)(2,1)S(1)}, bf16[2,32,1792]{2,1,0:T(8,128)(2,1)S(1)}, u32[]{:S(2)}, u32[]{:S(2)}) collective-permute-start(bf16[2,32,1792]{2,1,0:T(8,128)(2,1)S(1)} %pad_maximum_fusion.refs_0_), channel_id=1, source_target_pairs={{0,4},{2,6},{4,0},{6,2},{8,12},{10,14},{12,8},{14,10},{1,5},{3,7},... | collective-permute-start | bytes 688136 | tf_op jit(solution)/shard_map/ppermute | solution.py:23
  8.3 1.2 %collective-permute-start.1 = (bf16[32,1792]{1,0:T(8,128)(2,1)S(1)}, bf16[32,1792]{1,0:T(8,128)(2,1)S(1)}, u32[]{:S(2)}, u32[]{:S(2)}) collective-permute-start(bf16[32,1792]{1,0:T(8,128)(2,1)S(1)} %collective-permute-done), channel_id=1, source_target_pairs={{0,8},{2,10},{4,12},{6,14},{8,0},{10,2},{12,4},{14,6},{1,9},{3,11}... | collective-permute-start | bytes 344072 | tf_op jit(solution)/shard_map/ppermute | solution.py:23
  9.6 1.2 %copy-done = bf16[1,3584,128]{2,1,0:T(8,128)(2,1)S(1)} copy-done((bf16[1,3584,128]{2,1,0:T(8,128)(2,1)S(1)}, bf16[1,3584,128]{2,1,0:T(8,128)(2,1)}, u32[]{:S(2)}) %copy-start) | copy-done | bytes 917528
  10.7 1.2 %copy-done.1 = bf16[1,3584,128]{2,1,0:T(8,128)(2,1)S(1)} copy-done((bf16[1,3584,128]{2,1,0:T(8,128)(2,1)S(1)}, bf16[1,3584,128]{2,1,0:T(8,128)(2,1)}, u32[]{:S(2)}) %copy-start.1) | copy-done | bytes 917528
  11.9 1.2 %copy-done.2 = bf16[1,128,3584]{2,1,0:T(8,128)(2,1)S(1)} copy-done((bf16[1,128,3584]{2,1,0:T(8,128)(2,1)S(1)}, bf16[1,128,3584]{2,1,0:T(8,128)(2,1)}, u32[]{:S(2)}) %copy-start.2) | copy-done | bytes 917528
  13.1 0.8 %shard_map.65.refs_4_ = bf16[3584,384]{1,0:T(8,128)(2,1)S(1)} custom-call(bf16[3584,128]{1,0:T(8,128)(2,1)S(1)} %bitcast.28, bf16[3584,128]{1,0:T(8,128)(2,1)S(1)} %bitcast.29, bf16[128,3584]{1,0:T(8,128)(2,1)S(1)} %bitcast.30), custom_call_target="tpu_custom_call" | custom-call | flops 2300000000 | tf_op jit(solution)/shard_map/pallas_call | solution.py:49
  15.0 1.8 %collective-permute-done.1.from_ref = bf16[32,1792]{1,0:T(8,128)(2,1)S(1)} collective-permute-done((bf16[32,1792]{1,0:T(8,128)(2,1)S(1)}, bf16[32,1792]{1,0:T(8,128)(2,1)S(1)}, u32[]{:S(2)}, u32[]{:S(2)}) %collective-permute-start.1) | collective-permute-done | bytes 114720 | tf_op jit(solution)/shard_map/ppermute | solution.py:23
  16.8 0.8 %collective-permute-start.5 = (bf16[32,1792]{1,0:T(8,128)(2,1)S(1)}, bf16[32,1792]{1,0:T(8,128)(2,1)S(1)}, u32[]{:S(2)}, u32[]{:S(2)}) collective-permute-start(bf16[32,1792]{1,0:T(8,128)(2,1)S(1)} %shard_map.64.refs_1_), channel_id=1, source_target_pairs={{0,2},{2,0},{4,6},{6,4},{8,10},{10,8},{12,14},{14,12},{1,3},{3,1},... | collective-permute-start | bytes 344072 | tf_op jit(solution)/shard_map/ppermute | solution.py:23
  17.6 2.4 %collective-permute-start.12 = (bf16[32,1792]{1,0:T(8,128)(2,1)S(1)}, bf16[32,1792]{1,0:T(8,128)(2,1)S(1)}, u32[]{:S(2)}, u32[]{:S(2)}) collective-permute-start(bf16[32,1792]{1,0:T(8,128)(2,1)S(1)} %shard_map.64.refs_1_), channel_id=1, source_target_pairs={{0,4},{2,6},{4,0},{6,2},{8,12},{10,14},{12,8},{14,10},{1,5},{3,7},... | collective-permute-start | bytes 344072 | tf_op jit(solution)/shard_map/ppermute | solution.py:23
  20.0 0.8 %collective-permute-done.8.from_ref = bf16[32,1792]{1,0:T(8,128)(2,1)S(1)} collective-permute-done((bf16[32,1792]{1,0:T(8,128)(2,1)S(1)}, bf16[32,1792]{1,0:T(8,128)(2,1)S(1)}, u32[]{:S(2)}, u32[]{:S(2)}) %collective-permute-start.8) | collective-permute-done | bytes 114720 | tf_op jit(solution)/shard_map/ppermute | solution.py:23
  20.8 0.9 %collective-permute-start.9 = (bf16[32,1792]{1,0:T(8,128)(2,1)S(1)}, bf16[32,1792]{1,0:T(8,128)(2,1)S(1)}, u32[]{:S(2)}, u32[]{:S(2)}) collective-permute-start(bf16[32,1792]{1,0:T(8,128)(2,1)S(1)} %shard_map.67.refs_0_), channel_id=1, source_target_pairs={{0,2},{2,0},{4,6},{6,4},{8,10},{10,8},{12,14},{14,12},{1,3},{3,1},... | collective-permute-start | bytes 344072 | tf_op jit(solution)/shard_map/ppermute | solution.py:23
  21.8 1.6 %collective-permute-start.10 = (bf16[32,1792]{1,0:T(8,128)(2,1)S(1)}, bf16[32,1792]{1,0:T(8,128)(2,1)S(1)}, u32[]{:S(2)}, u32[]{:S(2)}) collective-permute-start(bf16[32,1792]{1,0:T(8,128)(2,1)S(1)} %collective-permute-done.5.refs_3_), channel_id=1, source_target_pairs={{0,4},{2,6},{4,0},{6,2},{8,12},{10,14},{12,8},{14,10},{1,5},{3,7},... | collective-permute-start | bytes 344072 | tf_op jit(solution)/shard_map/ppermute | solution.py:23
  23.3 1.5 %collective-permute-start.6 = (bf16[2,32,1792]{2,1,0:T(8,128)(2,1)S(1)}, bf16[2,32,1792]{2,1,0:T(8,128)(2,1)S(1)}, u32[]{:S(2)}, u32[]{:S(2)}) collective-permute-start(bf16[2,32,1792]{2,1,0:T(8,128)(2,1)S(1)} %collective-permute-done.2.refs_1_), channel_id=1, source_target_pairs={{0,4},{2,6},{4,0},{6,2},{8,12},{10,14},{12,8},{14,10},{1,5},{3,7},... | collective-permute-start | bytes 688136 | tf_op jit(solution)/shard_map/ppermute | solution.py:23
  25.1 1.1 %shard_map.68 = (f32[2,32,1792]{2,1,0:T(8,128)S(1)}, bf16[32,1792]{1,0:T(8,128)(2,1)S(1)}, f32[32,1792]{1,0:T(8,128)S(1)}) custom-call(bf16[32,1792]{1,0:T(8,128)(2,1)S(1)} %collective-permute-done.3.refs_0_, bf16[32,1792]{1,0:T(8,128)(2,1)S(1)} %shard_map.64.refs_1_, bf16[32,1792]{1,0:T(8,128)(2,1)S(1)} %collective-permute-done.11.refs_2_, ...), custom_call_target="tpu_custom_call" | custom-call | flops 1150000000 | tf_op jit(solution)/shard_map/pallas_call | solution.py:112
  26.2 1.5 %collective-permute-done.10.refs_3_ = bf16[32,1792]{1,0:T(8,128)(2,1)S(1)} collective-permute-done((bf16[32,1792]{1,0:T(8,128)(2,1)S(1)}, bf16[32,1792]{1,0:T(8,128)(2,1)S(1)}, u32[]{:S(2)}, u32[]{:S(2)}) %collective-permute-start.10) | collective-permute-done | bytes 114720 | tf_op jit(solution)/shard_map/ppermute | solution.py:23
  27.7 1.1 %shard_map.69 = (f32[2,32,1792]{2,1,0:T(8,128)S(1)}, bf16[32,1792]{1,0:T(8,128)(2,1)S(1)}, bf16[32,1792]{1,0:T(8,128)(2,1)S(1)}) custom-call(bf16[32,1792]{1,0:T(8,128)(2,1)S(1)} %shard_map.67.refs_0_, bf16[32,1792]{1,0:T(8,128)(2,1)S(1)} %collective-permute-done.12.refs_1_, bf16[32,1792]{1,0:T(8,128)(2,1)S(1)} %collective-permute-done.9.refs_2_, ...), custom_call_target="tpu_custom_call" | custom-call | flops 1150000000 | tf_op jit(solution)/shard_map/pallas_call | solution.py:112
  28.9 1.6 %collective-permute-start.13 = (bf16[32,1792]{1,0:T(8,128)(2,1)S(1)}, bf16[32,1792]{1,0:T(8,128)(2,1)S(1)}, u32[]{:S(2)}, u32[]{:S(2)}) collective-permute-start(bf16[32,1792]{1,0:T(8,128)(2,1)S(1)} %get-tuple-element.61), channel_id=1, source_target_pairs={{0,2},{2,0},{4,6},{6,4},{8,10},{10,8},{12,14},{14,12},{1,3},{3,1},... | collective-permute-start | bytes 344072 | tf_op jit(solution)/shard_map/ppermute | solution.py:23
  30.6 1.1 %collective-permute-start.16 = (bf16[32,1792]{1,0:T(8,128)(2,1)S(1)}, bf16[32,1792]{1,0:T(8,128)(2,1)S(1)}, u32[]{:S(2)}, u32[]{:S(2)}) collective-permute-start(bf16[32,1792]{1,0:T(8,128)(2,1)S(1)} %get-tuple-element.68), channel_id=1, source_target_pairs={{0,4},{2,6},{4,0},{6,2},{8,12},{10,14},{12,8},{14,10},{1,5},{3,7},... | collective-permute-start | bytes 344072 | tf_op jit(solution)/shard_map/ppermute | solution.py:23
  31.7 1.1 %collective-permute-start.15 = (bf16[32,1792]{1,0:T(8,128)(2,1)S(1)}, bf16[32,1792]{1,0:T(8,128)(2,1)S(1)}, u32[]{:S(2)}, u32[]{:S(2)}) collective-permute-start(bf16[32,1792]{1,0:T(8,128)(2,1)S(1)} %get-tuple-element.66), channel_id=1, source_target_pairs={{0,2},{2,0},{4,6},{6,4},{8,10},{10,8},{12,14},{14,12},{1,3},{3,1},... | collective-permute-start | bytes 344072 | tf_op jit(solution)/shard_map/ppermute | solution.py:23
  32.8 1.2 %shard_map.66 = (f32[2,32,1792]{2,1,0:T(8,128)S(1)}, bf16[2,32,1792]{2,1,0:T(8,128)(2,1)S(1)}, f32[2,32,1792]{2,1,0:T(8,128)S(1)}, bf16[2,32,1792]{2,1,0:T(8,128)(2,1)S(1)}) custom-call(bf16[2,32,1792]{2,1,0:T(8,128)(2,1)S(1)} %pad_maximum_fusion.refs_0_, bf16[2,32,1792]{2,1,0:T(8,128)(2,1)S(1)} %collective-permute-done.2.refs_1_, ...), custom_call_target="tpu_custom_call" | custom-call | flops 1150000000 | tf_op jit(solution)/shard_map/pallas_call | solution.py:112
  34.1 1.4 %collective-permute-start.14 = (bf16[2,32,1792]{2,1,0:T(8,128)(2,1)S(1)}, bf16[2,32,1792]{2,1,0:T(8,128)(2,1)S(1)}, u32[]{:S(2)}, u32[]{:S(2)}) collective-permute-start(bf16[2,32,1792]{2,1,0:T(8,128)(2,1)S(1)} %pad_maximum_fusion.1), channel_id=1, source_target_pairs={{0,4},{2,6},{4,0},{6,2},{8,12},{10,14},{12,8},{14,10},{1,5},{3,7},... | collective-permute-start | bytes 688136 | tf_op jit(solution)/shard_map/ppermute | solution.py:23
  35.5 1.1 %collective-permute-done.16.two_ref = bf16[32,1792]{1,0:T(8,128)(2,1)S(1)} collective-permute-done((bf16[32,1792]{1,0:T(8,128)(2,1)S(1)}, bf16[32,1792]{1,0:T(8,128)(2,1)S(1)}, u32[]{:S(2)}, u32[]{:S(2)}) %collective-permute-start.16) | collective-permute-done | bytes 114720 | tf_op jit(solution)/shard_map/ppermute | solution.py:23
  37.1 1.6 %collective-permute-start.19 = (bf16[2,32,1792]{2,1,0:T(8,128)(2,1)S(1)}, bf16[2,32,1792]{2,1,0:T(8,128)(2,1)S(1)}, u32[]{:S(2)}, u32[]{:S(2)}) collective-permute-start(bf16[2,32,1792]{2,1,0:T(8,128)(2,1)S(1)} %get-tuple-element.73), channel_id=1, source_target_pairs={{0,2},{2,0},{4,6},{6,4},{8,10},{10,8},{12,14},{14,12},{1,3},{3,1},... | collective-permute-start | bytes 688136 | tf_op jit(solution)/shard_map/ppermute | solution.py:23
  38.8 2.7 %collective-permute-done.17 = bf16[32,1792]{1,0:T(8,128)(2,1)S(1)} collective-permute-done((bf16[32,1792]{1,0:T(8,128)(2,1)S(1)}, bf16[32,1792]{1,0:T(8,128)(2,1)S(1)}, u32[]{:S(2)}, u32[]{:S(2)}) %collective-permute-start.17) | collective-permute-done | bytes 114720 | tf_op jit(solution)/shard_map/ppermute | solution.py:23
  41.6 2.7 %collective-permute-start.21 = (bf16[2,32,1792]{2,1,0:T(8,128)(2,1)S(1)}, bf16[2,32,1792]{2,1,0:T(8,128)(2,1)S(1)}, u32[]{:S(2)}, u32[]{:S(2)}) collective-permute-start(bf16[2,32,1792]{2,1,0:T(8,128)(2,1)S(1)} %add_convert_fusion), channel_id=1, source_target_pairs={{0,8},{2,10},{4,12},{6,14},{8,0},{10,2},{12,4},{14,6},{1,9},{3,11}... | collective-permute-start | bytes 688136 | tf_op jit(solution)/shard_map/ppermute | solution.py:23
  44.4 1.5 %collective-permute-start.20 = (bf16[2,32,1792]{2,1,0:T(8,128)(2,1)S(1)}, bf16[2,32,1792]{2,1,0:T(8,128)(2,1)S(1)}, u32[]{:S(2)}, u32[]{:S(2)}) collective-permute-start(bf16[2,32,1792]{2,1,0:T(8,128)(2,1)S(1)} %shard_map.72), channel_id=1, source_target_pairs={{0,4},{2,6},{4,0},{6,2},{8,12},{10,14},{12,8},{14,10},{1,5},{3,7},... | collective-permute-start | bytes 688136 | tf_op jit(solution)/shard_map/ppermute | solution.py:23
  46.6 4.8 %collective-permute-done.21.from_ref = bf16[2,32,1792]{2,1,0:T(8,128)(2,1)S(1)} collective-permute-done((bf16[2,32,1792]{2,1,0:T(8,128)(2,1)S(1)}, bf16[2,32,1792]{2,1,0:T(8,128)(2,1)S(1)}, u32[]{:S(2)}, u32[]{:S(2)}) %collective-permute-start.21) | collective-permute-done | bytes 229408 | tf_op jit(solution)/shard_map/ppermute | solution.py:23
  52.1 1.3 %collective-permute-done.22 = bf16[32,1792]{1,0:T(8,128)(2,1)S(1)} collective-permute-done((bf16[32,1792]{1,0:T(8,128)(2,1)S(1)}, bf16[32,1792]{1,0:T(8,128)(2,1)S(1)}, u32[]{:S(2)}, u32[]{:S(2)}) %collective-permute-start.22) | collective-permute-done | bytes 114720 | tf_op jit(solution)/shard_map/ppermute | solution.py:32
  53.5 0.7 %pad_maximum_fusion.2 = bf16[64,1792]{1,0:T(8,128)(2,1)} fusion(bf16[32,1792]{1,0:T(8,128)(2,1)S(1)} %get-tuple-element.76, bf16[32,1792]{1,0:T(8,128)(2,1)S(1)} %get-tuple-element.75), kind=kLoop, calls=%fused_computation.5 | loop fusion | flops 458752 | bytes 458752 | tf_op jit(solution)/shard_map/concatenate | solution.py:263
  (46 shorter events, 4.2 us)
Async XLA Ops:
  1.0 4.2 %collective-permute-start = (bf16[32,1792]{1,0:T(8,128)(2,1)S(1)}, bf16[32,1792]{1,0:T(8,128)(2,1)S(1)}, u32[]{:S(2)}, u32[]{:S(2)}) collective-permute-start(bf16[32,1792]{1,0:T(8,128)(2,1)S(1)} %get-tuple-element.42), channel_id=1, source_target_pairs={{0,1},{1,0},{2,3},{3,2},{4,5},{5,4},{6,7},{7,6},{8,9},{9,8},{10,11... | collective-permute-start | bytes 344072 | tf_op jit(solution)/shard_map/ppermute | solution.py:32
  1.5 12.4 %collective-permute-start.3 = (bf16[32,1792]{1,0:T(8,128)(2,1)S(1)}, bf16[32,1792]{1,0:T(8,128)(2,1)S(1)}, u32[]{:S(2)}, u32[]{:S(2)}) collective-permute-start(bf16[32,1792]{1,0:T(8,128)(2,1)S(1)} %get-tuple-element.41), channel_id=1, source_target_pairs={{0,8},{2,10},{4,12},{6,14},{8,0},{10,2},{12,4},{14,6},{1,9},{3,11}... | collective-permute-start | bytes 344072 | tf_op jit(solution)/shard_map/ppermute | solution.py:23
  5.2 11.6 %collective-permute-start.2 = (bf16[2,32,1792]{2,1,0:T(8,128)(2,1)S(1)}, bf16[2,32,1792]{2,1,0:T(8,128)(2,1)S(1)}, u32[]{:S(2)}, u32[]{:S(2)}) collective-permute-start(bf16[2,32,1792]{2,1,0:T(8,128)(2,1)S(1)} %pad_maximum_fusion.refs_0_), channel_id=1, source_target_pairs={{0,2},{2,0},{4,6},{6,4},{8,10},{10,8},{12,14},{14,12},{1,3},{3,1},... | collective-permute-start | bytes 688136 | tf_op jit(solution)/shard_map/ppermute | solution.py:23
  6.7 13.2 %collective-permute-start.4 = (bf16[2,32,1792]{2,1,0:T(8,128)(2,1)S(1)}, bf16[2,32,1792]{2,1,0:T(8,128)(2,1)S(1)}, u32[]{:S(2)}, u32[]{:S(2)}) collective-permute-start(bf16[2,32,1792]{2,1,0:T(8,128)(2,1)S(1)} %pad_maximum_fusion.refs_0_), channel_id=1, source_target_pairs={{0,4},{2,6},{4,0},{6,2},{8,12},{10,14},{12,8},{14,10},{1,5},{3,7},... | collective-permute-start | bytes 688136 | tf_op jit(solution)/shard_map/ppermute | solution.py:23
  8.3 8.5 %collective-permute-start.1 = (bf16[32,1792]{1,0:T(8,128)(2,1)S(1)}, bf16[32,1792]{1,0:T(8,128)(2,1)S(1)}, u32[]{:S(2)}, u32[]{:S(2)}) collective-permute-start(bf16[32,1792]{1,0:T(8,128)(2,1)S(1)} %collective-permute-done), channel_id=1, source_target_pairs={{0,8},{2,10},{4,12},{6,14},{8,0},{10,2},{12,4},{14,6},{1,9},{3,11}... | collective-permute-start | bytes 344072 | tf_op jit(solution)/shard_map/ppermute | solution.py:23
  9.6 1.2 %copy-start = (bf16[1,3584,128]{2,1,0:T(8,128)(2,1)S(1)}, bf16[1,3584,128]{2,1,0:T(8,128)(2,1)}, u32[]{:S(2)}) copy-start(bf16[1,3584,128]{2,1,0:T(8,128)(2,1)} %param.9) | copy-start | bytes 2752516
  10.7 1.2 %copy-start.1 = (bf16[1,3584,128]{2,1,0:T(8,128)(2,1)S(1)}, bf16[1,3584,128]{2,1,0:T(8,128)(2,1)}, u32[]{:S(2)}) copy-start(bf16[1,3584,128]{2,1,0:T(8,128)(2,1)} %param.10) | copy-start | bytes 2752516
  11.9 1.2 %copy-start.2 = (bf16[1,128,3584]{2,1,0:T(8,128)(2,1)S(1)}, bf16[1,128,3584]{2,1,0:T(8,128)(2,1)}, u32[]{:S(2)}) copy-start(bf16[1,128,3584]{2,1,0:T(8,128)(2,1)} %param.11) | copy-start | bytes 2752516
  13.9 6.9 %collective-permute-start.8 = (bf16[32,1792]{1,0:T(8,128)(2,1)S(1)}, bf16[32,1792]{1,0:T(8,128)(2,1)S(1)}, u32[]{:S(2)}, u32[]{:S(2)}) collective-permute-start(bf16[32,1792]{1,0:T(8,128)(2,1)S(1)} %collective-permute-done.3.refs_0_), channel_id=1, source_target_pairs={{0,4},{2,6},{4,0},{6,2},{8,12},{10,14},{12,8},{14,10},{1,5},{3,7},... | collective-permute-start | bytes 344072 | tf_op jit(solution)/shard_map/ppermute | solution.py:23
  14.4 8.9 %collective-permute-start.11 = (bf16[32,1792]{1,0:T(8,128)(2,1)S(1)}, bf16[32,1792]{1,0:T(8,128)(2,1)S(1)}, u32[]{:S(2)}, u32[]{:S(2)}) collective-permute-start(bf16[32,1792]{1,0:T(8,128)(2,1)S(1)} %collective-permute-done.3.refs_0_), channel_id=1, source_target_pairs={{0,2},{2,0},{4,6},{6,4},{8,10},{10,8},{12,14},{14,12},{1,3},{3,1},... | collective-permute-start | bytes 344072 | tf_op jit(solution)/shard_map/ppermute | solution.py:23
  16.8 4.9 %collective-permute-start.5 = (bf16[32,1792]{1,0:T(8,128)(2,1)S(1)}, bf16[32,1792]{1,0:T(8,128)(2,1)S(1)}, u32[]{:S(2)}, u32[]{:S(2)}) collective-permute-start(bf16[32,1792]{1,0:T(8,128)(2,1)S(1)} %shard_map.64.refs_1_), channel_id=1, source_target_pairs={{0,2},{2,0},{4,6},{6,4},{8,10},{10,8},{12,14},{14,12},{1,3},{3,1},... | collective-permute-start | bytes 344072 | tf_op jit(solution)/shard_map/ppermute | solution.py:23
  17.6 5.7 %collective-permute-start.12 = (bf16[32,1792]{1,0:T(8,128)(2,1)S(1)}, bf16[32,1792]{1,0:T(8,128)(2,1)S(1)}, u32[]{:S(2)}, u32[]{:S(2)}) collective-permute-start(bf16[32,1792]{1,0:T(8,128)(2,1)S(1)} %shard_map.64.refs_1_), channel_id=1, source_target_pairs={{0,4},{2,6},{4,0},{6,2},{8,12},{10,14},{12,8},{14,10},{1,5},{3,7},... | collective-permute-start | bytes 344072 | tf_op jit(solution)/shard_map/ppermute | solution.py:23
  20.0 5.1 %collective-permute-start.7 = (bf16[3584,384]{1,0:T(8,128)(2,1)S(1)}, bf16[3584,384]{1,0:T(8,128)(2,1)S(1)}, u32[]{:S(2)}, u32[]{:S(2)}) collective-permute-start(bf16[3584,384]{1,0:T(8,128)(2,1)S(1)} %shard_map.65.refs_4_), channel_id=1, source_target_pairs={{0,1},{1,0},{2,3},{3,2},{4,5},{5,4},{6,7},{7,6},{8,9},{9,8},{10,11... | collective-permute-start | bytes 8257544 | tf_op jit(solution)/shard_map/ppermute | solution.py:32
  20.8 5.4 %collective-permute-start.9 = (bf16[32,1792]{1,0:T(8,128)(2,1)S(1)}, bf16[32,1792]{1,0:T(8,128)(2,1)S(1)}, u32[]{:S(2)}, u32[]{:S(2)}) collective-permute-start(bf16[32,1792]{1,0:T(8,128)(2,1)S(1)} %shard_map.67.refs_0_), channel_id=1, source_target_pairs={{0,2},{2,0},{4,6},{6,4},{8,10},{10,8},{12,14},{14,12},{1,3},{3,1},... | collective-permute-start | bytes 344072 | tf_op jit(solution)/shard_map/ppermute | solution.py:23
  21.8 6.0 %collective-permute-start.10 = (bf16[32,1792]{1,0:T(8,128)(2,1)S(1)}, bf16[32,1792]{1,0:T(8,128)(2,1)S(1)}, u32[]{:S(2)}, u32[]{:S(2)}) collective-permute-start(bf16[32,1792]{1,0:T(8,128)(2,1)S(1)} %collective-permute-done.5.refs_3_), channel_id=1, source_target_pairs={{0,4},{2,6},{4,0},{6,2},{8,12},{10,14},{12,8},{14,10},{1,5},{3,7},... | collective-permute-start | bytes 344072 | tf_op jit(solution)/shard_map/ppermute | solution.py:23
  23.3 9.5 %collective-permute-start.6 = (bf16[2,32,1792]{2,1,0:T(8,128)(2,1)S(1)}, bf16[2,32,1792]{2,1,0:T(8,128)(2,1)S(1)}, u32[]{:S(2)}, u32[]{:S(2)}) collective-permute-start(bf16[2,32,1792]{2,1,0:T(8,128)(2,1)S(1)} %collective-permute-done.2.refs_1_), channel_id=1, source_target_pairs={{0,4},{2,6},{4,0},{6,2},{8,12},{10,14},{12,8},{14,10},{1,5},{3,7},... | collective-permute-start | bytes 688136 | tf_op jit(solution)/shard_map/ppermute | solution.py:23
  27.7 2.8 %copy-start.3 = (s32[64,1]{0,1:T(1,128)S(1)}, s32[64,1]{0,1:T(1,128)}, u32[]{:S(2)}) copy-start(s32[64,1]{0,1:T(1,128)} %param.8) | copy-start | bytes 772
  28.9 5.2 %collective-permute-start.13 = (bf16[32,1792]{1,0:T(8,128)(2,1)S(1)}, bf16[32,1792]{1,0:T(8,128)(2,1)S(1)}, u32[]{:S(2)}, u32[]{:S(2)}) collective-permute-start(bf16[32,1792]{1,0:T(8,128)(2,1)S(1)} %get-tuple-element.61), channel_id=1, source_target_pairs={{0,2},{2,0},{4,6},{6,4},{8,10},{10,8},{12,14},{14,12},{1,3},{3,1},... | collective-permute-start | bytes 344072 | tf_op jit(solution)/shard_map/ppermute | solution.py:23
  30.6 6.0 %collective-permute-start.16 = (bf16[32,1792]{1,0:T(8,128)(2,1)S(1)}, bf16[32,1792]{1,0:T(8,128)(2,1)S(1)}, u32[]{:S(2)}, u32[]{:S(2)}) collective-permute-start(bf16[32,1792]{1,0:T(8,128)(2,1)S(1)} %get-tuple-element.68), channel_id=1, source_target_pairs={{0,4},{2,6},{4,0},{6,2},{8,12},{10,14},{12,8},{14,10},{1,5},{3,7},... | collective-permute-start | bytes 344072 | tf_op jit(solution)/shard_map/ppermute | solution.py:23
  31.7 7.1 %collective-permute-start.15 = (bf16[32,1792]{1,0:T(8,128)(2,1)S(1)}, bf16[32,1792]{1,0:T(8,128)(2,1)S(1)}, u32[]{:S(2)}, u32[]{:S(2)}) collective-permute-start(bf16[32,1792]{1,0:T(8,128)(2,1)S(1)} %get-tuple-element.66), channel_id=1, source_target_pairs={{0,2},{2,0},{4,6},{6,4},{8,10},{10,8},{12,14},{14,12},{1,3},{3,1},... | collective-permute-start | bytes 344072 | tf_op jit(solution)/shard_map/ppermute | solution.py:23
  34.1 7.4 %collective-permute-start.14 = (bf16[2,32,1792]{2,1,0:T(8,128)(2,1)S(1)}, bf16[2,32,1792]{2,1,0:T(8,128)(2,1)S(1)}, u32[]{:S(2)}, u32[]{:S(2)}) collective-permute-start(bf16[2,32,1792]{2,1,0:T(8,128)(2,1)S(1)} %pad_maximum_fusion.1), channel_id=1, source_target_pairs={{0,4},{2,6},{4,0},{6,2},{8,12},{10,14},{12,8},{14,10},{1,5},{3,7},... | collective-permute-start | bytes 688136 | tf_op jit(solution)/shard_map/ppermute | solution.py:23
  36.6 9.9 %copy-start.4 = (s32[64,1]{0,1:T(1,128)S(1)}, s32[64,1]{0,1:T(1,128)}, u32[]{:S(2)}) copy-start(s32[64,1]{0,1:T(1,128)} %param.7) | copy-start | bytes 772
  36.6 4.9 %collective-permute-start.17 = (bf16[32,1792]{1,0:T(8,128)(2,1)S(1)}, bf16[32,1792]{1,0:T(8,128)(2,1)S(1)}, u32[]{:S(2)}, u32[]{:S(2)}) collective-permute-start(bf16[32,1792]{1,0:T(8,128)(2,1)S(1)} %shard_map.71), channel_id=1, source_target_pairs={{0,2},{2,0},{4,6},{6,4},{8,10},{10,8},{12,14},{14,12},{1,3},{3,1},... | collective-permute-start | bytes 344072 | tf_op jit(solution)/shard_map/ppermute | solution.py:23
  37.1 7.2 %collective-permute-start.19 = (bf16[2,32,1792]{2,1,0:T(8,128)(2,1)S(1)}, bf16[2,32,1792]{2,1,0:T(8,128)(2,1)S(1)}, u32[]{:S(2)}, u32[]{:S(2)}) collective-permute-start(bf16[2,32,1792]{2,1,0:T(8,128)(2,1)S(1)} %get-tuple-element.73), channel_id=1, source_target_pairs={{0,2},{2,0},{4,6},{6,4},{8,10},{10,8},{12,14},{14,12},{1,3},{3,1},... | collective-permute-start | bytes 688136 | tf_op jit(solution)/shard_map/ppermute | solution.py:23
  41.6 9.8 %collective-permute-start.21 = (bf16[2,32,1792]{2,1,0:T(8,128)(2,1)S(1)}, bf16[2,32,1792]{2,1,0:T(8,128)(2,1)S(1)}, u32[]{:S(2)}, u32[]{:S(2)}) collective-permute-start(bf16[2,32,1792]{2,1,0:T(8,128)(2,1)S(1)} %add_convert_fusion), channel_id=1, source_target_pairs={{0,8},{2,10},{4,12},{6,14},{8,0},{10,2},{12,4},{14,6},{1,9},{3,11}... | collective-permute-start | bytes 688136 | tf_op jit(solution)/shard_map/ppermute | solution.py:23
  44.4 7.6 %collective-permute-start.20 = (bf16[2,32,1792]{2,1,0:T(8,128)(2,1)S(1)}, bf16[2,32,1792]{2,1,0:T(8,128)(2,1)S(1)}, u32[]{:S(2)}, u32[]{:S(2)}) collective-permute-start(bf16[2,32,1792]{2,1,0:T(8,128)(2,1)S(1)} %shard_map.72), channel_id=1, source_target_pairs={{0,4},{2,6},{4,0},{6,2},{8,12},{10,14},{12,8},{14,10},{1,5},{3,7},... | collective-permute-start | bytes 688136 | tf_op jit(solution)/shard_map/ppermute | solution.py:23
  45.8 6.1 %collective-permute-start.18 = (bf16[2,32,1792]{2,1,0:T(8,128)(2,1)S(1)}, bf16[2,32,1792]{2,1,0:T(8,128)(2,1)S(1)}, u32[]{:S(2)}, u32[]{:S(2)}) collective-permute-start(bf16[2,32,1792]{2,1,0:T(8,128)(2,1)S(1)} %get-tuple-element.70), channel_id=1, source_target_pairs={{0,2},{2,0},{4,6},{6,4},{8,10},{10,8},{12,14},{14,12},{1,3},{3,1},... | collective-permute-start | bytes 688136 | tf_op jit(solution)/shard_map/ppermute | solution.py:23
  52.1 1.4 %collective-permute-start.22 = (bf16[32,1792]{1,0:T(8,128)(2,1)S(1)}, bf16[32,1792]{1,0:T(8,128)(2,1)S(1)}, u32[]{:S(2)}, u32[]{:S(2)}) collective-permute-start(bf16[32,1792]{1,0:T(8,128)(2,1)S(1)} %slice_bitcast_fusion), channel_id=1, source_target_pairs={{0,1},{1,0},{2,3},{3,2},{4,5},{5,4},{6,7},{7,6},{8,9},{9,8},{10,11... | collective-permute-start | bytes 344072 | tf_op jit(solution)/shard_map/ppermute | solution.py:32

commit v9 on v8

--- a/solution.py
+++ b/solution.py
@@ -213,7 +213,7 @@
 
     both0 = jnp.stack([a0, b0])
     z2a = swap(a0, 4)
-    z2b = cast(swap(b0, 4), bf16, 0.3)
+    z2b = swap(b0, 4)
     z1 = swap(both0, 2)
     x0 = swap(both0, 1)
     z2a, ours = tie((z2a, ours))
@@ -229,7 +229,7 @@
     m3 = swap(held, 2)
     m7a = swap(m6a, 1)
     m7b = swap(m5b, 2)
-    p4, p5a, p5b = expert(((z2a, z2b), (m5a, m5b)), ((f32,), (bf16, f32)))
+    p4, p5a, p5b = expert(((z2a, z2b), (m5a, m5b)), ((f32,), (bf16, f32)), 0.3)
     m7a, m7b, p4, p5a, p5b = tie((m7a, m7b, p4, p5a, p5b))
     p6, p7a, p7b = expert(((m6a, m6b), (m7a, m7b)), ((f32,), (bf16, bf16)))
     p0, p1, p2, p3 = expert(

time: 54.4 us -> 54.4 us (level)
  no operation moved by 1% of the time
where the time goes in v9:
time: 54.4 us; the launch traced here: 54.1 us
  starting transfers between devices  29.4 us (54%)
  waiting for transfers between devices  14.5 us (27%)
  Pallas kernels  4.43 us (8%)
  local copies, waits for them, and re-layouts  3.57 us (7%)
  other arithmetic  2.11 us (4%)
    ppermute x20, starting transfers between devices, swap(): return lax.ppermute(value, 'ep', pairs)  28.8 us
    ppermute x20, waiting for transfers between devices, swap(): return lax.ppermute(value, 'ep', pairs)  12.9 us
    unnamed x10, local copies, waits for them, and re-layouts  3.55 us
    pallas_call x3, Pallas kernels, expert_block(): pl.pallas_call(functools.partial(expert_kernel, [(None,) * len(b) for b i...  3.5 us
    ppermute x3, waiting for transfers between devices, swap_core(): return lax.ppermute(value, 'tp', [(0, 1), (1, 0)])  1.62 us
  transfers between devices with their start and end apart: 23, of which 9 were waited for; matrix products, arithmetic and copies ran while one was open for 1% of the time, Pallas kernels for 8%

profile of v9, /device:TPU:0, one launch (start us, length us, event | category | flops | bytes accessed | tf_op | source)
XLA Modules:
  0.0 54.1 jit_solution(14074474073694187664)
XLA Ops:
  0.0 1.0 %broadcast_select_fusion.2 = (bf16[32,1792]{1,0:T(8,128)(2,1)S(1)}, bf16[32,1792]{1,0:T(8,128)(2,1)S(1)}) fusion(pred[]{:T(512)S(6)} %eq.3, bf16[64,1792]{1,0:T(8,128)(2,1)} %param.6), kind=kLoop, calls=%fused_computation.13 | loop fusion | flops 114688 | bytes 458753 | tf_op jit(solution)/shard_map/jit(_where)/select_n | solution.py:206
  1.5 3.7 %collective-permute-start.3 = (bf16[32,1792]{1,0:T(8,128)(2,1)S(1)}, bf16[32,1792]{1,0:T(8,128)(2,1)S(1)}, u32[]{:S(2)}, u32[]{:S(2)}) collective-permute-start(bf16[32,1792]{1,0:T(8,128)(2,1)S(1)} %get-tuple-element.41), channel_id=1, source_target_pairs={{0,8},{2,10},{4,12},{6,14},{8,0},{10,2},{12,4},{14,6},{1,9},{3,11}... | collective-permute-start | bytes 344072 | tf_op jit(solution)/shard_map/ppermute | solution.py:23
  5.2 1.6 %collective-permute-start.2 = (bf16[2,32,1792]{2,1,0:T(8,128)(2,1)S(1)}, bf16[2,32,1792]{2,1,0:T(8,128)(2,1)S(1)}, u32[]{:S(2)}, u32[]{:S(2)}) collective-permute-start(bf16[2,32,1792]{2,1,0:T(8,128)(2,1)S(1)} %pad_maximum_fusion.refs_0_), channel_id=1, source_target_pairs={{0,2},{2,0},{4,6},{6,4},{8,10},{10,8},{12,14},{14,12},{1,3},{3,1},... | collective-permute-start | bytes 688136 | tf_op jit(solution)/shard_map/ppermute | solution.py:23
  6.7 1.6 %collective-permute-start.4 = (bf16[2,32,1792]{2,1,0:T(8,128)(2,1)S(1)}, bf16[2,32,1792]{2,1,0:T(8,128)(2,1)S(1)}, u32[]{:S(2)}, u32[]{:S(2)}) collective-permute-start(bf16[2,32,1792]{2,1,0:T(8,128)(2,1)S(1)} %pad_maximum_fusion.refs_0_), channel_id=1, source_target_pairs={{0,4},{2,6},{4,0},{6,2},{8,12},{10,14},{12,8},{14,10},{1,5},{3,7},... | collective-permute-start | bytes 688136 | tf_op jit(solution)/shard_map/ppermute | solution.py:23
  8.3 1.2 %collective-permute-start.1 = (bf16[32,1792]{1,0:T(8,128)(2,1)S(1)}, bf16[32,1792]{1,0:T(8,128)(2,1)S(1)}, u32[]{:S(2)}, u32[]{:S(2)}) collective-permute-start(bf16[32,1792]{1,0:T(8,128)(2,1)S(1)} %collective-permute-done), channel_id=1, source_target_pairs={{0,8},{2,10},{4,12},{6,14},{8,0},{10,2},{12,4},{14,6},{1,9},{3,11}... | collective-permute-start | bytes 344072 | tf_op jit(solution)/shard_map/ppermute | solution.py:23
  9.6 1.2 %copy-done = bf16[1,3584,128]{2,1,0:T(8,128)(2,1)S(1)} copy-done((bf16[1,3584,128]{2,1,0:T(8,128)(2,1)S(1)}, bf16[1,3584,128]{2,1,0:T(8,128)(2,1)}, u32[]{:S(2)}) %copy-start) | copy-done | bytes 917528
  10.7 1.2 %copy-done.1 = bf16[1,3584,128]{2,1,0:T(8,128)(2,1)S(1)} copy-done((bf16[1,3584,128]{2,1,0:T(8,128)(2,1)S(1)}, bf16[1,3584,128]{2,1,0:T(8,128)(2,1)}, u32[]{:S(2)}) %copy-start.1) | copy-done | bytes 917528
  11.9 1.2 %copy-done.2 = bf16[1,128,3584]{2,1,0:T(8,128)(2,1)S(1)} copy-done((bf16[1,128,3584]{2,1,0:T(8,128)(2,1)S(1)}, bf16[1,128,3584]{2,1,0:T(8,128)(2,1)}, u32[]{:S(2)}) %copy-start.2) | copy-done | bytes 917528
  13.1 0.8 %shard_map.64.refs_4_ = bf16[3584,384]{1,0:T(8,128)(2,1)S(1)} custom-call(bf16[3584,128]{1,0:T(8,128)(2,1)S(1)} %bitcast.28, bf16[3584,128]{1,0:T(8,128)(2,1)S(1)} %bitcast.29, bf16[128,3584]{1,0:T(8,128)(2,1)S(1)} %bitcast.30), custom_call_target="tpu_custom_call" | custom-call | flops 2300000000 | tf_op jit(solution)/shard_map/pallas_call | solution.py:49
  15.0 1.8 %collective-permute-done.1.refs_1_ = bf16[32,1792]{1,0:T(8,128)(2,1)S(1)} collective-permute-done((bf16[32,1792]{1,0:T(8,128)(2,1)S(1)}, bf16[32,1792]{1,0:T(8,128)(2,1)S(1)}, u32[]{:S(2)}, u32[]{:S(2)}) %collective-permute-start.1) | collective-permute-done | bytes 114720 | tf_op jit(solution)/shard_map/ppermute | solution.py:23
  16.8 0.7 %collective-permute-start.5 = (bf16[32,1792]{1,0:T(8,128)(2,1)S(1)}, bf16[32,1792]{1,0:T(8,128)(2,1)S(1)}, u32[]{:S(2)}, u32[]{:S(2)}) collective-permute-start(bf16[32,1792]{1,0:T(8,128)(2,1)S(1)} %collective-permute-done.1.refs_1_), channel_id=1, source_target_pairs={{0,2},{2,0},{4,6},{6,4},{8,10},{10,8},{12,14},{14,12},{1,3},{3,1},... | collective-permute-start | bytes 344072 | tf_op jit(solution)/shard_map/ppermute | solution.py:23
  17.5 2.4 %collective-permute-start.12 = (bf16[32,1792]{1,0:T(8,128)(2,1)S(1)}, bf16[32,1792]{1,0:T(8,128)(2,1)S(1)}, u32[]{:S(2)}, u32[]{:S(2)}) collective-permute-start(bf16[32,1792]{1,0:T(8,128)(2,1)S(1)} %collective-permute-done.1.refs_1_), channel_id=1, source_target_pairs={{0,4},{2,6},{4,0},{6,2},{8,12},{10,14},{12,8},{14,10},{1,5},{3,7},... | collective-permute-start | bytes 344072 | tf_op jit(solution)/shard_map/ppermute | solution.py:23
  19.9 1.0 %collective-permute-done.8.from_ref = bf16[32,1792]{1,0:T(8,128)(2,1)S(1)} collective-permute-done((bf16[32,1792]{1,0:T(8,128)(2,1)S(1)}, bf16[32,1792]{1,0:T(8,128)(2,1)S(1)}, u32[]{:S(2)}, u32[]{:S(2)}) %collective-permute-start.8) | collective-permute-done | bytes 114720 | tf_op jit(solution)/shard_map/ppermute | solution.py:23
  20.9 1.0 %collective-permute-start.9 = (bf16[32,1792]{1,0:T(8,128)(2,1)S(1)}, bf16[32,1792]{1,0:T(8,128)(2,1)S(1)}, u32[]{:S(2)}, u32[]{:S(2)}) collective-permute-start(bf16[32,1792]{1,0:T(8,128)(2,1)S(1)} %shard_map.66.refs_0_), channel_id=1, source_target_pairs={{0,2},{2,0},{4,6},{6,4},{8,10},{10,8},{12,14},{14,12},{1,3},{3,1},... | collective-permute-start | bytes 344072 | tf_op jit(solution)/shard_map/ppermute | solution.py:23
  21.9 1.5 %collective-permute-start.10 = (bf16[32,1792]{1,0:T(8,128)(2,1)S(1)}, bf16[32,1792]{1,0:T(8,128)(2,1)S(1)}, u32[]{:S(2)}, u32[]{:S(2)}) collective-permute-start(bf16[32,1792]{1,0:T(8,128)(2,1)S(1)} %collective-permute-done.5.refs_3_), channel_id=1, source_target_pairs={{0,4},{2,6},{4,0},{6,2},{8,12},{10,14},{12,8},{14,10},{1,5},{3,7},... | collective-permute-start | bytes 344072 | tf_op jit(solution)/shard_map/ppermute | solution.py:23
  23.4 1.3 %collective-permute-start.6 = (bf16[2,32,1792]{2,1,0:T(8,128)(2,1)S(1)}, bf16[2,32,1792]{2,1,0:T(8,128)(2,1)S(1)}, u32[]{:S(2)}, u32[]{:S(2)}) collective-permute-start(bf16[2,32,1792]{2,1,0:T(8,128)(2,1)S(1)} %collective-permute-done.2.refs_1_), channel_id=1, source_target_pairs={{0,4},{2,6},{4,0},{6,2},{8,12},{10,14},{12,8},{14,10},{1,5},{3,7},... | collective-permute-start | bytes 688136 | tf_op jit(solution)/shard_map/ppermute | solution.py:23
  25.0 1.1 %shard_map.67 = (f32[2,32,1792]{2,1,0:T(8,128)S(1)}, bf16[32,1792]{1,0:T(8,128)(2,1)S(1)}, f32[32,1792]{1,0:T(8,128)S(1)}) custom-call(bf16[32,1792]{1,0:T(8,128)(2,1)S(1)} %collective-permute-done.3.refs_0_, bf16[32,1792]{1,0:T(8,128)(2,1)S(1)} %collective-permute-done.1.refs_1_, bf16[32,1792]{1,0:T(8,128)(2,1)S(1)} %collective-permute-done.11.refs_2_, ...), custom_call_target="tpu_custom_call" | custom-call | flops 345000000 | tf_op jit(solution)/shard_map/pallas_call | solution.py:112
  26.2 1.7 %collective-permute-done.10.refs_3_ = bf16[32,1792]{1,0:T(8,128)(2,1)S(1)} collective-permute-done((bf16[32,1792]{1,0:T(8,128)(2,1)S(1)}, bf16[32,1792]{1,0:T(8,128)(2,1)S(1)}, u32[]{:S(2)}, u32[]{:S(2)}) %collective-permute-start.10) | collective-permute-done | bytes 114720 | tf_op jit(solution)/shard_map/ppermute | solution.py:23
  27.9 1.1 %shard_map.68 = (f32[2,32,1792]{2,1,0:T(8,128)S(1)}, bf16[32,1792]{1,0:T(8,128)(2,1)S(1)}, bf16[32,1792]{1,0:T(8,128)(2,1)S(1)}) custom-call(bf16[32,1792]{1,0:T(8,128)(2,1)S(1)} %shard_map.66.refs_0_, bf16[32,1792]{1,0:T(8,128)(2,1)S(1)} %collective-permute-done.12.refs_1_, bf16[32,1792]{1,0:T(8,128)(2,1)S(1)} %collective-permute-done.9.refs_2_, ...), custom_call_target="tpu_custom_call" | custom-call | flops 1150000000 | tf_op jit(solution)/shard_map/pallas_call | solution.py:112
  29.0 1.3 %collective-permute-start.13 = (bf16[32,1792]{1,0:T(8,128)(2,1)S(1)}, bf16[32,1792]{1,0:T(8,128)(2,1)S(1)}, u32[]{:S(2)}, u32[]{:S(2)}) collective-permute-start(bf16[32,1792]{1,0:T(8,128)(2,1)S(1)} %get-tuple-element.61), channel_id=1, source_target_pairs={{0,2},{2,0},{4,6},{6,4},{8,10},{10,8},{12,14},{14,12},{1,3},{3,1},... | collective-permute-start | bytes 344072 | tf_op jit(solution)/shard_map/ppermute | solution.py:23
  30.4 1.2 %collective-permute-start.16 = (bf16[32,1792]{1,0:T(8,128)(2,1)S(1)}, bf16[32,1792]{1,0:T(8,128)(2,1)S(1)}, u32[]{:S(2)}, u32[]{:S(2)}) collective-permute-start(bf16[32,1792]{1,0:T(8,128)(2,1)S(1)} %get-tuple-element.68), channel_id=1, source_target_pairs={{0,4},{2,6},{4,0},{6,2},{8,12},{10,14},{12,8},{14,10},{1,5},{3,7},... | collective-permute-start | bytes 344072 | tf_op jit(solution)/shard_map/ppermute | solution.py:23
  31.6 1.3 %collective-permute-start.15 = (bf16[32,1792]{1,0:T(8,128)(2,1)S(1)}, bf16[32,1792]{1,0:T(8,128)(2,1)S(1)}, u32[]{:S(2)}, u32[]{:S(2)}) collective-permute-start(bf16[32,1792]{1,0:T(8,128)(2,1)S(1)} %get-tuple-element.66), channel_id=1, source_target_pairs={{0,2},{2,0},{4,6},{6,4},{8,10},{10,8},{12,14},{14,12},{1,3},{3,1},... | collective-permute-start | bytes 344072 | tf_op jit(solution)/shard_map/ppermute | solution.py:23
  32.9 1.2 %shard_map.65 = (f32[2,32,1792]{2,1,0:T(8,128)S(1)}, bf16[2,32,1792]{2,1,0:T(8,128)(2,1)S(1)}, f32[2,32,1792]{2,1,0:T(8,128)S(1)}, bf16[2,32,1792]{2,1,0:T(8,128)(2,1)S(1)}) custom-call(bf16[2,32,1792]{2,1,0:T(8,128)(2,1)S(1)} %pad_maximum_fusion.refs_0_, bf16[2,32,1792]{2,1,0:T(8,128)(2,1)S(1)} %collective-permute-done.2.refs_1_, ...), custom_call_target="tpu_custom_call" | custom-call | flops 1150000000 | tf_op jit(solution)/shard_map/pallas_call | solution.py:112
  34.2 1.4 %collective-permute-start.14 = (bf16[2,32,1792]{2,1,0:T(8,128)(2,1)S(1)}, bf16[2,32,1792]{2,1,0:T(8,128)(2,1)S(1)}, u32[]{:S(2)}, u32[]{:S(2)}) collective-permute-start(bf16[2,32,1792]{2,1,0:T(8,128)(2,1)S(1)} %pad_maximum_fusion.1), channel_id=1, source_target_pairs={{0,4},{2,6},{4,0},{6,2},{8,12},{10,14},{12,8},{14,10},{1,5},{3,7},... | collective-permute-start | bytes 688136 | tf_op jit(solution)/shard_map/ppermute | solution.py:23
  36.4 0.9 %collective-permute-start.17 = (bf16[32,1792]{1,0:T(8,128)(2,1)S(1)}, bf16[32,1792]{1,0:T(8,128)(2,1)S(1)}, u32[]{:S(2)}, u32[]{:S(2)}) collective-permute-start(bf16[32,1792]{1,0:T(8,128)(2,1)S(1)} %shard_map.70), channel_id=1, source_target_pairs={{0,2},{2,0},{4,6},{6,4},{8,10},{10,8},{12,14},{14,12},{1,3},{3,1},... | collective-permute-start | bytes 344072 | tf_op jit(solution)/shard_map/ppermute | solution.py:23
  37.3 1.1 %collective-permute-start.19 = (bf16[2,32,1792]{2,1,0:T(8,128)(2,1)S(1)}, bf16[2,32,1792]{2,1,0:T(8,128)(2,1)S(1)}, u32[]{:S(2)}, u32[]{:S(2)}) collective-permute-start(bf16[2,32,1792]{2,1,0:T(8,128)(2,1)S(1)} %get-tuple-element.73), channel_id=1, source_target_pairs={{0,2},{2,0},{4,6},{6,4},{8,10},{10,8},{12,14},{14,12},{1,3},{3,1},... | collective-permute-start | bytes 688136 | tf_op jit(solution)/shard_map/ppermute | solution.py:23
  38.5 2.7 %collective-permute-done.17 = bf16[32,1792]{1,0:T(8,128)(2,1)S(1)} collective-permute-done((bf16[32,1792]{1,0:T(8,128)(2,1)S(1)}, bf16[32,1792]{1,0:T(8,128)(2,1)S(1)}, u32[]{:S(2)}, u32[]{:S(2)}) %collective-permute-start.17) | collective-permute-done | bytes 114720 | tf_op jit(solution)/shard_map/ppermute | solution.py:23
  41.3 2.9 %collective-permute-start.21 = (bf16[2,32,1792]{2,1,0:T(8,128)(2,1)S(1)}, bf16[2,32,1792]{2,1,0:T(8,128)(2,1)S(1)}, u32[]{:S(2)}, u32[]{:S(2)}) collective-permute-start(bf16[2,32,1792]{2,1,0:T(8,128)(2,1)S(1)} %add_convert_fusion), channel_id=1, source_target_pairs={{0,8},{2,10},{4,12},{6,14},{8,0},{10,2},{12,4},{14,6},{1,9},{3,11}... | collective-permute-start | bytes 688136 | tf_op jit(solution)/shard_map/ppermute | solution.py:23
  44.3 1.5 %collective-permute-start.20 = (bf16[2,32,1792]{2,1,0:T(8,128)(2,1)S(1)}, bf16[2,32,1792]{2,1,0:T(8,128)(2,1)S(1)}, u32[]{:S(2)}, u32[]{:S(2)}) collective-permute-start(bf16[2,32,1792]{2,1,0:T(8,128)(2,1)S(1)} %shard_map.71), channel_id=1, source_target_pairs={{0,4},{2,6},{4,0},{6,2},{8,12},{10,14},{12,8},{14,10},{1,5},{3,7},... | collective-permute-start | bytes 688136 | tf_op jit(solution)/shard_map/ppermute | solution.py:23
  45.8 1.2 %collective-permute-start.18 = (bf16[2,32,1792]{2,1,0:T(8,128)(2,1)S(1)}, bf16[2,32,1792]{2,1,0:T(8,128)(2,1)S(1)}, u32[]{:S(2)}, u32[]{:S(2)}) collective-permute-start(bf16[2,32,1792]{2,1,0:T(8,128)(2,1)S(1)} %get-tuple-element.70), channel_id=1, source_target_pairs={{0,2},{2,0},{4,6},{6,4},{8,10},{10,8},{12,14},{14,12},{1,3},{3,1},... | collective-permute-start | bytes 688136 | tf_op jit(solution)/shard_map/ppermute | solution.py:23
  47.0 4.3 %collective-permute-done.21.from_ref = bf16[2,32,1792]{2,1,0:T(8,128)(2,1)S(1)} collective-permute-done((bf16[2,32,1792]{2,1,0:T(8,128)(2,1)S(1)}, bf16[2,32,1792]{2,1,0:T(8,128)(2,1)S(1)}, u32[]{:S(2)}, u32[]{:S(2)}) %collective-permute-start.21) | collective-permute-done | bytes 229408 | tf_op jit(solution)/shard_map/ppermute | solution.py:23
  52.1 1.3 %collective-permute-done.22 = bf16[32,1792]{1,0:T(8,128)(2,1)S(1)} collective-permute-done((bf16[32,1792]{1,0:T(8,128)(2,1)S(1)}, bf16[32,1792]{1,0:T(8,128)(2,1)S(1)}, u32[]{:S(2)}, u32[]{:S(2)}) %collective-permute-start.22) | collective-permute-done | bytes 114720 | tf_op jit(solution)/shard_map/ppermute | solution.py:32
  (45 shorter events, 4.5 us)
Async XLA Ops:
  1.0 4.2 %collective-permute-start = (bf16[32,1792]{1,0:T(8,128)(2,1)S(1)}, bf16[32,1792]{1,0:T(8,128)(2,1)S(1)}, u32[]{:S(2)}, u32[]{:S(2)}) collective-permute-start(bf16[32,1792]{1,0:T(8,128)(2,1)S(1)} %get-tuple-element.42), channel_id=1, source_target_pairs={{0,1},{1,0},{2,3},{3,2},{4,5},{5,4},{6,7},{7,6},{8,9},{9,8},{10,11... | collective-permute-start | bytes 344072 | tf_op jit(solution)/shard_map/ppermute | solution.py:32
  1.5 12.4 %collective-permute-start.3 = (bf16[32,1792]{1,0:T(8,128)(2,1)S(1)}, bf16[32,1792]{1,0:T(8,128)(2,1)S(1)}, u32[]{:S(2)}, u32[]{:S(2)}) collective-permute-start(bf16[32,1792]{1,0:T(8,128)(2,1)S(1)} %get-tuple-element.41), channel_id=1, source_target_pairs={{0,8},{2,10},{4,12},{6,14},{8,0},{10,2},{12,4},{14,6},{1,9},{3,11}... | collective-permute-start | bytes 344072 | tf_op jit(solution)/shard_map/ppermute | solution.py:23
  5.2 11.6 %collective-permute-start.2 = (bf16[2,32,1792]{2,1,0:T(8,128)(2,1)S(1)}, bf16[2,32,1792]{2,1,0:T(8,128)(2,1)S(1)}, u32[]{:S(2)}, u32[]{:S(2)}) collective-permute-start(bf16[2,32,1792]{2,1,0:T(8,128)(2,1)S(1)} %pad_maximum_fusion.refs_0_), channel_id=1, source_target_pairs={{0,2},{2,0},{4,6},{6,4},{8,10},{10,8},{12,14},{14,12},{1,3},{3,1},... | collective-permute-start | bytes 688136 | tf_op jit(solution)/shard_map/ppermute | solution.py:23
  6.7 13.2 %collective-permute-start.4 = (bf16[2,32,1792]{2,1,0:T(8,128)(2,1)S(1)}, bf16[2,32,1792]{2,1,0:T(8,128)(2,1)S(1)}, u32[]{:S(2)}, u32[]{:S(2)}) collective-permute-start(bf16[2,32,1792]{2,1,0:T(8,128)(2,1)S(1)} %pad_maximum_fusion.refs_0_), channel_id=1, source_target_pairs={{0,4},{2,6},{4,0},{6,2},{8,12},{10,14},{12,8},{14,10},{1,5},{3,7},... | collective-permute-start | bytes 688136 | tf_op jit(solution)/shard_map/ppermute | solution.py:23
  8.3 8.5 %collective-permute-start.1 = (bf16[32,1792]{1,0:T(8,128)(2,1)S(1)}, bf16[32,1792]{1,0:T(8,128)(2,1)S(1)}, u32[]{:S(2)}, u32[]{:S(2)}) collective-permute-start(bf16[32,1792]{1,0:T(8,128)(2,1)S(1)} %collective-permute-done), channel_id=1, source_target_pairs={{0,8},{2,10},{4,12},{6,14},{8,0},{10,2},{12,4},{14,6},{1,9},{3,11}... | collective-permute-start | bytes 344072 | tf_op jit(solution)/shard_map/ppermute | solution.py:23
  9.6 1.2 %copy-start = (bf16[1,3584,128]{2,1,0:T(8,128)(2,1)S(1)}, bf16[1,3584,128]{2,1,0:T(8,128)(2,1)}, u32[]{:S(2)}) copy-start(bf16[1,3584,128]{2,1,0:T(8,128)(2,1)} %param.9) | copy-start | bytes 2752516
  10.7 1.2 %copy-start.1 = (bf16[1,3584,128]{2,1,0:T(8,128)(2,1)S(1)}, bf16[1,3584,128]{2,1,0:T(8,128)(2,1)}, u32[]{:S(2)}) copy-start(bf16[1,3584,128]{2,1,0:T(8,128)(2,1)} %param.10) | copy-start | bytes 2752516
  11.9 1.2 %copy-start.2 = (bf16[1,128,3584]{2,1,0:T(8,128)(2,1)S(1)}, bf16[1,128,3584]{2,1,0:T(8,128)(2,1)}, u32[]{:S(2)}) copy-start(bf16[1,128,3584]{2,1,0:T(8,128)(2,1)} %param.11) | copy-start | bytes 2752516
  13.9 7.0 %collective-permute-start.8 = (bf16[32,1792]{1,0:T(8,128)(2,1)S(1)}, bf16[32,1792]{1,0:T(8,128)(2,1)S(1)}, u32[]{:S(2)}, u32[]{:S(2)}) collective-permute-start(bf16[32,1792]{1,0:T(8,128)(2,1)S(1)} %collective-permute-done.3.refs_0_), channel_id=1, source_target_pairs={{0,4},{2,6},{4,0},{6,2},{8,12},{10,14},{12,8},{14,10},{1,5},{3,7},... | collective-permute-start | bytes 344072 | tf_op jit(solution)/shard_map/ppermute | solution.py:23
  14.4 9.0 %collective-permute-start.11 = (bf16[32,1792]{1,0:T(8,128)(2,1)S(1)}, bf16[32,1792]{1,0:T(8,128)(2,1)S(1)}, u32[]{:S(2)}, u32[]{:S(2)}) collective-permute-start(bf16[32,1792]{1,0:T(8,128)(2,1)S(1)} %collective-permute-done.3.refs_0_), channel_id=1, source_target_pairs={{0,2},{2,0},{4,6},{6,4},{8,10},{10,8},{12,14},{14,12},{1,3},{3,1},... | collective-permute-start | bytes 344072 | tf_op jit(solution)/shard_map/ppermute | solution.py:23
  16.8 5.1 %collective-permute-start.5 = (bf16[32,1792]{1,0:T(8,128)(2,1)S(1)}, bf16[32,1792]{1,0:T(8,128)(2,1)S(1)}, u32[]{:S(2)}, u32[]{:S(2)}) collective-permute-start(bf16[32,1792]{1,0:T(8,128)(2,1)S(1)} %collective-permute-done.1.refs_1_), channel_id=1, source_target_pairs={{0,2},{2,0},{4,6},{6,4},{8,10},{10,8},{12,14},{14,12},{1,3},{3,1},... | collective-permute-start | bytes 344072 | tf_op jit(solution)/shard_map/ppermute | solution.py:23
  17.5 5.9 %collective-permute-start.12 = (bf16[32,1792]{1,0:T(8,128)(2,1)S(1)}, bf16[32,1792]{1,0:T(8,128)(2,1)S(1)}, u32[]{:S(2)}, u32[]{:S(2)}) collective-permute-start(bf16[32,1792]{1,0:T(8,128)(2,1)S(1)} %collective-permute-done.1.refs_1_), channel_id=1, source_target_pairs={{0,4},{2,6},{4,0},{6,2},{8,12},{10,14},{12,8},{14,10},{1,5},{3,7},... | collective-permute-start | bytes 344072 | tf_op jit(solution)/shard_map/ppermute | solution.py:23
  19.9 5.1 %collective-permute-start.7 = (bf16[3584,384]{1,0:T(8,128)(2,1)S(1)}, bf16[3584,384]{1,0:T(8,128)(2,1)S(1)}, u32[]{:S(2)}, u32[]{:S(2)}) collective-permute-start(bf16[3584,384]{1,0:T(8,128)(2,1)S(1)} %shard_map.64.refs_4_), channel_id=1, source_target_pairs={{0,1},{1,0},{2,3},{3,2},{4,5},{5,4},{6,7},{7,6},{8,9},{9,8},{10,11... | collective-permute-start | bytes 8257544 | tf_op jit(solution)/shard_map/ppermute | solution.py:32
  20.9 5.2 %collective-permute-start.9 = (bf16[32,1792]{1,0:T(8,128)(2,1)S(1)}, bf16[32,1792]{1,0:T(8,128)(2,1)S(1)}, u32[]{:S(2)}, u32[]{:S(2)}) collective-permute-start(bf16[32,1792]{1,0:T(8,128)(2,1)S(1)} %shard_map.66.refs_0_), channel_id=1, source_target_pairs={{0,2},{2,0},{4,6},{6,4},{8,10},{10,8},{12,14},{14,12},{1,3},{3,1},... | collective-permute-start | bytes 344072 | tf_op jit(solution)/shard_map/ppermute | solution.py:23
  21.9 6.0 %collective-permute-start.10 = (bf16[32,1792]{1,0:T(8,128)(2,1)S(1)}, bf16[32,1792]{1,0:T(8,128)(2,1)S(1)}, u32[]{:S(2)}, u32[]{:S(2)}) collective-permute-start(bf16[32,1792]{1,0:T(8,128)(2,1)S(1)} %collective-permute-done.5.refs_3_), channel_id=1, source_target_pairs={{0,4},{2,6},{4,0},{6,2},{8,12},{10,14},{12,8},{14,10},{1,5},{3,7},... | collective-permute-start | bytes 344072 | tf_op jit(solution)/shard_map/ppermute | solution.py:23
  23.4 9.5 %collective-permute-start.6 = (bf16[2,32,1792]{2,1,0:T(8,128)(2,1)S(1)}, bf16[2,32,1792]{2,1,0:T(8,128)(2,1)S(1)}, u32[]{:S(2)}, u32[]{:S(2)}) collective-permute-start(bf16[2,32,1792]{2,1,0:T(8,128)(2,1)S(1)} %collective-permute-done.2.refs_1_), channel_id=1, source_target_pairs={{0,4},{2,6},{4,0},{6,2},{8,12},{10,14},{12,8},{14,10},{1,5},{3,7},... | collective-permute-start | bytes 688136 | tf_op jit(solution)/shard_map/ppermute | solution.py:23
  27.9 2.4 %copy-start.3 = (s32[64,1]{0,1:T(1,128)S(1)}, s32[64,1]{0,1:T(1,128)}, u32[]{:S(2)}) copy-start(s32[64,1]{0,1:T(1,128)} %param.8) | copy-start | bytes 772
  29.0 5.1 %collective-permute-start.13 = (bf16[32,1792]{1,0:T(8,128)(2,1)S(1)}, bf16[32,1792]{1,0:T(8,128)(2,1)S(1)}, u32[]{:S(2)}, u32[]{:S(2)}) collective-permute-start(bf16[32,1792]{1,0:T(8,128)(2,1)S(1)} %get-tuple-element.61), channel_id=1, source_target_pairs={{0,2},{2,0},{4,6},{6,4},{8,10},{10,8},{12,14},{14,12},{1,3},{3,1},... | collective-permute-start | bytes 344072 | tf_op jit(solution)/shard_map/ppermute | solution.py:23
  30.4 6.0 %collective-permute-start.16 = (bf16[32,1792]{1,0:T(8,128)(2,1)S(1)}, bf16[32,1792]{1,0:T(8,128)(2,1)S(1)}, u32[]{:S(2)}, u32[]{:S(2)}) collective-permute-start(bf16[32,1792]{1,0:T(8,128)(2,1)S(1)} %get-tuple-element.68), channel_id=1, source_target_pairs={{0,4},{2,6},{4,0},{6,2},{8,12},{10,14},{12,8},{14,10},{1,5},{3,7},... | collective-permute-start | bytes 344072 | tf_op jit(solution)/shard_map/ppermute | solution.py:23
  31.6 6.9 %collective-permute-start.15 = (bf16[32,1792]{1,0:T(8,128)(2,1)S(1)}, bf16[32,1792]{1,0:T(8,128)(2,1)S(1)}, u32[]{:S(2)}, u32[]{:S(2)}) collective-permute-start(bf16[32,1792]{1,0:T(8,128)(2,1)S(1)} %get-tuple-element.66), channel_id=1, source_target_pairs={{0,2},{2,0},{4,6},{6,4},{8,10},{10,8},{12,14},{14,12},{1,3},{3,1},... | collective-permute-start | bytes 344072 | tf_op jit(solution)/shard_map/ppermute | solution.py:23
  34.2 7.0 %collective-permute-start.14 = (bf16[2,32,1792]{2,1,0:T(8,128)(2,1)S(1)}, bf16[2,32,1792]{2,1,0:T(8,128)(2,1)S(1)}, u32[]{:S(2)}, u32[]{:S(2)}) collective-permute-start(bf16[2,32,1792]{2,1,0:T(8,128)(2,1)S(1)} %pad_maximum_fusion.1), channel_id=1, source_target_pairs={{0,4},{2,6},{4,0},{6,2},{8,12},{10,14},{12,8},{14,10},{1,5},{3,7},... | collective-permute-start | bytes 688136 | tf_op jit(solution)/shard_map/ppermute | solution.py:23
  36.4 10.6 %copy-start.4 = (s32[64,1]{0,1:T(1,128)S(1)}, s32[64,1]{0,1:T(1,128)}, u32[]{:S(2)}) copy-start(s32[64,1]{0,1:T(1,128)} %param.7) | copy-start | bytes 772
  36.4 4.9 %collective-permute-start.17 = (bf16[32,1792]{1,0:T(8,128)(2,1)S(1)}, bf16[32,1792]{1,0:T(8,128)(2,1)S(1)}, u32[]{:S(2)}, u32[]{:S(2)}) collective-permute-start(bf16[32,1792]{1,0:T(8,128)(2,1)S(1)} %shard_map.70), channel_id=1, source_target_pairs={{0,2},{2,0},{4,6},{6,4},{8,10},{10,8},{12,14},{14,12},{1,3},{3,1},... | collective-permute-start | bytes 344072 | tf_op jit(solution)/shard_map/ppermute | solution.py:23
  37.3 6.9 %collective-permute-start.19 = (bf16[2,32,1792]{2,1,0:T(8,128)(2,1)S(1)}, bf16[2,32,1792]{2,1,0:T(8,128)(2,1)S(1)}, u32[]{:S(2)}, u32[]{:S(2)}) collective-permute-start(bf16[2,32,1792]{2,1,0:T(8,128)(2,1)S(1)} %get-tuple-element.73), channel_id=1, source_target_pairs={{0,2},{2,0},{4,6},{6,4},{8,10},{10,8},{12,14},{14,12},{1,3},{3,1},... | collective-permute-start | bytes 688136 | tf_op jit(solution)/shard_map/ppermute | solution.py:23
  41.3 10.0 %collective-permute-start.21 = (bf16[2,32,1792]{2,1,0:T(8,128)(2,1)S(1)}, bf16[2,32,1792]{2,1,0:T(8,128)(2,1)S(1)}, u32[]{:S(2)}, u32[]{:S(2)}) collective-permute-start(bf16[2,32,1792]{2,1,0:T(8,128)(2,1)S(1)} %add_convert_fusion), channel_id=1, source_target_pairs={{0,8},{2,10},{4,12},{6,14},{8,0},{10,2},{12,4},{14,6},{1,9},{3,11}... | collective-permute-start | bytes 688136 | tf_op jit(solution)/shard_map/ppermute | solution.py:23
  44.3 7.6 %collective-permute-start.20 = (bf16[2,32,1792]{2,1,0:T(8,128)(2,1)S(1)}, bf16[2,32,1792]{2,1,0:T(8,128)(2,1)S(1)}, u32[]{:S(2)}, u32[]{:S(2)}) collective-permute-start(bf16[2,32,1792]{2,1,0:T(8,128)(2,1)S(1)} %shard_map.71), channel_id=1, source_target_pairs={{0,4},{2,6},{4,0},{6,2},{8,12},{10,14},{12,8},{14,10},{1,5},{3,7},... | collective-permute-start | bytes 688136 | tf_op jit(solution)/shard_map/ppermute | solution.py:23
  45.8 6.1 %collective-permute-start.18 = (bf16[2,32,1792]{2,1,0:T(8,128)(2,1)S(1)}, bf16[2,32,1792]{2,1,0:T(8,128)(2,1)S(1)}, u32[]{:S(2)}, u32[]{:S(2)}) collective-permute-start(bf16[2,32,1792]{2,1,0:T(8,128)(2,1)S(1)} %get-tuple-element.70), channel_id=1, source_target_pairs={{0,2},{2,0},{4,6},{6,4},{8,10},{10,8},{12,14},{14,12},{1,3},{3,1},... | collective-permute-start | bytes 688136 | tf_op jit(solution)/shard_map/ppermute | solution.py:23
  52.0 1.4 %collective-permute-start.22 = (bf16[32,1792]{1,0:T(8,128)(2,1)S(1)}, bf16[32,1792]{1,0:T(8,128)(2,1)S(1)}, u32[]{:S(2)}, u32[]{:S(2)}) collective-permute-start(bf16[32,1792]{1,0:T(8,128)(2,1)S(1)} %slice_bitcast_fusion), channel_id=1, source_target_pairs={{0,1},{1,0},{2,3},{3,2},{4,5},{5,4},{6,7},{7,6},{8,9},{9,8},{10,11... | collective-permute-start | bytes 344072 | tf_op jit(solution)/shard_map/ppermute | solution.py:32

commit v10 on v9

--- a/solution.py
+++ b/solution.py
@@ -249,7 +249,7 @@
     r3 = swap(p3, 1)
     s2 = add(p2, r3, 0.1)
     sent, p1 = tie((sent, p1))
-    other = cast(swap(sent, 4), f32, 0.5)
+    other = cast(swap(sent, 4), bf16, 0.5).astype(f32)
     r2 = swap(s2, 2)
     r1 = swap(p1, 1)
     near = p0 + r1.astype(f32) + r2.astype(f32)

time: 54.4 us -> 54.4 us (level)
  no operation moved by 1% of the time
where the time goes in v10:
time: 54.4 us; the launch traced here: 54.2 us
  starting transfers between devices  29.4 us (54%)
  waiting for transfers between devices  14.5 us (27%)
  Pallas kernels  4.41 us (8%)
  local copies, waits for them, and re-layouts  3.57 us (7%)
  other arithmetic  2.13 us (4%)
    ppermute x20, starting transfers between devices, swap(): return lax.ppermute(value, 'ep', pairs)  28.8 us
    ppermute x20, waiting for transfers between devices, swap(): return lax.ppermute(value, 'ep', pairs)  12.9 us
    unnamed x10, local copies, waits for them, and re-layouts  3.55 us
    pallas_call x3, Pallas kernels, expert_block(): pl.pallas_call(functools.partial(expert_kernel, [(None,) * len(b) for b i...  3.5 us
    ppermute x3, waiting for transfers between devices, swap_core(): return lax.ppermute(value, 'tp', [(0, 1), (1, 0)])  1.62 us
  transfers between devices with their start and end apart: 23, of which 9 were waited for; matrix products, arithmetic and copies ran while one was open for 1% of the time, Pallas kernels for 8%

profile of v10, /device:TPU:0, one launch (start us, length us, event | category | flops | bytes accessed | tf_op | source)
XLA Modules:
  0.0 54.2 jit_solution(3029728612615203176)
XLA Ops:
  0.0 1.0 %broadcast_select_fusion.2 = (bf16[32,1792]{1,0:T(8,128)(2,1)S(1)}, bf16[32,1792]{1,0:T(8,128)(2,1)S(1)}) fusion(pred[]{:T(512)S(6)} %eq.3, bf16[64,1792]{1,0:T(8,128)(2,1)} %param.6), kind=kLoop, calls=%fused_computation.13 | loop fusion | flops 114688 | bytes 458753 | tf_op jit(solution)/shard_map/jit(_where)/select_n | solution.py:206
  1.5 3.7 %collective-permute-start.3 = (bf16[32,1792]{1,0:T(8,128)(2,1)S(1)}, bf16[32,1792]{1,0:T(8,128)(2,1)S(1)}, u32[]{:S(2)}, u32[]{:S(2)}) collective-permute-start(bf16[32,1792]{1,0:T(8,128)(2,1)S(1)} %get-tuple-element.41), channel_id=1, source_target_pairs={{0,8},{2,10},{4,12},{6,14},{8,0},{10,2},{12,4},{14,6},{1,9},{3,11}... | collective-permute-start | bytes 344072 | tf_op jit(solution)/shard_map/ppermute | solution.py:23
  5.2 1.6 %collective-permute-start.2 = (bf16[2,32,1792]{2,1,0:T(8,128)(2,1)S(1)}, bf16[2,32,1792]{2,1,0:T(8,128)(2,1)S(1)}, u32[]{:S(2)}, u32[]{:S(2)}) collective-permute-start(bf16[2,32,1792]{2,1,0:T(8,128)(2,1)S(1)} %pad_maximum_fusion.refs_0_), channel_id=1, source_target_pairs={{0,2},{2,0},{4,6},{6,4},{8,10},{10,8},{12,14},{14,12},{1,3},{3,1},... | collective-permute-start | bytes 688136 | tf_op jit(solution)/shard_map/ppermute | solution.py:23
  6.7 1.6 %collective-permute-start.4 = (bf16[2,32,1792]{2,1,0:T(8,128)(2,1)S(1)}, bf16[2,32,1792]{2,1,0:T(8,128)(2,1)S(1)}, u32[]{:S(2)}, u32[]{:S(2)}) collective-permute-start(bf16[2,32,1792]{2,1,0:T(8,128)(2,1)S(1)} %pad_maximum_fusion.refs_0_), channel_id=1, source_target_pairs={{0,4},{2,6},{4,0},{6,2},{8,12},{10,14},{12,8},{14,10},{1,5},{3,7},... | collective-permute-start | bytes 688136 | tf_op jit(solution)/shard_map/ppermute | solution.py:23
  8.3 1.2 %collective-permute-start.1 = (bf16[32,1792]{1,0:T(8,128)(2,1)S(1)}, bf16[32,1792]{1,0:T(8,128)(2,1)S(1)}, u32[]{:S(2)}, u32[]{:S(2)}) collective-permute-start(bf16[32,1792]{1,0:T(8,128)(2,1)S(1)} %collective-permute-done), channel_id=1, source_target_pairs={{0,8},{2,10},{4,12},{6,14},{8,0},{10,2},{12,4},{14,6},{1,9},{3,11}... | collective-permute-start | bytes 344072 | tf_op jit(solution)/shard_map/ppermute | solution.py:23
  9.6 1.2 %copy-done = bf16[1,3584,128]{2,1,0:T(8,128)(2,1)S(1)} copy-done((bf16[1,3584,128]{2,1,0:T(8,128)(2,1)S(1)}, bf16[1,3584,128]{2,1,0:T(8,128)(2,1)}, u32[]{:S(2)}) %copy-start) | copy-done | bytes 917528
  10.7 1.2 %copy-done.1 = bf16[1,3584,128]{2,1,0:T(8,128)(2,1)S(1)} copy-done((bf16[1,3584,128]{2,1,0:T(8,128)(2,1)S(1)}, bf16[1,3584,128]{2,1,0:T(8,128)(2,1)}, u32[]{:S(2)}) %copy-start.1) | copy-done | bytes 917528
  11.9 1.2 %copy-done.2 = bf16[1,128,3584]{2,1,0:T(8,128)(2,1)S(1)} copy-done((bf16[1,128,3584]{2,1,0:T(8,128)(2,1)S(1)}, bf16[1,128,3584]{2,1,0:T(8,128)(2,1)}, u32[]{:S(2)}) %copy-start.2) | copy-done | bytes 917528
  13.1 0.8 %shard_map.64.refs_4_ = bf16[3584,384]{1,0:T(8,128)(2,1)S(1)} custom-call(bf16[3584,128]{1,0:T(8,128)(2,1)S(1)} %bitcast.28, bf16[3584,128]{1,0:T(8,128)(2,1)S(1)} %bitcast.29, bf16[128,3584]{1,0:T(8,128)(2,1)S(1)} %bitcast.30), custom_call_target="tpu_custom_call" | custom-call | flops 2300000000 | tf_op jit(solution)/shard_map/pallas_call | solution.py:49
  15.0 1.8 %collective-permute-done.1.refs_1_ = bf16[32,1792]{1,0:T(8,128)(2,1)S(1)} collective-permute-done((bf16[32,1792]{1,0:T(8,128)(2,1)S(1)}, bf16[32,1792]{1,0:T(8,128)(2,1)S(1)}, u32[]{:S(2)}, u32[]{:S(2)}) %collective-permute-start.1) | collective-permute-done | bytes 114720 | tf_op jit(solution)/shard_map/ppermute | solution.py:23
  16.8 0.7 %collective-permute-start.5 = (bf16[32,1792]{1,0:T(8,128)(2,1)S(1)}, bf16[32,1792]{1,0:T(8,128)(2,1)S(1)}, u32[]{:S(2)}, u32[]{:S(2)}) collective-permute-start(bf16[32,1792]{1,0:T(8,128)(2,1)S(1)} %collective-permute-done.1.refs_1_), channel_id=1, source_target_pairs={{0,2},{2,0},{4,6},{6,4},{8,10},{10,8},{12,14},{14,12},{1,3},{3,1},... | collective-permute-start | bytes 344072 | tf_op jit(solution)/shard_map/ppermute | solution.py:23
  17.5 2.4 %collective-permute-start.12 = (bf16[32,1792]{1,0:T(8,128)(2,1)S(1)}, bf16[32,1792]{1,0:T(8,128)(2,1)S(1)}, u32[]{:S(2)}, u32[]{:S(2)}) collective-permute-start(bf16[32,1792]{1,0:T(8,128)(2,1)S(1)} %collective-permute-done.1.refs_1_), channel_id=1, source_target_pairs={{0,4},{2,6},{4,0},{6,2},{8,12},{10,14},{12,8},{14,10},{1,5},{3,7},... | collective-permute-start | bytes 344072 | tf_op jit(solution)/shard_map/ppermute | solution.py:23
  19.9 1.0 %collective-permute-done.8.from_ref = bf16[32,1792]{1,0:T(8,128)(2,1)S(1)} collective-permute-done((bf16[32,1792]{1,0:T(8,128)(2,1)S(1)}, bf16[32,1792]{1,0:T(8,128)(2,1)S(1)}, u32[]{:S(2)}, u32[]{:S(2)}) %collective-permute-start.8) | collective-permute-done | bytes 114720 | tf_op jit(solution)/shard_map/ppermute | solution.py:23
  20.9 1.0 %collective-permute-start.9 = (bf16[32,1792]{1,0:T(8,128)(2,1)S(1)}, bf16[32,1792]{1,0:T(8,128)(2,1)S(1)}, u32[]{:S(2)}, u32[]{:S(2)}) collective-permute-start(bf16[32,1792]{1,0:T(8,128)(2,1)S(1)} %shard_map.66.refs_0_), channel_id=1, source_target_pairs={{0,2},{2,0},{4,6},{6,4},{8,10},{10,8},{12,14},{14,12},{1,3},{3,1},... | collective-permute-start | bytes 344072 | tf_op jit(solution)/shard_map/ppermute | solution.py:23
  21.9 1.5 %collective-permute-start.10 = (bf16[32,1792]{1,0:T(8,128)(2,1)S(1)}, bf16[32,1792]{1,0:T(8,128)(2,1)S(1)}, u32[]{:S(2)}, u32[]{:S(2)}) collective-permute-start(bf16[32,1792]{1,0:T(8,128)(2,1)S(1)} %collective-permute-done.5.refs_3_), channel_id=1, source_target_pairs={{0,4},{2,6},{4,0},{6,2},{8,12},{10,14},{12,8},{14,10},{1,5},{3,7},... | collective-permute-start | bytes 344072 | tf_op jit(solution)/shard_map/ppermute | solution.py:23
  23.4 1.3 %collective-permute-start.6 = (bf16[2,32,1792]{2,1,0:T(8,128)(2,1)S(1)}, bf16[2,32,1792]{2,1,0:T(8,128)(2,1)S(1)}, u32[]{:S(2)}, u32[]{:S(2)}) collective-permute-start(bf16[2,32,1792]{2,1,0:T(8,128)(2,1)S(1)} %collective-permute-done.2.refs_1_), channel_id=1, source_target_pairs={{0,4},{2,6},{4,0},{6,2},{8,12},{10,14},{12,8},{14,10},{1,5},{3,7},... | collective-permute-start | bytes 688136 | tf_op jit(solution)/shard_map/ppermute | solution.py:23
  25.0 1.1 %shard_map.67 = (f32[2,32,1792]{2,1,0:T(8,128)S(1)}, bf16[32,1792]{1,0:T(8,128)(2,1)S(1)}, f32[32,1792]{1,0:T(8,128)S(1)}) custom-call(bf16[32,1792]{1,0:T(8,128)(2,1)S(1)} %collective-permute-done.3.refs_0_, bf16[32,1792]{1,0:T(8,128)(2,1)S(1)} %collective-permute-done.1.refs_1_, bf16[32,1792]{1,0:T(8,128)(2,1)S(1)} %collective-permute-done.11.refs_2_, ...), custom_call_target="tpu_custom_call" | custom-call | flops 345000000 | tf_op jit(solution)/shard_map/pallas_call | solution.py:112
  26.2 1.7 %collective-permute-done.10.refs_3_ = bf16[32,1792]{1,0:T(8,128)(2,1)S(1)} collective-permute-done((bf16[32,1792]{1,0:T(8,128)(2,1)S(1)}, bf16[32,1792]{1,0:T(8,128)(2,1)S(1)}, u32[]{:S(2)}, u32[]{:S(2)}) %collective-permute-start.10) | collective-permute-done | bytes 114720 | tf_op jit(solution)/shard_map/ppermute | solution.py:23
  27.9 1.1 %shard_map.68 = (f32[2,32,1792]{2,1,0:T(8,128)S(1)}, bf16[32,1792]{1,0:T(8,128)(2,1)S(1)}, bf16[32,1792]{1,0:T(8,128)(2,1)S(1)}) custom-call(bf16[32,1792]{1,0:T(8,128)(2,1)S(1)} %shard_map.66.refs_0_, bf16[32,1792]{1,0:T(8,128)(2,1)S(1)} %collective-permute-done.12.refs_1_, bf16[32,1792]{1,0:T(8,128)(2,1)S(1)} %collective-permute-done.9.refs_2_, ...), custom_call_target="tpu_custom_call" | custom-call | flops 1150000000 | tf_op jit(solution)/shard_map/pallas_call | solution.py:112
  29.0 1.3 %collective-permute-start.13 = (bf16[32,1792]{1,0:T(8,128)(2,1)S(1)}, bf16[32,1792]{1,0:T(8,128)(2,1)S(1)}, u32[]{:S(2)}, u32[]{:S(2)}) collective-permute-start(bf16[32,1792]{1,0:T(8,128)(2,1)S(1)} %get-tuple-element.61), channel_id=1, source_target_pairs={{0,2},{2,0},{4,6},{6,4},{8,10},{10,8},{12,14},{14,12},{1,3},{3,1},... | collective-permute-start | bytes 344072 | tf_op jit(solution)/shard_map/ppermute | solution.py:23
  30.4 1.2 %collective-permute-start.16 = (bf16[32,1792]{1,0:T(8,128)(2,1)S(1)}, bf16[32,1792]{1,0:T(8,128)(2,1)S(1)}, u32[]{:S(2)}, u32[]{:S(2)}) collective-permute-start(bf16[32,1792]{1,0:T(8,128)(2,1)S(1)} %get-tuple-element.68), channel_id=1, source_target_pairs={{0,4},{2,6},{4,0},{6,2},{8,12},{10,14},{12,8},{14,10},{1,5},{3,7},... | collective-permute-start | bytes 344072 | tf_op jit(solution)/shard_map/ppermute | solution.py:23
  31.6 1.3 %collective-permute-start.15 = (bf16[32,1792]{1,0:T(8,128)(2,1)S(1)}, bf16[32,1792]{1,0:T(8,128)(2,1)S(1)}, u32[]{:S(2)}, u32[]{:S(2)}) collective-permute-start(bf16[32,1792]{1,0:T(8,128)(2,1)S(1)} %get-tuple-element.66), channel_id=1, source_target_pairs={{0,2},{2,0},{4,6},{6,4},{8,10},{10,8},{12,14},{14,12},{1,3},{3,1},... | collective-permute-start | bytes 344072 | tf_op jit(solution)/shard_map/ppermute | solution.py:23
  32.9 1.2 %shard_map.65 = (f32[2,32,1792]{2,1,0:T(8,128)S(1)}, bf16[2,32,1792]{2,1,0:T(8,128)(2,1)S(1)}, f32[2,32,1792]{2,1,0:T(8,128)S(1)}, bf16[2,32,1792]{2,1,0:T(8,128)(2,1)S(1)}) custom-call(bf16[2,32,1792]{2,1,0:T(8,128)(2,1)S(1)} %pad_maximum_fusion.refs_0_, bf16[2,32,1792]{2,1,0:T(8,128)(2,1)S(1)} %collective-permute-done.2.refs_1_, ...), custom_call_target="tpu_custom_call" | custom-call | flops 1150000000 | tf_op jit(solution)/shard_map/pallas_call | solution.py:112
  34.2 1.4 %collective-permute-start.14 = (bf16[2,32,1792]{2,1,0:T(8,128)(2,1)S(1)}, bf16[2,32,1792]{2,1,0:T(8,128)(2,1)S(1)}, u32[]{:S(2)}, u32[]{:S(2)}) collective-permute-start(bf16[2,32,1792]{2,1,0:T(8,128)(2,1)S(1)} %pad_maximum_fusion.1), channel_id=1, source_target_pairs={{0,4},{2,6},{4,0},{6,2},{8,12},{10,14},{12,8},{14,10},{1,5},{3,7},... | collective-permute-start | bytes 688136 | tf_op jit(solution)/shard_map/ppermute | solution.py:23
  36.4 0.9 %collective-permute-start.17 = (bf16[32,1792]{1,0:T(8,128)(2,1)S(1)}, bf16[32,1792]{1,0:T(8,128)(2,1)S(1)}, u32[]{:S(2)}, u32[]{:S(2)}) collective-permute-start(bf16[32,1792]{1,0:T(8,128)(2,1)S(1)} %shard_map.70), channel_id=1, source_target_pairs={{0,2},{2,0},{4,6},{6,4},{8,10},{10,8},{12,14},{14,12},{1,3},{3,1},... | collective-permute-start | bytes 344072 | tf_op jit(solution)/shard_map/ppermute | solution.py:23
  37.3 1.1 %collective-permute-start.19 = (bf16[2,32,1792]{2,1,0:T(8,128)(2,1)S(1)}, bf16[2,32,1792]{2,1,0:T(8,128)(2,1)S(1)}, u32[]{:S(2)}, u32[]{:S(2)}) collective-permute-start(bf16[2,32,1792]{2,1,0:T(8,128)(2,1)S(1)} %get-tuple-element.73), channel_id=1, source_target_pairs={{0,2},{2,0},{4,6},{6,4},{8,10},{10,8},{12,14},{14,12},{1,3},{3,1},... | collective-permute-start | bytes 688136 | tf_op jit(solution)/shard_map/ppermute | solution.py:23
  38.5 2.7 %collective-permute-done.17 = bf16[32,1792]{1,0:T(8,128)(2,1)S(1)} collective-permute-done((bf16[32,1792]{1,0:T(8,128)(2,1)S(1)}, bf16[32,1792]{1,0:T(8,128)(2,1)S(1)}, u32[]{:S(2)}, u32[]{:S(2)}) %collective-permute-start.17) | collective-permute-done | bytes 114720 | tf_op jit(solution)/shard_map/ppermute | solution.py:23
  41.3 2.9 %collective-permute-start.21 = (bf16[2,32,1792]{2,1,0:T(8,128)(2,1)S(1)}, bf16[2,32,1792]{2,1,0:T(8,128)(2,1)S(1)}, u32[]{:S(2)}, u32[]{:S(2)}) collective-permute-start(bf16[2,32,1792]{2,1,0:T(8,128)(2,1)S(1)} %add_convert_fusion), channel_id=1, source_target_pairs={{0,8},{2,10},{4,12},{6,14},{8,0},{10,2},{12,4},{14,6},{1,9},{3,11}... | collective-permute-start | bytes 688136 | tf_op jit(solution)/shard_map/ppermute | solution.py:23
  44.3 1.5 %collective-permute-start.20 = (bf16[2,32,1792]{2,1,0:T(8,128)(2,1)S(1)}, bf16[2,32,1792]{2,1,0:T(8,128)(2,1)S(1)}, u32[]{:S(2)}, u32[]{:S(2)}) collective-permute-start(bf16[2,32,1792]{2,1,0:T(8,128)(2,1)S(1)} %shard_map.71), channel_id=1, source_target_pairs={{0,4},{2,6},{4,0},{6,2},{8,12},{10,14},{12,8},{14,10},{1,5},{3,7},... | collective-permute-start | bytes 688136 | tf_op jit(solution)/shard_map/ppermute | solution.py:23
  45.8 1.2 %collective-permute-start.18 = (bf16[2,32,1792]{2,1,0:T(8,128)(2,1)S(1)}, bf16[2,32,1792]{2,1,0:T(8,128)(2,1)S(1)}, u32[]{:S(2)}, u32[]{:S(2)}) collective-permute-start(bf16[2,32,1792]{2,1,0:T(8,128)(2,1)S(1)} %get-tuple-element.70), channel_id=1, source_target_pairs={{0,2},{2,0},{4,6},{6,4},{8,10},{10,8},{12,14},{14,12},{1,3},{3,1},... | collective-permute-start | bytes 688136 | tf_op jit(solution)/shard_map/ppermute | solution.py:23
  47.0 4.3 %collective-permute-done.21.from_ref = bf16[2,32,1792]{2,1,0:T(8,128)(2,1)S(1)} collective-permute-done((bf16[2,32,1792]{2,1,0:T(8,128)(2,1)S(1)}, bf16[2,32,1792]{2,1,0:T(8,128)(2,1)S(1)}, u32[]{:S(2)}, u32[]{:S(2)}) %collective-permute-start.21) | collective-permute-done | bytes 229408 | tf_op jit(solution)/shard_map/ppermute | solution.py:23
  52.1 1.3 %collective-permute-done.22 = bf16[32,1792]{1,0:T(8,128)(2,1)S(1)} collective-permute-done((bf16[32,1792]{1,0:T(8,128)(2,1)S(1)}, bf16[32,1792]{1,0:T(8,128)(2,1)S(1)}, u32[]{:S(2)}, u32[]{:S(2)}) %collective-permute-start.22) | collective-permute-done | bytes 114720 | tf_op jit(solution)/shard_map/ppermute | solution.py:32
  (45 shorter events, 4.5 us)
Async XLA Ops:
  1.0 4.2 %collective-permute-start = (bf16[32,1792]{1,0:T(8,128)(2,1)S(1)}, bf16[32,1792]{1,0:T(8,128)(2,1)S(1)}, u32[]{:S(2)}, u32[]{:S(2)}) collective-permute-start(bf16[32,1792]{1,0:T(8,128)(2,1)S(1)} %get-tuple-element.42), channel_id=1, source_target_pairs={{0,1},{1,0},{2,3},{3,2},{4,5},{5,4},{6,7},{7,6},{8,9},{9,8},{10,11... | collective-permute-start | bytes 344072 | tf_op jit(solution)/shard_map/ppermute | solution.py:32
  1.5 12.4 %collective-permute-start.3 = (bf16[32,1792]{1,0:T(8,128)(2,1)S(1)}, bf16[32,1792]{1,0:T(8,128)(2,1)S(1)}, u32[]{:S(2)}, u32[]{:S(2)}) collective-permute-start(bf16[32,1792]{1,0:T(8,128)(2,1)S(1)} %get-tuple-element.41), channel_id=1, source_target_pairs={{0,8},{2,10},{4,12},{6,14},{8,0},{10,2},{12,4},{14,6},{1,9},{3,11}... | collective-permute-start | bytes 344072 | tf_op jit(solution)/shard_map/ppermute | solution.py:23
  5.2 11.6 %collective-permute-start.2 = (bf16[2,32,1792]{2,1,0:T(8,128)(2,1)S(1)}, bf16[2,32,1792]{2,1,0:T(8,128)(2,1)S(1)}, u32[]{:S(2)}, u32[]{:S(2)}) collective-permute-start(bf16[2,32,1792]{2,1,0:T(8,128)(2,1)S(1)} %pad_maximum_fusion.refs_0_), channel_id=1, source_target_pairs={{0,2},{2,0},{4,6},{6,4},{8,10},{10,8},{12,14},{14,12},{1,3},{3,1},... | collective-permute-start | bytes 688136 | tf_op jit(solution)/shard_map/ppermute | solution.py:23
  6.7 13.2 %collective-permute-start.4 = (bf16[2,32,1792]{2,1,0:T(8,128)(2,1)S(1)}, bf16[2,32,1792]{2,1,0:T(8,128)(2,1)S(1)}, u32[]{:S(2)}, u32[]{:S(2)}) collective-permute-start(bf16[2,32,1792]{2,1,0:T(8,128)(2,1)S(1)} %pad_maximum_fusion.refs_0_), channel_id=1, source_target_pairs={{0,4},{2,6},{4,0},{6,2},{8,12},{10,14},{12,8},{14,10},{1,5},{3,7},... | collective-permute-start | bytes 688136 | tf_op jit(solution)/shard_map/ppermute | solution.py:23
  8.3 8.5 %collective-permute-start.1 = (bf16[32,1792]{1,0:T(8,128)(2,1)S(1)}, bf16[32,1792]{1,0:T(8,128)(2,1)S(1)}, u32[]{:S(2)}, u32[]{:S(2)}) collective-permute-start(bf16[32,1792]{1,0:T(8,128)(2,1)S(1)} %collective-permute-done), channel_id=1, source_target_pairs={{0,8},{2,10},{4,12},{6,14},{8,0},{10,2},{12,4},{14,6},{1,9},{3,11}... | collective-permute-start | bytes 344072 | tf_op jit(solution)/shard_map/ppermute | solution.py:23
  9.6 1.2 %copy-start = (bf16[1,3584,128]{2,1,0:T(8,128)(2,1)S(1)}, bf16[1,3584,128]{2,1,0:T(8,128)(2,1)}, u32[]{:S(2)}) copy-start(bf16[1,3584,128]{2,1,0:T(8,128)(2,1)} %param.9) | copy-start | bytes 2752516
  10.7 1.2 %copy-start.1 = (bf16[1,3584,128]{2,1,0:T(8,128)(2,1)S(1)}, bf16[1,3584,128]{2,1,0:T(8,128)(2,1)}, u32[]{:S(2)}) copy-start(bf16[1,3584,128]{2,1,0:T(8,128)(2,1)} %param.10) | copy-start | bytes 2752516
  11.9 1.2 %copy-start.2 = (bf16[1,128,3584]{2,1,0:T(8,128)(2,1)S(1)}, bf16[1,128,3584]{2,1,0:T(8,128)(2,1)}, u32[]{:S(2)}) copy-start(bf16[1,128,3584]{2,1,0:T(8,128)(2,1)} %param.11) | copy-start | bytes 2752516
  13.9 7.0 %collective-permute-start.8 = (bf16[32,1792]{1,0:T(8,128)(2,1)S(1)}, bf16[32,1792]{1,0:T(8,128)(2,1)S(1)}, u32[]{:S(2)}, u32[]{:S(2)}) collective-permute-start(bf16[32,1792]{1,0:T(8,128)(2,1)S(1)} %collective-permute-done.3.refs_0_), channel_id=1, source_target_pairs={{0,4},{2,6},{4,0},{6,2},{8,12},{10,14},{12,8},{14,10},{1,5},{3,7},... | collective-permute-start | bytes 344072 | tf_op jit(solution)/shard_map/ppermute | solution.py:23
  14.4 9.0 %collective-permute-start.11 = (bf16[32,1792]{1,0:T(8,128)(2,1)S(1)}, bf16[32,1792]{1,0:T(8,128)(2,1)S(1)}, u32[]{:S(2)}, u32[]{:S(2)}) collective-permute-start(bf16[32,1792]{1,0:T(8,128)(2,1)S(1)} %collective-permute-done.3.refs_0_), channel_id=1, source_target_pairs={{0,2},{2,0},{4,6},{6,4},{8,10},{10,8},{12,14},{14,12},{1,3},{3,1},... | collective-permute-start | bytes 344072 | tf_op jit(solution)/shard_map/ppermute | solution.py:23
  16.8 5.1 %collective-permute-start.5 = (bf16[32,1792]{1,0:T(8,128)(2,1)S(1)}, bf16[32,1792]{1,0:T(8,128)(2,1)S(1)}, u32[]{:S(2)}, u32[]{:S(2)}) collective-permute-start(bf16[32,1792]{1,0:T(8,128)(2,1)S(1)} %collective-permute-done.1.refs_1_), channel_id=1, source_target_pairs={{0,2},{2,0},{4,6},{6,4},{8,10},{10,8},{12,14},{14,12},{1,3},{3,1},... | collective-permute-start | bytes 344072 | tf_op jit(solution)/shard_map/ppermute | solution.py:23
  17.5 5.9 %collective-permute-start.12 = (bf16[32,1792]{1,0:T(8,128)(2,1)S(1)}, bf16[32,1792]{1,0:T(8,128)(2,1)S(1)}, u32[]{:S(2)}, u32[]{:S(2)}) collective-permute-start(bf16[32,1792]{1,0:T(8,128)(2,1)S(1)} %collective-permute-done.1.refs_1_), channel_id=1, source_target_pairs={{0,4},{2,6},{4,0},{6,2},{8,12},{10,14},{12,8},{14,10},{1,5},{3,7},... | collective-permute-start | bytes 344072 | tf_op jit(solution)/shard_map/ppermute | solution.py:23
  19.9 5.1 %collective-permute-start.7 = (bf16[3584,384]{1,0:T(8,128)(2,1)S(1)}, bf16[3584,384]{1,0:T(8,128)(2,1)S(1)}, u32[]{:S(2)}, u32[]{:S(2)}) collective-permute-start(bf16[3584,384]{1,0:T(8,128)(2,1)S(1)} %shard_map.64.refs_4_), channel_id=1, source_target_pairs={{0,1},{1,0},{2,3},{3,2},{4,5},{5,4},{6,7},{7,6},{8,9},{9,8},{10,11... | collective-permute-start | bytes 8257544 | tf_op jit(solution)/shard_map/ppermute | solution.py:32
  20.9 5.2 %collective-permute-start.9 = (bf16[32,1792]{1,0:T(8,128)(2,1)S(1)}, bf16[32,1792]{1,0:T(8,128)(2,1)S(1)}, u32[]{:S(2)}, u32[]{:S(2)}) collective-permute-start(bf16[32,1792]{1,0:T(8,128)(2,1)S(1)} %shard_map.66.refs_0_), channel_id=1, source_target_pairs={{0,2},{2,0},{4,6},{6,4},{8,10},{10,8},{12,14},{14,12},{1,3},{3,1},... | collective-permute-start | bytes 344072 | tf_op jit(solution)/shard_map/ppermute | solution.py:23
  21.9 6.0 %collective-permute-start.10 = (bf16[32,1792]{1,0:T(8,128)(2,1)S(1)}, bf16[32,1792]{1,0:T(8,128)(2,1)S(1)}, u32[]{:S(2)}, u32[]{:S(2)}) collective-permute-start(bf16[32,1792]{1,0:T(8,128)(2,1)S(1)} %collective-permute-done.5.refs_3_), channel_id=1, source_target_pairs={{0,4},{2,6},{4,0},{6,2},{8,12},{10,14},{12,8},{14,10},{1,5},{3,7},... | collective-permute-start | bytes 344072 | tf_op jit(solution)/shard_map/ppermute | solution.py:23
  23.4 9.5 %collective-permute-start.6 = (bf16[2,32,1792]{2,1,0:T(8,128)(2,1)S(1)}, bf16[2,32,1792]{2,1,0:T(8,128)(2,1)S(1)}, u32[]{:S(2)}, u32[]{:S(2)}) collective-permute-start(bf16[2,32,1792]{2,1,0:T(8,128)(2,1)S(1)} %collective-permute-done.2.refs_1_), channel_id=1, source_target_pairs={{0,4},{2,6},{4,0},{6,2},{8,12},{10,14},{12,8},{14,10},{1,5},{3,7},... | collective-permute-start | bytes 688136 | tf_op jit(solution)/shard_map/ppermute | solution.py:23
  27.9 2.4 %copy-start.3 = (s32[64,1]{0,1:T(1,128)S(1)}, s32[64,1]{0,1:T(1,128)}, u32[]{:S(2)}) copy-start(s32[64,1]{0,1:T(1,128)} %param.8) | copy-start | bytes 772
  29.0 5.1 %collective-permute-start.13 = (bf16[32,1792]{1,0:T(8,128)(2,1)S(1)}, bf16[32,1792]{1,0:T(8,128)(2,1)S(1)}, u32[]{:S(2)}, u32[]{:S(2)}) collective-permute-start(bf16[32,1792]{1,0:T(8,128)(2,1)S(1)} %get-tuple-element.61), channel_id=1, source_target_pairs={{0,2},{2,0},{4,6},{6,4},{8,10},{10,8},{12,14},{14,12},{1,3},{3,1},... | collective-permute-start | bytes 344072 | tf_op jit(solution)/shard_map/ppermute | solution.py:23
  30.4 6.0 %collective-permute-start.16 = (bf16[32,1792]{1,0:T(8,128)(2,1)S(1)}, bf16[32,1792]{1,0:T(8,128)(2,1)S(1)}, u32[]{:S(2)}, u32[]{:S(2)}) collective-permute-start(bf16[32,1792]{1,0:T(8,128)(2,1)S(1)} %get-tuple-element.68), channel_id=1, source_target_pairs={{0,4},{2,6},{4,0},{6,2},{8,12},{10,14},{12,8},{14,10},{1,5},{3,7},... | collective-permute-start | bytes 344072 | tf_op jit(solution)/shard_map/ppermute | solution.py:23
  31.6 6.9 %collective-permute-start.15 = (bf16[32,1792]{1,0:T(8,128)(2,1)S(1)}, bf16[32,1792]{1,0:T(8,128)(2,1)S(1)}, u32[]{:S(2)}, u32[]{:S(2)}) collective-permute-start(bf16[32,1792]{1,0:T(8,128)(2,1)S(1)} %get-tuple-element.66), channel_id=1, source_target_pairs={{0,2},{2,0},{4,6},{6,4},{8,10},{10,8},{12,14},{14,12},{1,3},{3,1},... | collective-permute-start | bytes 344072 | tf_op jit(solution)/shard_map/ppermute | solution.py:23
  34.2 7.0 %collective-permute-start.14 = (bf16[2,32,1792]{2,1,0:T(8,128)(2,1)S(1)}, bf16[2,32,1792]{2,1,0:T(8,128)(2,1)S(1)}, u32[]{:S(2)}, u32[]{:S(2)}) collective-permute-start(bf16[2,32,1792]{2,1,0:T(8,128)(2,1)S(1)} %pad_maximum_fusion.1), channel_id=1, source_target_pairs={{0,4},{2,6},{4,0},{6,2},{8,12},{10,14},{12,8},{14,10},{1,5},{3,7},... | collective-permute-start | bytes 688136 | tf_op jit(solution)/shard_map/ppermute | solution.py:23
  36.4 10.6 %copy-start.4 = (s32[64,1]{0,1:T(1,128)S(1)}, s32[64,1]{0,1:T(1,128)}, u32[]{:S(2)}) copy-start(s32[64,1]{0,1:T(1,128)} %param.7) | copy-start | bytes 772
  36.4 4.9 %collective-permute-start.17 = (bf16[32,1792]{1,0:T(8,128)(2,1)S(1)}, bf16[32,1792]{1,0:T(8,128)(2,1)S(1)}, u32[]{:S(2)}, u32[]{:S(2)}) collective-permute-start(bf16[32,1792]{1,0:T(8,128)(2,1)S(1)} %shard_map.70), channel_id=1, source_target_pairs={{0,2},{2,0},{4,6},{6,4},{8,10},{10,8},{12,14},{14,12},{1,3},{3,1},... | collective-permute-start | bytes 344072 | tf_op jit(solution)/shard_map/ppermute | solution.py:23
  37.3 6.9 %collective-permute-start.19 = (bf16[2,32,1792]{2,1,0:T(8,128)(2,1)S(1)}, bf16[2,32,1792]{2,1,0:T(8,128)(2,1)S(1)}, u32[]{:S(2)}, u32[]{:S(2)}) collective-permute-start(bf16[2,32,1792]{2,1,0:T(8,128)(2,1)S(1)} %get-tuple-element.73), channel_id=1, source_target_pairs={{0,2},{2,0},{4,6},{6,4},{8,10},{10,8},{12,14},{14,12},{1,3},{3,1},... | collective-permute-start | bytes 688136 | tf_op jit(solution)/shard_map/ppermute | solution.py:23
  41.3 10.0 %collective-permute-start.21 = (bf16[2,32,1792]{2,1,0:T(8,128)(2,1)S(1)}, bf16[2,32,1792]{2,1,0:T(8,128)(2,1)S(1)}, u32[]{:S(2)}, u32[]{:S(2)}) collective-permute-start(bf16[2,32,1792]{2,1,0:T(8,128)(2,1)S(1)} %add_convert_fusion), channel_id=1, source_target_pairs={{0,8},{2,10},{4,12},{6,14},{8,0},{10,2},{12,4},{14,6},{1,9},{3,11}... | collective-permute-start | bytes 688136 | tf_op jit(solution)/shard_map/ppermute | solution.py:23
  44.3 7.6 %collective-permute-start.20 = (bf16[2,32,1792]{2,1,0:T(8,128)(2,1)S(1)}, bf16[2,32,1792]{2,1,0:T(8,128)(2,1)S(1)}, u32[]{:S(2)}, u32[]{:S(2)}) collective-permute-start(bf16[2,32,1792]{2,1,0:T(8,128)(2,1)S(1)} %shard_map.71), channel_id=1, source_target_pairs={{0,4},{2,6},{4,0},{6,2},{8,12},{10,14},{12,8},{14,10},{1,5},{3,7},... | collective-permute-start | bytes 688136 | tf_op jit(solution)/shard_map/ppermute | solution.py:23
  45.8 6.1 %collective-permute-start.18 = (bf16[2,32,1792]{2,1,0:T(8,128)(2,1)S(1)}, bf16[2,32,1792]{2,1,0:T(8,128)(2,1)S(1)}, u32[]{:S(2)}, u32[]{:S(2)}) collective-permute-start(bf16[2,32,1792]{2,1,0:T(8,128)(2,1)S(1)} %get-tuple-element.70), channel_id=1, source_target_pairs={{0,2},{2,0},{4,6},{6,4},{8,10},{10,8},{12,14},{14,12},{1,3},{3,1},... | collective-permute-start | bytes 688136 | tf_op jit(solution)/shard_map/ppermute | solution.py:23
  52.0 1.4 %collective-permute-start.22 = (bf16[32,1792]{1,0:T(8,128)(2,1)S(1)}, bf16[32,1792]{1,0:T(8,128)(2,1)S(1)}, u32[]{:S(2)}, u32[]{:S(2)}) collective-permute-start(bf16[32,1792]{1,0:T(8,128)(2,1)S(1)} %slice_bitcast_fusion), channel_id=1, source_target_pairs={{0,1},{1,0},{2,3},{3,2},{4,5},{5,4},{6,7},{7,6},{8,9},{9,8},{10,11... | collective-permute-start | bytes 344072 | tf_op jit(solution)/shard_map/ppermute | solution.py:32
